TPU v7x, 256 devices: a whole 4x4x8 slice. The times are simulated.
256 devices in a mesh: section: 8 (over x, z_lo), dp: 32 (over z_hi, y, core).
Axes of the slice: x: 4, y: 4, z: 8 (z_hi: 4, z_lo: 2; z = z_hi * 2 + z_lo), core: 2. Of those that a mesh axis runs over, the one named last changes fastest.
Arguments:
- entries: bfloat16 [2, 3, 1024, 3072], P(None, None, 'dp'), may hold values from -6 to 6
- cotangents: bfloat16 [2, 3, 1024, 3072], P(None, None, 'dp'), may hold values from -6 to 6
- scales: bfloat16 [8, 2, 3072], P('section', None, 'dp'), may hold values from 0.5 to 1.5
- key_weight: bfloat16 [8, 3072, 256], P('section', 'dp'), may hold values from -0.109375 to 0.109375
- rate_weight: bfloat16 [8, 3072, 24], P('section', 'dp'), may hold values from -0.109375 to 0.109375
- rate_bias: bfloat16 [8, 24], P('section'), may hold values from -7 to -3
Outputs:
- grad_scales: float32 [8, 2, 3072], P('section', None, 'dp')
- grad_keys: float32 [8, 3072, 256], P('section', 'dp')
- grad_rates: float32 [8, 3072, 24], P('section', 'dp')
- grad_bias: float32 [8, 24], P('section')
All inputs are finite; a program needn't handle non-finite values.
Results may differ from a plain program's by a relative error of at most 0.025.
Values may be sent and summed in bfloat16 or wider, within the bound.
No kernel may reach another device: no remote copies, remote signals or barrier semaphores. Data moves between devices by JAX's collectives and lax.ppermute only.
A program may use at most 128 MiB of HBM per device.

v0:
```python
import functools

import jax
import jax.numpy as jnp
from jax import lax
from jax.experimental import pallas as pl
from jax.experimental.pallas import tpu as pltpu
from jax.sharding import Mesh, PartitionSpec as P

F32 = jnp.float32
BF16 = jnp.bfloat16
SECTION = ("x", "zl")
DP = ("zh", "y", "c")

T = 32
D = 3072
C = 128
H = 24
GROUPS = H // 4
W = H * T
LAYERS = 8
SEQS = 6
ROWS = 96
PIECE = 112
TOK = LAYERS * T
BLOCK = 384
BLOCKS = D // BLOCK
SENT = BLOCKS * T + T + 16


def iota(shape, axis):
    return lax.broadcasted_iota(jnp.int32, shape, axis)


def nt(a, b):
    return lax.dot_general(
        a, b, (((1,), (1,)), ((), ())), preferred_element_type=F32
    )


def tn(a, b):
    return lax.dot_general(
        a, b, (((0,), (0,)), ((), ())), preferred_element_type=F32
    )


def nn(a, b):
    return jnp.dot(a, b, preferred_element_type=F32)


def split3(a):
    hi = a.astype(BF16)
    rest = a - hi.astype(F32)
    mid = rest.astype(BF16)
    low = (rest - mid.astype(F32)).astype(BF16)
    return jnp.concatenate([hi, mid, low, jnp.zeros_like(hi)], axis=1)


def masks():
    row = iota((T, W), 0)
    col = iota((T, W), 1) % T
    spread = (iota((C, W), 0) % T == iota((C, W), 1) // T) & (iota((C, W), 0) < 3 * T)
    spread = jnp.where(spread, 1.0, 0.0).astype(BF16)
    block = iota((C, C), 0) // T == iota((C, C), 1) // T
    tri = jnp.where(iota((T, T), 0) >= iota((T, T), 1), 1.0, 0.0).astype(BF16)
    return row >= col, row == col, spread, block, tri


def tile4(a):
    return jnp.concatenate([a] * 4, axis=0)


def stack_heads(a, g):
    return jnp.concatenate([a[:, C * (4 * g + j) : C * (4 * g + j + 1)] for j in range(4)], axis=0)


def unstack_heads(parts):
    return jnp.concatenate([p[T * j : T * (j + 1)] for p in parts for j in range(4)], axis=1)


def block_diag(mixing, g, block):
    return jnp.where(block, tile4(mixing[:, C * g : C * (g + 1)]), 0.0).astype(BF16)


def assemble_rows(piece):
    out = []
    lane = iota((T, C), 1)
    for m in range(8):
        p = []
        for i in range(4):
            z = piece(4 * m + i).astype(F32)
            p.append(jnp.concatenate([z[:, :C], z[:, C:]], axis=0))
        p1 = pltpu.roll(p[1], 96, 1)
        p2 = pltpu.roll(p[2], 64, 1)
        p3 = pltpu.roll(p[3], 32, 1)
        out.append(jnp.where(lane < 96, p[0], p1))
        out.append(jnp.where(lane < 64, p1, p2))
        out.append(jnp.where(lane < 32, p2, p3))
    return jnp.concatenate(out, axis=1)


def cut_rows(rows):
    lane = iota((T, C), 1)
    a, b, c = rows[:, :C], rows[:, C : 2 * C], rows[:, 2 * C :]
    one = jnp.where(lane < 32, pltpu.roll(a, 32, 1), pltpu.roll(b, 32, 1))
    two = jnp.where(lane < 64, pltpu.roll(b, 64, 1), pltpu.roll(c, 64, 1))
    parts = [a, one, two, pltpu.roll(c, 96, 1)]
    return [jnp.concatenate([p[:16], p[16:]], axis=1) for p in parts]


def gray(i):
    return jnp.where(i >= 2, 5 - i, i)


def partner(i, c, first):
    return jnp.where((c == 0) == first, i ^ 1, 3 - i)


def sequence_kernel(pos_ref, *refs):
    left, right = refs[:8], refs[8:16]
    entry_ref, cot_ref, sent_ref = refs[16:19]
    w_scr, rows_scr, xs, ns, mixed_scr, decay_scr, write_scr, small_scr, proj_scr, sem_a, sem_b = refs[19:]
    x, y, c, valid = pos_ref[0], pos_ref[1], pos_ref[2], pos_ref[3]

    def ring(i, core):
        one, two = partner(i, core, True), partner(i, core, False)
        return [i, one, two, partner(two, core, True)]

    copies = []
    for kc in range(2):
        cc = (c + kc) % 2
        ys, xx = ring(y, cc), ring(x, cc)
        for i in range(4):
            for j in range(4):
                at = pl.ds(2 * xx[j], 2)
                copy = pltpu.make_async_copy(
                    left[kc * 4 + i].at[j],
                    w_scr.at[at, :, ys[i], cc, :, :C],
                    sem_a.at[xx[j]],
                )
                copy.start()
                at = pl.ds(2 * xx[i], 2)
                copy = pltpu.make_async_copy(
                    right[kc * 4 + i].at[j],
                    w_scr.at[at, :, ys[j], cc, :, C:],
                    sem_b.at[xx[i]],
                )
                copy.start()

    def wait_layers(at):
        for sem, src in ((sem_a, left[0]), (sem_b, right[0])):
            for _ in range(8):
                pltpu.make_async_copy(
                    src.at[0], w_scr.at[0:2, :, 0, 0, :, :C], sem.at[at]
                ).wait()

    causal, diag, spread, block, tri = masks()

    def keys_of(layer, m):
        parts = [w_scr[layer, m // 2, (m % 2) * 2 + i // 2, i % 2, :ROWS] for i in range(4)]
        return jnp.concatenate(parts, axis=0)

    def forward(layer, stream):
        @pl.when(layer % 2 == 0)
        def _():
            wait_layers(layer // 2)

        rows = assemble_rows(lambda d: w_scr[layer, d // 8, d // 2 % 4, d % 2, ROWS:])
        rows_low = rows.astype(BF16)
        rows_scr[layer] = rows_low
        gain, scale, bias = rows[24:25], rows[25:26], rows[26:27, :T]
        xs[layer] = stream
        x_f = stream.astype(F32)
        inv_rms = lax.rsqrt(jnp.sum(x_f * x_f, axis=1, keepdims=True) * (1.0 / D) + 1e-05)
        normed = (x_f * inv_rms * gain).astype(BF16)
        ns[layer] = normed
        for m in range(BLOCKS):
            sent_ref[layer, T * m : T * (m + 1)] = normed[:, BLOCK * m : BLOCK * (m + 1)]
        logits = nt(normed, rows_low) + bias
        key_query = sum(
            nn(normed[:, BLOCK * m : BLOCK * (m + 1)], keys_of(layer, m)) for m in range(BLOCKS)
        )
        head = iota((T, T), 1) < H
        rate = jnp.maximum(logits, 0.0) + jnp.log1p(jnp.exp(-jnp.abs(logits)))
        rate = jnp.where(head, rate, 0.0)
        keep = 1.0 / (1.0 + rate)
        write = rate * keep
        total = nn(tri, split3(-jnp.log1p(rate)))
        total = total[:, :T] + total[:, T : 2 * T] + total[:, 2 * T : 3 * T]
        wide = nn(jnp.concatenate([split3(total), split3(write)], axis=0), spread)
        total_t, write_t = wide[:T], wide[T:]
        total_s = jnp.sum(jnp.where(diag, total_t, 0.0), axis=0, keepdims=True)
        write_s = jnp.sum(jnp.where(diag, write_t, 0.0), axis=0, keepdims=True)
        decay = jnp.where(causal, jnp.exp(jnp.where(causal, total_t - total_s, 0.0)), 0.0)
        k = key_query[:, :C]
        q = key_query[:, C:]
        inv = lax.rsqrt(jnp.sum(k * k, axis=1, keepdims=True) + 1e-06)
        scores = nt(q.astype(BF16), tile4((k * inv).astype(BF16)))
        decay_scr[layer] = decay
        write_scr[layer] = write_s
        proj_scr[layer] = key_query
        small_scr[layer] = jnp.concatenate([scores, logits, keep, jnp.zeros((T, 64), F32)], axis=1)
        mixing = decay * write_s * jnp.concatenate([scores] * GROUPS, axis=1)
        mixed = unstack_heads(
            [nn(block_diag(mixing, g, block), stack_heads(normed, g)) for g in range(GROUPS)]
        )
        mixed_scr[layer] = mixed.astype(BF16)
        return (x_f + scale * mixed).astype(BF16)

    lax.fori_loop(0, LAYERS, forward, entry_ref[...])

    def backward(step, back):
        layer = LAYERS - 1 - step
        x_f = xs[layer].astype(F32)
        normed = ns[layer]
        rows_low = rows_scr[layer]
        rows = rows_low[16:].astype(F32)
        gain, scale = rows[8:9], rows[9:10]
        dy = back.astype(F32)
        decay = decay_scr[layer]
        write_s = write_scr[layer]
        small = small_scr[layer]
        scores, logits, keep = small[:, :C], small[:, C : C + T], small[:, C + T : C + 2 * T]
        scores6 = jnp.concatenate([scores] * GROUPS, axis=1)
        mixing = decay * write_s * scores6
        d_scale = jnp.sum(dy * mixed_scr[layer].astype(F32), axis=0, keepdims=True)
        d_out = (dy * scale).astype(BF16)
        d_mix = []
        d_values = []
        for g in range(GROUPS):
            grad = stack_heads(d_out, g)
            full = jnp.where(block, nt(grad, stack_heads(normed, g)), 0.0)
            d_mix.append(full[:T] + full[T : 2 * T] + full[2 * T : 3 * T] + full[3 * T :])
            d_values.append(tn(block_diag(mixing, g, block), grad))
        d_mix = jnp.concatenate(d_mix, axis=1)
        d_values = unstack_heads(d_values)
        near = d_mix * decay
        scored = near * scores6
        d_write_s = jnp.sum(scored, axis=0, keepdims=True)
        weighted = near * write_s
        d_scores = sum(weighted[:, C * g : C * (g + 1)] for g in range(GROUPS)).astype(BF16)
        d_total = scored * write_s - jnp.where(diag, d_write_s * write_s, 0.0)
        gathered = []
        for part in (d_total, jnp.where(diag, d_write_s, 0.0)):
            hi = part.astype(BF16)
            gathered += [hi, (part - hi.astype(F32)).astype(BF16)]
        summed = nt(jnp.concatenate(gathered, axis=0), spread[:T])
        d_total = summed[:T] + summed[T : 2 * T]
        d_write = summed[2 * T : 3 * T] + summed[3 * T :]
        d_log = tn(tri, split3(d_total))
        d_log = d_log[:, :T] + d_log[:, T : 2 * T] + d_log[:, 2 * T : 3 * T]
        d_rate = keep * (d_write * keep - d_log)
        d_logits = d_rate / (1.0 + jnp.exp(-logits))
        d_low = jnp.where(iota((T, T), 1) < H, d_logits, 0.0).astype(BF16)
        k = proj_scr[layer][:, :C]
        q = proj_scr[layer][:, C:]
        inv = lax.rsqrt(jnp.sum(k * k, axis=1, keepdims=True) + 1e-06)
        d_q = nn(d_scores, tile4((k * inv).astype(BF16)))
        d_unit = tn(d_scores, q.astype(BF16))
        d_unit = d_unit[:T] + d_unit[T : 2 * T] + d_unit[2 * T : 3 * T] + d_unit[3 * T :]
        d_k = inv * d_unit - k * (inv * inv * inv * jnp.sum(d_unit * k, axis=1, keepdims=True))
        d_keyq = jnp.concatenate([d_k, d_q], axis=1).astype(BF16)
        through = jnp.concatenate([nt(d_keyq, keys_of(layer, m)) for m in range(BLOCKS)], axis=1)
        d_normed = d_values + through + nn(d_low, rows_low)
        inv_rms = lax.rsqrt(jnp.sum(x_f * x_f, axis=1, keepdims=True) * (1.0 / D) + 1e-05)
        x_hat = x_f * inv_rms
        d_gain = jnp.sum(d_normed * x_hat, axis=0, keepdims=True)
        d_hat = d_normed * gain
        mean = jnp.sum(d_hat * x_hat, axis=1, keepdims=True) * (1.0 / D)
        sent_ref[layer, TOK : TOK + T, :256] = d_keyq
        sent_ref[layer, TOK : TOK + T, 256:] = jnp.concatenate(
            [d_low, jnp.zeros((T, 96), BF16)], axis=1
        )
        sent_ref[layer, TOK + T :] = jnp.concatenate(
            [d[:, BLOCK * i : BLOCK * (i + 1)] for d in (d_gain, d_scale) for i in range(8)], axis=0
        ).astype(BF16)
        return (dy + inv_rms * (d_hat - x_hat * mean)).astype(BF16)

    cot = jnp.where(valid > 0, cot_ref[...].astype(F32), 0.0).astype(BF16)
    lax.fori_loop(0, LAYERS, backward, cot)


def weight_kernel(pos_ref, got_ref, keep_ref, send_ref, scr, sem):
    zh, y, c = pos_ref[0], pos_ref[1], pos_ref[2]

    def slot(there, here, core):
        bits = gray(jnp.int32(there)) ^ gray(here)
        return bits if core else (bits & 1) * 2 + (bits >> 1)

    tokens = jnp.concatenate([got_ref[s, TOK : TOK + T] for s in range(LAYERS)], axis=0)
    extra = sum(got_ref[s, TOK + T :].astype(F32) for s in range(LAYERS))
    bias = jnp.sum(tokens[:, 256:].astype(F32), axis=0, keepdims=True)
    bias = jnp.concatenate([bias[:, :ROWS]] * 4, axis=1)
    for m in range(BLOCKS):
        normed = jnp.concatenate([got_ref[s, T * m : T * (m + 1)] for s in range(LAYERS)], axis=0)
        keys = tn(normed, tokens[:, :256])
        rates = tn(tokens[:, 256:], normed)[:H]
        rows = jnp.concatenate(
            [rates, extra[m : m + 1], extra[m + 8 : m + 9], bias, jnp.zeros((5, BLOCK), F32)],
            axis=0,
        )
        low = cut_rows(rows)
        for i in range(4):
            d = 4 * m + i
            z_at, y_at = slot(d // 8, zh, d % 2), slot(d // 2 % 4, y, d % 2)
            c_at = (d + c) % 2
            scr[c_at, z_at, y_at, :ROWS] = keys[ROWS * i : ROWS * (i + 1)].astype(BF16)
            scr[c_at, z_at, y_at, ROWS:] = low[i].astype(BF16)
    for i, ref in enumerate((keep_ref, send_ref)):
        pltpu.make_async_copy(scr.at[i], ref, sem.at[i]).start()
    for i, ref in enumerate((keep_ref, send_ref)):
        pltpu.make_async_copy(scr.at[i], ref, sem.at[i]).wait()


def add_kernel(axis, a_ref, b_ref, keep_ref, send_ref):
    total = (a_ref[...].astype(F32) + b_ref[...].astype(F32)).astype(BF16)
    if axis == 1:
        half = total.shape[1] // 2
        keep_ref[...] = total[:, :half]
        send_ref[...] = total[:, half:]
    else:
        half = total.shape[0] // 2
        keep_ref[...] = total[:half]
        send_ref[...] = total[half:]


def final_kernel(a_ref, b_ref, scales_ref, keys_ref, rates_ref, bias_ref):
    total = a_ref[0].astype(F32) + b_ref[0].astype(F32)
    keys_ref[...] = total[:ROWS]
    rates = jnp.concatenate([total[ROWS:, :C], total[ROWS:, C:]], axis=0)
    wide = jnp.concatenate([rates, jnp.zeros((C - T, C), F32)], axis=0)
    rates_ref[...] = wide.T[:ROWS, :H]
    scales_ref[...] = rates[24:26, :ROWS]
    bias_ref[...] = rates[26:27, :H]


ANY = pl.BlockSpec(memory_space=pl.ANY)
VMEM = pl.BlockSpec(memory_space=pltpu.VMEM)
SMEM = pl.BlockSpec(memory_space=pltpu.SMEM)
PARAMS = pltpu.CompilerParams(vmem_limit_bytes=56 * 1024 * 1024)


def shape(*dims, dtype=BF16):
    return jax.ShapeDtypeStruct(dims, dtype)


def call(kernel, outs, ins, scratch, out_spec=None, cost=None):
    flops, moved = cost
    return pl.pallas_call(
        kernel,
        out_shape=outs,
        in_specs=ins,
        out_specs=out_spec or [VMEM] * len(outs),
        scratch_shapes=scratch,
        compiler_params=PARAMS,
        cost_estimate=pl.CostEstimate(flops=flops, bytes_accessed=moved, transcendentals=0),
    )


def ring_pairs(first):
    pairs = []
    for i in range(4):
        for c in range(2):
            to = i ^ 1 if (c == 0) == first else 3 - i
            pairs.append((i * 2 + c, to * 2 + c))
    return pairs


def swap(array, axis, first):
    return lax.ppermute(array, (axis, "c"), ring_pairs(first))


def other_core(array):
    return lax.ppermute(array, "c", [(0, 1), (1, 0)])


def gather_ring(array, axis):
    one = swap(array, axis, True)
    two = swap(array, axis, False)
    return [array, one, two, swap(one, axis, False)]


def per_device(entries, cotangents, scales, key_weight, rate_weight, rate_bias):
    x, zl, zh, y, c = (lax.axis_index(a) for a in ("x", "zl", "zh", "y", "c"))
    section = x * 2 + zl
    mine = jnp.minimum(section, SEQS - 1)
    stream = lax.dynamic_index_in_dim(entries.reshape(SEQS, T, D), mine, 0, keepdims=False)
    back = lax.dynamic_index_in_dim(cotangents.reshape(SEQS, T, D), mine, 0, keepdims=False)

    wide = jnp.pad(rate_weight[0].T, ((0, 0), (0, C - ROWS)))
    small = jnp.pad(scales[0], ((0, 0), (0, C - ROWS)))
    line = jnp.pad(rate_bias, ((0, 0), (0, C - H)))
    right = jnp.concatenate([wide[16:], small, line, jnp.zeros((5, C), BF16)], axis=0)
    packed = jnp.concatenate(
        [key_weight[0], jnp.concatenate([wide[:16], right], axis=1)], axis=0
    )

    along = jnp.stack(gather_ring(packed, "zh"))
    first, second = partner(zh, c, True), partner(zh, c, False)
    across = partner(second, c, True)
    order = [jnp.where(j == first, 1, jnp.where(j == second, 2, jnp.where(j == across, 3, 0))) for j in range(4)]
    along = jnp.take(along, jnp.stack(order), axis=0)
    pairs = []
    for z in range(8):
        for core in range(2):
            to = z ^ 1 if core == 0 else (z + 1 if z % 2 else z - 1) % 8
            pairs.append(tuple(((i % 2) * 4 + i // 2) * 2 + core for i in (z, to)))
    other = lax.ppermute(along, ("zl", "zh", "c"), pairs)
    both = jnp.where(zl == 0, jnp.stack([along, other]), jnp.stack([other, along]))

    left = jnp.stack(gather_ring(both[..., :C], "x"))
    right = jnp.stack(gather_ring(both[..., C:], "y"))
    left = gather_ring(left, "y")
    right = gather_ring(right, "x")
    left = left + [other_core(a) for a in left]
    right = right + [other_core(a) for a in right]

    pos = jnp.stack([x, y, c, jnp.where(section < SEQS, 1, 0)]).astype(jnp.int32)
    sent = call(
        sequence_kernel,
        [shape(LAYERS, SENT, BLOCK)],
        [SMEM] + [ANY] * 16 + [VMEM] * 2,
        [
            pltpu.VMEM((LAYERS, 4, 4, 2, PIECE, 256), BF16),
            pltpu.VMEM((LAYERS, T, D), BF16),
            pltpu.VMEM((LAYERS, T, D), BF16),
            pltpu.VMEM((LAYERS, T, D), BF16),
            pltpu.VMEM((LAYERS, T, D), BF16),
            pltpu.VMEM((LAYERS, T, W), F32),
            pltpu.VMEM((LAYERS, 1, W), F32),
            pltpu.VMEM((LAYERS, T, 256), F32),
            pltpu.VMEM((LAYERS, T, 256), F32),
            pltpu.SemaphoreType.DMA((4,)),
            pltpu.SemaphoreType.DMA((4,)),
        ],
        cost=(8_000_000_000, 30_000_000),
    )(pos, *left, *right, stream, back)[0]

    got = lax.all_to_all(sent, SECTION, 0, 0, tiled=True)
    pos = jnp.stack([zh, y, c]).astype(jnp.int32)
    half = shape(4, 4, PIECE, 256)
    keep, send = call(
        weight_kernel,
        [half, half],
        [SMEM, VMEM],
        [pltpu.VMEM((2, 4, 4, PIECE, 256), BF16), pltpu.SemaphoreType.DMA((2,))],
        [ANY] * 2,
        cost=(600_000_000, 4_000_000),
    )(pos, got)
    got = other_core(send)
    for axis, first, out in (
        (1, True, (4, 2, PIECE, 256)),
        (1, False, (4, 1, PIECE, 256)),
        (0, True, (2, 1, PIECE, 256)),
        (0, False, (1, 1, PIECE, 256)),
    ):
        keep, send = call(
            functools.partial(add_kernel, axis),
            [shape(*out), shape(*out)],
            [VMEM] * 2,
            [],
            cost=(1_000_000, 4_000_000),
        )(keep, got)
        got = swap(send, "y" if axis == 1 else "zh", first)
    g_scales, g_keys, g_rates, g_bias = call(
        final_kernel,
        [
            shape(2, ROWS, dtype=F32),
            shape(ROWS, 256, dtype=F32),
            shape(ROWS, H, dtype=F32),
            shape(1, H, dtype=F32),
        ],
        [VMEM] * 2,
        [],
        cost=(0, 500_000),
    )(keep[0], got[0])
    return g_scales[None], g_keys[None], g_rates[None], g_bias


def solution(mesh):
    fine = Mesh(mesh.devices.reshape(4, 2, 4, 4, 2), ("x", "zl", "zh", "y", "c"))
    placed = (
        P(None, None, DP, None),
        P(None, None, DP, None),
        P(SECTION, None, DP),
        P(SECTION, DP, None),
        P(SECTION, DP, None),
        P(SECTION, None),
    )
    return jax.shard_map(
        per_device,
        mesh=fine,
        in_specs=placed,
        out_specs=(
            P(SECTION, None, DP),
            P(SECTION, DP, None),
            P(SECTION, DP, None),
            P(SECTION, None),
        ),
        check_vma=False,
    )
```

profile of v0, /device:TPU:2, one launch (start us, length us, event | category | flops | bytes accessed | tf_op | source)
XLA Modules:
  0.0 196.7 jit_solution(10209925235090818603)
XLA Ops:
  2.0 0.8 maximum_maximum_fusion
  2.9 3.4 %collective-permute-start = (bf16[112,256]{1,0:T(8,128)(2,1)S(1)}, bf16[112,256]{1,0:T(8,128)(2,1)S(1)}, u32[]{:S(2)}, u32[]{:S(2)}) collective-permute-start(bf16[112,256]{1,0:T(8,128)(2,1)S(1)} %maximum_maximum_fusion), channel_id=1, source_target_pairs={{0,8},{1,25},{8,0},{9,17},{16,24},{17,9},{24,16},{25,1},{2,10},{3,... | collective-permute-start | bytes 172040 | tf_op jit(solution)/shard_map/ppermute | solution.py:370
  6.2 4.5 %collective-permute-start.1 = (bf16[112,256]{1,0:T(8,128)(2,1)S(1)}, bf16[112,256]{1,0:T(8,128)(2,1)S(1)}, u32[]{:S(2)}, u32[]{:S(2)}) collective-permute-start(bf16[112,256]{1,0:T(8,128)(2,1)S(1)} %maximum_maximum_fusion), channel_id=1, source_target_pairs={{0,24},{1,9},{8,16},{9,1},{16,8},{17,25},{24,0},{25,17},{2,26},{3,... | collective-permute-start | bytes 172040 | tf_op jit(solution)/shard_map/ppermute | solution.py:370
  10.7 0.8 fusion.12
  11.7 2.6 %collective-permute-start.2 = (bf16[112,256]{1,0:T(8,128)(2,1)S(1)}, bf16[112,256]{1,0:T(8,128)(2,1)S(1)}, u32[]{:S(2)}, u32[]{:S(2)}) collective-permute-start(bf16[112,256]{1,0:T(8,128)(2,1)S(1)} %collective-permute-done), channel_id=1, source_target_pairs={{0,24},{1,9},{8,16},{9,1},{16,8},{17,25},{24,0},{25,17},{2,26},{3,... | collective-permute-start | bytes 172040 | tf_op jit(solution)/shard_map/ppermute | solution.py:370
  14.4 3.8 %collective-permute-done.2 = bf16[112,256]{1,0:T(8,128)(2,1)S(1)} collective-permute-done((bf16[112,256]{1,0:T(8,128)(2,1)S(1)}, bf16[112,256]{1,0:T(8,128)(2,1)S(1)}, u32[]{:S(2)}, u32[]{:S(2)}) %collective-permute-start.2) | collective-permute-done | bytes 57376 | tf_op jit(solution)/shard_map/ppermute | solution.py:370
  18.9 1.6 collective-permute-start.3
  20.6 4.4 %collective-permute-done.3 = bf16[4,112,256]{2,1,0:T(8,128)(2,1)S(1)} collective-permute-done((bf16[4,112,256]{2,1,0:T(8,128)(2,1)S(1)}, bf16[4,112,256]{2,1,0:T(8,128)(2,1)S(1)}, u32[]{:S(2)}, u32[]{:S(2)}) %collective-permute-start.3) | collective-permute-done | bytes 229408 | tf_op jit(solution)/shard_map/ppermute | solution.py:408
  25.8 1.6 collective-permute-start.14
  27.4 2.2 %collective-permute-start.5 = (bf16[2,4,112,128]{3,2,1,0:T(8,128)(2,1)S(1)}, bf16[2,4,112,128]{3,2,1,0:T(8,128)(2,1)S(1)}, u32[]{:S(2)}, u32[]{:S(2)}) collective-permute-start(bf16[2,4,112,128]{3,2,1,0:T(8,128)(2,1)S(1)} %get-tuple-element.39), channel_id=1, source_target_pairs={{0,192},{1,65},{64,128},{65,1},{128,64},{129,193},{192,0},{193,129... | collective-permute-start | bytes 688136 | tf_op jit(solution)/shard_map/ppermute | solution.py:370
  29.6 3.8 %collective-permute-done.4 = bf16[2,4,112,128]{3,2,1,0:T(8,128)(2,1)S(1)} collective-permute-done((bf16[2,4,112,128]{3,2,1,0:T(8,128)(2,1)S(1)}, bf16[2,4,112,128]{3,2,1,0:T(8,128)(2,1)S(1)}, u32[]{:S(2)}, u32[]{:S(2)}) %collective-permute-start.4) | collective-permute-done | bytes 229408 | tf_op jit(solution)/shard_map/ppermute | solution.py:370
  33.3 1.9 collective-permute-start.6
  35.2 1.0 collective-permute-start.15
  36.2 2.3 %collective-permute-start.16 = (bf16[2,4,112,128]{3,2,1,0:T(8,128)(2,1)S(1)}, bf16[2,4,112,128]{3,2,1,0:T(8,128)(2,1)S(1)}, u32[]{:S(2)}, u32[]{:S(2)}) collective-permute-start(bf16[2,4,112,128]{3,2,1,0:T(8,128)(2,1)S(1)} %collective-permute-done.14), channel_id=1, source_target_pairs={{0,6},{1,3},{2,4},{3,1},{4,2},{5,7},{6,0},{7,5},{8,14},{9,11},{10,... | collective-permute-start | bytes 688136 | tf_op jit(solution)/shard_map/ppermute | solution.py:370
  38.4 0.9 collective-permute-done.6
  39.6 2.6 %collective-permute-start.8 = (bf16[4,2,4,112,128]{4,3,2,1,0:T(8,128)(2,1)S(1)}, bf16[4,2,4,112,128]{4,3,2,1,0:T(8,128)(2,1)S(1)}, u32[]{:S(2)}, u32[]{:S(2)}) collective-permute-start(bf16[4,2,4,112,128]{4,3,2,1,0:T(8,128)(2,1)S(1)} %pad_maximum_fusion.refs_0_), channel_id=1, source_target_pairs={{0,6},{1,3},{2,4},{3,1},{4,2},{5,7},{6,0},{7,5},{8,14},{9,11},{10,... | collective-permute-start | bytes 2752520 | tf_op jit(solution)/shard_map/ppermute | solution.py:370
  42.6 2.2 %collective-permute-done.16 = bf16[2,4,112,128]{3,2,1,0:T(8,128)(2,1)S(1)} collective-permute-done((bf16[2,4,112,128]{3,2,1,0:T(8,128)(2,1)S(1)}, bf16[2,4,112,128]{3,2,1,0:T(8,128)(2,1)S(1)}, u32[]{:S(2)}, u32[]{:S(2)}) %collective-permute-start.16) | collective-permute-done | bytes 229408 | tf_op jit(solution)/shard_map/ppermute | solution.py:370
  45.0 1.9 collective-permute-start.17
  47.5 16.2 %collective-permute-done.8.refs_2_ = bf16[4,2,4,112,128]{4,3,2,1,0:T(8,128)(2,1)S(1)} collective-permute-done((bf16[4,2,4,112,128]{4,3,2,1,0:T(8,128)(2,1)S(1)}, bf16[4,2,4,112,128]{4,3,2,1,0:T(8,128)(2,1)S(1)}, u32[]{:S(2)}, u32[]{:S(2)}) %collective-permute-start.8) | collective-permute-done | bytes 917536 | tf_op jit(solution)/shard_map/ppermute | solution.py:370
  63.8 2.7 %collective-permute-start.9 = (bf16[4,2,4,112,128]{4,3,2,1,0:T(8,128)(2,1)}, bf16[4,2,4,112,128]{4,3,2,1,0:T(8,128)(2,1)}, u32[]{:S(2)}, u32[]{:S(2)}) collective-permute-start(bf16[4,2,4,112,128]{4,3,2,1,0:T(8,128)(2,1)} %collective-permute-done.7.refs_1_), channel_id=1, source_target_pairs={{0,6},{1,3},{2,4},{3,1},{4,2},{5,7},{6,0},{7,5},{8,14},{9,11},{10,... | collective-permute-start | bytes 2752520 | tf_op jit(solution)/shard_map/ppermute | solution.py:370
  66.5 1.2 collective-permute-done.17.refs_9_
  68.9 1.0 copy-done.11
  69.9 8.9 %collective-permute-done.9.refs_3_ = bf16[4,2,4,112,128]{4,3,2,1,0:T(8,128)(2,1)} collective-permute-done((bf16[4,2,4,112,128]{4,3,2,1,0:T(8,128)(2,1)}, bf16[4,2,4,112,128]{4,3,2,1,0:T(8,128)(2,1)}, u32[]{:S(2)}, u32[]{:S(2)}) %collective-permute-start.9) | collective-permute-done | bytes 917536 | tf_op jit(solution)/shard_map/ppermute | solution.py:370
  78.8 2.6 %collective-permute-done.19.refs_11_ = bf16[4,2,4,112,128]{4,3,2,1,0:T(8,128)(2,1)} collective-permute-done((bf16[4,2,4,112,128]{4,3,2,1,0:T(8,128)(2,1)}, bf16[4,2,4,112,128]{4,3,2,1,0:T(8,128)(2,1)}, u32[]{:S(2)}, u32[]{:S(2)}) %collective-permute-start.19) | collective-permute-done | bytes 917536 | tf_op jit(solution)/shard_map/ppermute | solution.py:370
  82.0 1.8 dynamic-slice_bitcast_fusion
  84.2 29.6 %shard_map.93 = bf16[8,304,384]{2,1,0:T(8,128)(2,1)} custom-call(s32[4]{0:T(128)} %pad_add_fusion.1.pos_ref, bf16[4,2,4,112,128]{4,3,2,1,0:T(8,128)(2,1)} %copy-done.1, bf16[4,2,4,112,128]{4,3,2,1,0:T(8,128)(2,1)} %collective-permute-done.7.refs_1_, bf16[4,2,4,112,128]{4,3,2,1,0:T(8,128)(2,1)} %copy-done.9, ...), custom_call_target="tpu_custom_call" | custom-call | flops 8000000000 | bytes 30000000 | tf_op jit(solution)/shard_map/pallas_call | solution.py:419
  113.8 7.5 %all-to-all-start = ((bf16[8,304,384]{2,1,0:T(8,128)(2,1)}), bf16[8,304,384]{2,1,0:T(8,128)(2,1)S(1)}, u32[]{:S(2)}, u32[]{:S(2)}) async-start(bf16[8,304,384]{2,1,0:T(8,128)(2,1)} %shard_map.93), calls=%async_computation | async-start | bytes 3735552 | tf_op jit(solution)/shard_map/all_to_all | solution.py:439
  121.8 22.7 %all-to-all-done.got_ref = bf16[8,304,384]{2,1,0:T(8,128)(2,1)S(1)} async-done(((bf16[8,304,384]{2,1,0:T(8,128)(2,1)}), bf16[8,304,384]{2,1,0:T(8,128)(2,1)S(1)}, u32[]{:S(2)}, u32[]{:S(2)}) %all-to-all-start) | async-done | bytes 1867808 | tf_op jit(solution)/shard_map/all_to_all | solution.py:439
  144.5 1.3 copy-done
  145.8 3.8 %shard_map.94 = (bf16[4,4,112,256]{3,2,1,0:T(8,128)(2,1)}, bf16[4,4,112,256]{3,2,1,0:T(8,128)(2,1)}) custom-call(s32[3]{0:T(128)} %pad_add_fusion.pos_ref, bf16[8,304,384]{2,1,0:T(8,128)(2,1)} %copy-done), custom_call_target="tpu_custom_call" | custom-call | flops 600000000 | bytes 4000000 | tf_op jit(solution)/shard_map/pallas_call | solution.py:442
  149.6 2.7 %collective-permute-done.24.b_ref = bf16[4,4,112,256]{3,2,1,0:T(8,128)(2,1)S(1)} collective-permute-done((bf16[4,4,112,256]{3,2,1,0:T(8,128)(2,1)}, bf16[4,4,112,256]{3,2,1,0:T(8,128)(2,1)S(1)}, u32[]{:S(2)}, u32[]{:S(2)}) %collective-permute-start.24) | collective-permute-done | bytes 917536 | tf_op jit(solution)/shard_map/ppermute | solution.py:374
  152.3 1.0 copy-done.3
  153.3 2.5 %shard_map.95 = (bf16[4,2,112,256]{3,2,1,0:T(8,128)(2,1)}, bf16[4,2,112,256]{3,2,1,0:T(8,128)(2,1)}) custom-call(bf16[4,4,112,256]{3,2,1,0:T(8,128)(2,1)} %get-tuple-element.18.a_ref, bf16[4,4,112,256]{3,2,1,0:T(8,128)(2,1)} %copy-done.3), custom_call_target="tpu_custom_call" | custom-call | flops 1000000 | bytes 4000000 | tf_op jit(solution)/shard_map/pallas_call | solution.py:457
  155.8 1.0 collective-permute-start.25
  156.7 7.7 %collective-permute-done.25.b_ref = bf16[4,2,112,256]{3,2,1,0:T(8,128)(2,1)S(1)} collective-permute-done((bf16[4,2,112,256]{3,2,1,0:T(8,128)(2,1)}, bf16[4,2,112,256]{3,2,1,0:T(8,128)(2,1)S(1)}, u32[]{:S(2)}, u32[]{:S(2)}) %collective-permute-start.25) | collective-permute-done | bytes 458784 | tf_op jit(solution)/shard_map/ppermute | solution.py:370
  164.5 0.8 copy-done.4
  165.2 2.0 %shard_map.96 = (bf16[4,1,112,256]{3,2,1,0:T(8,128)(2,1)}, bf16[4,1,112,256]{3,2,1,0:T(8,128)(2,1)}) custom-call(bf16[4,2,112,256]{3,2,1,0:T(8,128)(2,1)} %get-tuple-element.20.a_ref, bf16[4,2,112,256]{3,2,1,0:T(8,128)(2,1)} %copy-done.4), custom_call_target="tpu_custom_call" | custom-call | flops 1000000 | bytes 4000000 | tf_op jit(solution)/shard_map/pallas_call | solution.py:457
  167.2 1.7 collective-permute-start.26
  169.0 5.7 %collective-permute-done.26.b_ref = bf16[4,1,112,256]{3,2,1,0:T(8,128)(2,1)S(1)} collective-permute-done((bf16[4,1,112,256]{3,2,1,0:T(8,128)(2,1)}, bf16[4,1,112,256]{3,2,1,0:T(8,128)(2,1)S(1)}, u32[]{:S(2)}, u32[]{:S(2)}) %collective-permute-start.26) | collective-permute-done | bytes 229408 | tf_op jit(solution)/shard_map/ppermute | solution.py:370
  174.7 0.7 copy-done.5
  175.4 1.8 shard_map.97
  177.2 1.7 collective-permute-start.27
  178.8 5.5 %collective-permute-done.27.b_ref = bf16[2,1,112,256]{3,2,1,0:T(8,128)(2,1)S(1)} collective-permute-done((bf16[2,1,112,256]{3,2,1,0:T(8,128)(2,1)}, bf16[2,1,112,256]{3,2,1,0:T(8,128)(2,1)S(1)}, u32[]{:S(2)}, u32[]{:S(2)}) %collective-permute-start.27) | collective-permute-done | bytes 114720 | tf_op jit(solution)/shard_map/ppermute | solution.py:370
  184.9 1.6 shard_map.98
  186.6 1.3 collective-permute-start.28
  187.8 5.2 %collective-permute-done.28 = bf16[1,1,112,256]{3,2,1,0:T(8,128)(2,1)S(1)} collective-permute-done((bf16[1,1,112,256]{3,2,1,0:T(8,128)(2,1)}, bf16[1,1,112,256]{3,2,1,0:T(8,128)(2,1)S(1)}, u32[]{:S(2)}, u32[]{:S(2)}) %collective-permute-start.28) | collective-permute-done | bytes 57376 | tf_op jit(solution)/shard_map/ppermute | solution.py:370
  193.7 1.6 shard_map.99
  195.2 1.5 copy.10
  (63 shorter events, 8.8 us)
Async XLA Ops:
  2.9 8.8 %collective-permute-start = (bf16[112,256]{1,0:T(8,128)(2,1)S(1)}, bf16[112,256]{1,0:T(8,128)(2,1)S(1)}, u32[]{:S(2)}, u32[]{:S(2)}) collective-permute-start(bf16[112,256]{1,0:T(8,128)(2,1)S(1)} %maximum_maximum_fusion), channel_id=1, source_target_pairs={{0,8},{1,25},{8,0},{9,17},{16,24},{17,9},{24,16},{25,1},{2,10},{3,... | collective-permute-start | bytes 172040 | tf_op jit(solution)/shard_map/ppermute | solution.py:370
  6.2 8.2 %collective-permute-start.1 = (bf16[112,256]{1,0:T(8,128)(2,1)S(1)}, bf16[112,256]{1,0:T(8,128)(2,1)S(1)}, u32[]{:S(2)}, u32[]{:S(2)}) collective-permute-start(bf16[112,256]{1,0:T(8,128)(2,1)S(1)} %maximum_maximum_fusion), channel_id=1, source_target_pairs={{0,24},{1,9},{8,16},{9,1},{16,8},{17,25},{24,0},{25,17},{2,26},{3,... | collective-permute-start | bytes 172040 | tf_op jit(solution)/shard_map/ppermute | solution.py:370
  11.7 6.5 %collective-permute-start.2 = (bf16[112,256]{1,0:T(8,128)(2,1)S(1)}, bf16[112,256]{1,0:T(8,128)(2,1)S(1)}, u32[]{:S(2)}, u32[]{:S(2)}) collective-permute-start(bf16[112,256]{1,0:T(8,128)(2,1)S(1)} %collective-permute-done), channel_id=1, source_target_pairs={{0,24},{1,9},{8,16},{9,1},{16,8},{17,25},{24,0},{25,17},{2,26},{3,... | collective-permute-start | bytes 172040 | tf_op jit(solution)/shard_map/ppermute | solution.py:370
  18.9 6.1 %collective-permute-start.3 = (bf16[4,112,256]{2,1,0:T(8,128)(2,1)S(1)}, bf16[4,112,256]{2,1,0:T(8,128)(2,1)S(1)}, u32[]{:S(2)}, u32[]{:S(2)}) collective-permute-start(bf16[4,112,256]{2,1,0:T(8,128)(2,1)S(1)} %broadcast_select_fusion), channel_id=1, source_target_pairs={{0,32},{1,57},{32,0},{33,9},{8,40},{9,33},{40,8},{41,17},{16,48},{... | collective-permute-start | bytes 688136 | tf_op jit(solution)/shard_map/ppermute | solution.py:408
  25.2 8.1 %collective-permute-start.4 = (bf16[2,4,112,128]{3,2,1,0:T(8,128)(2,1)S(1)}, bf16[2,4,112,128]{3,2,1,0:T(8,128)(2,1)S(1)}, u32[]{:S(2)}, u32[]{:S(2)}) collective-permute-start(bf16[2,4,112,128]{3,2,1,0:T(8,128)(2,1)S(1)} %get-tuple-element.39), channel_id=1, source_target_pairs={{0,64},{1,193},{64,0},{65,129},{128,192},{129,65},{192,128},{193,1... | collective-permute-start | bytes 688136 | tf_op jit(solution)/shard_map/ppermute | solution.py:370
  25.8 10.3 %collective-permute-start.14 = (bf16[2,4,112,128]{3,2,1,0:T(8,128)(2,1)S(1)}, bf16[2,4,112,128]{3,2,1,0:T(8,128)(2,1)S(1)}, u32[]{:S(2)}, u32[]{:S(2)}) collective-permute-start(bf16[2,4,112,128]{3,2,1,0:T(8,128)(2,1)S(1)} %get-tuple-element.38), channel_id=1, source_target_pairs={{0,2},{1,7},{2,0},{3,5},{4,6},{5,3},{6,4},{7,1},{8,10},{9,15},{10,... | collective-permute-start | bytes 688136 | tf_op jit(solution)/shard_map/ppermute | solution.py:370
  27.4 11.0 %collective-permute-start.5 = (bf16[2,4,112,128]{3,2,1,0:T(8,128)(2,1)S(1)}, bf16[2,4,112,128]{3,2,1,0:T(8,128)(2,1)S(1)}, u32[]{:S(2)}, u32[]{:S(2)}) collective-permute-start(bf16[2,4,112,128]{3,2,1,0:T(8,128)(2,1)S(1)} %get-tuple-element.39), channel_id=1, source_target_pairs={{0,192},{1,65},{64,128},{65,1},{128,64},{129,193},{192,0},{193,129... | collective-permute-start | bytes 688136 | tf_op jit(solution)/shard_map/ppermute | solution.py:370
  33.3 6.0 %collective-permute-start.6 = (bf16[2,4,112,128]{3,2,1,0:T(8,128)(2,1)S(1)}, bf16[2,4,112,128]{3,2,1,0:T(8,128)(2,1)S(1)}, u32[]{:S(2)}, u32[]{:S(2)}) collective-permute-start(bf16[2,4,112,128]{3,2,1,0:T(8,128)(2,1)S(1)} %collective-permute-done.4), channel_id=1, source_target_pairs={{0,192},{1,65},{64,128},{65,1},{128,64},{129,193},{192,0},{193,129... | collective-permute-start | bytes 688136 | tf_op jit(solution)/shard_map/ppermute | solution.py:370
  35.2 7.5 %collective-permute-start.15 = (bf16[2,4,112,128]{3,2,1,0:T(8,128)(2,1)S(1)}, bf16[2,4,112,128]{3,2,1,0:T(8,128)(2,1)S(1)}, u32[]{:S(2)}, u32[]{:S(2)}) collective-permute-start(bf16[2,4,112,128]{3,2,1,0:T(8,128)(2,1)S(1)} %get-tuple-element.38), channel_id=1, source_target_pairs={{0,6},{1,3},{2,4},{3,1},{4,2},{5,7},{6,0},{7,5},{8,14},{9,11},{10,... | collective-permute-start | bytes 688136 | tf_op jit(solution)/shard_map/ppermute | solution.py:370
  36.2 8.7 %collective-permute-start.16 = (bf16[2,4,112,128]{3,2,1,0:T(8,128)(2,1)S(1)}, bf16[2,4,112,128]{3,2,1,0:T(8,128)(2,1)S(1)}, u32[]{:S(2)}, u32[]{:S(2)}) collective-permute-start(bf16[2,4,112,128]{3,2,1,0:T(8,128)(2,1)S(1)} %collective-permute-done.14), channel_id=1, source_target_pairs={{0,6},{1,3},{2,4},{3,1},{4,2},{5,7},{6,0},{7,5},{8,14},{9,11},{10,... | collective-permute-start | bytes 688136 | tf_op jit(solution)/shard_map/ppermute | solution.py:370
  39.5 44.4 %copy-start.1 = (bf16[4,2,4,112,128]{4,3,2,1,0:T(8,128)(2,1)}, bf16[4,2,4,112,128]{4,3,2,1,0:T(8,128)(2,1)S(1)}, u32[]{:S(2)}) copy-start(bf16[4,2,4,112,128]{4,3,2,1,0:T(8,128)(2,1)S(1)} %pad_maximum_fusion.refs_0_) | copy-start | bytes 2752516
  39.5 7.4 %collective-permute-start.10 = (bf16[4,2,4,112,128]{4,3,2,1,0:T(8,128)(2,1)S(1)}, bf16[4,2,4,112,128]{4,3,2,1,0:T(8,128)(2,1)S(1)}, u32[]{:S(2)}, u32[]{:S(2)}) collective-permute-start(bf16[4,2,4,112,128]{4,3,2,1,0:T(8,128)(2,1)S(1)} %pad_maximum_fusion.refs_0_), channel_id=1, source_target_pairs={{0,1},{1,0},{2,3},{3,2},{4,5},{5,4},{6,7},{7,6},{8,9},{9,8},{10,11... | collective-permute-start | bytes 2752520 | tf_op jit(solution)/shard_map/ppermute | solution.py:374
  39.6 24.2 %collective-permute-start.8 = (bf16[4,2,4,112,128]{4,3,2,1,0:T(8,128)(2,1)S(1)}, bf16[4,2,4,112,128]{4,3,2,1,0:T(8,128)(2,1)S(1)}, u32[]{:S(2)}, u32[]{:S(2)}) collective-permute-start(bf16[4,2,4,112,128]{4,3,2,1,0:T(8,128)(2,1)S(1)} %pad_maximum_fusion.refs_0_), channel_id=1, source_target_pairs={{0,6},{1,3},{2,4},{3,1},{4,2},{5,7},{6,0},{7,5},{8,14},{9,11},{10,... | collective-permute-start | bytes 2752520 | tf_op jit(solution)/shard_map/ppermute | solution.py:370
  42.2 21.6 %collective-permute-start.7 = (bf16[4,2,4,112,128]{4,3,2,1,0:T(8,128)(2,1)S(1)}, bf16[4,2,4,112,128]{4,3,2,1,0:T(8,128)(2,1)}, u32[]{:S(2)}, u32[]{:S(2)}) collective-permute-start(bf16[4,2,4,112,128]{4,3,2,1,0:T(8,128)(2,1)S(1)} %pad_maximum_fusion.refs_0_), channel_id=1, source_target_pairs={{0,2},{1,7},{2,0},{3,5},{4,6},{5,3},{6,4},{7,1},{8,10},{9,15},{10,... | collective-permute-start | bytes 2752520 | tf_op jit(solution)/shard_map/ppermute | solution.py:370
  45.0 39.2 %copy-start.2 = (bf16[4,2,4,112,128]{4,3,2,1,0:T(8,128)(2,1)}, bf16[4,2,4,112,128]{4,3,2,1,0:T(8,128)(2,1)S(1)}, u32[]{:S(2)}) copy-start(bf16[4,2,4,112,128]{4,3,2,1,0:T(8,128)(2,1)S(1)} %pad_maximum_fusion.1.refs_8_) | copy-start | bytes 2752516
  45.0 22.6 %collective-permute-start.17 = (bf16[4,2,4,112,128]{4,3,2,1,0:T(8,128)(2,1)S(1)}, bf16[4,2,4,112,128]{4,3,2,1,0:T(8,128)(2,1)}, u32[]{:S(2)}, u32[]{:S(2)}) collective-permute-start(bf16[4,2,4,112,128]{4,3,2,1,0:T(8,128)(2,1)S(1)} %pad_maximum_fusion.1.refs_8_), channel_id=1, source_target_pairs={{0,64},{1,193},{64,0},{65,129},{128,192},{129,65},{192,128},{193,1... | collective-permute-start | bytes 2752520 | tf_op jit(solution)/shard_map/ppermute | solution.py:370
  46.9 21.1 %collective-permute-start.20 = (bf16[4,2,4,112,128]{4,3,2,1,0:T(8,128)(2,1)S(1)}, bf16[4,2,4,112,128]{4,3,2,1,0:T(8,128)(2,1)S(1)}, u32[]{:S(2)}, u32[]{:S(2)}) collective-permute-start(bf16[4,2,4,112,128]{4,3,2,1,0:T(8,128)(2,1)S(1)} %pad_maximum_fusion.1.refs_8_), channel_id=1, source_target_pairs={{0,1},{1,0},{2,3},{3,2},{4,5},{5,4},{6,7},{7,6},{8,9},{9,8},{10,11... | collective-permute-start | bytes 2752520 | tf_op jit(solution)/shard_map/ppermute | solution.py:374
  46.9 37.3 %copy-start.8 = (bf16[4,2,4,112,128]{4,3,2,1,0:T(8,128)(2,1)}, bf16[4,2,4,112,128]{4,3,2,1,0:T(8,128)(2,1)S(1)}, u32[]{:S(2)}) copy-start(bf16[4,2,4,112,128]{4,3,2,1,0:T(8,128)(2,1)S(1)} %collective-permute-done.10.refs_4_) | copy-start | bytes 2752516
  46.9 21.1 %collective-permute-start.18 = (bf16[4,2,4,112,128]{4,3,2,1,0:T(8,128)(2,1)S(1)}, bf16[4,2,4,112,128]{4,3,2,1,0:T(8,128)(2,1)}, u32[]{:S(2)}, u32[]{:S(2)}) collective-permute-start(bf16[4,2,4,112,128]{4,3,2,1,0:T(8,128)(2,1)S(1)} %pad_maximum_fusion.1.refs_8_), channel_id=1, source_target_pairs={{0,192},{1,65},{64,128},{65,1},{128,64},{129,193},{192,0},{193,129... | collective-permute-start | bytes 2752520 | tf_op jit(solution)/shard_map/ppermute | solution.py:370
  63.7 4.3 %copy-start.9 = (bf16[4,2,4,112,128]{4,3,2,1,0:T(8,128)(2,1)}, bf16[4,2,4,112,128]{4,3,2,1,0:T(8,128)(2,1)S(1)}, u32[]{:S(2)}) copy-start(bf16[4,2,4,112,128]{4,3,2,1,0:T(8,128)(2,1)S(1)} %collective-permute-done.8.refs_2_) | copy-start | bytes 2752516
  63.7 4.8 %collective-permute-start.12 = (bf16[4,2,4,112,128]{4,3,2,1,0:T(8,128)(2,1)S(1)}, bf16[4,2,4,112,128]{4,3,2,1,0:T(8,128)(2,1)S(1)}, u32[]{:S(2)}, u32[]{:S(2)}) collective-permute-start(bf16[4,2,4,112,128]{4,3,2,1,0:T(8,128)(2,1)S(1)} %collective-permute-done.8.refs_2_), channel_id=1, source_target_pairs={{0,1},{1,0},{2,3},{3,2},{4,5},{5,4},{6,7},{7,6},{8,9},{9,8},{10,11... | collective-permute-start | bytes 2752520 | tf_op jit(solution)/shard_map/ppermute | solution.py:374
  63.8 15.0 %collective-permute-start.9 = (bf16[4,2,4,112,128]{4,3,2,1,0:T(8,128)(2,1)}, bf16[4,2,4,112,128]{4,3,2,1,0:T(8,128)(2,1)}, u32[]{:S(2)}, u32[]{:S(2)}) collective-permute-start(bf16[4,2,4,112,128]{4,3,2,1,0:T(8,128)(2,1)} %collective-permute-done.7.refs_1_), channel_id=1, source_target_pairs={{0,6},{1,3},{2,4},{3,1},{4,2},{5,7},{6,0},{7,5},{8,14},{9,11},{10,... | collective-permute-start | bytes 2752520 | tf_op jit(solution)/shard_map/ppermute | solution.py:370
  67.6 13.7 %collective-permute-start.19 = (bf16[4,2,4,112,128]{4,3,2,1,0:T(8,128)(2,1)}, bf16[4,2,4,112,128]{4,3,2,1,0:T(8,128)(2,1)}, u32[]{:S(2)}, u32[]{:S(2)}) collective-permute-start(bf16[4,2,4,112,128]{4,3,2,1,0:T(8,128)(2,1)} %collective-permute-done.17.refs_9_), channel_id=1, source_target_pairs={{0,192},{1,65},{64,128},{65,1},{128,64},{129,193},{192,0},{193,129... | collective-permute-start | bytes 2752520 | tf_op jit(solution)/shard_map/ppermute | solution.py:370
  68.0 0.9 copy-start.10
  68.0 15.8 %collective-permute-start.11 = (bf16[4,2,4,112,128]{4,3,2,1,0:T(8,128)(2,1)}, bf16[4,2,4,112,128]{4,3,2,1,0:T(8,128)(2,1)}, u32[]{:S(2)}, u32[]{:S(2)}) collective-permute-start(bf16[4,2,4,112,128]{4,3,2,1,0:T(8,128)(2,1)} %collective-permute-done.7.refs_1_), channel_id=1, source_target_pairs={{0,1},{1,0},{2,3},{3,2},{4,5},{5,4},{6,7},{7,6},{8,9},{9,8},{10,11... | collective-permute-start | bytes 2752520 | tf_op jit(solution)/shard_map/ppermute | solution.py:374
  68.0 15.8 %collective-permute-start.21 = (bf16[4,2,4,112,128]{4,3,2,1,0:T(8,128)(2,1)}, bf16[4,2,4,112,128]{4,3,2,1,0:T(8,128)(2,1)}, u32[]{:S(2)}, u32[]{:S(2)}) collective-permute-start(bf16[4,2,4,112,128]{4,3,2,1,0:T(8,128)(2,1)} %collective-permute-done.17.refs_9_), channel_id=1, source_target_pairs={{0,1},{1,0},{2,3},{3,2},{4,5},{5,4},{6,7},{7,6},{8,9},{9,8},{10,11... | collective-permute-start | bytes 2752520 | tf_op jit(solution)/shard_map/ppermute | solution.py:374
  68.9 1.0 copy-start.11
  68.9 14.9 %collective-permute-start.22 = (bf16[4,2,4,112,128]{4,3,2,1,0:T(8,128)(2,1)}, bf16[4,2,4,112,128]{4,3,2,1,0:T(8,128)(2,1)}, u32[]{:S(2)}, u32[]{:S(2)}) collective-permute-start(bf16[4,2,4,112,128]{4,3,2,1,0:T(8,128)(2,1)} %collective-permute-done.18.refs_10_), channel_id=1, source_target_pairs={{0,1},{1,0},{2,3},{3,2},{4,5},{5,4},{6,7},{7,6},{8,9},{9,8},{10,11... | collective-permute-start | bytes 2752520 | tf_op jit(solution)/shard_map/ppermute | solution.py:374
  78.8 5.1 %collective-permute-start.13 = (bf16[4,2,4,112,128]{4,3,2,1,0:T(8,128)(2,1)}, bf16[4,2,4,112,128]{4,3,2,1,0:T(8,128)(2,1)}, u32[]{:S(2)}, u32[]{:S(2)}) collective-permute-start(bf16[4,2,4,112,128]{4,3,2,1,0:T(8,128)(2,1)} %collective-permute-done.9.refs_3_), channel_id=1, source_target_pairs={{0,1},{1,0},{2,3},{3,2},{4,5},{5,4},{6,7},{7,6},{8,9},{9,8},{10,11... | collective-permute-start | bytes 2752520 | tf_op jit(solution)/shard_map/ppermute | solution.py:374
  81.3 2.8 %collective-permute-start.23 = (bf16[4,2,4,112,128]{4,3,2,1,0:T(8,128)(2,1)}, bf16[4,2,4,112,128]{4,3,2,1,0:T(8,128)(2,1)}, u32[]{:S(2)}, u32[]{:S(2)}) collective-permute-start(bf16[4,2,4,112,128]{4,3,2,1,0:T(8,128)(2,1)} %collective-permute-done.19.refs_11_), channel_id=1, source_target_pairs={{0,1},{1,0},{2,3},{3,2},{4,5},{5,4},{6,7},{7,6},{8,9},{9,8},{10,11... | collective-permute-start | bytes 2752520 | tf_op jit(solution)/shard_map/ppermute | solution.py:374
  113.8 30.8 %all-to-all-start = ((bf16[8,304,384]{2,1,0:T(8,128)(2,1)}), bf16[8,304,384]{2,1,0:T(8,128)(2,1)S(1)}, u32[]{:S(2)}, u32[]{:S(2)}) async-start(bf16[8,304,384]{2,1,0:T(8,128)(2,1)} %shard_map.93), calls=%async_computation | async-start | bytes 3735552 | tf_op jit(solution)/shard_map/all_to_all | solution.py:439
  144.5 1.3 copy-start
  149.5 2.8 %collective-permute-start.24 = (bf16[4,4,112,256]{3,2,1,0:T(8,128)(2,1)}, bf16[4,4,112,256]{3,2,1,0:T(8,128)(2,1)S(1)}, u32[]{:S(2)}, u32[]{:S(2)}) collective-permute-start(bf16[4,4,112,256]{3,2,1,0:T(8,128)(2,1)} %get-tuple-element.19), channel_id=1, source_target_pairs={{0,1},{1,0},{2,3},{3,2},{4,5},{5,4},{6,7},{7,6},{8,9},{9,8},{10,11... | collective-permute-start | bytes 2752520 | tf_op jit(solution)/shard_map/ppermute | solution.py:374
  152.3 1.0 copy-start.3
  155.8 8.7 %collective-permute-start.25 = (bf16[4,2,112,256]{3,2,1,0:T(8,128)(2,1)}, bf16[4,2,112,256]{3,2,1,0:T(8,128)(2,1)S(1)}, u32[]{:S(2)}, u32[]{:S(2)}) collective-permute-start(bf16[4,2,112,256]{3,2,1,0:T(8,128)(2,1)} %get-tuple-element.21), channel_id=1, source_target_pairs={{0,2},{1,7},{2,0},{3,5},{4,6},{5,3},{6,4},{7,1},{8,10},{9,15},{10,... | collective-permute-start | bytes 1376264 | tf_op jit(solution)/shard_map/ppermute | solution.py:370
  164.5 0.8 copy-start.4
  167.2 7.4 %collective-permute-start.26 = (bf16[4,1,112,256]{3,2,1,0:T(8,128)(2,1)}, bf16[4,1,112,256]{3,2,1,0:T(8,128)(2,1)S(1)}, u32[]{:S(2)}, u32[]{:S(2)}) collective-permute-start(bf16[4,1,112,256]{3,2,1,0:T(8,128)(2,1)} %get-tuple-element.23), channel_id=1, source_target_pairs={{0,6},{1,3},{2,4},{3,1},{4,2},{5,7},{6,0},{7,5},{8,14},{9,11},{10,... | collective-permute-start | bytes 688136 | tf_op jit(solution)/shard_map/ppermute | solution.py:370
  174.7 0.7 copy-start.5
  177.2 7.1 %collective-permute-start.27 = (bf16[2,1,112,256]{3,2,1,0:T(8,128)(2,1)}, bf16[2,1,112,256]{3,2,1,0:T(8,128)(2,1)S(1)}, u32[]{:S(2)}, u32[]{:S(2)}) collective-permute-start(bf16[2,1,112,256]{3,2,1,0:T(8,128)(2,1)} %get-tuple-element.25), channel_id=1, source_target_pairs={{0,8},{1,25},{8,0},{9,17},{16,24},{17,9},{24,16},{25,1},{2,10},{3,... | collective-permute-start | bytes 344072 | tf_op jit(solution)/shard_map/ppermute | solution.py:370
  184.3 0.6 copy-start.6
  186.6 6.5 %collective-permute-start.28 = (bf16[1,1,112,256]{3,2,1,0:T(8,128)(2,1)}, bf16[1,1,112,256]{3,2,1,0:T(8,128)(2,1)S(1)}, u32[]{:S(2)}, u32[]{:S(2)}) collective-permute-start(bf16[1,1,112,256]{3,2,1,0:T(8,128)(2,1)} %get-tuple-element.27), channel_id=1, source_target_pairs={{0,24},{1,9},{8,16},{9,1},{16,8},{17,25},{24,0},{25,17},{2,26},{3,... | collective-permute-start | bytes 172040 | tf_op jit(solution)/shard_map/ppermute | solution.py:370
  193.1 0.6 copy-start.7
where the time goes:
time: 197 us
  waiting for transfers between devices  93.8 us (48%)
  starting transfers between devices  43.9 us (22%)
  Pallas kernels  42.8 us (22%)
  local copies, waits for them, and re-layouts  11.7 us (6%)
  other arithmetic  3.62 us (2%)
    ppermute x19, waiting for transfers between devices, swap(): return lax.ppermute(array, (axis, 'c'), ring_pairs(first))  63.7 us
    ppermute x19, starting transfers between devices, swap(): return lax.ppermute(array, (axis, 'c'), ring_pairs(first))  34.1 us
    pallas_call x1, Pallas kernels, per_device(): call(sequence_kernel, [shape(LAYERS, SENT, BLOCK)], [SMEM] + [ANY] * 16 +...  29.6 us
    all_to_all x1, waiting for transfers between devices, per_device(): got = lax.all_to_all(sent, SECTION, 0, 0, tiled=True)  22.7 us
    pallas_call x4, Pallas kernels, per_device(): call(functools.partial(add_kernel, axis), [shape(*out), shape(*out)], [VM...  7.89 us
    unnamed x25, local copies, waits for them, and re-layouts  7.88 us
    all_to_all x1, starting transfers between devices, per_device(): got = lax.all_to_all(sent, SECTION, 0, 0, tiled=True)  7.49 us
    ppermute x1, waiting for transfers between devices, per_device(): other = lax.ppermute(along, ('zl', 'zh', 'c'), pairs)  4.4 us
  transfers between devices with their start and end apart: 30, of which 16 were waited for; matrix products, arithmetic and copies ran while one was open for 2% of the time, Pallas kernels for 0%

commit v1 on v0

--- a/solution.py
+++ b/solution.py
@@ -1,5 +1,3 @@
-import functools
-
 import jax
 import jax.numpy as jnp
 from jax import lax
@@ -119,8 +117,17 @@
 def sequence_kernel(pos_ref, *refs):
     left, right = refs[:8], refs[8:16]
     entry_ref, cot_ref, sent_ref = refs[16:19]
-    w_scr, rows_scr, xs, ns, mixed_scr, decay_scr, write_scr, small_scr, proj_scr, sem_a, sem_b = refs[19:]
-    x, y, c, valid = pos_ref[0], pos_ref[1], pos_ref[2], pos_ref[3]
+    w_scr, rows_scr, xs, ns, mixed_scr, decay_scr, write_scr, small_scr, proj_scr = refs[19:28]
+    first_scr, sem_a, sem_b, sem_c = refs[28:]
+    x, y, c, zh, section = (pos_ref[i] for i in range(5))
+    mine = jnp.minimum(section, SEQS - 1)
+    loads = []
+    for i, ref in enumerate((entry_ref, cot_ref)):
+        copy = pltpu.make_async_copy(
+            ref.at[mine // 3, mine % 3], first_scr.at[i], sem_c.at[i]
+        )
+        copy.start()
+        loads.append(copy)
 
     def ring(i, core):
         one, two = partner(i, core, True), partner(i, core, False)
@@ -207,7 +214,9 @@
         mixed_scr[layer] = mixed.astype(BF16)
         return (x_f + scale * mixed).astype(BF16)
 
-    lax.fori_loop(0, LAYERS, forward, entry_ref[...])
+    loads[0].wait()
+    loads[1].wait()
+    lax.fori_loop(0, LAYERS, forward, first_scr[0])
 
     def backward(step, back):
         layer = LAYERS - 1 - step
@@ -276,23 +285,32 @@
         ).astype(BF16)
         return (dy + inv_rms * (d_hat - x_hat * mean)).astype(BF16)
 
-    cot = jnp.where(valid > 0, cot_ref[...].astype(F32), 0.0).astype(BF16)
+    cot = jnp.where(section < SEQS, first_scr[1].astype(F32), 0.0).astype(BF16)
     lax.fori_loop(0, LAYERS, backward, cot)
 
 
-def weight_kernel(pos_ref, got_ref, keep_ref, send_ref, scr, sem):
-    zh, y, c = pos_ref[0], pos_ref[1], pos_ref[2]
+def weight_kernel(pos_ref, got_ref, keep_ref, send_ref, got, scr, sem_in, sem):
+    y, c, zh = pos_ref[1], pos_ref[2], pos_ref[3]
+    loads = []
+    for m in list(range(BLOCKS)) + [BLOCKS]:
+        at = pl.ds(T * m, T if m < BLOCKS else T + 16)
+        loads.append(pltpu.make_async_copy(got_ref.at[:, at], got.at[:, at], sem_in.at[m]))
+    loads[-1].start()
+    for copy in loads[:-1]:
+        copy.start()
 
     def slot(there, here, core):
         bits = gray(jnp.int32(there)) ^ gray(here)
         return bits if core else (bits & 1) * 2 + (bits >> 1)
 
-    tokens = jnp.concatenate([got_ref[s, TOK : TOK + T] for s in range(LAYERS)], axis=0)
-    extra = sum(got_ref[s, TOK + T :].astype(F32) for s in range(LAYERS))
+    loads[-1].wait()
+    tokens = jnp.concatenate([got[s, TOK : TOK + T] for s in range(LAYERS)], axis=0)
+    extra = sum(got[s, TOK + T :].astype(F32) for s in range(LAYERS))
     bias = jnp.sum(tokens[:, 256:].astype(F32), axis=0, keepdims=True)
     bias = jnp.concatenate([bias[:, :ROWS]] * 4, axis=1)
     for m in range(BLOCKS):
-        normed = jnp.concatenate([got_ref[s, T * m : T * (m + 1)] for s in range(LAYERS)], axis=0)
+        loads[m].wait()
+        normed = jnp.concatenate([got[s, T * m : T * (m + 1)] for s in range(LAYERS)], axis=0)
         keys = tn(normed, tokens[:, :256])
         rates = tn(tokens[:, 256:], normed)[:H]
         rows = jnp.concatenate(
@@ -302,34 +320,22 @@
         low = cut_rows(rows)
         for i in range(4):
             d = 4 * m + i
-            z_at, y_at = slot(d // 8, zh, d % 2), slot(d // 2 % 4, y, d % 2)
+            y_at, z_at = slot(d // 2 % 4, y, d % 2), slot(d // 8, zh, d % 2)
             c_at = (d + c) % 2
-            scr[c_at, z_at, y_at, :ROWS] = keys[ROWS * i : ROWS * (i + 1)].astype(BF16)
-            scr[c_at, z_at, y_at, ROWS:] = low[i].astype(BF16)
+            scr[c_at, y_at, z_at, :ROWS] = keys[ROWS * i : ROWS * (i + 1)].astype(BF16)
+            scr[c_at, y_at, z_at, ROWS:] = low[i].astype(BF16)
     for i, ref in enumerate((keep_ref, send_ref)):
         pltpu.make_async_copy(scr.at[i], ref, sem.at[i]).start()
     for i, ref in enumerate((keep_ref, send_ref)):
         pltpu.make_async_copy(scr.at[i], ref, sem.at[i]).wait()
 
 
-def add_kernel(axis, a_ref, b_ref, keep_ref, send_ref):
-    total = (a_ref[...].astype(F32) + b_ref[...].astype(F32)).astype(BF16)
-    if axis == 1:
-        half = total.shape[1] // 2
-        keep_ref[...] = total[:, :half]
-        send_ref[...] = total[:, half:]
-    else:
-        half = total.shape[0] // 2
-        keep_ref[...] = total[:half]
-        send_ref[...] = total[half:]
-
-
-def final_kernel(a_ref, b_ref, scales_ref, keys_ref, rates_ref, bias_ref):
-    total = a_ref[0].astype(F32) + b_ref[0].astype(F32)
+def final_kernel(a_ref, b_ref, c_ref, d_ref, scales_ref, keys_ref, rates_ref, bias_ref):
+    total = a_ref[...].astype(F32) + b_ref[...].astype(F32)
+    total = total + c_ref[...].astype(F32) + d_ref[...].astype(F32)
     keys_ref[...] = total[:ROWS]
     rates = jnp.concatenate([total[ROWS:, :C], total[ROWS:, C:]], axis=0)
-    wide = jnp.concatenate([rates, jnp.zeros((C - T, C), F32)], axis=0)
-    rates_ref[...] = wide.T[:ROWS, :H]
+    rates_ref[...] = rates[:H, :ROWS]
     scales_ref[...] = rates[24:26, :ROWS]
     bias_ref[...] = rates[26:27, :H]
 
@@ -374,18 +380,24 @@
     return lax.ppermute(array, "c", [(0, 1), (1, 0)])
 
 
-def gather_ring(array, axis):
+def opposite(array, axis):
+    return lax.ppermute(array, axis, [(i, i ^ 2) for i in range(4)])
+
+
+def gather_ring(array, axis, direct=False):
     one = swap(array, axis, True)
     two = swap(array, axis, False)
-    return [array, one, two, swap(one, axis, False)]
+    return [array, one, two, opposite(array, axis) if direct else swap(one, axis, False)]
+
+
+def add(a, b):
+    return (a.astype(F32) + b.astype(F32)).astype(BF16)
 
 
 def per_device(entries, cotangents, scales, key_weight, rate_weight, rate_bias):
     x, zl, zh, y, c = (lax.axis_index(a) for a in ("x", "zl", "zh", "y", "c"))
     section = x * 2 + zl
-    mine = jnp.minimum(section, SEQS - 1)
-    stream = lax.dynamic_index_in_dim(entries.reshape(SEQS, T, D), mine, 0, keepdims=False)
-    back = lax.dynamic_index_in_dim(cotangents.reshape(SEQS, T, D), mine, 0, keepdims=False)
+    pos = jnp.stack([x, y, c, zh, section]).astype(jnp.int32)
 
     wide = jnp.pad(rate_weight[0].T, ((0, 0), (0, C - ROWS)))
     small = jnp.pad(scales[0], ((0, 0), (0, C - ROWS)))
@@ -395,7 +407,7 @@
         [key_weight[0], jnp.concatenate([wide[:16], right], axis=1)], axis=0
     )
 
-    along = jnp.stack(gather_ring(packed, "zh"))
+    along = jnp.stack(gather_ring(packed, "zh", direct=True))
     first, second = partner(zh, c, True), partner(zh, c, False)
     across = partner(second, c, True)
     order = [jnp.where(j == first, 1, jnp.where(j == second, 2, jnp.where(j == across, 3, 0))) for j in range(4)]
@@ -415,11 +427,10 @@
     left = left + [other_core(a) for a in left]
     right = right + [other_core(a) for a in right]
 
-    pos = jnp.stack([x, y, c, jnp.where(section < SEQS, 1, 0)]).astype(jnp.int32)
     sent = call(
         sequence_kernel,
         [shape(LAYERS, SENT, BLOCK)],
-        [SMEM] + [ANY] * 16 + [VMEM] * 2,
+        [SMEM] + [ANY] * 18,
         [
             pltpu.VMEM((LAYERS, 4, 4, 2, PIECE, 256), BF16),
             pltpu.VMEM((LAYERS, T, D), BF16),
@@ -430,51 +441,54 @@
             pltpu.VMEM((LAYERS, 1, W), F32),
             pltpu.VMEM((LAYERS, T, 256), F32),
             pltpu.VMEM((LAYERS, T, 256), F32),
+            pltpu.VMEM((2, T, D), BF16),
             pltpu.SemaphoreType.DMA((4,)),
             pltpu.SemaphoreType.DMA((4,)),
+            pltpu.SemaphoreType.DMA((2,)),
         ],
         cost=(8_000_000_000, 30_000_000),
-    )(pos, *left, *right, stream, back)[0]
+    )(pos, *left, *right, entries, cotangents)[0]
 
     got = lax.all_to_all(sent, SECTION, 0, 0, tiled=True)
-    pos = jnp.stack([zh, y, c]).astype(jnp.int32)
     half = shape(4, 4, PIECE, 256)
     keep, send = call(
         weight_kernel,
         [half, half],
-        [SMEM, VMEM],
-        [pltpu.VMEM((2, 4, 4, PIECE, 256), BF16), pltpu.SemaphoreType.DMA((2,))],
+        [SMEM, ANY],
+        [
+            pltpu.VMEM((LAYERS, SENT, BLOCK), BF16),
+            pltpu.VMEM((2, 4, 4, PIECE, 256), BF16),
+            pltpu.SemaphoreType.DMA((BLOCKS + 1,)),
+            pltpu.SemaphoreType.DMA((2,)),
+        ],
         [ANY] * 2,
         cost=(600_000_000, 4_000_000),
     )(pos, got)
     got = other_core(send)
-    for axis, first, out in (
-        (1, True, (4, 2, PIECE, 256)),
-        (1, False, (4, 1, PIECE, 256)),
-        (0, True, (2, 1, PIECE, 256)),
-        (0, False, (1, 1, PIECE, 256)),
-    ):
-        keep, send = call(
-            functools.partial(add_kernel, axis),
-            [shape(*out), shape(*out)],
-            [VMEM] * 2,
-            [],
-            cost=(1_000_000, 4_000_000),
-        )(keep, got)
-        got = swap(send, "y" if axis == 1 else "zh", first)
+    got = swap(add(keep[2:], got[2:]), "y", True), keep[:2], got[:2]
+    keep = add(got[1], got[2])
+    got = got[0]
+    got, keep = swap(add(keep[1], got[1]), "y", False), add(keep[0], got[0])
+    got = add(keep, got)
+    parts = [
+        got[0],
+        swap(got[2], "zh", True),
+        swap(got[1], "zh", False),
+        opposite(got[3], "zh"),
+    ]
     g_scales, g_keys, g_rates, g_bias = call(
         final_kernel,
         [
             shape(2, ROWS, dtype=F32),
             shape(ROWS, 256, dtype=F32),
-            shape(ROWS, H, dtype=F32),
+            shape(H, ROWS, dtype=F32),
             shape(1, H, dtype=F32),
         ],
-        [VMEM] * 2,
+        [VMEM] * 4,
         [],
         cost=(0, 500_000),
-    )(keep[0], got[0])
-    return g_scales[None], g_keys[None], g_rates[None], g_bias
+    )(*parts)
+    return g_scales[None], g_keys[None], g_rates.T[None], g_bias
 
 
 def solution(mesh):

time: 197 us -> 186 us (0.944)
  blocking collectives: 0 us -> 31 us
  waiting for transfers between devices: 93.8 us -> 65.3 us
  Pallas kernels: 42.8 us -> 36.3 us
  local copies, waits for them, and re-layouts: 11.7 us -> 5.39 us
    all_to_all x0 -> x1, blocking collectives: none -> 31 us  [per_device(): got = lax.all_to_all(sent, SECTION, 0, 0, tiled=True)]
    all_to_all x1 -> x0, waiting for transfers between devices: 22.7 us -> none  [per_device(): got = lax.all_to_all(sent, SECTION, 0, 0, tiled=True)]
    ppermute x19 -> x18, waiting for transfers between devices: 63.7 us -> 49.8 us  [swap(): return lax.ppermute(array, (axis, 'c'), ring_pairs(first))]
    all_to_all x1 -> x0, starting transfers between devices: 7.49 us -> none  [per_device(): got = lax.all_to_all(sent, SECTION, 0, 0, tiled=True)]
    pallas_call x6 -> x2, Pallas kernels: 41.2 us -> 34.7 us  [the longest x1 29.3 us: per_device(): call(sequence_kernel, [shape(LAYERS, SENT, BLOCK)], [SMEM] + [ANY] * 18,...]
    ppermute x0 -> x2, waiting for transfers between devices: none -> 5.87 us  [opposite(): return lax.ppermute(array, axis, [(i, i ^ 2) for i in range(4)])]
    unnamed x25 -> x18, local copies, waits for them, and re-layouts: 7.88 us -> 2.06 us
    ppermute x19 -> x18, starting transfers between devices: 34.1 us -> 38.6 us  [swap(): return lax.ppermute(array, (axis, 'c'), ring_pairs(first))]
  transfers between devices with their start and end apart: 30 -> 30, of which waited for: 16 -> 18; matrix products, arithmetic and copies ran while one was open for 2% -> 1% of each run, Pallas kernels for 0% -> 0%
where the time goes in v1:
time: 186 us
  waiting for transfers between devices  65.3 us (35%)
  starting transfers between devices  42.8 us (23%)
  Pallas kernels  36.3 us (20%)
  blocking collectives  31 us (17%)
  local copies, waits for them, and re-layouts  5.39 us (3%)
  other arithmetic  3.93 us (2%)
    ppermute x18, waiting for transfers between devices, swap(): return lax.ppermute(array, (axis, 'c'), ring_pairs(first))  49.8 us
    ppermute x18, starting transfers between devices, swap(): return lax.ppermute(array, (axis, 'c'), ring_pairs(first))  38.6 us
    all_to_all x1, blocking collectives, per_device(): got = lax.all_to_all(sent, SECTION, 0, 0, tiled=True)  31 us
    pallas_call x1, Pallas kernels, per_device(): call(sequence_kernel, [shape(LAYERS, SENT, BLOCK)], [SMEM] + [ANY] * 18,...  29.3 us
    ppermute x2, waiting for transfers between devices, opposite(): return lax.ppermute(array, axis, [(i, i ^ 2) for i in range(4)])  5.87 us
    pallas_call x1, Pallas kernels, per_device(): call(weight_kernel, [half, half], [SMEM, ANY], [pltpu.VMEM((LAYERS, SENT,...  5.38 us
    ppermute x9, waiting for transfers between devices, other_core(): return lax.ppermute(array, 'c', [(0, 1), (1, 0)])  4.85 us
    ppermute x1, waiting for transfers between devices, per_device(): other = lax.ppermute(along, ('zl', 'zh', 'c'), pairs)  4.83 us
  transfers between devices with their start and end apart: 30, of which 18 were waited for; matrix products, arithmetic and copies ran while one was open for 1% of the time, Pallas kernels for 0%

profile of v1, /device:TPU:2, one launch (start us, length us, event | category | flops | bytes accessed | tf_op | source)
XLA Modules:
  0.0 185.5 jit_solution(16468305269219320981)
XLA Ops:
  0.6 0.7 pad_slice_fusion
  1.3 0.7 pad_slice_fusion.1
  2.0 0.8 maximum_maximum_fusion
  2.9 6.4 %collective-permute-start.1 = (bf16[112,256]{1,0:T(8,128)(2,1)S(1)}, bf16[112,256]{1,0:T(8,128)(2,1)S(1)}, u32[]{:S(2)}, u32[]{:S(2)}) collective-permute-start(bf16[112,256]{1,0:T(8,128)(2,1)S(1)} %maximum_maximum_fusion), channel_id=1, source_target_pairs={{0,24},{1,9},{8,16},{9,1},{16,8},{17,25},{24,0},{25,17},{2,26},{3,... | collective-permute-start | bytes 172040 | tf_op jit(solution)/shard_map/ppermute | solution.py:376
  9.2 1.5 collective-permute-start
  10.7 1.0 collective-permute-start.2
  11.7 0.8 fusion.15
  12.8 1.6 collective-permute-done.1
  14.4 1.1 collective-permute-done
  15.6 3.6 %collective-permute-done.2 = bf16[112,256]{1,0:T(8,128)(2,1)S(1)} collective-permute-done((bf16[112,256]{1,0:T(8,128)(2,1)S(1)}, bf16[112,256]{1,0:T(8,128)(2,1)S(1)}, u32[]{:S(2)}, u32[]{:S(2)}) %collective-permute-start.2) | collective-permute-done | bytes 57376 | tf_op jit(solution)/shard_map/ppermute | solution.py:384
  19.9 1.2 collective-permute-start.3
  21.2 4.8 %collective-permute-done.3 = bf16[4,112,256]{2,1,0:T(8,128)(2,1)S(1)} collective-permute-done((bf16[4,112,256]{2,1,0:T(8,128)(2,1)S(1)}, bf16[4,112,256]{2,1,0:T(8,128)(2,1)S(1)}, u32[]{:S(2)}, u32[]{:S(2)}) %collective-permute-start.3) | collective-permute-done | bytes 229408 | tf_op jit(solution)/shard_map/ppermute | solution.py:420
  26.2 0.6 collective-permute-start.4
  26.8 1.6 collective-permute-start.14
  28.4 2.2 %collective-permute-start.5 = (bf16[2,4,112,128]{3,2,1,0:T(8,128)(2,1)S(1)}, bf16[2,4,112,128]{3,2,1,0:T(8,128)(2,1)S(1)}, u32[]{:S(2)}, u32[]{:S(2)}) collective-permute-start(bf16[2,4,112,128]{3,2,1,0:T(8,128)(2,1)S(1)} %get-tuple-element.21), channel_id=1, source_target_pairs={{0,192},{1,65},{64,128},{65,1},{128,64},{129,193},{192,0},{193,129... | collective-permute-start | bytes 688136 | tf_op jit(solution)/shard_map/ppermute | solution.py:376
  30.5 2.3 %collective-permute-done.4 = bf16[2,4,112,128]{3,2,1,0:T(8,128)(2,1)S(1)} collective-permute-done((bf16[2,4,112,128]{3,2,1,0:T(8,128)(2,1)S(1)}, bf16[2,4,112,128]{3,2,1,0:T(8,128)(2,1)S(1)}, u32[]{:S(2)}, u32[]{:S(2)}) %collective-permute-start.4) | collective-permute-done | bytes 229408 | tf_op jit(solution)/shard_map/ppermute | solution.py:376
  32.9 2.6 %collective-permute-start.6 = (bf16[2,4,112,128]{3,2,1,0:T(8,128)(2,1)S(1)}, bf16[2,4,112,128]{3,2,1,0:T(8,128)(2,1)S(1)}, u32[]{:S(2)}, u32[]{:S(2)}) collective-permute-start(bf16[2,4,112,128]{3,2,1,0:T(8,128)(2,1)S(1)} %collective-permute-done.4), channel_id=1, source_target_pairs={{0,192},{1,65},{64,128},{65,1},{128,64},{129,193},{192,0},{193,129... | collective-permute-start | bytes 688136 | tf_op jit(solution)/shard_map/ppermute | solution.py:376
  35.5 2.3 %collective-permute-start.15 = (bf16[2,4,112,128]{3,2,1,0:T(8,128)(2,1)S(1)}, bf16[2,4,112,128]{3,2,1,0:T(8,128)(2,1)S(1)}, u32[]{:S(2)}, u32[]{:S(2)}) collective-permute-start(bf16[2,4,112,128]{3,2,1,0:T(8,128)(2,1)S(1)} %get-tuple-element.20), channel_id=1, source_target_pairs={{0,6},{1,3},{2,4},{3,1},{4,2},{5,7},{6,0},{7,5},{8,14},{9,11},{10,... | collective-permute-start | bytes 688136 | tf_op jit(solution)/shard_map/ppermute | solution.py:376
  37.8 1.0 collective-permute-start.16
  38.7 0.8 collective-permute-done.6
  39.7 4.4 %collective-permute-start.8 = (bf16[4,2,4,112,128]{4,3,2,1,0:T(8,128)(2,1)S(1)}, bf16[4,2,4,112,128]{4,3,2,1,0:T(8,128)(2,1)S(1)}, u32[]{:S(2)}, u32[]{:S(2)}) collective-permute-start(bf16[4,2,4,112,128]{4,3,2,1,0:T(8,128)(2,1)S(1)} %pad_maximum_fusion.refs_0_), channel_id=1, source_target_pairs={{0,6},{1,3},{2,4},{3,1},{4,2},{5,7},{6,0},{7,5},{8,14},{9,11},{10,... | collective-permute-start | bytes 2752520 | tf_op jit(solution)/shard_map/ppermute | solution.py:376
  44.2 1.0 collective-permute-done.16
  45.3 1.9 %collective-permute-start.17 = (bf16[4,2,4,112,128]{4,3,2,1,0:T(8,128)(2,1)S(1)}, bf16[4,2,4,112,128]{4,3,2,1,0:T(8,128)(2,1)}, u32[]{:S(2)}, u32[]{:S(2)}) collective-permute-start(bf16[4,2,4,112,128]{4,3,2,1,0:T(8,128)(2,1)S(1)} %pad_maximum_fusion.1.refs_8_), channel_id=1, source_target_pairs={{0,64},{1,193},{64,0},{65,129},{128,192},{129,65},{192,128},{193,1... | collective-permute-start | bytes 2752520 | tf_op jit(solution)/shard_map/ppermute | solution.py:376
  47.3 0.9 collective-permute-start.18
  48.2 16.5 %collective-permute-done.8.refs_2_ = bf16[4,2,4,112,128]{4,3,2,1,0:T(8,128)(2,1)S(1)} collective-permute-done((bf16[4,2,4,112,128]{4,3,2,1,0:T(8,128)(2,1)S(1)}, bf16[4,2,4,112,128]{4,3,2,1,0:T(8,128)(2,1)S(1)}, u32[]{:S(2)}, u32[]{:S(2)}) %collective-permute-start.8) | collective-permute-done | bytes 917536 | tf_op jit(solution)/shard_map/ppermute | solution.py:376
  64.7 3.8 %collective-permute-start.9 = (bf16[4,2,4,112,128]{4,3,2,1,0:T(8,128)(2,1)}, bf16[4,2,4,112,128]{4,3,2,1,0:T(8,128)(2,1)}, u32[]{:S(2)}, u32[]{:S(2)}) collective-permute-start(bf16[4,2,4,112,128]{4,3,2,1,0:T(8,128)(2,1)} %collective-permute-done.7.refs_1_), channel_id=1, source_target_pairs={{0,6},{1,3},{2,4},{3,1},{4,2},{5,7},{6,0},{7,5},{8,14},{9,11},{10,... | collective-permute-start | bytes 2752520 | tf_op jit(solution)/shard_map/ppermute | solution.py:376
  68.5 1.7 collective-permute-start.19
  71.2 1.0 copy-done.8
  72.2 8.0 %collective-permute-done.9.refs_3_ = bf16[4,2,4,112,128]{4,3,2,1,0:T(8,128)(2,1)} collective-permute-done((bf16[4,2,4,112,128]{4,3,2,1,0:T(8,128)(2,1)}, bf16[4,2,4,112,128]{4,3,2,1,0:T(8,128)(2,1)}, u32[]{:S(2)}, u32[]{:S(2)}) %collective-permute-start.9) | collective-permute-done | bytes 917536 | tf_op jit(solution)/shard_map/ppermute | solution.py:376
  80.2 2.0 %collective-permute-done.19.refs_11_ = bf16[4,2,4,112,128]{4,3,2,1,0:T(8,128)(2,1)} collective-permute-done((bf16[4,2,4,112,128]{4,3,2,1,0:T(8,128)(2,1)}, bf16[4,2,4,112,128]{4,3,2,1,0:T(8,128)(2,1)}, u32[]{:S(2)}, u32[]{:S(2)}) %collective-permute-start.19) | collective-permute-done | bytes 917536 | tf_op jit(solution)/shard_map/ppermute | solution.py:376
  82.2 0.6 stack.105.pos_ref
  83.0 2.0 %collective-permute-done.23.refs_15_ = bf16[4,2,4,112,128]{4,3,2,1,0:T(8,128)(2,1)} collective-permute-done((bf16[4,2,4,112,128]{4,3,2,1,0:T(8,128)(2,1)}, bf16[4,2,4,112,128]{4,3,2,1,0:T(8,128)(2,1)}, u32[]{:S(2)}, u32[]{:S(2)}) %collective-permute-start.23) | collective-permute-done | bytes 917536 | tf_op jit(solution)/shard_map/ppermute | solution.py:380
  85.0 29.3 %shard_map.93 = bf16[8,304,384]{2,1,0:T(8,128)(2,1)} custom-call(s32[5]{0:T(128)} %stack.105.pos_ref, bf16[4,2,4,112,128]{4,3,2,1,0:T(8,128)(2,1)} %copy-done, bf16[4,2,4,112,128]{4,3,2,1,0:T(8,128)(2,1)} %collective-permute-done.7.refs_1_, bf16[4,2,4,112,128]{4,3,2,1,0:T(8,128)(2,1)} %copy-done.6, ...), custom_call_target="tpu_custom_call" | custom-call | flops 8000000000 | bytes 30000000 | tf_op jit(solution)/shard_map/pallas_call | solution.py:430
  114.4 31.0 %all_to_all.5.got_ref = bf16[8,304,384]{2,1,0:T(8,128)(2,1)} all-to-all(bf16[8,304,384]{2,1,0:T(8,128)(2,1)} %shard_map.93), channel_id=1, replica_groups=mesh['x'=4,'zl'=2,'zh'=4,'y'=4,'c'=2] {'x','zl'}, dimensions={0} | all-to-all | bytes 3735552 | tf_op jit(solution)/shard_map/all_to_all | solution.py:452
  145.3 5.4 %shard_map.94 = (bf16[4,4,112,256]{3,2,1,0:T(8,128)(2,1)}, bf16[4,4,112,256]{3,2,1,0:T(8,128)(2,1)}) custom-call(s32[5]{0:T(128)} %stack.105.pos_ref, bf16[8,304,384]{2,1,0:T(8,128)(2,1)} %all_to_all.5.got_ref), custom_call_target="tpu_custom_call" | custom-call | flops 600000000 | bytes 4000000 | tf_op jit(solution)/shard_map/pallas_call | solution.py:454
  150.8 2.7 %collective-permute-done.24 = bf16[4,4,112,256]{3,2,1,0:T(8,128)(2,1)S(1)} collective-permute-done((bf16[4,4,112,256]{3,2,1,0:T(8,128)(2,1)}, bf16[4,4,112,256]{3,2,1,0:T(8,128)(2,1)S(1)}, u32[]{:S(2)}, u32[]{:S(2)}) %collective-permute-start.24) | collective-permute-done | bytes 917536 | tf_op jit(solution)/shard_map/ppermute | solution.py:380
  153.5 1.4 add_convert_fusion.1
  154.9 0.7 collective-permute-start.25
  155.7 7.8 %collective-permute-done.25 = bf16[2,4,112,256]{3,2,1,0:T(8,128)(2,1)S(1)} collective-permute-done((bf16[2,4,112,256]{3,2,1,0:T(8,128)(2,1)S(1)}, bf16[2,4,112,256]{3,2,1,0:T(8,128)(2,1)S(1)}, u32[]{:S(2)}, u32[]{:S(2)}) %collective-permute-start.25) | collective-permute-done | bytes 458784 | tf_op jit(solution)/shard_map/ppermute | solution.py:376
  163.6 1.7 collective-permute-start.26
  165.3 5.6 %collective-permute-done.26 = bf16[4,112,256]{2,1,0:T(8,128)(2,1)S(1)} collective-permute-done((bf16[4,112,256]{2,1,0:T(8,128)(2,1)S(1)}, bf16[4,112,256]{2,1,0:T(8,128)(2,1)S(1)}, u32[]{:S(2)}, u32[]{:S(2)}) %collective-permute-start.26) | collective-permute-done | bytes 229408 | tf_op jit(solution)/shard_map/ppermute | solution.py:376
  171.0 0.6 slice_bitcast_fusion
  171.6 1.2 collective-permute-start.29
  172.8 4.8 %collective-permute-start.28 = (bf16[112,256]{1,0:T(8,128)(2,1)S(1)}, bf16[112,256]{1,0:T(8,128)(2,1)S(1)}, u32[]{:S(2)}, u32[]{:S(2)}) collective-permute-start(bf16[112,256]{1,0:T(8,128)(2,1)S(1)} %get-tuple-element.23), channel_id=1, source_target_pairs={{0,24},{1,9},{8,16},{9,1},{16,8},{17,25},{24,0},{25,17},{2,26},{3,... | collective-permute-start | bytes 172040 | tf_op jit(solution)/shard_map/ppermute | solution.py:376
  178.1 2.2 %collective-permute-done.29.d_ref = bf16[112,256]{1,0:T(8,128)(2,1)S(1)} collective-permute-done((bf16[112,256]{1,0:T(8,128)(2,1)S(1)}, bf16[112,256]{1,0:T(8,128)(2,1)S(1)}, u32[]{:S(2)}, u32[]{:S(2)}) %collective-permute-start.29) | collective-permute-done | bytes 57376 | tf_op jit(solution)/shard_map/ppermute | solution.py:384
  180.3 1.2 collective-permute-done.28.c_ref
  181.5 1.8 collective-permute-done.27.b_ref
  184.0 1.6 shard_map.95
  (55 shorter events, 4.0 us)
Async XLA Ops:
  2.9 11.6 %collective-permute-start.1 = (bf16[112,256]{1,0:T(8,128)(2,1)S(1)}, bf16[112,256]{1,0:T(8,128)(2,1)S(1)}, u32[]{:S(2)}, u32[]{:S(2)}) collective-permute-start(bf16[112,256]{1,0:T(8,128)(2,1)S(1)} %maximum_maximum_fusion), channel_id=1, source_target_pairs={{0,24},{1,9},{8,16},{9,1},{16,8},{17,25},{24,0},{25,17},{2,26},{3,... | collective-permute-start | bytes 172040 | tf_op jit(solution)/shard_map/ppermute | solution.py:376
  9.2 6.3 %collective-permute-start = (bf16[112,256]{1,0:T(8,128)(2,1)S(1)}, bf16[112,256]{1,0:T(8,128)(2,1)S(1)}, u32[]{:S(2)}, u32[]{:S(2)}) collective-permute-start(bf16[112,256]{1,0:T(8,128)(2,1)S(1)} %maximum_maximum_fusion), channel_id=1, source_target_pairs={{0,8},{1,25},{8,0},{9,17},{16,24},{17,9},{24,16},{25,1},{2,10},{3,... | collective-permute-start | bytes 172040 | tf_op jit(solution)/shard_map/ppermute | solution.py:376
  10.7 8.5 %collective-permute-start.2 = (bf16[112,256]{1,0:T(8,128)(2,1)S(1)}, bf16[112,256]{1,0:T(8,128)(2,1)S(1)}, u32[]{:S(2)}, u32[]{:S(2)}) collective-permute-start(bf16[112,256]{1,0:T(8,128)(2,1)S(1)} %maximum_maximum_fusion), channel_id=1, source_target_pairs={{0,16},{8,24},{16,0},{24,8},{1,17},{9,25},{17,1},{25,9},{2,18},{10... | collective-permute-start | bytes 172040 | tf_op jit(solution)/shard_map/ppermute | solution.py:384
  19.9 6.1 %collective-permute-start.3 = (bf16[4,112,256]{2,1,0:T(8,128)(2,1)S(1)}, bf16[4,112,256]{2,1,0:T(8,128)(2,1)S(1)}, u32[]{:S(2)}, u32[]{:S(2)}) collective-permute-start(bf16[4,112,256]{2,1,0:T(8,128)(2,1)S(1)} %broadcast_select_fusion), channel_id=1, source_target_pairs={{0,32},{1,57},{32,0},{33,9},{8,40},{9,33},{40,8},{41,17},{16,48},{... | collective-permute-start | bytes 688136 | tf_op jit(solution)/shard_map/ppermute | solution.py:420
  26.2 6.7 %collective-permute-start.4 = (bf16[2,4,112,128]{3,2,1,0:T(8,128)(2,1)S(1)}, bf16[2,4,112,128]{3,2,1,0:T(8,128)(2,1)S(1)}, u32[]{:S(2)}, u32[]{:S(2)}) collective-permute-start(bf16[2,4,112,128]{3,2,1,0:T(8,128)(2,1)S(1)} %get-tuple-element.21), channel_id=1, source_target_pairs={{0,64},{1,193},{64,0},{65,129},{128,192},{129,65},{192,128},{193,1... | collective-permute-start | bytes 688136 | tf_op jit(solution)/shard_map/ppermute | solution.py:376
  26.8 10.9 %collective-permute-start.14 = (bf16[2,4,112,128]{3,2,1,0:T(8,128)(2,1)S(1)}, bf16[2,4,112,128]{3,2,1,0:T(8,128)(2,1)S(1)}, u32[]{:S(2)}, u32[]{:S(2)}) collective-permute-start(bf16[2,4,112,128]{3,2,1,0:T(8,128)(2,1)S(1)} %get-tuple-element.20), channel_id=1, source_target_pairs={{0,2},{1,7},{2,0},{3,5},{4,6},{5,3},{6,4},{7,1},{8,10},{9,15},{10,... | collective-permute-start | bytes 688136 | tf_op jit(solution)/shard_map/ppermute | solution.py:376
  28.4 10.3 %collective-permute-start.5 = (bf16[2,4,112,128]{3,2,1,0:T(8,128)(2,1)S(1)}, bf16[2,4,112,128]{3,2,1,0:T(8,128)(2,1)S(1)}, u32[]{:S(2)}, u32[]{:S(2)}) collective-permute-start(bf16[2,4,112,128]{3,2,1,0:T(8,128)(2,1)S(1)} %get-tuple-element.21), channel_id=1, source_target_pairs={{0,192},{1,65},{64,128},{65,1},{128,64},{129,193},{192,0},{193,129... | collective-permute-start | bytes 688136 | tf_op jit(solution)/shard_map/ppermute | solution.py:376
  32.9 6.6 %collective-permute-start.6 = (bf16[2,4,112,128]{3,2,1,0:T(8,128)(2,1)S(1)}, bf16[2,4,112,128]{3,2,1,0:T(8,128)(2,1)S(1)}, u32[]{:S(2)}, u32[]{:S(2)}) collective-permute-start(bf16[2,4,112,128]{3,2,1,0:T(8,128)(2,1)S(1)} %collective-permute-done.4), channel_id=1, source_target_pairs={{0,192},{1,65},{64,128},{65,1},{128,64},{129,193},{192,0},{193,129... | collective-permute-start | bytes 688136 | tf_op jit(solution)/shard_map/ppermute | solution.py:376
  35.5 8.7 %collective-permute-start.15 = (bf16[2,4,112,128]{3,2,1,0:T(8,128)(2,1)S(1)}, bf16[2,4,112,128]{3,2,1,0:T(8,128)(2,1)S(1)}, u32[]{:S(2)}, u32[]{:S(2)}) collective-permute-start(bf16[2,4,112,128]{3,2,1,0:T(8,128)(2,1)S(1)} %get-tuple-element.20), channel_id=1, source_target_pairs={{0,6},{1,3},{2,4},{3,1},{4,2},{5,7},{6,0},{7,5},{8,14},{9,11},{10,... | collective-permute-start | bytes 688136 | tf_op jit(solution)/shard_map/ppermute | solution.py:376
  37.8 7.4 %collective-permute-start.16 = (bf16[2,4,112,128]{3,2,1,0:T(8,128)(2,1)S(1)}, bf16[2,4,112,128]{3,2,1,0:T(8,128)(2,1)S(1)}, u32[]{:S(2)}, u32[]{:S(2)}) collective-permute-start(bf16[2,4,112,128]{3,2,1,0:T(8,128)(2,1)S(1)} %collective-permute-done.14), channel_id=1, source_target_pairs={{0,6},{1,3},{2,4},{3,1},{4,2},{5,7},{6,0},{7,5},{8,14},{9,11},{10,... | collective-permute-start | bytes 688136 | tf_op jit(solution)/shard_map/ppermute | solution.py:376
  39.6 45.4 %copy-start = (bf16[4,2,4,112,128]{4,3,2,1,0:T(8,128)(2,1)}, bf16[4,2,4,112,128]{4,3,2,1,0:T(8,128)(2,1)S(1)}, u32[]{:S(2)}) copy-start(bf16[4,2,4,112,128]{4,3,2,1,0:T(8,128)(2,1)S(1)} %pad_maximum_fusion.refs_0_) | copy-start | bytes 2752516
  39.6 7.6 %collective-permute-start.10 = (bf16[4,2,4,112,128]{4,3,2,1,0:T(8,128)(2,1)S(1)}, bf16[4,2,4,112,128]{4,3,2,1,0:T(8,128)(2,1)S(1)}, u32[]{:S(2)}, u32[]{:S(2)}) collective-permute-start(bf16[4,2,4,112,128]{4,3,2,1,0:T(8,128)(2,1)S(1)} %pad_maximum_fusion.refs_0_), channel_id=1, source_target_pairs={{0,1},{1,0},{2,3},{3,2},{4,5},{5,4},{6,7},{7,6},{8,9},{9,8},{10,11... | collective-permute-start | bytes 2752520 | tf_op jit(solution)/shard_map/ppermute | solution.py:380
  39.7 25.0 %collective-permute-start.8 = (bf16[4,2,4,112,128]{4,3,2,1,0:T(8,128)(2,1)S(1)}, bf16[4,2,4,112,128]{4,3,2,1,0:T(8,128)(2,1)S(1)}, u32[]{:S(2)}, u32[]{:S(2)}) collective-permute-start(bf16[4,2,4,112,128]{4,3,2,1,0:T(8,128)(2,1)S(1)} %pad_maximum_fusion.refs_0_), channel_id=1, source_target_pairs={{0,6},{1,3},{2,4},{3,1},{4,2},{5,7},{6,0},{7,5},{8,14},{9,11},{10,... | collective-permute-start | bytes 2752520 | tf_op jit(solution)/shard_map/ppermute | solution.py:376
  44.1 20.6 %collective-permute-start.7 = (bf16[4,2,4,112,128]{4,3,2,1,0:T(8,128)(2,1)S(1)}, bf16[4,2,4,112,128]{4,3,2,1,0:T(8,128)(2,1)}, u32[]{:S(2)}, u32[]{:S(2)}) collective-permute-start(bf16[4,2,4,112,128]{4,3,2,1,0:T(8,128)(2,1)S(1)} %pad_maximum_fusion.refs_0_), channel_id=1, source_target_pairs={{0,2},{1,7},{2,0},{3,5},{4,6},{5,3},{6,4},{7,1},{8,10},{9,15},{10,... | collective-permute-start | bytes 2752520 | tf_op jit(solution)/shard_map/ppermute | solution.py:376
  45.3 39.8 %copy-start.1 = (bf16[4,2,4,112,128]{4,3,2,1,0:T(8,128)(2,1)}, bf16[4,2,4,112,128]{4,3,2,1,0:T(8,128)(2,1)S(1)}, u32[]{:S(2)}) copy-start(bf16[4,2,4,112,128]{4,3,2,1,0:T(8,128)(2,1)S(1)} %pad_maximum_fusion.1.refs_8_) | copy-start | bytes 2752516
  45.3 23.2 %collective-permute-start.17 = (bf16[4,2,4,112,128]{4,3,2,1,0:T(8,128)(2,1)S(1)}, bf16[4,2,4,112,128]{4,3,2,1,0:T(8,128)(2,1)}, u32[]{:S(2)}, u32[]{:S(2)}) collective-permute-start(bf16[4,2,4,112,128]{4,3,2,1,0:T(8,128)(2,1)S(1)} %pad_maximum_fusion.1.refs_8_), channel_id=1, source_target_pairs={{0,64},{1,193},{64,0},{65,129},{128,192},{129,65},{192,128},{193,1... | collective-permute-start | bytes 2752520 | tf_op jit(solution)/shard_map/ppermute | solution.py:376
  47.2 23.0 %collective-permute-start.20 = (bf16[4,2,4,112,128]{4,3,2,1,0:T(8,128)(2,1)S(1)}, bf16[4,2,4,112,128]{4,3,2,1,0:T(8,128)(2,1)S(1)}, u32[]{:S(2)}, u32[]{:S(2)}) collective-permute-start(bf16[4,2,4,112,128]{4,3,2,1,0:T(8,128)(2,1)S(1)} %pad_maximum_fusion.1.refs_8_), channel_id=1, source_target_pairs={{0,1},{1,0},{2,3},{3,2},{4,5},{5,4},{6,7},{7,6},{8,9},{9,8},{10,11... | collective-permute-start | bytes 2752520 | tf_op jit(solution)/shard_map/ppermute | solution.py:380
  47.3 37.8 %copy-start.5 = (bf16[4,2,4,112,128]{4,3,2,1,0:T(8,128)(2,1)}, bf16[4,2,4,112,128]{4,3,2,1,0:T(8,128)(2,1)S(1)}, u32[]{:S(2)}) copy-start(bf16[4,2,4,112,128]{4,3,2,1,0:T(8,128)(2,1)S(1)} %collective-permute-done.10.refs_4_) | copy-start | bytes 2752516
  47.3 23.0 %collective-permute-start.18 = (bf16[4,2,4,112,128]{4,3,2,1,0:T(8,128)(2,1)S(1)}, bf16[4,2,4,112,128]{4,3,2,1,0:T(8,128)(2,1)}, u32[]{:S(2)}, u32[]{:S(2)}) collective-permute-start(bf16[4,2,4,112,128]{4,3,2,1,0:T(8,128)(2,1)S(1)} %pad_maximum_fusion.1.refs_8_), channel_id=1, source_target_pairs={{0,192},{1,65},{64,128},{65,1},{128,64},{129,193},{192,0},{193,129... | collective-permute-start | bytes 2752520 | tf_op jit(solution)/shard_map/ppermute | solution.py:376
  64.7 5.5 %copy-start.6 = (bf16[4,2,4,112,128]{4,3,2,1,0:T(8,128)(2,1)}, bf16[4,2,4,112,128]{4,3,2,1,0:T(8,128)(2,1)S(1)}, u32[]{:S(2)}) copy-start(bf16[4,2,4,112,128]{4,3,2,1,0:T(8,128)(2,1)S(1)} %collective-permute-done.8.refs_2_) | copy-start | bytes 2752516
  64.7 6.0 %collective-permute-start.12 = (bf16[4,2,4,112,128]{4,3,2,1,0:T(8,128)(2,1)S(1)}, bf16[4,2,4,112,128]{4,3,2,1,0:T(8,128)(2,1)S(1)}, u32[]{:S(2)}, u32[]{:S(2)}) collective-permute-start(bf16[4,2,4,112,128]{4,3,2,1,0:T(8,128)(2,1)S(1)} %collective-permute-done.8.refs_2_), channel_id=1, source_target_pairs={{0,1},{1,0},{2,3},{3,2},{4,5},{5,4},{6,7},{7,6},{8,9},{9,8},{10,11... | collective-permute-start | bytes 2752520 | tf_op jit(solution)/shard_map/ppermute | solution.py:380
  64.7 15.5 %collective-permute-start.9 = (bf16[4,2,4,112,128]{4,3,2,1,0:T(8,128)(2,1)}, bf16[4,2,4,112,128]{4,3,2,1,0:T(8,128)(2,1)}, u32[]{:S(2)}, u32[]{:S(2)}) collective-permute-start(bf16[4,2,4,112,128]{4,3,2,1,0:T(8,128)(2,1)} %collective-permute-done.7.refs_1_), channel_id=1, source_target_pairs={{0,6},{1,3},{2,4},{3,1},{4,2},{5,7},{6,0},{7,5},{8,14},{9,11},{10,... | collective-permute-start | bytes 2752520 | tf_op jit(solution)/shard_map/ppermute | solution.py:376
  68.5 13.7 %collective-permute-start.19 = (bf16[4,2,4,112,128]{4,3,2,1,0:T(8,128)(2,1)}, bf16[4,2,4,112,128]{4,3,2,1,0:T(8,128)(2,1)}, u32[]{:S(2)}, u32[]{:S(2)}) collective-permute-start(bf16[4,2,4,112,128]{4,3,2,1,0:T(8,128)(2,1)} %collective-permute-done.17.refs_9_), channel_id=1, source_target_pairs={{0,192},{1,65},{64,128},{65,1},{128,64},{129,193},{192,0},{193,129... | collective-permute-start | bytes 2752520 | tf_op jit(solution)/shard_map/ppermute | solution.py:376
  70.2 0.9 copy-start.7
  70.2 12.6 %collective-permute-start.11 = (bf16[4,2,4,112,128]{4,3,2,1,0:T(8,128)(2,1)}, bf16[4,2,4,112,128]{4,3,2,1,0:T(8,128)(2,1)}, u32[]{:S(2)}, u32[]{:S(2)}) collective-permute-start(bf16[4,2,4,112,128]{4,3,2,1,0:T(8,128)(2,1)} %collective-permute-done.7.refs_1_), channel_id=1, source_target_pairs={{0,1},{1,0},{2,3},{3,2},{4,5},{5,4},{6,7},{7,6},{8,9},{9,8},{10,11... | collective-permute-start | bytes 2752520 | tf_op jit(solution)/shard_map/ppermute | solution.py:380
  70.3 12.6 %collective-permute-start.21 = (bf16[4,2,4,112,128]{4,3,2,1,0:T(8,128)(2,1)}, bf16[4,2,4,112,128]{4,3,2,1,0:T(8,128)(2,1)}, u32[]{:S(2)}, u32[]{:S(2)}) collective-permute-start(bf16[4,2,4,112,128]{4,3,2,1,0:T(8,128)(2,1)} %collective-permute-done.17.refs_9_), channel_id=1, source_target_pairs={{0,1},{1,0},{2,3},{3,2},{4,5},{5,4},{6,7},{7,6},{8,9},{9,8},{10,11... | collective-permute-start | bytes 2752520 | tf_op jit(solution)/shard_map/ppermute | solution.py:380
  71.2 1.0 copy-start.8
  71.2 11.7 %collective-permute-start.22 = (bf16[4,2,4,112,128]{4,3,2,1,0:T(8,128)(2,1)}, bf16[4,2,4,112,128]{4,3,2,1,0:T(8,128)(2,1)}, u32[]{:S(2)}, u32[]{:S(2)}) collective-permute-start(bf16[4,2,4,112,128]{4,3,2,1,0:T(8,128)(2,1)} %collective-permute-done.18.refs_10_), channel_id=1, source_target_pairs={{0,1},{1,0},{2,3},{3,2},{4,5},{5,4},{6,7},{7,6},{8,9},{9,8},{10,11... | collective-permute-start | bytes 2752520 | tf_op jit(solution)/shard_map/ppermute | solution.py:380
  80.2 2.8 %collective-permute-start.13 = (bf16[4,2,4,112,128]{4,3,2,1,0:T(8,128)(2,1)}, bf16[4,2,4,112,128]{4,3,2,1,0:T(8,128)(2,1)}, u32[]{:S(2)}, u32[]{:S(2)}) collective-permute-start(bf16[4,2,4,112,128]{4,3,2,1,0:T(8,128)(2,1)} %collective-permute-done.9.refs_3_), channel_id=1, source_target_pairs={{0,1},{1,0},{2,3},{3,2},{4,5},{5,4},{6,7},{7,6},{8,9},{9,8},{10,11... | collective-permute-start | bytes 2752520 | tf_op jit(solution)/shard_map/ppermute | solution.py:380
  82.2 2.8 %collective-permute-start.23 = (bf16[4,2,4,112,128]{4,3,2,1,0:T(8,128)(2,1)}, bf16[4,2,4,112,128]{4,3,2,1,0:T(8,128)(2,1)}, u32[]{:S(2)}, u32[]{:S(2)}) collective-permute-start(bf16[4,2,4,112,128]{4,3,2,1,0:T(8,128)(2,1)} %collective-permute-done.19.refs_11_), channel_id=1, source_target_pairs={{0,1},{1,0},{2,3},{3,2},{4,5},{5,4},{6,7},{7,6},{8,9},{9,8},{10,11... | collective-permute-start | bytes 2752520 | tf_op jit(solution)/shard_map/ppermute | solution.py:380
  150.7 2.8 %collective-permute-start.24 = (bf16[4,4,112,256]{3,2,1,0:T(8,128)(2,1)}, bf16[4,4,112,256]{3,2,1,0:T(8,128)(2,1)S(1)}, u32[]{:S(2)}, u32[]{:S(2)}) collective-permute-start(bf16[4,4,112,256]{3,2,1,0:T(8,128)(2,1)} %get-tuple-element.11), channel_id=1, source_target_pairs={{0,1},{1,0},{2,3},{3,2},{4,5},{5,4},{6,7},{7,6},{8,9},{9,8},{10,11... | collective-permute-start | bytes 2752520 | tf_op jit(solution)/shard_map/ppermute | solution.py:380
  154.9 8.6 %collective-permute-start.25 = (bf16[2,4,112,256]{3,2,1,0:T(8,128)(2,1)S(1)}, bf16[2,4,112,256]{3,2,1,0:T(8,128)(2,1)S(1)}, u32[]{:S(2)}, u32[]{:S(2)}) collective-permute-start(bf16[2,4,112,256]{3,2,1,0:T(8,128)(2,1)S(1)} %get-tuple-element.17), channel_id=1, source_target_pairs={{0,2},{1,7},{2,0},{3,5},{4,6},{5,3},{6,4},{7,1},{8,10},{9,15},{10,... | collective-permute-start | bytes 1376264 | tf_op jit(solution)/shard_map/ppermute | solution.py:376
  163.6 7.3 %collective-permute-start.26 = (bf16[4,112,256]{2,1,0:T(8,128)(2,1)S(1)}, bf16[4,112,256]{2,1,0:T(8,128)(2,1)S(1)}, u32[]{:S(2)}, u32[]{:S(2)}) collective-permute-start(bf16[4,112,256]{2,1,0:T(8,128)(2,1)S(1)} %fusion.2), channel_id=1, source_target_pairs={{0,6},{1,3},{2,4},{3,1},{4,2},{5,7},{6,0},{7,5},{8,14},{9,11},{10,... | collective-permute-start | bytes 688136 | tf_op jit(solution)/shard_map/ppermute | solution.py:376
  171.6 8.7 %collective-permute-start.29 = (bf16[112,256]{1,0:T(8,128)(2,1)S(1)}, bf16[112,256]{1,0:T(8,128)(2,1)S(1)}, u32[]{:S(2)}, u32[]{:S(2)}) collective-permute-start(bf16[112,256]{1,0:T(8,128)(2,1)S(1)} %get-tuple-element.22), channel_id=1, source_target_pairs={{0,16},{8,24},{16,0},{24,8},{1,17},{9,25},{17,1},{25,9},{2,18},{10... | collective-permute-start | bytes 172040 | tf_op jit(solution)/shard_map/ppermute | solution.py:384
  172.8 8.7 %collective-permute-start.28 = (bf16[112,256]{1,0:T(8,128)(2,1)S(1)}, bf16[112,256]{1,0:T(8,128)(2,1)S(1)}, u32[]{:S(2)}, u32[]{:S(2)}) collective-permute-start(bf16[112,256]{1,0:T(8,128)(2,1)S(1)} %get-tuple-element.23), channel_id=1, source_target_pairs={{0,24},{1,9},{8,16},{9,1},{16,8},{17,25},{24,0},{25,17},{2,26},{3,... | collective-permute-start | bytes 172040 | tf_op jit(solution)/shard_map/ppermute | solution.py:376
  177.6 5.7 %collective-permute-start.27 = (bf16[112,256]{1,0:T(8,128)(2,1)S(1)}, bf16[112,256]{1,0:T(8,128)(2,1)S(1)}, u32[]{:S(2)}, u32[]{:S(2)}) collective-permute-start(bf16[112,256]{1,0:T(8,128)(2,1)S(1)} %get-tuple-element.24), channel_id=1, source_target_pairs={{0,8},{1,25},{8,0},{9,17},{16,24},{17,9},{24,16},{25,1},{2,10},{3,... | collective-permute-start | bytes 172040 | tf_op jit(solution)/shard_map/ppermute | solution.py:376
  180.3 3.0 %copy-start.2 = (bf16[112,256]{1,0:T(8,128)(2,1)}, bf16[112,256]{1,0:T(8,128)(2,1)S(1)}, u32[]{:S(2)}) copy-start(bf16[112,256]{1,0:T(8,128)(2,1)S(1)} %collective-permute-done.29.d_ref) | copy-start | bytes 172036
  181.5 1.8 copy-start.3
  183.3 0.6 copy-start.4

commit v2 on v1

--- a/solution.py
+++ b/solution.py
@@ -23,7 +23,7 @@
 TOK = LAYERS * T
 BLOCK = 384
 BLOCKS = D // BLOCK
-SENT = BLOCKS * T + T + 16
+PAY = T + 16
 
 
 def iota(shape, axis):
@@ -114,26 +114,13 @@
     return jnp.where((c == 0) == first, i ^ 1, 3 - i)
 
 
-def sequence_kernel(pos_ref, *refs):
-    left, right = refs[:8], refs[8:16]
-    entry_ref, cot_ref, sent_ref = refs[16:19]
-    w_scr, rows_scr, xs, ns, mixed_scr, decay_scr, write_scr, small_scr, proj_scr = refs[19:28]
-    first_scr, sem_a, sem_b, sem_c = refs[28:]
-    x, y, c, zh, section = (pos_ref[i] for i in range(5))
-    mine = jnp.minimum(section, SEQS - 1)
-    loads = []
-    for i, ref in enumerate((entry_ref, cot_ref)):
-        copy = pltpu.make_async_copy(
-            ref.at[mine // 3, mine % 3], first_scr.at[i], sem_c.at[i]
-        )
-        copy.start()
-        loads.append(copy)
+def load_weights(pos_ref, left, right, w_scr, sem_a, sem_b):
+    x, y, c = pos_ref[0], pos_ref[1], pos_ref[2]
 
     def ring(i, core):
         one, two = partner(i, core, True), partner(i, core, False)
         return [i, one, two, partner(two, core, True)]
 
-    copies = []
     for kc in range(2):
         cc = (c + kc) % 2
         ys, xx = ring(y, cc), ring(x, cc)
@@ -161,11 +148,24 @@
                     src.at[0], w_scr.at[0:2, :, 0, 0, :, :C], sem.at[at]
                 ).wait()
 
+    return wait_layers
+
+
+def keys_of(w_scr, layer, m):
+    parts = [w_scr[layer, m // 2, (m % 2) * 2 + i // 2, i % 2, :ROWS] for i in range(4)]
+    return jnp.concatenate(parts, axis=0)
+
+
+def forward_kernel(pos_ref, *refs):
+    left, right, entry_ref, sent_ref, kept = refs[:8], refs[8:16], refs[16], refs[17], refs[18:22]
+    w_scr, first_scr = refs[22:24]
+    scrs, (sem_a, sem_b, sem_c, sem_k) = refs[24:28], refs[28:]
+    rows_scr, xs, mixed_scr, wide_scr = scrs
+    mine = jnp.minimum(pos_ref[4], SEQS - 1)
+    first = pltpu.make_async_copy(entry_ref.at[mine // 3, mine % 3], first_scr, sem_c)
+    first.start()
+    wait_layers = load_weights(pos_ref, left, right, w_scr, sem_a, sem_b)
     causal, diag, spread, block, tri = masks()
-
-    def keys_of(layer, m):
-        parts = [w_scr[layer, m // 2, (m % 2) * 2 + i // 2, i % 2, :ROWS] for i in range(4)]
-        return jnp.concatenate(parts, axis=0)
 
     def forward(layer, stream):
         @pl.when(layer % 2 == 0)
@@ -180,12 +180,11 @@
         x_f = stream.astype(F32)
         inv_rms = lax.rsqrt(jnp.sum(x_f * x_f, axis=1, keepdims=True) * (1.0 / D) + 1e-05)
         normed = (x_f * inv_rms * gain).astype(BF16)
-        ns[layer] = normed
         for m in range(BLOCKS):
             sent_ref[layer, T * m : T * (m + 1)] = normed[:, BLOCK * m : BLOCK * (m + 1)]
         logits = nt(normed, rows_low) + bias
         key_query = sum(
-            nn(normed[:, BLOCK * m : BLOCK * (m + 1)], keys_of(layer, m)) for m in range(BLOCKS)
+            nn(normed[:, BLOCK * m : BLOCK * (m + 1)], keys_of(w_scr, layer, m)) for m in range(BLOCKS)
         )
         head = iota((T, T), 1) < H
         rate = jnp.maximum(logits, 0.0) + jnp.log1p(jnp.exp(-jnp.abs(logits)))
@@ -203,32 +202,62 @@
         q = key_query[:, C:]
         inv = lax.rsqrt(jnp.sum(k * k, axis=1, keepdims=True) + 1e-06)
         scores = nt(q.astype(BF16), tile4((k * inv).astype(BF16)))
-        decay_scr[layer] = decay
-        write_scr[layer] = write_s
-        proj_scr[layer] = key_query
-        small_scr[layer] = jnp.concatenate([scores, logits, keep, jnp.zeros((T, 64), F32)], axis=1)
+        wide_scr[layer, :T, :W] = decay
+        wide_scr[layer, T:, :W] = jnp.broadcast_to(write_s, (8, W))
+        wide_scr[layer, :T, W : W + 256] = key_query
+        wide_scr[layer, :T, W + 256 :] = jnp.concatenate(
+            [scores, logits, keep, jnp.zeros((T, 64), F32)], axis=1
+        )
         mixing = decay * write_s * jnp.concatenate([scores] * GROUPS, axis=1)
         mixed = unstack_heads(
             [nn(block_diag(mixing, g, block), stack_heads(normed, g)) for g in range(GROUPS)]
         )
         mixed_scr[layer] = mixed.astype(BF16)
+        for i in range(4):
+            pltpu.make_async_copy(scrs[i].at[layer], kept[i].at[layer], sem_k.at[i]).start()
         return (x_f + scale * mixed).astype(BF16)
 
-    loads[0].wait()
-    loads[1].wait()
-    lax.fori_loop(0, LAYERS, forward, first_scr[0])
+    first.wait()
+    lax.fori_loop(0, LAYERS, forward, first_scr[...])
+    for i in range(4):
+        pltpu.make_async_copy(scrs[i], kept[i], sem_k.at[i]).wait()
+
+
+def backward_kernel(pos_ref, *refs):
+    left, right, cot_ref, kept, sent_ref = refs[:8], refs[8:16], refs[16], refs[17:22], refs[22]
+    w_scr, first_scr = refs[23:25]
+    scrs, (sem_a, sem_b, sem_c, sem_k) = refs[25:30], refs[30:]
+    rows_scr, xs, mixed_scr, wide_scr, n_scr = scrs
+    mine = jnp.minimum(pos_ref[4], SEQS - 1)
+    first = pltpu.make_async_copy(cot_ref.at[mine // 3, mine % 3], first_scr, sem_c)
+    first.start()
+
+    def load(layer, start):
+        for i in range(5):
+            copy = pltpu.make_async_copy(kept[i].at[layer], scrs[i].at[layer], sem_k.at[layer])
+            if start:
+                copy.start()
+            else:
+                copy.wait()
+
+    load(LAYERS - 1, True)
+    wait_layers = load_weights(pos_ref, left, right, w_scr, sem_a, sem_b)
+    for layer in reversed(range(LAYERS - 1)):
+        load(layer, True)
+    causal, diag, spread, block, tri = masks()
 
     def backward(step, back):
         layer = LAYERS - 1 - step
+        load(layer, False)
         x_f = xs[layer].astype(F32)
-        normed = ns[layer]
+        normed = jnp.concatenate([n_scr[layer, T * m : T * (m + 1)] for m in range(BLOCKS)], axis=1)
         rows_low = rows_scr[layer]
         rows = rows_low[16:].astype(F32)
         gain, scale = rows[8:9], rows[9:10]
         dy = back.astype(F32)
-        decay = decay_scr[layer]
-        write_s = write_scr[layer]
-        small = small_scr[layer]
+        decay = wide_scr[layer, :T, :W]
+        write_s = wide_scr[layer, T : T + 1, :W]
+        small = wide_scr[layer, :T, W + 256 :]
         scores, logits, keep = small[:, :C], small[:, C : C + T], small[:, C + T : C + 2 * T]
         scores6 = jnp.concatenate([scores] * GROUPS, axis=1)
         mixing = decay * write_s * scores6
@@ -261,40 +290,47 @@
         d_rate = keep * (d_write * keep - d_log)
         d_logits = d_rate / (1.0 + jnp.exp(-logits))
         d_low = jnp.where(iota((T, T), 1) < H, d_logits, 0.0).astype(BF16)
-        k = proj_scr[layer][:, :C]
-        q = proj_scr[layer][:, C:]
+        k = wide_scr[layer, :T, W : W + C]
+        q = wide_scr[layer, :T, W + C : W + 256]
         inv = lax.rsqrt(jnp.sum(k * k, axis=1, keepdims=True) + 1e-06)
         d_q = nn(d_scores, tile4((k * inv).astype(BF16)))
         d_unit = tn(d_scores, q.astype(BF16))
         d_unit = d_unit[:T] + d_unit[T : 2 * T] + d_unit[2 * T : 3 * T] + d_unit[3 * T :]
         d_k = inv * d_unit - k * (inv * inv * inv * jnp.sum(d_unit * k, axis=1, keepdims=True))
         d_keyq = jnp.concatenate([d_k, d_q], axis=1).astype(BF16)
-        through = jnp.concatenate([nt(d_keyq, keys_of(layer, m)) for m in range(BLOCKS)], axis=1)
+
+        @pl.when(layer % 2 == 1)
+        def _():
+            wait_layers(layer // 2)
+
+        through = jnp.concatenate([nt(d_keyq, keys_of(w_scr, layer, m)) for m in range(BLOCKS)], axis=1)
         d_normed = d_values + through + nn(d_low, rows_low)
         inv_rms = lax.rsqrt(jnp.sum(x_f * x_f, axis=1, keepdims=True) * (1.0 / D) + 1e-05)
         x_hat = x_f * inv_rms
         d_gain = jnp.sum(d_normed * x_hat, axis=0, keepdims=True)
         d_hat = d_normed * gain
         mean = jnp.sum(d_hat * x_hat, axis=1, keepdims=True) * (1.0 / D)
-        sent_ref[layer, TOK : TOK + T, :256] = d_keyq
-        sent_ref[layer, TOK : TOK + T, 256:] = jnp.concatenate(
+        sent_ref[layer, :T, :256] = d_keyq
+        sent_ref[layer, :T, 256:] = jnp.concatenate(
             [d_low, jnp.zeros((T, 96), BF16)], axis=1
         )
-        sent_ref[layer, TOK + T :] = jnp.concatenate(
+        sent_ref[layer, T:] = jnp.concatenate(
             [d[:, BLOCK * i : BLOCK * (i + 1)] for d in (d_gain, d_scale) for i in range(8)], axis=0
         ).astype(BF16)
         return (dy + inv_rms * (d_hat - x_hat * mean)).astype(BF16)
 
-    cot = jnp.where(section < SEQS, first_scr[1].astype(F32), 0.0).astype(BF16)
+    first.wait()
+    cot = jnp.where(pos_ref[4] < SEQS, first_scr[...].astype(F32), 0.0).astype(BF16)
     lax.fori_loop(0, LAYERS, backward, cot)
 
 
-def weight_kernel(pos_ref, got_ref, keep_ref, send_ref, got, scr, sem_in, sem):
+def weight_kernel(pos_ref, got_ref, pay_ref, keep_ref, send_ref, got, pay, scr, sem_in, sem):
     y, c, zh = pos_ref[1], pos_ref[2], pos_ref[3]
     loads = []
-    for m in list(range(BLOCKS)) + [BLOCKS]:
-        at = pl.ds(T * m, T if m < BLOCKS else T + 16)
+    for m in range(BLOCKS):
+        at = pl.ds(T * m, T)
         loads.append(pltpu.make_async_copy(got_ref.at[:, at], got.at[:, at], sem_in.at[m]))
+    loads.append(pltpu.make_async_copy(pay_ref, pay, sem_in.at[BLOCKS]))
     loads[-1].start()
     for copy in loads[:-1]:
         copy.start()
@@ -304,8 +340,8 @@
         return bits if core else (bits & 1) * 2 + (bits >> 1)
 
     loads[-1].wait()
-    tokens = jnp.concatenate([got[s, TOK : TOK + T] for s in range(LAYERS)], axis=0)
-    extra = sum(got[s, TOK + T :].astype(F32) for s in range(LAYERS))
+    tokens = jnp.concatenate([pay[s, :T] for s in range(LAYERS)], axis=0)
+    extra = sum(pay[s, T:].astype(F32) for s in range(LAYERS))
     bias = jnp.sum(tokens[:, 256:].astype(F32), axis=0, keepdims=True)
     bias = jnp.concatenate([bias[:, :ROWS]] * 4, axis=1)
     for m in range(BLOCKS):
@@ -427,43 +463,50 @@
     left = left + [other_core(a) for a in left]
     right = right + [other_core(a) for a in right]
 
-    sent = call(
-        sequence_kernel,
-        [shape(LAYERS, SENT, BLOCK)],
-        [SMEM] + [ANY] * 18,
-        [
-            pltpu.VMEM((LAYERS, 4, 4, 2, PIECE, 256), BF16),
-            pltpu.VMEM((LAYERS, T, D), BF16),
-            pltpu.VMEM((LAYERS, T, D), BF16),
-            pltpu.VMEM((LAYERS, T, D), BF16),
-            pltpu.VMEM((LAYERS, T, D), BF16),
-            pltpu.VMEM((LAYERS, T, W), F32),
-            pltpu.VMEM((LAYERS, 1, W), F32),
-            pltpu.VMEM((LAYERS, T, 256), F32),
-            pltpu.VMEM((LAYERS, T, 256), F32),
-            pltpu.VMEM((2, T, D), BF16),
-            pltpu.SemaphoreType.DMA((4,)),
-            pltpu.SemaphoreType.DMA((4,)),
-            pltpu.SemaphoreType.DMA((2,)),
-        ],
-        cost=(8_000_000_000, 30_000_000),
-    )(pos, *left, *right, entries, cotangents)[0]
-
-    got = lax.all_to_all(sent, SECTION, 0, 0, tiled=True)
+    wide = shape(LAYERS, T + 8, W + 512, dtype=F32)
+    stored = shape(LAYERS, T, D)
+    normed = shape(LAYERS, TOK, BLOCK)
+    held = [
+        pltpu.VMEM((LAYERS, 4, 4, 2, PIECE, 256), BF16),
+        pltpu.VMEM((T, D), BF16),
+        pltpu.VMEM(stored.shape, BF16),
+        pltpu.VMEM(stored.shape, BF16),
+        pltpu.VMEM(stored.shape, BF16),
+        pltpu.VMEM(wide.shape, F32),
+    ]
+    sems = [pltpu.SemaphoreType.DMA((4,)), pltpu.SemaphoreType.DMA((4,)), pltpu.SemaphoreType.DMA]
+    normed, *kept = call(
+        forward_kernel,
+        [normed, stored, stored, stored, wide],
+        [SMEM] + [ANY] * 17,
+        held + sems + [pltpu.SemaphoreType.DMA((4,))],
+        [VMEM] + [ANY] * 4,
+        cost=(3_000_000_000, 30_000_000),
+    )(pos, *left, *right, entries)
+    got = lax.all_to_all(normed, SECTION, 0, 0, tiled=True)
+    pay = call(
+        backward_kernel,
+        [shape(LAYERS, PAY, BLOCK)],
+        [SMEM] + [ANY] * 22,
+        held + [pltpu.VMEM((LAYERS, TOK, BLOCK), BF16)] + sems + [pltpu.SemaphoreType.DMA((LAYERS,))],
+        cost=(8_000_000_000, 40_000_000),
+    )(pos, *left, *right, cotangents, *kept, normed)[0]
+    pay = lax.all_to_all(pay, SECTION, 0, 0, tiled=True)
     half = shape(4, 4, PIECE, 256)
     keep, send = call(
         weight_kernel,
         [half, half],
-        [SMEM, ANY],
+        [SMEM, ANY, ANY],
         [
-            pltpu.VMEM((LAYERS, SENT, BLOCK), BF16),
+            pltpu.VMEM((LAYERS, TOK, BLOCK), BF16),
+            pltpu.VMEM((LAYERS, PAY, BLOCK), BF16),
             pltpu.VMEM((2, 4, 4, PIECE, 256), BF16),
             pltpu.SemaphoreType.DMA((BLOCKS + 1,)),
             pltpu.SemaphoreType.DMA((2,)),
         ],
         [ANY] * 2,
         cost=(600_000_000, 4_000_000),
-    )(pos, got)
+    )(pos, got, pay)
     got = other_core(send)
     got = swap(add(keep[2:], got[2:]), "y", True), keep[:2], got[:2]
     keep = add(got[1], got[2])

time: 186 us -> 201 us (1.081)
  Pallas kernels: 36.3 us -> 45 us
  blocking collectives: 31 us -> 37.3 us
    pallas_call x2 -> x3, Pallas kernels: 34.7 us -> 43.5 us  [the longest x1 20.8 us: per_device(): call(backward_kernel, [shape(LAYERS, PAY, BLOCK)], [SMEM] + [ANY] * 22, h...]
    all_to_all x1 -> x2, blocking collectives: 31 us -> 37.3 us  [the longest x1 23.7 us: per_device(): got = lax.all_to_all(normed, SECTION, 0, 0, tiled=True)]
where the time goes in v2:
time: 201 us; the launch traced here: 200 us
  waiting for transfers between devices  65 us (32%)
  Pallas kernels  45 us (22%)
  starting transfers between devices  42.6 us (21%)
  blocking collectives  37.3 us (19%)
  local copies, waits for them, and re-layouts  5.29 us (3%)
  other arithmetic  3.93 us (2%)
    ppermute x18, waiting for transfers between devices, swap(): return lax.ppermute(array, (axis, 'c'), ring_pairs(first))  49.8 us
    ppermute x18, starting transfers between devices, swap(): return lax.ppermute(array, (axis, 'c'), ring_pairs(first))  38.4 us
    all_to_all x1, blocking collectives, per_device(): got = lax.all_to_all(normed, SECTION, 0, 0, tiled=True)  23.7 us
    pallas_call x1, Pallas kernels, per_device(): call(backward_kernel, [shape(LAYERS, PAY, BLOCK)], [SMEM] + [ANY] * 22, h...  20.8 us
    pallas_call x1, Pallas kernels, per_device(): call(forward_kernel, [normed, stored, stored, stored, wide], [SMEM] + [AN...  17.3 us
    all_to_all x1, blocking collectives, per_device(): pay = lax.all_to_all(pay, SECTION, 0, 0, tiled=True)  13.6 us
    ppermute x2, waiting for transfers between devices, opposite(): return lax.ppermute(array, axis, [(i, i ^ 2) for i in range(4)])  5.56 us
    pallas_call x1, Pallas kernels, per_device(): call(weight_kernel, [half, half], [SMEM, ANY, ANY], [pltpu.VMEM((LAYERS,...  5.35 us
  transfers between devices with their start and end apart: 30, of which 18 were waited for; matrix products, arithmetic and copies ran while one was open for 1% of the time, Pallas kernels for 0%

profile of v2, /device:TPU:2, one launch (start us, length us, event | category | flops | bytes accessed | tf_op | source)
XLA Modules:
  0.0 200.1 jit_solution(16859013626127806836)
XLA Ops:
  0.6 0.7 pad_slice_fusion
  1.3 0.7 pad_slice_fusion.1
  2.0 0.8 maximum_maximum_fusion
  2.9 6.4 %collective-permute-start.1 = (bf16[112,256]{1,0:T(8,128)(2,1)S(1)}, bf16[112,256]{1,0:T(8,128)(2,1)S(1)}, u32[]{:S(2)}, u32[]{:S(2)}) collective-permute-start(bf16[112,256]{1,0:T(8,128)(2,1)S(1)} %maximum_maximum_fusion), channel_id=1, source_target_pairs={{0,24},{1,9},{8,16},{9,1},{16,8},{17,25},{24,0},{25,17},{2,26},{3,... | collective-permute-start | bytes 172040 | tf_op jit(solution)/shard_map/ppermute | solution.py:412
  9.2 1.5 collective-permute-start
  10.7 1.0 collective-permute-start.2
  11.7 0.8 fusion.15
  12.8 1.6 collective-permute-done.1
  14.4 1.1 collective-permute-done
  15.6 3.6 %collective-permute-done.2 = bf16[112,256]{1,0:T(8,128)(2,1)S(1)} collective-permute-done((bf16[112,256]{1,0:T(8,128)(2,1)S(1)}, bf16[112,256]{1,0:T(8,128)(2,1)S(1)}, u32[]{:S(2)}, u32[]{:S(2)}) %collective-permute-start.2) | collective-permute-done | bytes 57376 | tf_op jit(solution)/shard_map/ppermute | solution.py:420
  19.9 1.2 collective-permute-start.3
  21.2 4.8 %collective-permute-done.3 = bf16[4,112,256]{2,1,0:T(8,128)(2,1)S(1)} collective-permute-done((bf16[4,112,256]{2,1,0:T(8,128)(2,1)S(1)}, bf16[4,112,256]{2,1,0:T(8,128)(2,1)S(1)}, u32[]{:S(2)}, u32[]{:S(2)}) %collective-permute-start.3) | collective-permute-done | bytes 229408 | tf_op jit(solution)/shard_map/ppermute | solution.py:456
  26.8 1.6 collective-permute-start.14
  28.4 2.2 %collective-permute-start.5 = (bf16[2,4,112,128]{3,2,1,0:T(8,128)(2,1)S(1)}, bf16[2,4,112,128]{3,2,1,0:T(8,128)(2,1)S(1)}, u32[]{:S(2)}, u32[]{:S(2)}) collective-permute-start(bf16[2,4,112,128]{3,2,1,0:T(8,128)(2,1)S(1)} %get-tuple-element.31), channel_id=1, source_target_pairs={{0,192},{1,65},{64,128},{65,1},{128,64},{129,193},{192,0},{193,129... | collective-permute-start | bytes 688136 | tf_op jit(solution)/shard_map/ppermute | solution.py:412
  30.5 2.3 %collective-permute-done.4 = bf16[2,4,112,128]{3,2,1,0:T(8,128)(2,1)S(1)} collective-permute-done((bf16[2,4,112,128]{3,2,1,0:T(8,128)(2,1)S(1)}, bf16[2,4,112,128]{3,2,1,0:T(8,128)(2,1)S(1)}, u32[]{:S(2)}, u32[]{:S(2)}) %collective-permute-start.4) | collective-permute-done | bytes 229408 | tf_op jit(solution)/shard_map/ppermute | solution.py:412
  32.9 2.6 %collective-permute-start.6 = (bf16[2,4,112,128]{3,2,1,0:T(8,128)(2,1)S(1)}, bf16[2,4,112,128]{3,2,1,0:T(8,128)(2,1)S(1)}, u32[]{:S(2)}, u32[]{:S(2)}) collective-permute-start(bf16[2,4,112,128]{3,2,1,0:T(8,128)(2,1)S(1)} %collective-permute-done.4), channel_id=1, source_target_pairs={{0,192},{1,65},{64,128},{65,1},{128,64},{129,193},{192,0},{193,129... | collective-permute-start | bytes 688136 | tf_op jit(solution)/shard_map/ppermute | solution.py:412
  35.5 2.3 %collective-permute-start.15 = (bf16[2,4,112,128]{3,2,1,0:T(8,128)(2,1)S(1)}, bf16[2,4,112,128]{3,2,1,0:T(8,128)(2,1)S(1)}, u32[]{:S(2)}, u32[]{:S(2)}) collective-permute-start(bf16[2,4,112,128]{3,2,1,0:T(8,128)(2,1)S(1)} %get-tuple-element.30), channel_id=1, source_target_pairs={{0,6},{1,3},{2,4},{3,1},{4,2},{5,7},{6,0},{7,5},{8,14},{9,11},{10,... | collective-permute-start | bytes 688136 | tf_op jit(solution)/shard_map/ppermute | solution.py:412
  37.8 1.0 collective-permute-start.16
  38.7 0.8 collective-permute-done.6
  39.7 4.4 %collective-permute-start.8 = (bf16[4,2,4,112,128]{4,3,2,1,0:T(8,128)(2,1)S(1)}, bf16[4,2,4,112,128]{4,3,2,1,0:T(8,128)(2,1)S(1)}, u32[]{:S(2)}, u32[]{:S(2)}) collective-permute-start(bf16[4,2,4,112,128]{4,3,2,1,0:T(8,128)(2,1)S(1)} %pad_maximum_fusion.refs_0_), channel_id=1, source_target_pairs={{0,6},{1,3},{2,4},{3,1},{4,2},{5,7},{6,0},{7,5},{8,14},{9,11},{10,... | collective-permute-start | bytes 2752520 | tf_op jit(solution)/shard_map/ppermute | solution.py:412
  44.2 1.0 collective-permute-done.16
  45.3 1.9 collective-permute-start.17
  47.3 0.9 collective-permute-start.18
  48.2 16.5 %collective-permute-done.8.refs_2_ = bf16[4,2,4,112,128]{4,3,2,1,0:T(8,128)(2,1)S(1)} collective-permute-done((bf16[4,2,4,112,128]{4,3,2,1,0:T(8,128)(2,1)S(1)}, bf16[4,2,4,112,128]{4,3,2,1,0:T(8,128)(2,1)S(1)}, u32[]{:S(2)}, u32[]{:S(2)}) %collective-permute-start.8) | collective-permute-done | bytes 917536 | tf_op jit(solution)/shard_map/ppermute | solution.py:412
  64.7 3.8 %collective-permute-start.9 = (bf16[4,2,4,112,128]{4,3,2,1,0:T(8,128)(2,1)}, bf16[4,2,4,112,128]{4,3,2,1,0:T(8,128)(2,1)}, u32[]{:S(2)}, u32[]{:S(2)}) collective-permute-start(bf16[4,2,4,112,128]{4,3,2,1,0:T(8,128)(2,1)} %collective-permute-done.7.refs_1_), channel_id=1, source_target_pairs={{0,6},{1,3},{2,4},{3,1},{4,2},{5,7},{6,0},{7,5},{8,14},{9,11},{10,... | collective-permute-start | bytes 2752520 | tf_op jit(solution)/shard_map/ppermute | solution.py:412
  68.5 1.7 collective-permute-start.19
  71.2 0.9 copy-done.6
  72.1 8.1 %collective-permute-done.9.refs_3_ = bf16[4,2,4,112,128]{4,3,2,1,0:T(8,128)(2,1)} collective-permute-done((bf16[4,2,4,112,128]{4,3,2,1,0:T(8,128)(2,1)}, bf16[4,2,4,112,128]{4,3,2,1,0:T(8,128)(2,1)}, u32[]{:S(2)}, u32[]{:S(2)}) %collective-permute-start.9) | collective-permute-done | bytes 917536 | tf_op jit(solution)/shard_map/ppermute | solution.py:412
  80.2 2.0 %collective-permute-done.19.refs_11_ = bf16[4,2,4,112,128]{4,3,2,1,0:T(8,128)(2,1)} collective-permute-done((bf16[4,2,4,112,128]{4,3,2,1,0:T(8,128)(2,1)}, bf16[4,2,4,112,128]{4,3,2,1,0:T(8,128)(2,1)}, u32[]{:S(2)}, u32[]{:S(2)}) %collective-permute-start.19) | collective-permute-done | bytes 917536 | tf_op jit(solution)/shard_map/ppermute | solution.py:412
  83.0 2.0 %collective-permute-done.23.refs_15_ = bf16[4,2,4,112,128]{4,3,2,1,0:T(8,128)(2,1)} collective-permute-done((bf16[4,2,4,112,128]{4,3,2,1,0:T(8,128)(2,1)}, bf16[4,2,4,112,128]{4,3,2,1,0:T(8,128)(2,1)}, u32[]{:S(2)}, u32[]{:S(2)}) %collective-permute-start.23) | collective-permute-done | bytes 917536 | tf_op jit(solution)/shard_map/ppermute | solution.py:416
  85.0 17.3 %shard_map.93 = (bf16[8,256,384]{2,1,0:T(8,128)(2,1)}, bf16[8,32,3072]{2,1,0:T(8,128)(2,1)}, bf16[8,32,3072]{2,1,0:T(8,128)(2,1)}, bf16[8,32,3072]{2,1,0:T(8,128)(2,1)}, f32[8,40,1280]{2,1,0:T(8,128)}) custom-call(s32[5]{0:T(128)} %stack.105.pos_ref, bf16[4,2,4,112,128]{4,3,2,1,0:T(8,128)(2,1)} %copy-done, ...), custom_call_target="tpu_custom_call" | custom-call | flops 3000000000 | bytes 30000000 | tf_op jit(solution)/shard_map/pallas_call | solution.py:478
  102.3 20.8 %shard_map.94 = bf16[8,48,384]{2,1,0:T(8,128)(2,1)} custom-call(s32[5]{0:T(128)} %stack.105.pos_ref, bf16[4,2,4,112,128]{4,3,2,1,0:T(8,128)(2,1)} %copy-done, bf16[4,2,4,112,128]{4,3,2,1,0:T(8,128)(2,1)} %collective-permute-done.7.refs_1_, bf16[4,2,4,112,128]{4,3,2,1,0:T(8,128)(2,1)} %copy-done.4, ...), custom_call_target="tpu_custom_call" | custom-call | flops 8000000000 | bytes 40000000 | tf_op jit(solution)/shard_map/pallas_call | solution.py:487
  123.2 13.6 %all_to_all.10.pay_ref = bf16[8,48,384]{2,1,0:T(8,128)(2,1)} all-to-all(bf16[8,48,384]{2,1,0:T(8,128)(2,1)} %shard_map.94), channel_id=1, replica_groups=mesh['x'=4,'zl'=2,'zh'=4,'y'=4,'c'=2] {'x','zl'}, dimensions={0} | all-to-all | bytes 589824 | tf_op jit(solution)/shard_map/all_to_all | solution.py:494
  136.8 23.7 %all_to_all.11.got_ref = bf16[8,256,384]{2,1,0:T(8,128)(2,1)} all-to-all(bf16[8,256,384]{2,1,0:T(8,128)(2,1)S(1)} %copy-done.2), channel_id=1, replica_groups=mesh['x'=4,'zl'=2,'zh'=4,'y'=4,'c'=2] {'x','zl'}, dimensions={0} | all-to-all | bytes 3145728 | tf_op jit(solution)/shard_map/all_to_all | solution.py:486
  160.5 5.3 %shard_map.95 = (bf16[4,4,112,256]{3,2,1,0:T(8,128)(2,1)}, bf16[4,4,112,256]{3,2,1,0:T(8,128)(2,1)}) custom-call(s32[5]{0:T(128)} %stack.105.pos_ref, bf16[8,256,384]{2,1,0:T(8,128)(2,1)} %all_to_all.11.got_ref, bf16[8,48,384]{2,1,0:T(8,128)(2,1)} %all_to_all.10.pay_ref), custom_call_target="tpu_custom_call" | custom-call | flops 600000000 | bytes 4000000 | tf_op jit(solution)/shard_map/pallas_call | solution.py:496
  166.0 2.7 %collective-permute-done.24 = bf16[4,4,112,256]{3,2,1,0:T(8,128)(2,1)S(1)} collective-permute-done((bf16[4,4,112,256]{3,2,1,0:T(8,128)(2,1)}, bf16[4,4,112,256]{3,2,1,0:T(8,128)(2,1)S(1)}, u32[]{:S(2)}, u32[]{:S(2)}) %collective-permute-start.24) | collective-permute-done | bytes 917536 | tf_op jit(solution)/shard_map/ppermute | solution.py:416
  168.7 1.4 add_convert_fusion.1
  170.1 0.7 collective-permute-start.25
  170.8 7.8 %collective-permute-done.25 = bf16[2,4,112,256]{3,2,1,0:T(8,128)(2,1)S(1)} collective-permute-done((bf16[2,4,112,256]{3,2,1,0:T(8,128)(2,1)S(1)}, bf16[2,4,112,256]{3,2,1,0:T(8,128)(2,1)S(1)}, u32[]{:S(2)}, u32[]{:S(2)}) %collective-permute-start.25) | collective-permute-done | bytes 458784 | tf_op jit(solution)/shard_map/ppermute | solution.py:412
  178.7 1.5 collective-permute-start.26
  180.2 5.8 %collective-permute-done.26 = bf16[4,112,256]{2,1,0:T(8,128)(2,1)S(1)} collective-permute-done((bf16[4,112,256]{2,1,0:T(8,128)(2,1)S(1)}, bf16[4,112,256]{2,1,0:T(8,128)(2,1)S(1)}, u32[]{:S(2)}, u32[]{:S(2)}) %collective-permute-start.26) | collective-permute-done | bytes 229408 | tf_op jit(solution)/shard_map/ppermute | solution.py:412
  186.1 0.6 slice_bitcast_fusion
  186.7 1.3 collective-permute-start.29
  188.0 4.8 %collective-permute-start.28 = (bf16[112,256]{1,0:T(8,128)(2,1)S(1)}, bf16[112,256]{1,0:T(8,128)(2,1)S(1)}, u32[]{:S(2)}, u32[]{:S(2)}) collective-permute-start(bf16[112,256]{1,0:T(8,128)(2,1)S(1)} %get-tuple-element.33), channel_id=1, source_target_pairs={{0,24},{1,9},{8,16},{9,1},{16,8},{17,25},{24,0},{25,17},{2,26},{3,... | collective-permute-start | bytes 172040 | tf_op jit(solution)/shard_map/ppermute | solution.py:412
  193.2 1.9 collective-permute-done.29.d_ref
  195.2 1.2 collective-permute-done.28.c_ref
  196.4 1.5 collective-permute-done.27.b_ref
  198.5 1.6 shard_map.96
  (59 shorter events, 5.2 us)
Async XLA Ops:
  2.9 11.6 %collective-permute-start.1 = (bf16[112,256]{1,0:T(8,128)(2,1)S(1)}, bf16[112,256]{1,0:T(8,128)(2,1)S(1)}, u32[]{:S(2)}, u32[]{:S(2)}) collective-permute-start(bf16[112,256]{1,0:T(8,128)(2,1)S(1)} %maximum_maximum_fusion), channel_id=1, source_target_pairs={{0,24},{1,9},{8,16},{9,1},{16,8},{17,25},{24,0},{25,17},{2,26},{3,... | collective-permute-start | bytes 172040 | tf_op jit(solution)/shard_map/ppermute | solution.py:412
  9.2 6.3 %collective-permute-start = (bf16[112,256]{1,0:T(8,128)(2,1)S(1)}, bf16[112,256]{1,0:T(8,128)(2,1)S(1)}, u32[]{:S(2)}, u32[]{:S(2)}) collective-permute-start(bf16[112,256]{1,0:T(8,128)(2,1)S(1)} %maximum_maximum_fusion), channel_id=1, source_target_pairs={{0,8},{1,25},{8,0},{9,17},{16,24},{17,9},{24,16},{25,1},{2,10},{3,... | collective-permute-start | bytes 172040 | tf_op jit(solution)/shard_map/ppermute | solution.py:412
  10.7 8.5 %collective-permute-start.2 = (bf16[112,256]{1,0:T(8,128)(2,1)S(1)}, bf16[112,256]{1,0:T(8,128)(2,1)S(1)}, u32[]{:S(2)}, u32[]{:S(2)}) collective-permute-start(bf16[112,256]{1,0:T(8,128)(2,1)S(1)} %maximum_maximum_fusion), channel_id=1, source_target_pairs={{0,16},{8,24},{16,0},{24,8},{1,17},{9,25},{17,1},{25,9},{2,18},{10... | collective-permute-start | bytes 172040 | tf_op jit(solution)/shard_map/ppermute | solution.py:420
  19.9 6.1 %collective-permute-start.3 = (bf16[4,112,256]{2,1,0:T(8,128)(2,1)S(1)}, bf16[4,112,256]{2,1,0:T(8,128)(2,1)S(1)}, u32[]{:S(2)}, u32[]{:S(2)}) collective-permute-start(bf16[4,112,256]{2,1,0:T(8,128)(2,1)S(1)} %broadcast_select_fusion), channel_id=1, source_target_pairs={{0,32},{1,57},{32,0},{33,9},{8,40},{9,33},{40,8},{41,17},{16,48},{... | collective-permute-start | bytes 688136 | tf_op jit(solution)/shard_map/ppermute | solution.py:456
  26.2 6.7 %collective-permute-start.4 = (bf16[2,4,112,128]{3,2,1,0:T(8,128)(2,1)S(1)}, bf16[2,4,112,128]{3,2,1,0:T(8,128)(2,1)S(1)}, u32[]{:S(2)}, u32[]{:S(2)}) collective-permute-start(bf16[2,4,112,128]{3,2,1,0:T(8,128)(2,1)S(1)} %get-tuple-element.31), channel_id=1, source_target_pairs={{0,64},{1,193},{64,0},{65,129},{128,192},{129,65},{192,128},{193,1... | collective-permute-start | bytes 688136 | tf_op jit(solution)/shard_map/ppermute | solution.py:412
  26.8 10.9 %collective-permute-start.14 = (bf16[2,4,112,128]{3,2,1,0:T(8,128)(2,1)S(1)}, bf16[2,4,112,128]{3,2,1,0:T(8,128)(2,1)S(1)}, u32[]{:S(2)}, u32[]{:S(2)}) collective-permute-start(bf16[2,4,112,128]{3,2,1,0:T(8,128)(2,1)S(1)} %get-tuple-element.30), channel_id=1, source_target_pairs={{0,2},{1,7},{2,0},{3,5},{4,6},{5,3},{6,4},{7,1},{8,10},{9,15},{10,... | collective-permute-start | bytes 688136 | tf_op jit(solution)/shard_map/ppermute | solution.py:412
  28.4 10.3 %collective-permute-start.5 = (bf16[2,4,112,128]{3,2,1,0:T(8,128)(2,1)S(1)}, bf16[2,4,112,128]{3,2,1,0:T(8,128)(2,1)S(1)}, u32[]{:S(2)}, u32[]{:S(2)}) collective-permute-start(bf16[2,4,112,128]{3,2,1,0:T(8,128)(2,1)S(1)} %get-tuple-element.31), channel_id=1, source_target_pairs={{0,192},{1,65},{64,128},{65,1},{128,64},{129,193},{192,0},{193,129... | collective-permute-start | bytes 688136 | tf_op jit(solution)/shard_map/ppermute | solution.py:412
  32.9 6.6 %collective-permute-start.6 = (bf16[2,4,112,128]{3,2,1,0:T(8,128)(2,1)S(1)}, bf16[2,4,112,128]{3,2,1,0:T(8,128)(2,1)S(1)}, u32[]{:S(2)}, u32[]{:S(2)}) collective-permute-start(bf16[2,4,112,128]{3,2,1,0:T(8,128)(2,1)S(1)} %collective-permute-done.4), channel_id=1, source_target_pairs={{0,192},{1,65},{64,128},{65,1},{128,64},{129,193},{192,0},{193,129... | collective-permute-start | bytes 688136 | tf_op jit(solution)/shard_map/ppermute | solution.py:412
  35.5 8.7 %collective-permute-start.15 = (bf16[2,4,112,128]{3,2,1,0:T(8,128)(2,1)S(1)}, bf16[2,4,112,128]{3,2,1,0:T(8,128)(2,1)S(1)}, u32[]{:S(2)}, u32[]{:S(2)}) collective-permute-start(bf16[2,4,112,128]{3,2,1,0:T(8,128)(2,1)S(1)} %get-tuple-element.30), channel_id=1, source_target_pairs={{0,6},{1,3},{2,4},{3,1},{4,2},{5,7},{6,0},{7,5},{8,14},{9,11},{10,... | collective-permute-start | bytes 688136 | tf_op jit(solution)/shard_map/ppermute | solution.py:412
  37.8 7.4 %collective-permute-start.16 = (bf16[2,4,112,128]{3,2,1,0:T(8,128)(2,1)S(1)}, bf16[2,4,112,128]{3,2,1,0:T(8,128)(2,1)S(1)}, u32[]{:S(2)}, u32[]{:S(2)}) collective-permute-start(bf16[2,4,112,128]{3,2,1,0:T(8,128)(2,1)S(1)} %collective-permute-done.14), channel_id=1, source_target_pairs={{0,6},{1,3},{2,4},{3,1},{4,2},{5,7},{6,0},{7,5},{8,14},{9,11},{10,... | collective-permute-start | bytes 688136 | tf_op jit(solution)/shard_map/ppermute | solution.py:412
  39.6 45.4 %copy-start = (bf16[4,2,4,112,128]{4,3,2,1,0:T(8,128)(2,1)}, bf16[4,2,4,112,128]{4,3,2,1,0:T(8,128)(2,1)S(1)}, u32[]{:S(2)}) copy-start(bf16[4,2,4,112,128]{4,3,2,1,0:T(8,128)(2,1)S(1)} %pad_maximum_fusion.refs_0_) | copy-start | bytes 2752516
  39.6 7.6 %collective-permute-start.10 = (bf16[4,2,4,112,128]{4,3,2,1,0:T(8,128)(2,1)S(1)}, bf16[4,2,4,112,128]{4,3,2,1,0:T(8,128)(2,1)S(1)}, u32[]{:S(2)}, u32[]{:S(2)}) collective-permute-start(bf16[4,2,4,112,128]{4,3,2,1,0:T(8,128)(2,1)S(1)} %pad_maximum_fusion.refs_0_), channel_id=1, source_target_pairs={{0,1},{1,0},{2,3},{3,2},{4,5},{5,4},{6,7},{7,6},{8,9},{9,8},{10,11... | collective-permute-start | bytes 2752520 | tf_op jit(solution)/shard_map/ppermute | solution.py:416
  39.7 25.0 %collective-permute-start.8 = (bf16[4,2,4,112,128]{4,3,2,1,0:T(8,128)(2,1)S(1)}, bf16[4,2,4,112,128]{4,3,2,1,0:T(8,128)(2,1)S(1)}, u32[]{:S(2)}, u32[]{:S(2)}) collective-permute-start(bf16[4,2,4,112,128]{4,3,2,1,0:T(8,128)(2,1)S(1)} %pad_maximum_fusion.refs_0_), channel_id=1, source_target_pairs={{0,6},{1,3},{2,4},{3,1},{4,2},{5,7},{6,0},{7,5},{8,14},{9,11},{10,... | collective-permute-start | bytes 2752520 | tf_op jit(solution)/shard_map/ppermute | solution.py:412
  44.1 20.6 %collective-permute-start.7 = (bf16[4,2,4,112,128]{4,3,2,1,0:T(8,128)(2,1)S(1)}, bf16[4,2,4,112,128]{4,3,2,1,0:T(8,128)(2,1)}, u32[]{:S(2)}, u32[]{:S(2)}) collective-permute-start(bf16[4,2,4,112,128]{4,3,2,1,0:T(8,128)(2,1)S(1)} %pad_maximum_fusion.refs_0_), channel_id=1, source_target_pairs={{0,2},{1,7},{2,0},{3,5},{4,6},{5,3},{6,4},{7,1},{8,10},{9,15},{10,... | collective-permute-start | bytes 2752520 | tf_op jit(solution)/shard_map/ppermute | solution.py:412
  45.3 39.8 %copy-start.1 = (bf16[4,2,4,112,128]{4,3,2,1,0:T(8,128)(2,1)}, bf16[4,2,4,112,128]{4,3,2,1,0:T(8,128)(2,1)S(1)}, u32[]{:S(2)}) copy-start(bf16[4,2,4,112,128]{4,3,2,1,0:T(8,128)(2,1)S(1)} %pad_maximum_fusion.1.refs_8_) | copy-start | bytes 2752516
  45.3 23.2 %collective-permute-start.17 = (bf16[4,2,4,112,128]{4,3,2,1,0:T(8,128)(2,1)S(1)}, bf16[4,2,4,112,128]{4,3,2,1,0:T(8,128)(2,1)}, u32[]{:S(2)}, u32[]{:S(2)}) collective-permute-start(bf16[4,2,4,112,128]{4,3,2,1,0:T(8,128)(2,1)S(1)} %pad_maximum_fusion.1.refs_8_), channel_id=1, source_target_pairs={{0,64},{1,193},{64,0},{65,129},{128,192},{129,65},{192,128},{193,1... | collective-permute-start | bytes 2752520 | tf_op jit(solution)/shard_map/ppermute | solution.py:412
  47.2 23.0 %collective-permute-start.20 = (bf16[4,2,4,112,128]{4,3,2,1,0:T(8,128)(2,1)S(1)}, bf16[4,2,4,112,128]{4,3,2,1,0:T(8,128)(2,1)S(1)}, u32[]{:S(2)}, u32[]{:S(2)}) collective-permute-start(bf16[4,2,4,112,128]{4,3,2,1,0:T(8,128)(2,1)S(1)} %pad_maximum_fusion.1.refs_8_), channel_id=1, source_target_pairs={{0,1},{1,0},{2,3},{3,2},{4,5},{5,4},{6,7},{7,6},{8,9},{9,8},{10,11... | collective-permute-start | bytes 2752520 | tf_op jit(solution)/shard_map/ppermute | solution.py:416
  47.3 37.8 %copy-start.3 = (bf16[4,2,4,112,128]{4,3,2,1,0:T(8,128)(2,1)}, bf16[4,2,4,112,128]{4,3,2,1,0:T(8,128)(2,1)S(1)}, u32[]{:S(2)}) copy-start(bf16[4,2,4,112,128]{4,3,2,1,0:T(8,128)(2,1)S(1)} %collective-permute-done.10.refs_4_) | copy-start | bytes 2752516
  47.3 23.0 %collective-permute-start.18 = (bf16[4,2,4,112,128]{4,3,2,1,0:T(8,128)(2,1)S(1)}, bf16[4,2,4,112,128]{4,3,2,1,0:T(8,128)(2,1)}, u32[]{:S(2)}, u32[]{:S(2)}) collective-permute-start(bf16[4,2,4,112,128]{4,3,2,1,0:T(8,128)(2,1)S(1)} %pad_maximum_fusion.1.refs_8_), channel_id=1, source_target_pairs={{0,192},{1,65},{64,128},{65,1},{128,64},{129,193},{192,0},{193,129... | collective-permute-start | bytes 2752520 | tf_op jit(solution)/shard_map/ppermute | solution.py:412
  64.7 5.5 %copy-start.4 = (bf16[4,2,4,112,128]{4,3,2,1,0:T(8,128)(2,1)}, bf16[4,2,4,112,128]{4,3,2,1,0:T(8,128)(2,1)S(1)}, u32[]{:S(2)}) copy-start(bf16[4,2,4,112,128]{4,3,2,1,0:T(8,128)(2,1)S(1)} %collective-permute-done.8.refs_2_) | copy-start | bytes 2752516
  64.7 6.0 %collective-permute-start.12 = (bf16[4,2,4,112,128]{4,3,2,1,0:T(8,128)(2,1)S(1)}, bf16[4,2,4,112,128]{4,3,2,1,0:T(8,128)(2,1)S(1)}, u32[]{:S(2)}, u32[]{:S(2)}) collective-permute-start(bf16[4,2,4,112,128]{4,3,2,1,0:T(8,128)(2,1)S(1)} %collective-permute-done.8.refs_2_), channel_id=1, source_target_pairs={{0,1},{1,0},{2,3},{3,2},{4,5},{5,4},{6,7},{7,6},{8,9},{9,8},{10,11... | collective-permute-start | bytes 2752520 | tf_op jit(solution)/shard_map/ppermute | solution.py:416
  64.7 15.5 %collective-permute-start.9 = (bf16[4,2,4,112,128]{4,3,2,1,0:T(8,128)(2,1)}, bf16[4,2,4,112,128]{4,3,2,1,0:T(8,128)(2,1)}, u32[]{:S(2)}, u32[]{:S(2)}) collective-permute-start(bf16[4,2,4,112,128]{4,3,2,1,0:T(8,128)(2,1)} %collective-permute-done.7.refs_1_), channel_id=1, source_target_pairs={{0,6},{1,3},{2,4},{3,1},{4,2},{5,7},{6,0},{7,5},{8,14},{9,11},{10,... | collective-permute-start | bytes 2752520 | tf_op jit(solution)/shard_map/ppermute | solution.py:412
  68.5 13.7 %collective-permute-start.19 = (bf16[4,2,4,112,128]{4,3,2,1,0:T(8,128)(2,1)}, bf16[4,2,4,112,128]{4,3,2,1,0:T(8,128)(2,1)}, u32[]{:S(2)}, u32[]{:S(2)}) collective-permute-start(bf16[4,2,4,112,128]{4,3,2,1,0:T(8,128)(2,1)} %collective-permute-done.17.refs_9_), channel_id=1, source_target_pairs={{0,192},{1,65},{64,128},{65,1},{128,64},{129,193},{192,0},{193,129... | collective-permute-start | bytes 2752520 | tf_op jit(solution)/shard_map/ppermute | solution.py:412
  70.2 0.9 copy-start.5
  70.2 12.6 %collective-permute-start.11 = (bf16[4,2,4,112,128]{4,3,2,1,0:T(8,128)(2,1)}, bf16[4,2,4,112,128]{4,3,2,1,0:T(8,128)(2,1)}, u32[]{:S(2)}, u32[]{:S(2)}) collective-permute-start(bf16[4,2,4,112,128]{4,3,2,1,0:T(8,128)(2,1)} %collective-permute-done.7.refs_1_), channel_id=1, source_target_pairs={{0,1},{1,0},{2,3},{3,2},{4,5},{5,4},{6,7},{7,6},{8,9},{9,8},{10,11... | collective-permute-start | bytes 2752520 | tf_op jit(solution)/shard_map/ppermute | solution.py:416
  70.3 12.6 %collective-permute-start.21 = (bf16[4,2,4,112,128]{4,3,2,1,0:T(8,128)(2,1)}, bf16[4,2,4,112,128]{4,3,2,1,0:T(8,128)(2,1)}, u32[]{:S(2)}, u32[]{:S(2)}) collective-permute-start(bf16[4,2,4,112,128]{4,3,2,1,0:T(8,128)(2,1)} %collective-permute-done.17.refs_9_), channel_id=1, source_target_pairs={{0,1},{1,0},{2,3},{3,2},{4,5},{5,4},{6,7},{7,6},{8,9},{9,8},{10,11... | collective-permute-start | bytes 2752520 | tf_op jit(solution)/shard_map/ppermute | solution.py:416
  71.2 0.9 copy-start.6
  71.2 11.7 %collective-permute-start.22 = (bf16[4,2,4,112,128]{4,3,2,1,0:T(8,128)(2,1)}, bf16[4,2,4,112,128]{4,3,2,1,0:T(8,128)(2,1)}, u32[]{:S(2)}, u32[]{:S(2)}) collective-permute-start(bf16[4,2,4,112,128]{4,3,2,1,0:T(8,128)(2,1)} %collective-permute-done.18.refs_10_), channel_id=1, source_target_pairs={{0,1},{1,0},{2,3},{3,2},{4,5},{5,4},{6,7},{7,6},{8,9},{9,8},{10,11... | collective-permute-start | bytes 2752520 | tf_op jit(solution)/shard_map/ppermute | solution.py:416
  80.2 2.8 %collective-permute-start.13 = (bf16[4,2,4,112,128]{4,3,2,1,0:T(8,128)(2,1)}, bf16[4,2,4,112,128]{4,3,2,1,0:T(8,128)(2,1)}, u32[]{:S(2)}, u32[]{:S(2)}) collective-permute-start(bf16[4,2,4,112,128]{4,3,2,1,0:T(8,128)(2,1)} %collective-permute-done.9.refs_3_), channel_id=1, source_target_pairs={{0,1},{1,0},{2,3},{3,2},{4,5},{5,4},{6,7},{7,6},{8,9},{9,8},{10,11... | collective-permute-start | bytes 2752520 | tf_op jit(solution)/shard_map/ppermute | solution.py:416
  82.2 2.8 %collective-permute-start.23 = (bf16[4,2,4,112,128]{4,3,2,1,0:T(8,128)(2,1)}, bf16[4,2,4,112,128]{4,3,2,1,0:T(8,128)(2,1)}, u32[]{:S(2)}, u32[]{:S(2)}) collective-permute-start(bf16[4,2,4,112,128]{4,3,2,1,0:T(8,128)(2,1)} %collective-permute-done.19.refs_11_), channel_id=1, source_target_pairs={{0,1},{1,0},{2,3},{3,2},{4,5},{5,4},{6,7},{7,6},{8,9},{9,8},{10,11... | collective-permute-start | bytes 2752520 | tf_op jit(solution)/shard_map/ppermute | solution.py:416
  102.3 34.5 %copy-start.2 = (bf16[8,256,384]{2,1,0:T(8,128)(2,1)S(1)}, bf16[8,256,384]{2,1,0:T(8,128)(2,1)}, u32[]{:S(2)}) copy-start(bf16[8,256,384]{2,1,0:T(8,128)(2,1)} %get-tuple-element.15.refs_21_) | copy-start | bytes 4718596
  165.9 2.8 %collective-permute-start.24 = (bf16[4,4,112,256]{3,2,1,0:T(8,128)(2,1)}, bf16[4,4,112,256]{3,2,1,0:T(8,128)(2,1)S(1)}, u32[]{:S(2)}, u32[]{:S(2)}) collective-permute-start(bf16[4,4,112,256]{3,2,1,0:T(8,128)(2,1)} %get-tuple-element.21), channel_id=1, source_target_pairs={{0,1},{1,0},{2,3},{3,2},{4,5},{5,4},{6,7},{7,6},{8,9},{9,8},{10,11... | collective-permute-start | bytes 2752520 | tf_op jit(solution)/shard_map/ppermute | solution.py:416
  170.1 8.6 %collective-permute-start.25 = (bf16[2,4,112,256]{3,2,1,0:T(8,128)(2,1)S(1)}, bf16[2,4,112,256]{3,2,1,0:T(8,128)(2,1)S(1)}, u32[]{:S(2)}, u32[]{:S(2)}) collective-permute-start(bf16[2,4,112,256]{3,2,1,0:T(8,128)(2,1)S(1)} %get-tuple-element.27), channel_id=1, source_target_pairs={{0,2},{1,7},{2,0},{3,5},{4,6},{5,3},{6,4},{7,1},{8,10},{9,15},{10,... | collective-permute-start | bytes 1376264 | tf_op jit(solution)/shard_map/ppermute | solution.py:412
  178.7 7.3 %collective-permute-start.26 = (bf16[4,112,256]{2,1,0:T(8,128)(2,1)S(1)}, bf16[4,112,256]{2,1,0:T(8,128)(2,1)S(1)}, u32[]{:S(2)}, u32[]{:S(2)}) collective-permute-start(bf16[4,112,256]{2,1,0:T(8,128)(2,1)S(1)} %fusion.2), channel_id=1, source_target_pairs={{0,6},{1,3},{2,4},{3,1},{4,2},{5,7},{6,0},{7,5},{8,14},{9,11},{10,... | collective-permute-start | bytes 688136 | tf_op jit(solution)/shard_map/ppermute | solution.py:412
  186.7 8.4 %collective-permute-start.29 = (bf16[112,256]{1,0:T(8,128)(2,1)S(1)}, bf16[112,256]{1,0:T(8,128)(2,1)S(1)}, u32[]{:S(2)}, u32[]{:S(2)}) collective-permute-start(bf16[112,256]{1,0:T(8,128)(2,1)S(1)} %get-tuple-element.32), channel_id=1, source_target_pairs={{0,16},{8,24},{16,0},{24,8},{1,17},{9,25},{17,1},{25,9},{2,18},{10... | collective-permute-start | bytes 172040 | tf_op jit(solution)/shard_map/ppermute | solution.py:420
  188.0 8.4 %collective-permute-start.28 = (bf16[112,256]{1,0:T(8,128)(2,1)S(1)}, bf16[112,256]{1,0:T(8,128)(2,1)S(1)}, u32[]{:S(2)}, u32[]{:S(2)}) collective-permute-start(bf16[112,256]{1,0:T(8,128)(2,1)S(1)} %get-tuple-element.33), channel_id=1, source_target_pairs={{0,24},{1,9},{8,16},{9,1},{16,8},{17,25},{24,0},{25,17},{2,26},{3,... | collective-permute-start | bytes 172040 | tf_op jit(solution)/shard_map/ppermute | solution.py:412
  192.8 5.1 %collective-permute-start.27 = (bf16[112,256]{1,0:T(8,128)(2,1)S(1)}, bf16[112,256]{1,0:T(8,128)(2,1)S(1)}, u32[]{:S(2)}, u32[]{:S(2)}) collective-permute-start(bf16[112,256]{1,0:T(8,128)(2,1)S(1)} %get-tuple-element.34), channel_id=1, source_target_pairs={{0,8},{1,25},{8,0},{9,17},{16,24},{17,9},{24,16},{25,1},{2,10},{3,... | collective-permute-start | bytes 172040 | tf_op jit(solution)/shard_map/ppermute | solution.py:412
  195.2 2.7 %copy-start.7 = (bf16[112,256]{1,0:T(8,128)(2,1)}, bf16[112,256]{1,0:T(8,128)(2,1)S(1)}, u32[]{:S(2)}) copy-start(bf16[112,256]{1,0:T(8,128)(2,1)S(1)} %collective-permute-done.29.d_ref) | copy-start | bytes 172036
  196.4 1.5 copy-start.8
  197.9 0.6 copy-start.9

commit v3 on v1

--- a/solution.py
+++ b/solution.py
@@ -115,10 +115,10 @@
 
 
 def sequence_kernel(pos_ref, *refs):
-    left, right = refs[:8], refs[8:16]
-    entry_ref, cot_ref, sent_ref = refs[16:19]
-    w_scr, rows_scr, xs, ns, mixed_scr, decay_scr, write_scr, small_scr, proj_scr = refs[19:28]
-    first_scr, sem_a, sem_b, sem_c = refs[28:]
+    left, right = refs[:16], refs[16:32]
+    entry_ref, cot_ref, sent_ref = refs[32:35]
+    w_scr, rows_scr, xs, ns, mixed_scr, decay_scr, write_scr, small_scr, proj_scr = refs[35:44]
+    first_scr, sem_a, sem_b, sem_c = refs[44:]
     x, y, c, zh, section = (pos_ref[i] for i in range(5))
     mine = jnp.minimum(section, SEQS - 1)
     loads = []
@@ -133,33 +133,30 @@
         one, two = partner(i, core, True), partner(i, core, False)
         return [i, one, two, partner(two, core, True)]
 
-    copies = []
-    for kc in range(2):
-        cc = (c + kc) % 2
-        ys, xx = ring(y, cc), ring(x, cc)
-        for i in range(4):
-            for j in range(4):
-                at = pl.ds(2 * xx[j], 2)
-                copy = pltpu.make_async_copy(
-                    left[kc * 4 + i].at[j],
-                    w_scr.at[at, :, ys[i], cc, :, :C],
-                    sem_a.at[xx[j]],
-                )
-                copy.start()
-                at = pl.ds(2 * xx[i], 2)
-                copy = pltpu.make_async_copy(
-                    right[kc * 4 + i].at[j],
-                    w_scr.at[at, :, ys[j], cc, :, C:],
-                    sem_b.at[xx[i]],
-                )
-                copy.start()
-
-    def wait_layers(at):
-        for sem, src in ((sem_a, left[0]), (sem_b, right[0])):
-            for _ in range(8):
+    for part in range(2):
+        for kc in range(2):
+            cc = (c + kc) % 2
+            ys, xx = ring(y, cc), ring(x, cc)
+            for i in range(4):
+                at = (kc * 2 + part) * 4 + i
                 pltpu.make_async_copy(
-                    src.at[0], w_scr.at[0:2, :, 0, 0, :, :C], sem.at[at]
-                ).wait()
+                    left[at],
+                    w_scr.at[4 * part : 4 * part + 4, :, ys[i], cc, :, :C],
+                    sem_a.at[part],
+                ).start()
+                pltpu.make_async_copy(
+                    right[at], w_scr.at[2 * xx[i] + part, :, :, cc, :, C:], sem_b.at[xx[i]]
+                ).start()
+
+    def wait_left(part):
+        for _ in range(8):
+            pltpu.make_async_copy(
+                left[0], w_scr.at[0:4, :, 0, 0, :, :C], sem_a.at[part]
+            ).wait()
+
+    def wait_right(at):
+        for _ in range(4):
+            pltpu.make_async_copy(right[0], w_scr.at[0, :, :, 0, :, C:], sem_b.at[at]).wait()
 
     causal, diag, spread, block, tri = masks()
 
@@ -168,9 +165,13 @@
         return jnp.concatenate(parts, axis=0)
 
     def forward(layer, stream):
+        @pl.when(layer % 4 == 0)
+        def _():
+            wait_left(layer // 4)
+
         @pl.when(layer % 2 == 0)
         def _():
-            wait_layers(layer // 2)
+            wait_right(layer // 2)
 
         rows = assemble_rows(lambda d: w_scr[layer, d // 8, d // 2 % 4, d % 2, ROWS:])
         rows_low = rows.astype(BF16)
@@ -384,14 +385,14 @@
     return lax.ppermute(array, axis, [(i, i ^ 2) for i in range(4)])
 
 
-def gather_ring(array, axis, direct=False):
+def gather_ring(array, axis):
     one = swap(array, axis, True)
     two = swap(array, axis, False)
-    return [array, one, two, opposite(array, axis) if direct else swap(one, axis, False)]
-
-
-def add(a, b):
-    return (a.astype(F32) + b.astype(F32)).astype(BF16)
+    return [array, one, two, swap(one, axis, False)]
+
+
+def add(*parts):
+    return sum(a.astype(F32) for a in parts).astype(BF16)
 
 
 def per_device(entries, cotangents, scales, key_weight, rate_weight, rate_bias):
@@ -407,30 +408,38 @@
         [key_weight[0], jnp.concatenate([wide[:16], right], axis=1)], axis=0
     )
 
-    along = jnp.stack(gather_ring(packed, "zh", direct=True))
-    first, second = partner(zh, c, True), partner(zh, c, False)
-    across = partner(second, c, True)
-    order = [jnp.where(j == first, 1, jnp.where(j == second, 2, jnp.where(j == across, 3, 0))) for j in range(4)]
-    along = jnp.take(along, jnp.stack(order), axis=0)
-    pairs = []
-    for z in range(8):
-        for core in range(2):
-            to = z ^ 1 if core == 0 else (z + 1 if z % 2 else z - 1) % 8
-            pairs.append(tuple(((i % 2) * 4 + i // 2) * 2 + core for i in (z, to)))
-    other = lax.ppermute(along, ("zl", "zh", "c"), pairs)
-    both = jnp.where(zl == 0, jnp.stack([along, other]), jnp.stack([other, along]))
+    along = [packed] + [None] * 7
+    for k in (4, 3, 5, 2, 6, 1, 7):
+        pairs = []
+        for z in range(8):
+            for core in range(2):
+                to = (z + k if core == 0 else z - k) % 8
+                pairs.append(tuple(((i % 2) * 4 + i // 2) * 2 + core for i in (z, to)))
+        along[k] = lax.ppermute(packed, ("zl", "zh", "c"), pairs)
+    z = zh * 2 + zl
+    there = jnp.arange(4)[None] * 2 + jnp.arange(2)[:, None]
+    both = jnp.take(jnp.stack(along), jnp.where(c == 0, z - there, there - z) % 8, axis=0)
+
+    def order(i):
+        bits = gray(jnp.arange(4)) ^ gray(i)
+        return jnp.where(c == 0, jnp.array([0, 1, 2, 3])[bits], jnp.array([0, 2, 1, 3])[bits])
 
     left = jnp.stack(gather_ring(both[..., :C], "x"))
-    right = jnp.stack(gather_ring(both[..., C:], "y"))
-    left = gather_ring(left, "y")
-    right = gather_ring(right, "x")
-    left = left + [other_core(a) for a in left]
-    right = right + [other_core(a) for a in right]
+    right = jnp.stack(gather_ring(both[..., C:], "y"), axis=2)
+    x_order, y_order = order(x), order(y)
+    lefts, rights = [], []
+    for part in range(2):
+        own = jnp.take(left, x_order[2 * part : 2 * part + 2], axis=0)
+        lefts += gather_ring(own.reshape(4, 4, PIECE, C), "y")
+        own = jnp.take(right[part], y_order, axis=1)
+        rights += gather_ring(own, "x")
+    left = lefts + [other_core(a) for a in lefts]
+    right = rights + [other_core(a) for a in rights]
 
     sent = call(
         sequence_kernel,
         [shape(LAYERS, SENT, BLOCK)],
-        [SMEM] + [ANY] * 18,
+        [SMEM] + [ANY] * 34,
         [
             pltpu.VMEM((LAYERS, 4, 4, 2, PIECE, 256), BF16),
             pltpu.VMEM((LAYERS, T, D), BF16),
@@ -442,7 +451,7 @@
             pltpu.VMEM((LAYERS, T, 256), F32),
             pltpu.VMEM((LAYERS, T, 256), F32),
             pltpu.VMEM((2, T, D), BF16),
-            pltpu.SemaphoreType.DMA((4,)),
+            pltpu.SemaphoreType.DMA((2,)),
             pltpu.SemaphoreType.DMA((4,)),
             pltpu.SemaphoreType.DMA((2,)),
         ],
@@ -465,11 +474,10 @@
         cost=(600_000_000, 4_000_000),
     )(pos, got)
     got = other_core(send)
-    got = swap(add(keep[2:], got[2:]), "y", True), keep[:2], got[:2]
-    keep = add(got[1], got[2])
-    got = got[0]
-    got, keep = swap(add(keep[1], got[1]), "y", False), add(keep[0], got[0])
-    got = add(keep, got)
+    total = [add(keep[i], got[i]) for i in range(4)]
+    got = add(
+        total[0], swap(total[2], "y", True), swap(total[1], "y", False), opposite(total[3], "y")
+    )
     parts = [
         got[0],
         swap(got[2], "zh", True),

time: 186 us -> 210 us (1.13)
  starting transfers between devices: 42.8 us -> 57.2 us
  local copies, waits for them, and re-layouts: 5.39 us -> 10 us
  waiting for transfers between devices: 65.3 us -> 68.8 us
    ppermute x1 -> x7, starting transfers between devices: 1.18 us -> 16.1 us  [per_device(): along[k] = lax.ppermute(packed, ('zl', 'zh', 'c'), pairs)]
    ppermute x18 -> x22, starting transfers between devices: 38.6 us -> 25.8 us  [swap(): return lax.ppermute(array, (axis, 'c'), ring_pairs(first))]
    ppermute x2, starting transfers between devices: 2.26 us -> 9.05 us  [opposite(): return lax.ppermute(array, axis, [(i, i ^ 2) for i in range(4)])]
    gather x1 -> x9, local copies, waits for them, and re-layouts: 0.56 us -> 6.33 us  [the longest x2 1.93 us: order(): jnp.array([0, 2, 1, 3])[bits]]
    ppermute x9 -> x17, starting transfers between devices: 0.69 us -> 6.19 us  [other_core(): return lax.ppermute(array, 'c', [(0, 1), (1, 0)])]
    ppermute x1 -> x7, waiting for transfers between devices: 4.83 us -> 9.6 us  [per_device(): along[k] = lax.ppermute(packed, ('zl', 'zh', 'c'), pairs)]
    ppermute x18 -> x22, waiting for transfers between devices: 49.8 us -> 45.9 us  [swap(): return lax.ppermute(array, (axis, 'c'), ring_pairs(first))]
    ppermute x2, waiting for transfers between devices: 5.87 us -> 9.19 us  [opposite(): return lax.ppermute(array, axis, [(i, i ^ 2) for i in range(4)])]
  transfers between devices with their start and end apart: 30 -> 48, of which waited for: 18 -> 20; matrix products, arithmetic and copies ran while one was open for 1% -> 4% of each run, Pallas kernels for 0% -> 0%
where the time goes in v3:
time: 210 us; the launch traced here: 209 us
  waiting for transfers between devices  68.8 us (33%)
  starting transfers between devices  57.2 us (27%)
  Pallas kernels  36.2 us (17%)
  blocking collectives  30.8 us (15%)
  local copies, waits for them, and re-layouts  10 us (5%)
  other arithmetic  4.98 us (2%)
    ppermute x22, waiting for transfers between devices, swap(): return lax.ppermute(array, (axis, 'c'), ring_pairs(first))  45.9 us
    all_to_all x1, blocking collectives, per_device(): got = lax.all_to_all(sent, SECTION, 0, 0, tiled=True)  30.8 us
    pallas_call x1, Pallas kernels, per_device(): call(sequence_kernel, [shape(LAYERS, SENT, BLOCK)], [SMEM] + [ANY] * 34,...  29.3 us
    ppermute x22, starting transfers between devices, swap(): return lax.ppermute(array, (axis, 'c'), ring_pairs(first))  25.8 us
    ppermute x7, starting transfers between devices, per_device(): along[k] = lax.ppermute(packed, ('zl', 'zh', 'c'), pairs)  16.1 us
    ppermute x7, waiting for transfers between devices, per_device(): along[k] = lax.ppermute(packed, ('zl', 'zh', 'c'), pairs)  9.6 us
    ppermute x2, waiting for transfers between devices, opposite(): return lax.ppermute(array, axis, [(i, i ^ 2) for i in range(4)])  9.19 us
    ppermute x2, starting transfers between devices, opposite(): return lax.ppermute(array, axis, [(i, i ^ 2) for i in range(4)])  9.05 us
  transfers between devices with their start and end apart: 48, of which 20 were waited for; matrix products, arithmetic and copies ran while one was open for 4% of the time, Pallas kernels for 0%

profile of v3, /device:TPU:2, one launch (start us, length us, event | category | flops | bytes accessed | tf_op | source)
XLA Modules:
  0.0 209.2 jit_solution(11355255860080367560)
XLA Ops:
  1.3 0.7 pad_slice_fusion.1
  2.0 0.8 maximum_maximum_fusion
  2.9 6.4 %collective-permute-start.5 = (bf16[112,256]{1,0:T(8,128)(2,1)S(1)}, bf16[112,256]{1,0:T(8,128)(2,1)S(1)}, u32[]{:S(2)}, u32[]{:S(2)}) collective-permute-start(bf16[112,256]{1,0:T(8,128)(2,1)S(1)} %maximum_maximum_fusion), channel_id=1, source_target_pairs={{0,24},{1,9},{32,56},{33,41},{8,0},{9,17},{40,32},{41,49},{16,8},{... | collective-permute-start | bytes 172040 | tf_op jit(solution)/shard_map/ppermute | solution.py:418
  9.2 1.0 collective-permute-start.4
  10.2 4.5 %collective-permute-start.3 = (bf16[112,256]{1,0:T(8,128)(2,1)S(1)}, bf16[112,256]{1,0:T(8,128)(2,1)S(1)}, u32[]{:S(2)}, u32[]{:S(2)}) collective-permute-start(bf16[112,256]{1,0:T(8,128)(2,1)S(1)} %maximum_maximum_fusion), channel_id=1, source_target_pairs={{0,16},{1,17},{32,48},{33,49},{8,24},{9,25},{40,56},{41,57},{16,0}... | collective-permute-start | bytes 172040 | tf_op jit(solution)/shard_map/ppermute | solution.py:418
  14.7 2.0 collective-permute-start
  16.8 0.8 bitcast_dynamic-update-slice_fusion.7
  17.7 1.3 gather_fusion.4
  19.7 0.9 collective-permute-done
  20.6 2.3 %collective-permute-start.1 = (bf16[112,256]{1,0:T(8,128)(2,1)S(1)}, bf16[112,256]{1,0:T(8,128)(2,1)S(1)}, u32[]{:S(2)}, u32[]{:S(2)}) collective-permute-start(bf16[112,256]{1,0:T(8,128)(2,1)S(1)} %maximum_maximum_fusion), channel_id=1, source_target_pairs={{0,8},{1,25},{32,40},{33,57},{8,16},{9,1},{40,48},{41,33},{16,24},... | collective-permute-start | bytes 172040 | tf_op jit(solution)/shard_map/ppermute | solution.py:418
  22.9 4.6 %collective-permute-done.1 = bf16[112,256]{1,0:T(8,128)(2,1)S(1)} collective-permute-done((bf16[112,256]{1,0:T(8,128)(2,1)S(1)}, bf16[112,256]{1,0:T(8,128)(2,1)S(1)}, u32[]{:S(2)}, u32[]{:S(2)}) %collective-permute-start.1) | collective-permute-done | bytes 57376 | tf_op jit(solution)/shard_map/ppermute | solution.py:418
  27.6 4.1 %collective-permute-done.6 = bf16[112,256]{1,0:T(8,128)(2,1)S(1)} collective-permute-done((bf16[112,256]{1,0:T(8,128)(2,1)S(1)}, bf16[112,256]{1,0:T(8,128)(2,1)S(1)}, u32[]{:S(2)}, u32[]{:S(2)}) %collective-permute-start.6) | collective-permute-done | bytes 57376 | tf_op jit(solution)/shard_map/ppermute | solution.py:418
  34.4 2.2 %collective-permute-start.8 = (bf16[2,4,112,128]{3,2,1,0:T(8,128)(2,1)S(1)}, bf16[2,4,112,128]{3,2,1,0:T(8,128)(2,1)S(1)}, u32[]{:S(2)}, u32[]{:S(2)}) collective-permute-start(bf16[2,4,112,128]{3,2,1,0:T(8,128)(2,1)S(1)} %get-tuple-element.32), channel_id=1, source_target_pairs={{0,192},{1,65},{64,128},{65,1},{128,64},{129,193},{192,0},{193,129... | collective-permute-start | bytes 688136 | tf_op jit(solution)/shard_map/ppermute | solution.py:377
  36.7 1.6 collective-permute-start.24
  38.2 2.2 %collective-permute-done.7 = bf16[2,4,112,128]{3,2,1,0:T(8,128)(2,1)S(1)} collective-permute-done((bf16[2,4,112,128]{3,2,1,0:T(8,128)(2,1)S(1)}, bf16[2,4,112,128]{3,2,1,0:T(8,128)(2,1)S(1)}, u32[]{:S(2)}, u32[]{:S(2)}) %collective-permute-start.7) | collective-permute-done | bytes 229408 | tf_op jit(solution)/shard_map/ppermute | solution.py:377
  40.5 0.8 collective-permute-start.9
  41.3 3.1 %collective-permute-start.25 = (bf16[2,4,112,128]{3,2,1,0:T(8,128)(2,1)S(1)}, bf16[2,4,112,128]{3,2,1,0:T(8,128)(2,1)S(1)}, u32[]{:S(2)}, u32[]{:S(2)}) collective-permute-start(bf16[2,4,112,128]{3,2,1,0:T(8,128)(2,1)S(1)} %get-tuple-element.31), channel_id=1, source_target_pairs={{0,6},{1,3},{2,4},{3,1},{4,2},{5,7},{6,0},{7,5},{8,14},{9,11},{10,... | collective-permute-start | bytes 688136 | tf_op jit(solution)/shard_map/ppermute | solution.py:377
  45.1 2.8 %collective-permute-start.26 = (bf16[2,4,112,128]{3,2,1,0:T(8,128)(2,1)S(1)}, bf16[2,4,112,128]{3,2,1,0:T(8,128)(2,1)S(1)}, u32[]{:S(2)}, u32[]{:S(2)}) collective-permute-start(bf16[2,4,112,128]{3,2,1,0:T(8,128)(2,1)S(1)} %collective-permute-done.24), channel_id=1, source_target_pairs={{0,6},{1,3},{2,4},{3,1},{4,2},{5,7},{6,0},{7,5},{8,14},{9,11},{10,... | collective-permute-start | bytes 688136 | tf_op jit(solution)/shard_map/ppermute | solution.py:377
  48.9 2.3 %collective-permute-start.11 = (bf16[4,4,112,128]{3,2,1,0:T(8,128)(2,1)S(1)}, bf16[4,4,112,128]{3,2,1,0:T(8,128)(2,1)}, u32[]{:S(2)}, u32[]{:S(2)}) collective-permute-start(bf16[4,4,112,128]{3,2,1,0:T(8,128)(2,1)S(1)} %bitcast.85), channel_id=1, source_target_pairs={{0,6},{1,3},{2,4},{3,1},{4,2},{5,7},{6,0},{7,5},{8,14},{9,11},{10,... | collective-permute-start | bytes 1376264 | tf_op jit(solution)/shard_map/ppermute | solution.py:377
  52.7 2.5 %collective-permute-start.14 = (bf16[4,4,112,128]{3,2,1,0:T(8,128)(2,1)S(1)}, bf16[4,4,112,128]{3,2,1,0:T(8,128)(2,1)}, u32[]{:S(2)}, u32[]{:S(2)}) collective-permute-start(bf16[4,4,112,128]{3,2,1,0:T(8,128)(2,1)S(1)} %bitcast.89), channel_id=1, source_target_pairs={{0,6},{1,3},{2,4},{3,1},{4,2},{5,7},{6,0},{7,5},{8,14},{9,11},{10,... | collective-permute-start | bytes 1376264 | tf_op jit(solution)/shard_map/ppermute | solution.py:377
  56.9 6.8 %collective-permute-done.11.refs_2_ = bf16[4,4,112,128]{3,2,1,0:T(8,128)(2,1)} collective-permute-done((bf16[4,4,112,128]{3,2,1,0:T(8,128)(2,1)S(1)}, bf16[4,4,112,128]{3,2,1,0:T(8,128)(2,1)}, u32[]{:S(2)}, u32[]{:S(2)}) %collective-permute-start.11) | collective-permute-done | bytes 458784 | tf_op jit(solution)/shard_map/ppermute | solution.py:377
  63.7 1.1 collective-permute-done.10.refs_1_
  64.9 2.4 %collective-permute-start.30 = (bf16[4,4,112,128]{3,2,1,0:T(8,128)(2,1)S(1)}, bf16[4,4,112,128]{3,2,1,0:T(8,128)(2,1)S(1)}, u32[]{:S(2)}, u32[]{:S(2)}) collective-permute-start(bf16[4,4,112,128]{3,2,1,0:T(8,128)(2,1)S(1)} %get-tuple-element.37.refs_20_), channel_id=1, source_target_pairs={{0,64},{1,193},{64,0},{65,129},{128,192},{129,65},{192,128},{193,1... | collective-permute-start | bytes 1376264 | tf_op jit(solution)/shard_map/ppermute | solution.py:377
  67.3 6.2 %collective-permute-done.14.refs_6_ = bf16[4,4,112,128]{3,2,1,0:T(8,128)(2,1)} collective-permute-done((bf16[4,4,112,128]{3,2,1,0:T(8,128)(2,1)S(1)}, bf16[4,4,112,128]{3,2,1,0:T(8,128)(2,1)}, u32[]{:S(2)}, u32[]{:S(2)}) %collective-permute-start.14) | collective-permute-done | bytes 458784 | tf_op jit(solution)/shard_map/ppermute | solution.py:377
  73.6 2.4 %collective-permute-start.27 = (bf16[4,4,112,128]{3,2,1,0:T(8,128)(2,1)S(1)}, bf16[4,4,112,128]{3,2,1,0:T(8,128)(2,1)}, u32[]{:S(2)}, u32[]{:S(2)}) collective-permute-start(bf16[4,4,112,128]{3,2,1,0:T(8,128)(2,1)S(1)} %get-tuple-element.38.refs_16_), channel_id=1, source_target_pairs={{0,64},{1,193},{64,0},{65,129},{128,192},{129,65},{192,128},{193,1... | collective-permute-start | bytes 1376264 | tf_op jit(solution)/shard_map/ppermute | solution.py:377
  76.1 2.1 %collective-permute-done.31.refs_22_ = bf16[4,4,112,128]{3,2,1,0:T(8,128)(2,1)S(1)} collective-permute-done((bf16[4,4,112,128]{3,2,1,0:T(8,128)(2,1)S(1)}, bf16[4,4,112,128]{3,2,1,0:T(8,128)(2,1)S(1)}, u32[]{:S(2)}, u32[]{:S(2)}) %collective-permute-start.31) | collective-permute-done | bytes 458784 | tf_op jit(solution)/shard_map/ppermute | solution.py:377
  79.2 8.3 %collective-permute-done.28.refs_18_ = bf16[4,4,112,128]{3,2,1,0:T(8,128)(2,1)S(1)} collective-permute-done((bf16[4,4,112,128]{3,2,1,0:T(8,128)(2,1)S(1)}, bf16[4,4,112,128]{3,2,1,0:T(8,128)(2,1)S(1)}, u32[]{:S(2)}, u32[]{:S(2)}) %collective-permute-start.28) | collective-permute-done | bytes 458784 | tf_op jit(solution)/shard_map/ppermute | solution.py:377
  88.0 1.4 collective-permute-start.15
  90.1 2.5 %collective-permute-start.35 = (bf16[4,4,112,128]{3,2,1,0:T(8,128)(2,1)S(1)}, bf16[4,4,112,128]{3,2,1,0:T(8,128)(2,1)S(1)}, u32[]{:S(2)}, u32[]{:S(2)}) collective-permute-start(bf16[4,4,112,128]{3,2,1,0:T(8,128)(2,1)S(1)} %collective-permute-done.28.refs_18_), channel_id=1, source_target_pairs={{0,1},{1,0},{2,3},{3,2},{4,5},{5,4},{6,7},{7,6},{8,9},{9,8},{10,11... | collective-permute-start | bytes 1376264 | tf_op jit(solution)/shard_map/ppermute | solution.py:381
  92.6 5.1 %collective-permute-done.15.refs_7_ = bf16[4,4,112,128]{3,2,1,0:T(8,128)(2,1)} collective-permute-done((bf16[4,4,112,128]{3,2,1,0:T(8,128)(2,1)S(1)}, bf16[4,4,112,128]{3,2,1,0:T(8,128)(2,1)}, u32[]{:S(2)}, u32[]{:S(2)}) %collective-permute-start.15) | collective-permute-done | bytes 458784 | tf_op jit(solution)/shard_map/ppermute | solution.py:377
  98.9 0.7 collective-permute-start.40
  99.6 6.9 %collective-permute-done.29.refs_19_ = bf16[4,4,112,128]{3,2,1,0:T(8,128)(2,1)} collective-permute-done((bf16[4,4,112,128]{3,2,1,0:T(8,128)(2,1)}, bf16[4,4,112,128]{3,2,1,0:T(8,128)(2,1)}, u32[]{:S(2)}, u32[]{:S(2)}) %collective-permute-start.29) | collective-permute-done | bytes 458784 | tf_op jit(solution)/shard_map/ppermute | solution.py:377
  107.4 1.4 collective-permute-done.36.refs_27_
  108.9 29.3 %shard_map.129 = bf16[8,304,384]{2,1,0:T(8,128)(2,1)} custom-call(s32[5]{0:T(128)} %stack.80.pos_ref, bf16[4,4,112,128]{3,2,1,0:T(8,128)(2,1)} %bitcast.87, bf16[4,4,112,128]{3,2,1,0:T(8,128)(2,1)} %collective-permute-done.10.refs_1_, bf16[4,4,112,128]{3,2,1,0:T(8,128)(2,1)} %collective-permute-done.11.refs_2_, ...), custom_call_target="tpu_custom_call" | custom-call | flops 8000000000 | bytes 30000000 | tf_op jit(solution)/shard_map/pallas_call | solution.py:439
  138.1 30.8 %all_to_all.5.got_ref = bf16[8,304,384]{2,1,0:T(8,128)(2,1)} all-to-all(bf16[8,304,384]{2,1,0:T(8,128)(2,1)} %shard_map.129), channel_id=1, replica_groups=mesh['x'=4,'zl'=2,'zh'=4,'y'=4,'c'=2] {'x','zl'}, dimensions={0} | all-to-all | bytes 3735552 | tf_op jit(solution)/shard_map/all_to_all | solution.py:461
  168.9 5.4 %shard_map.130 = (bf16[4,4,112,256]{3,2,1,0:T(8,128)(2,1)}, bf16[4,4,112,256]{3,2,1,0:T(8,128)(2,1)}) custom-call(s32[5]{0:T(128)} %stack.80.pos_ref, bf16[8,304,384]{2,1,0:T(8,128)(2,1)} %all_to_all.5.got_ref), custom_call_target="tpu_custom_call" | custom-call | flops 600000000 | bytes 4000000 | tf_op jit(solution)/shard_map/pallas_call | solution.py:463
  174.4 2.7 %collective-permute-done.41 = bf16[4,4,112,256]{3,2,1,0:T(8,128)(2,1)S(1)} collective-permute-done((bf16[4,4,112,256]{3,2,1,0:T(8,128)(2,1)}, bf16[4,4,112,256]{3,2,1,0:T(8,128)(2,1)S(1)}, u32[]{:S(2)}, u32[]{:S(2)}) %collective-permute-start.41) | collective-permute-done | bytes 917536 | tf_op jit(solution)/shard_map/ppermute | solution.py:381
  177.1 1.3 fusion.6
  178.5 3.8 %collective-permute-start.44 = (bf16[4,112,256]{2,1,0:T(8,128)(2,1)S(1)}, bf16[4,112,256]{2,1,0:T(8,128)(2,1)S(1)}, u32[]{:S(2)}, u32[]{:S(2)}) collective-permute-start(bf16[4,112,256]{2,1,0:T(8,128)(2,1)S(1)} %get-tuple-element.25), channel_id=1, source_target_pairs={{0,4},{2,6},{4,0},{6,2},{1,5},{3,7},{5,1},{7,3},{8,12},{10,14},{12... | collective-permute-start | bytes 688136 | tf_op jit(solution)/shard_map/ppermute | solution.py:385
  182.3 0.9 collective-permute-start.43
  183.2 2.8 %collective-permute-done.42 = bf16[4,112,256]{2,1,0:T(8,128)(2,1)S(1)} collective-permute-done((bf16[4,112,256]{2,1,0:T(8,128)(2,1)S(1)}, bf16[4,112,256]{2,1,0:T(8,128)(2,1)S(1)}, u32[]{:S(2)}, u32[]{:S(2)}) %collective-permute-start.42) | collective-permute-done | bytes 229408 | tf_op jit(solution)/shard_map/ppermute | solution.py:377
  186.0 6.7 %collective-permute-done.44 = bf16[4,112,256]{2,1,0:T(8,128)(2,1)S(1)} collective-permute-done((bf16[4,112,256]{2,1,0:T(8,128)(2,1)S(1)}, bf16[4,112,256]{2,1,0:T(8,128)(2,1)S(1)}, u32[]{:S(2)}, u32[]{:S(2)}) %collective-permute-start.44) | collective-permute-done | bytes 229408 | tf_op jit(solution)/shard_map/ppermute | solution.py:385
  193.3 1.1 fusion.2
  195.0 5.3 %collective-permute-start.47 = (bf16[112,256]{1,0:T(8,128)(2,1)S(1)}, bf16[112,256]{1,0:T(8,128)(2,1)S(1)}, u32[]{:S(2)}, u32[]{:S(2)}) collective-permute-start(bf16[112,256]{1,0:T(8,128)(2,1)S(1)} %get-tuple-element.33), channel_id=1, source_target_pairs={{0,16},{8,24},{16,0},{24,8},{1,17},{9,25},{17,1},{25,9},{2,18},{10... | collective-permute-start | bytes 172040 | tf_op jit(solution)/shard_map/ppermute | solution.py:385
  200.3 1.0 collective-permute-start.46
  201.5 2.5 %collective-permute-done.47.d_ref = bf16[112,256]{1,0:T(8,128)(2,1)S(1)} collective-permute-done((bf16[112,256]{1,0:T(8,128)(2,1)S(1)}, bf16[112,256]{1,0:T(8,128)(2,1)S(1)}, u32[]{:S(2)}, u32[]{:S(2)}) %collective-permute-start.47) | collective-permute-done | bytes 57376 | tf_op jit(solution)/shard_map/ppermute | solution.py:385
  204.0 2.6 %collective-permute-done.46.c_ref = bf16[112,256]{1,0:T(8,128)(2,1)S(1)} collective-permute-done((bf16[112,256]{1,0:T(8,128)(2,1)S(1)}, bf16[112,256]{1,0:T(8,128)(2,1)S(1)}, u32[]{:S(2)}, u32[]{:S(2)}) %collective-permute-start.46) | collective-permute-done | bytes 57376 | tf_op jit(solution)/shard_map/ppermute | solution.py:377
  207.6 1.6 shard_map.131
  (142 shorter events, 16.2 us)
Async XLA Ops:
  2.9 24.7 %collective-permute-start.5 = (bf16[112,256]{1,0:T(8,128)(2,1)S(1)}, bf16[112,256]{1,0:T(8,128)(2,1)S(1)}, u32[]{:S(2)}, u32[]{:S(2)}) collective-permute-start(bf16[112,256]{1,0:T(8,128)(2,1)S(1)} %maximum_maximum_fusion), channel_id=1, source_target_pairs={{0,24},{1,9},{32,56},{33,41},{8,0},{9,17},{40,32},{41,49},{16,8},{... | collective-permute-start | bytes 172040 | tf_op jit(solution)/shard_map/ppermute | solution.py:418
  9.2 18.3 %collective-permute-start.4 = (bf16[112,256]{1,0:T(8,128)(2,1)S(1)}, bf16[112,256]{1,0:T(8,128)(2,1)S(1)}, u32[]{:S(2)}, u32[]{:S(2)}) collective-permute-start(bf16[112,256]{1,0:T(8,128)(2,1)S(1)} %maximum_maximum_fusion), channel_id=1, source_target_pairs={{0,48},{1,41},{32,24},{33,17},{8,56},{9,49},{40,0},{41,25},{16,32}... | collective-permute-start | bytes 172040 | tf_op jit(solution)/shard_map/ppermute | solution.py:418
  10.2 17.3 %collective-permute-start.3 = (bf16[112,256]{1,0:T(8,128)(2,1)S(1)}, bf16[112,256]{1,0:T(8,128)(2,1)S(1)}, u32[]{:S(2)}, u32[]{:S(2)}) collective-permute-start(bf16[112,256]{1,0:T(8,128)(2,1)S(1)} %maximum_maximum_fusion), channel_id=1, source_target_pairs={{0,16},{1,17},{32,48},{33,49},{8,24},{9,25},{40,56},{41,57},{16,0}... | collective-permute-start | bytes 172040 | tf_op jit(solution)/shard_map/ppermute | solution.py:418
  14.7 12.8 %collective-permute-start.2 = (bf16[112,256]{1,0:T(8,128)(2,1)S(1)}, bf16[112,256]{1,0:T(8,128)(2,1)S(1)}, u32[]{:S(2)}, u32[]{:S(2)}) collective-permute-start(bf16[112,256]{1,0:T(8,128)(2,1)S(1)} %maximum_maximum_fusion), channel_id=1, source_target_pairs={{0,40},{1,49},{32,16},{33,25},{8,48},{9,57},{40,24},{41,1},{16,56}... | collective-permute-start | bytes 172040 | tf_op jit(solution)/shard_map/ppermute | solution.py:418
  14.7 5.9 %collective-permute-start = (bf16[112,256]{1,0:T(8,128)(2,1)S(1)}, bf16[112,256]{1,0:T(8,128)(2,1)S(1)}, u32[]{:S(2)}, u32[]{:S(2)}) collective-permute-start(bf16[112,256]{1,0:T(8,128)(2,1)S(1)} %maximum_maximum_fusion), channel_id=1, source_target_pairs={{0,32},{1,57},{32,8},{33,1},{8,40},{9,33},{40,16},{41,9},{16,48},{... | collective-permute-start | bytes 172040 | tf_op jit(solution)/shard_map/ppermute | solution.py:418
  20.6 6.9 %collective-permute-start.1 = (bf16[112,256]{1,0:T(8,128)(2,1)S(1)}, bf16[112,256]{1,0:T(8,128)(2,1)S(1)}, u32[]{:S(2)}, u32[]{:S(2)}) collective-permute-start(bf16[112,256]{1,0:T(8,128)(2,1)S(1)} %maximum_maximum_fusion), channel_id=1, source_target_pairs={{0,8},{1,25},{32,40},{33,57},{8,16},{9,1},{40,48},{41,33},{16,24},... | collective-permute-start | bytes 172040 | tf_op jit(solution)/shard_map/ppermute | solution.py:418
  27.5 4.2 %collective-permute-start.6 = (bf16[112,256]{1,0:T(8,128)(2,1)S(1)}, bf16[112,256]{1,0:T(8,128)(2,1)S(1)}, u32[]{:S(2)}, u32[]{:S(2)}) collective-permute-start(bf16[112,256]{1,0:T(8,128)(2,1)S(1)} %maximum_maximum_fusion), channel_id=1, source_target_pairs={{0,56},{1,33},{32,0},{33,9},{8,32},{9,41},{40,8},{41,17},{16,40},{... | collective-permute-start | bytes 172040 | tf_op jit(solution)/shard_map/ppermute | solution.py:418
  32.5 8.0 %collective-permute-start.7 = (bf16[2,4,112,128]{3,2,1,0:T(8,128)(2,1)S(1)}, bf16[2,4,112,128]{3,2,1,0:T(8,128)(2,1)S(1)}, u32[]{:S(2)}, u32[]{:S(2)}) collective-permute-start(bf16[2,4,112,128]{3,2,1,0:T(8,128)(2,1)S(1)} %get-tuple-element.32), channel_id=1, source_target_pairs={{0,64},{1,193},{64,0},{65,129},{128,192},{129,65},{192,128},{193,1... | collective-permute-start | bytes 688136 | tf_op jit(solution)/shard_map/ppermute | solution.py:377
  34.4 13.5 %collective-permute-start.8 = (bf16[2,4,112,128]{3,2,1,0:T(8,128)(2,1)S(1)}, bf16[2,4,112,128]{3,2,1,0:T(8,128)(2,1)S(1)}, u32[]{:S(2)}, u32[]{:S(2)}) collective-permute-start(bf16[2,4,112,128]{3,2,1,0:T(8,128)(2,1)S(1)} %get-tuple-element.32), channel_id=1, source_target_pairs={{0,192},{1,65},{64,128},{65,1},{128,64},{129,193},{192,0},{193,129... | collective-permute-start | bytes 688136 | tf_op jit(solution)/shard_map/ppermute | solution.py:377
  36.7 8.4 %collective-permute-start.24 = (bf16[2,4,112,128]{3,2,1,0:T(8,128)(2,1)S(1)}, bf16[2,4,112,128]{3,2,1,0:T(8,128)(2,1)S(1)}, u32[]{:S(2)}, u32[]{:S(2)}) collective-permute-start(bf16[2,4,112,128]{3,2,1,0:T(8,128)(2,1)S(1)} %get-tuple-element.31), channel_id=1, source_target_pairs={{0,2},{1,7},{2,0},{3,5},{4,6},{5,3},{6,4},{7,1},{8,10},{9,15},{10,... | collective-permute-start | bytes 688136 | tf_op jit(solution)/shard_map/ppermute | solution.py:377
  40.5 7.4 %collective-permute-start.9 = (bf16[2,4,112,128]{3,2,1,0:T(8,128)(2,1)S(1)}, bf16[2,4,112,128]{3,2,1,0:T(8,128)(2,1)S(1)}, u32[]{:S(2)}, u32[]{:S(2)}) collective-permute-start(bf16[2,4,112,128]{3,2,1,0:T(8,128)(2,1)S(1)} %collective-permute-done.7), channel_id=1, source_target_pairs={{0,192},{1,65},{64,128},{65,1},{128,64},{129,193},{192,0},{193,129... | collective-permute-start | bytes 688136 | tf_op jit(solution)/shard_map/ppermute | solution.py:377
  41.3 10.8 %collective-permute-start.25 = (bf16[2,4,112,128]{3,2,1,0:T(8,128)(2,1)S(1)}, bf16[2,4,112,128]{3,2,1,0:T(8,128)(2,1)S(1)}, u32[]{:S(2)}, u32[]{:S(2)}) collective-permute-start(bf16[2,4,112,128]{3,2,1,0:T(8,128)(2,1)S(1)} %get-tuple-element.31), channel_id=1, source_target_pairs={{0,6},{1,3},{2,4},{3,1},{4,2},{5,7},{6,0},{7,5},{8,14},{9,11},{10,... | collective-permute-start | bytes 688136 | tf_op jit(solution)/shard_map/ppermute | solution.py:377
  45.1 7.6 %collective-permute-start.26 = (bf16[2,4,112,128]{3,2,1,0:T(8,128)(2,1)S(1)}, bf16[2,4,112,128]{3,2,1,0:T(8,128)(2,1)S(1)}, u32[]{:S(2)}, u32[]{:S(2)}) collective-permute-start(bf16[2,4,112,128]{3,2,1,0:T(8,128)(2,1)S(1)} %collective-permute-done.24), channel_id=1, source_target_pairs={{0,6},{1,3},{2,4},{3,1},{4,2},{5,7},{6,0},{7,5},{8,14},{9,11},{10,... | collective-permute-start | bytes 688136 | tf_op jit(solution)/shard_map/ppermute | solution.py:377
  48.8 8.0 %collective-permute-start.16 = (bf16[4,4,112,128]{3,2,1,0:T(8,128)(2,1)S(1)}, bf16[4,4,112,128]{3,2,1,0:T(8,128)(2,1)}, u32[]{:S(2)}, u32[]{:S(2)}) collective-permute-start(bf16[4,4,112,128]{3,2,1,0:T(8,128)(2,1)S(1)} %bitcast.84), channel_id=1, source_target_pairs={{0,1},{1,0},{2,3},{3,2},{4,5},{5,4},{6,7},{7,6},{8,9},{9,8},{10,11... | collective-permute-start | bytes 1376264 | tf_op jit(solution)/shard_map/ppermute | solution.py:381
  48.9 14.8 %collective-permute-start.11 = (bf16[4,4,112,128]{3,2,1,0:T(8,128)(2,1)S(1)}, bf16[4,4,112,128]{3,2,1,0:T(8,128)(2,1)}, u32[]{:S(2)}, u32[]{:S(2)}) collective-permute-start(bf16[4,4,112,128]{3,2,1,0:T(8,128)(2,1)S(1)} %bitcast.85), channel_id=1, source_target_pairs={{0,6},{1,3},{2,4},{3,1},{4,2},{5,7},{6,0},{7,5},{8,14},{9,11},{10,... | collective-permute-start | bytes 1376264 | tf_op jit(solution)/shard_map/ppermute | solution.py:377
  51.2 13.6 %collective-permute-start.10 = (bf16[4,4,112,128]{3,2,1,0:T(8,128)(2,1)S(1)}, bf16[4,4,112,128]{3,2,1,0:T(8,128)(2,1)}, u32[]{:S(2)}, u32[]{:S(2)}) collective-permute-start(bf16[4,4,112,128]{3,2,1,0:T(8,128)(2,1)S(1)} %bitcast.86), channel_id=1, source_target_pairs={{0,2},{1,7},{2,0},{3,5},{4,6},{5,3},{6,4},{7,1},{8,10},{9,15},{10,... | collective-permute-start | bytes 1376264 | tf_op jit(solution)/shard_map/ppermute | solution.py:377
  52.1 12.8 %collective-permute-start.20 = (bf16[4,4,112,128]{3,2,1,0:T(8,128)(2,1)S(1)}, bf16[4,4,112,128]{3,2,1,0:T(8,128)(2,1)}, u32[]{:S(2)}, u32[]{:S(2)}) collective-permute-start(bf16[4,4,112,128]{3,2,1,0:T(8,128)(2,1)S(1)} %bitcast.88), channel_id=1, source_target_pairs={{0,1},{1,0},{2,3},{3,2},{4,5},{5,4},{6,7},{7,6},{8,9},{9,8},{10,11... | collective-permute-start | bytes 1376264 | tf_op jit(solution)/shard_map/ppermute | solution.py:381
  52.7 20.8 %collective-permute-start.14 = (bf16[4,4,112,128]{3,2,1,0:T(8,128)(2,1)S(1)}, bf16[4,4,112,128]{3,2,1,0:T(8,128)(2,1)}, u32[]{:S(2)}, u32[]{:S(2)}) collective-permute-start(bf16[4,4,112,128]{3,2,1,0:T(8,128)(2,1)S(1)} %bitcast.89), channel_id=1, source_target_pairs={{0,6},{1,3},{2,4},{3,1},{4,2},{5,7},{6,0},{7,5},{8,14},{9,11},{10,... | collective-permute-start | bytes 1376264 | tf_op jit(solution)/shard_map/ppermute | solution.py:377
  56.8 16.7 %collective-permute-start.13 = (bf16[4,4,112,128]{3,2,1,0:T(8,128)(2,1)S(1)}, bf16[4,4,112,128]{3,2,1,0:T(8,128)(2,1)S(1)}, u32[]{:S(2)}, u32[]{:S(2)}) collective-permute-start(bf16[4,4,112,128]{3,2,1,0:T(8,128)(2,1)S(1)} %bitcast.90), channel_id=1, source_target_pairs={{0,2},{1,7},{2,0},{3,5},{4,6},{5,3},{6,4},{7,1},{8,10},{9,15},{10,... | collective-permute-start | bytes 1376264 | tf_op jit(solution)/shard_map/ppermute | solution.py:377
  63.7 9.9 %collective-permute-start.37 = (bf16[4,4,112,128]{3,2,1,0:T(8,128)(2,1)S(1)}, bf16[4,4,112,128]{3,2,1,0:T(8,128)(2,1)S(1)}, u32[]{:S(2)}, u32[]{:S(2)}) collective-permute-start(bf16[4,4,112,128]{3,2,1,0:T(8,128)(2,1)S(1)} %get-tuple-element.37.refs_20_), channel_id=1, source_target_pairs={{0,1},{1,0},{2,3},{3,2},{4,5},{5,4},{6,7},{7,6},{8,9},{9,8},{10,11... | collective-permute-start | bytes 1376264 | tf_op jit(solution)/shard_map/ppermute | solution.py:381
  64.8 13.4 %collective-permute-start.31 = (bf16[4,4,112,128]{3,2,1,0:T(8,128)(2,1)S(1)}, bf16[4,4,112,128]{3,2,1,0:T(8,128)(2,1)S(1)}, u32[]{:S(2)}, u32[]{:S(2)}) collective-permute-start(bf16[4,4,112,128]{3,2,1,0:T(8,128)(2,1)S(1)} %get-tuple-element.37.refs_20_), channel_id=1, source_target_pairs={{0,192},{1,65},{64,128},{65,1},{128,64},{129,193},{192,0},{193,129... | collective-permute-start | bytes 1376264 | tf_op jit(solution)/shard_map/ppermute | solution.py:377
  64.9 13.3 %collective-permute-start.30 = (bf16[4,4,112,128]{3,2,1,0:T(8,128)(2,1)S(1)}, bf16[4,4,112,128]{3,2,1,0:T(8,128)(2,1)S(1)}, u32[]{:S(2)}, u32[]{:S(2)}) collective-permute-start(bf16[4,4,112,128]{3,2,1,0:T(8,128)(2,1)S(1)} %get-tuple-element.37.refs_20_), channel_id=1, source_target_pairs={{0,64},{1,193},{64,0},{65,129},{128,192},{129,65},{192,128},{193,1... | collective-permute-start | bytes 1376264 | tf_op jit(solution)/shard_map/ppermute | solution.py:377
  73.5 5.2 %collective-permute-start.33 = (bf16[4,4,112,128]{3,2,1,0:T(8,128)(2,1)S(1)}, bf16[4,4,112,128]{3,2,1,0:T(8,128)(2,1)S(1)}, u32[]{:S(2)}, u32[]{:S(2)}) collective-permute-start(bf16[4,4,112,128]{3,2,1,0:T(8,128)(2,1)S(1)} %get-tuple-element.38.refs_16_), channel_id=1, source_target_pairs={{0,1},{1,0},{2,3},{3,2},{4,5},{5,4},{6,7},{7,6},{8,9},{9,8},{10,11... | collective-permute-start | bytes 1376264 | tf_op jit(solution)/shard_map/ppermute | solution.py:381
  73.5 13.9 %collective-permute-start.28 = (bf16[4,4,112,128]{3,2,1,0:T(8,128)(2,1)S(1)}, bf16[4,4,112,128]{3,2,1,0:T(8,128)(2,1)S(1)}, u32[]{:S(2)}, u32[]{:S(2)}) collective-permute-start(bf16[4,4,112,128]{3,2,1,0:T(8,128)(2,1)S(1)} %get-tuple-element.38.refs_16_), channel_id=1, source_target_pairs={{0,192},{1,65},{64,128},{65,1},{128,64},{129,193},{192,0},{193,129... | collective-permute-start | bytes 1376264 | tf_op jit(solution)/shard_map/ppermute | solution.py:377
  73.6 13.8 %collective-permute-start.27 = (bf16[4,4,112,128]{3,2,1,0:T(8,128)(2,1)S(1)}, bf16[4,4,112,128]{3,2,1,0:T(8,128)(2,1)}, u32[]{:S(2)}, u32[]{:S(2)}) collective-permute-start(bf16[4,4,112,128]{3,2,1,0:T(8,128)(2,1)S(1)} %get-tuple-element.38.refs_16_), channel_id=1, source_target_pairs={{0,64},{1,193},{64,0},{65,129},{128,192},{129,65},{192,128},{193,1... | collective-permute-start | bytes 1376264 | tf_op jit(solution)/shard_map/ppermute | solution.py:377
  78.2 9.8 %collective-permute-start.18 = (bf16[4,4,112,128]{3,2,1,0:T(8,128)(2,1)}, bf16[4,4,112,128]{3,2,1,0:T(8,128)(2,1)S(1)}, u32[]{:S(2)}, u32[]{:S(2)}) collective-permute-start(bf16[4,4,112,128]{3,2,1,0:T(8,128)(2,1)} %collective-permute-done.11.refs_2_), channel_id=1, source_target_pairs={{0,1},{1,0},{2,3},{3,2},{4,5},{5,4},{6,7},{7,6},{8,9},{9,8},{10,11... | collective-permute-start | bytes 1376264 | tf_op jit(solution)/shard_map/ppermute | solution.py:381
  78.2 11.1 %collective-permute-start.17 = (bf16[4,4,112,128]{3,2,1,0:T(8,128)(2,1)}, bf16[4,4,112,128]{3,2,1,0:T(8,128)(2,1)S(1)}, u32[]{:S(2)}, u32[]{:S(2)}) collective-permute-start(bf16[4,4,112,128]{3,2,1,0:T(8,128)(2,1)} %collective-permute-done.10.refs_1_), channel_id=1, source_target_pairs={{0,1},{1,0},{2,3},{3,2},{4,5},{5,4},{6,7},{7,6},{8,9},{9,8},{10,11... | collective-permute-start | bytes 1376264 | tf_op jit(solution)/shard_map/ppermute | solution.py:381
  78.7 10.6 %collective-permute-start.12 = (bf16[4,4,112,128]{3,2,1,0:T(8,128)(2,1)}, bf16[4,4,112,128]{3,2,1,0:T(8,128)(2,1)}, u32[]{:S(2)}, u32[]{:S(2)}) collective-permute-start(bf16[4,4,112,128]{3,2,1,0:T(8,128)(2,1)} %collective-permute-done.10.refs_1_), channel_id=1, source_target_pairs={{0,6},{1,3},{2,4},{3,1},{4,2},{5,7},{6,0},{7,5},{8,14},{9,11},{10,... | collective-permute-start | bytes 1376264 | tf_op jit(solution)/shard_map/ppermute | solution.py:377
  87.4 2.4 %collective-permute-start.22 = (bf16[4,4,112,128]{3,2,1,0:T(8,128)(2,1)}, bf16[4,4,112,128]{3,2,1,0:T(8,128)(2,1)S(1)}, u32[]{:S(2)}, u32[]{:S(2)}) collective-permute-start(bf16[4,4,112,128]{3,2,1,0:T(8,128)(2,1)} %collective-permute-done.14.refs_6_), channel_id=1, source_target_pairs={{0,1},{1,0},{2,3},{3,2},{4,5},{5,4},{6,7},{7,6},{8,9},{9,8},{10,11... | collective-permute-start | bytes 1376264 | tf_op jit(solution)/shard_map/ppermute | solution.py:381
  87.4 2.6 %collective-permute-start.21 = (bf16[4,4,112,128]{3,2,1,0:T(8,128)(2,1)S(1)}, bf16[4,4,112,128]{3,2,1,0:T(8,128)(2,1)S(1)}, u32[]{:S(2)}, u32[]{:S(2)}) collective-permute-start(bf16[4,4,112,128]{3,2,1,0:T(8,128)(2,1)S(1)} %collective-permute-done.13.refs_5_), channel_id=1, source_target_pairs={{0,1},{1,0},{2,3},{3,2},{4,5},{5,4},{6,7},{7,6},{8,9},{9,8},{10,11... | collective-permute-start | bytes 1376264 | tf_op jit(solution)/shard_map/ppermute | solution.py:381
  88.0 9.8 %collective-permute-start.15 = (bf16[4,4,112,128]{3,2,1,0:T(8,128)(2,1)S(1)}, bf16[4,4,112,128]{3,2,1,0:T(8,128)(2,1)}, u32[]{:S(2)}, u32[]{:S(2)}) collective-permute-start(bf16[4,4,112,128]{3,2,1,0:T(8,128)(2,1)S(1)} %collective-permute-done.13.refs_5_), channel_id=1, source_target_pairs={{0,6},{1,3},{2,4},{3,1},{4,2},{5,7},{6,0},{7,5},{8,14},{9,11},{10,... | collective-permute-start | bytes 1376264 | tf_op jit(solution)/shard_map/ppermute | solution.py:377
  89.3 8.9 %collective-permute-start.39 = (bf16[4,4,112,128]{3,2,1,0:T(8,128)(2,1)S(1)}, bf16[4,4,112,128]{3,2,1,0:T(8,128)(2,1)S(1)}, u32[]{:S(2)}, u32[]{:S(2)}) collective-permute-start(bf16[4,4,112,128]{3,2,1,0:T(8,128)(2,1)S(1)} %collective-permute-done.31.refs_22_), channel_id=1, source_target_pairs={{0,1},{1,0},{2,3},{3,2},{4,5},{5,4},{6,7},{7,6},{8,9},{9,8},{10,11... | collective-permute-start | bytes 1376264 | tf_op jit(solution)/shard_map/ppermute | solution.py:381
  89.3 8.9 %collective-permute-start.38 = (bf16[4,4,112,128]{3,2,1,0:T(8,128)(2,1)S(1)}, bf16[4,4,112,128]{3,2,1,0:T(8,128)(2,1)S(1)}, u32[]{:S(2)}, u32[]{:S(2)}) collective-permute-start(bf16[4,4,112,128]{3,2,1,0:T(8,128)(2,1)S(1)} %collective-permute-done.30.refs_21_), channel_id=1, source_target_pairs={{0,1},{1,0},{2,3},{3,2},{4,5},{5,4},{6,7},{7,6},{8,9},{9,8},{10,11... | collective-permute-start | bytes 1376264 | tf_op jit(solution)/shard_map/ppermute | solution.py:381
  89.8 8.9 %collective-permute-start.32 = (bf16[4,4,112,128]{3,2,1,0:T(8,128)(2,1)S(1)}, bf16[4,4,112,128]{3,2,1,0:T(8,128)(2,1)}, u32[]{:S(2)}, u32[]{:S(2)}) collective-permute-start(bf16[4,4,112,128]{3,2,1,0:T(8,128)(2,1)S(1)} %collective-permute-done.30.refs_21_), channel_id=1, source_target_pairs={{0,192},{1,65},{64,128},{65,1},{128,64},{129,193},{192,0},{193,129... | collective-permute-start | bytes 1376264 | tf_op jit(solution)/shard_map/ppermute | solution.py:377
  90.1 8.8 %collective-permute-start.35 = (bf16[4,4,112,128]{3,2,1,0:T(8,128)(2,1)S(1)}, bf16[4,4,112,128]{3,2,1,0:T(8,128)(2,1)S(1)}, u32[]{:S(2)}, u32[]{:S(2)}) collective-permute-start(bf16[4,4,112,128]{3,2,1,0:T(8,128)(2,1)S(1)} %collective-permute-done.28.refs_18_), channel_id=1, source_target_pairs={{0,1},{1,0},{2,3},{3,2},{4,5},{5,4},{6,7},{7,6},{8,9},{9,8},{10,11... | collective-permute-start | bytes 1376264 | tf_op jit(solution)/shard_map/ppermute | solution.py:381
  97.7 8.8 %collective-permute-start.29 = (bf16[4,4,112,128]{3,2,1,0:T(8,128)(2,1)}, bf16[4,4,112,128]{3,2,1,0:T(8,128)(2,1)}, u32[]{:S(2)}, u32[]{:S(2)}) collective-permute-start(bf16[4,4,112,128]{3,2,1,0:T(8,128)(2,1)} %collective-permute-done.27.refs_17_), channel_id=1, source_target_pairs={{0,192},{1,65},{64,128},{65,1},{128,64},{129,193},{192,0},{193,129... | collective-permute-start | bytes 1376264 | tf_op jit(solution)/shard_map/ppermute | solution.py:377
  98.2 9.1 %collective-permute-start.34 = (bf16[4,4,112,128]{3,2,1,0:T(8,128)(2,1)}, bf16[4,4,112,128]{3,2,1,0:T(8,128)(2,1)}, u32[]{:S(2)}, u32[]{:S(2)}) collective-permute-start(bf16[4,4,112,128]{3,2,1,0:T(8,128)(2,1)} %collective-permute-done.27.refs_17_), channel_id=1, source_target_pairs={{0,1},{1,0},{2,3},{3,2},{4,5},{5,4},{6,7},{7,6},{8,9},{9,8},{10,11... | collective-permute-start | bytes 1376264 | tf_op jit(solution)/shard_map/ppermute | solution.py:381
  98.3 9.1 %collective-permute-start.19 = (bf16[4,4,112,128]{3,2,1,0:T(8,128)(2,1)}, bf16[4,4,112,128]{3,2,1,0:T(8,128)(2,1)}, u32[]{:S(2)}, u32[]{:S(2)}) collective-permute-start(bf16[4,4,112,128]{3,2,1,0:T(8,128)(2,1)} %collective-permute-done.12.refs_3_), channel_id=1, source_target_pairs={{0,1},{1,0},{2,3},{3,2},{4,5},{5,4},{6,7},{7,6},{8,9},{9,8},{10,11... | collective-permute-start | bytes 1376264 | tf_op jit(solution)/shard_map/ppermute | solution.py:381
  98.8 8.6 %collective-permute-start.23 = (bf16[4,4,112,128]{3,2,1,0:T(8,128)(2,1)}, bf16[4,4,112,128]{3,2,1,0:T(8,128)(2,1)}, u32[]{:S(2)}, u32[]{:S(2)}) collective-permute-start(bf16[4,4,112,128]{3,2,1,0:T(8,128)(2,1)} %collective-permute-done.15.refs_7_), channel_id=1, source_target_pairs={{0,1},{1,0},{2,3},{3,2},{4,5},{5,4},{6,7},{7,6},{8,9},{9,8},{10,11... | collective-permute-start | bytes 1376264 | tf_op jit(solution)/shard_map/ppermute | solution.py:381
  98.9 8.5 %collective-permute-start.40 = (bf16[4,4,112,128]{3,2,1,0:T(8,128)(2,1)}, bf16[4,4,112,128]{3,2,1,0:T(8,128)(2,1)}, u32[]{:S(2)}, u32[]{:S(2)}) collective-permute-start(bf16[4,4,112,128]{3,2,1,0:T(8,128)(2,1)} %collective-permute-done.32.refs_23_), channel_id=1, source_target_pairs={{0,1},{1,0},{2,3},{3,2},{4,5},{5,4},{6,7},{7,6},{8,9},{9,8},{10,11... | collective-permute-start | bytes 1376264 | tf_op jit(solution)/shard_map/ppermute | solution.py:381
  106.6 2.2 %collective-permute-start.36 = (bf16[4,4,112,128]{3,2,1,0:T(8,128)(2,1)}, bf16[4,4,112,128]{3,2,1,0:T(8,128)(2,1)}, u32[]{:S(2)}, u32[]{:S(2)}) collective-permute-start(bf16[4,4,112,128]{3,2,1,0:T(8,128)(2,1)} %collective-permute-done.29.refs_19_), channel_id=1, source_target_pairs={{0,1},{1,0},{2,3},{3,2},{4,5},{5,4},{6,7},{7,6},{8,9},{9,8},{10,11... | collective-permute-start | bytes 1376264 | tf_op jit(solution)/shard_map/ppermute | solution.py:381
  174.3 2.8 %collective-permute-start.41 = (bf16[4,4,112,256]{3,2,1,0:T(8,128)(2,1)}, bf16[4,4,112,256]{3,2,1,0:T(8,128)(2,1)S(1)}, u32[]{:S(2)}, u32[]{:S(2)}) collective-permute-start(bf16[4,4,112,256]{3,2,1,0:T(8,128)(2,1)} %get-tuple-element.13), channel_id=1, source_target_pairs={{0,1},{1,0},{2,3},{3,2},{4,5},{5,4},{6,7},{7,6},{8,9},{9,8},{10,11... | collective-permute-start | bytes 2752520 | tf_op jit(solution)/shard_map/ppermute | solution.py:381
  178.4 7.6 %collective-permute-start.42 = (bf16[4,112,256]{2,1,0:T(8,128)(2,1)S(1)}, bf16[4,112,256]{2,1,0:T(8,128)(2,1)S(1)}, u32[]{:S(2)}, u32[]{:S(2)}) collective-permute-start(bf16[4,112,256]{2,1,0:T(8,128)(2,1)S(1)} %get-tuple-element.24), channel_id=1, source_target_pairs={{0,2},{1,7},{2,0},{3,5},{4,6},{5,3},{6,4},{7,1},{8,10},{9,15},{10,... | collective-permute-start | bytes 688136 | tf_op jit(solution)/shard_map/ppermute | solution.py:377
  178.5 14.2 %collective-permute-start.44 = (bf16[4,112,256]{2,1,0:T(8,128)(2,1)S(1)}, bf16[4,112,256]{2,1,0:T(8,128)(2,1)S(1)}, u32[]{:S(2)}, u32[]{:S(2)}) collective-permute-start(bf16[4,112,256]{2,1,0:T(8,128)(2,1)S(1)} %get-tuple-element.25), channel_id=1, source_target_pairs={{0,4},{2,6},{4,0},{6,2},{1,5},{3,7},{5,1},{7,3},{8,12},{10,14},{12... | collective-permute-start | bytes 688136 | tf_op jit(solution)/shard_map/ppermute | solution.py:385
  182.3 11.0 %collective-permute-start.43 = (bf16[4,112,256]{2,1,0:T(8,128)(2,1)S(1)}, bf16[4,112,256]{2,1,0:T(8,128)(2,1)S(1)}, u32[]{:S(2)}, u32[]{:S(2)}) collective-permute-start(bf16[4,112,256]{2,1,0:T(8,128)(2,1)S(1)} %get-tuple-element.26), channel_id=1, source_target_pairs={{0,6},{1,3},{2,4},{3,1},{4,2},{5,7},{6,0},{7,5},{8,14},{9,11},{10,... | collective-permute-start | bytes 688136 | tf_op jit(solution)/shard_map/ppermute | solution.py:377
  195.0 9.0 %collective-permute-start.47 = (bf16[112,256]{1,0:T(8,128)(2,1)S(1)}, bf16[112,256]{1,0:T(8,128)(2,1)S(1)}, u32[]{:S(2)}, u32[]{:S(2)}) collective-permute-start(bf16[112,256]{1,0:T(8,128)(2,1)S(1)} %get-tuple-element.33), channel_id=1, source_target_pairs={{0,16},{8,24},{16,0},{24,8},{1,17},{9,25},{17,1},{25,9},{2,18},{10... | collective-permute-start | bytes 172040 | tf_op jit(solution)/shard_map/ppermute | solution.py:385
  200.3 6.3 %collective-permute-start.46 = (bf16[112,256]{1,0:T(8,128)(2,1)S(1)}, bf16[112,256]{1,0:T(8,128)(2,1)S(1)}, u32[]{:S(2)}, u32[]{:S(2)}) collective-permute-start(bf16[112,256]{1,0:T(8,128)(2,1)S(1)} %get-tuple-element.34), channel_id=1, source_target_pairs={{0,24},{1,9},{8,16},{9,1},{16,8},{17,25},{24,0},{25,17},{2,26},{3,... | collective-permute-start | bytes 172040 | tf_op jit(solution)/shard_map/ppermute | solution.py:377
  201.3 5.7 %collective-permute-start.45 = (bf16[112,256]{1,0:T(8,128)(2,1)S(1)}, bf16[112,256]{1,0:T(8,128)(2,1)S(1)}, u32[]{:S(2)}, u32[]{:S(2)}) collective-permute-start(bf16[112,256]{1,0:T(8,128)(2,1)S(1)} %get-tuple-element.35), channel_id=1, source_target_pairs={{0,8},{1,25},{8,0},{9,17},{16,24},{17,9},{24,16},{25,1},{2,10},{3,... | collective-permute-start | bytes 172040 | tf_op jit(solution)/shard_map/ppermute | solution.py:377
  (21 other events, 373.8 us)

commit v4 on v1

--- a/solution.py
+++ b/solution.py
@@ -133,26 +133,26 @@
         one, two = partner(i, core, True), partner(i, core, False)
         return [i, one, two, partner(two, core, True)]
 
-    copies = []
-    for kc in range(2):
-        cc = (c + kc) % 2
-        ys, xx = ring(y, cc), ring(x, cc)
-        for i in range(4):
-            for j in range(4):
-                at = pl.ds(2 * xx[j], 2)
-                copy = pltpu.make_async_copy(
-                    left[kc * 4 + i].at[j],
-                    w_scr.at[at, :, ys[i], cc, :, :C],
-                    sem_a.at[xx[j]],
-                )
-                copy.start()
-                at = pl.ds(2 * xx[i], 2)
-                copy = pltpu.make_async_copy(
-                    right[kc * 4 + i].at[j],
-                    w_scr.at[at, :, ys[j], cc, :, C:],
-                    sem_b.at[xx[i]],
-                )
-                copy.start()
+    for target in range(4):
+        for kc in range(2):
+            cc = (c + kc) % 2
+            ys, xx = ring(y, cc), ring(x, cc)
+            slot = sum(jnp.where(xx[j] == target, j, 0) for j in range(4))
+            for i in range(4):
+                pltpu.make_async_copy(
+                    left[kc * 4 + i].at[slot],
+                    w_scr.at[2 * target : 2 * target + 2, :, ys[i], cc, :, :C],
+                    sem_a.at[target],
+                ).start()
+
+                @pl.when(xx[i] == target)
+                def _(i=i, kc=kc, cc=cc, ys=ys, target=target):
+                    for j in range(4):
+                        pltpu.make_async_copy(
+                            right[kc * 4 + i].at[j],
+                            w_scr.at[2 * target : 2 * target + 2, :, ys[j], cc, :, C:],
+                            sem_b.at[target],
+                        ).start()
 
     def wait_layers(at):
         for sem, src in ((sem_a, left[0]), (sem_b, right[0])):
@@ -216,7 +216,7 @@
 
     loads[0].wait()
     loads[1].wait()
-    lax.fori_loop(0, LAYERS, forward, first_scr[0])
+    lax.fori_loop(0, LAYERS, forward, first_scr[0], unroll=2)
 
     def backward(step, back):
         layer = LAYERS - 1 - step
@@ -286,7 +286,7 @@
         return (dy + inv_rms * (d_hat - x_hat * mean)).astype(BF16)
 
     cot = jnp.where(section < SEQS, first_scr[1].astype(F32), 0.0).astype(BF16)
-    lax.fori_loop(0, LAYERS, backward, cot)
+    lax.fori_loop(0, LAYERS, backward, cot, unroll=2)
 
 
 def weight_kernel(pos_ref, got_ref, keep_ref, send_ref, got, scr, sem_in, sem):
@@ -324,8 +324,15 @@
             c_at = (d + c) % 2
             scr[c_at, y_at, z_at, :ROWS] = keys[ROWS * i : ROWS * (i + 1)].astype(BF16)
             scr[c_at, y_at, z_at, ROWS:] = low[i].astype(BF16)
-    for i, ref in enumerate((keep_ref, send_ref)):
-        pltpu.make_async_copy(scr.at[i], ref, sem.at[i]).start()
+        if m % 2:
+            for core in range(2):
+                z_at = slot(m // 2, zh, core)
+                for i, ref in enumerate((keep_ref, send_ref)):
+
+                    @pl.when((core + c) % 2 == i)
+                    def _(i=i, ref=ref, z_at=z_at):
+                        pltpu.make_async_copy(scr.at[i, :, z_at], ref.at[:, z_at], sem.at[i]).start()
+
     for i, ref in enumerate((keep_ref, send_ref)):
         pltpu.make_async_copy(scr.at[i], ref, sem.at[i]).wait()
 
@@ -449,7 +456,18 @@
         cost=(8_000_000_000, 30_000_000),
     )(pos, *left, *right, entries, cotangents)[0]
 
-    got = lax.all_to_all(sent, SECTION, 0, 0, tiled=True)
+    groups = [
+        [
+            (((i * 4) + (z - i % 2 * core) % 4) * 4 + row) * 2 + core
+            for i in range(LAYERS)
+        ]
+        for z in range(4)
+        for row in range(4)
+        for core in range(2)
+    ]
+    got = lax.all_to_all(
+        sent, ("x", "zl", "zh", "y", "c"), 0, 0, axis_index_groups=groups, tiled=True
+    )
     half = shape(4, 4, PIECE, 256)
     keep, send = call(
         weight_kernel,

time: 186 us -> 181 us (0.973)
  Pallas kernels: 36.3 us -> 32.3 us
    pallas_call x1, Pallas kernels: 29.3 us -> 25.9 us  [per_device(): call(sequence_kernel, [shape(LAYERS, SENT, BLOCK)], [SMEM] + [ANY] * 18,...]
where the time goes in v4:
time: 181 us
  waiting for transfers between devices  65.3 us (36%)
  starting transfers between devices  42.8 us (24%)
  Pallas kernels  32.3 us (18%)
  blocking collectives  30.4 us (17%)
  local copies, waits for them, and re-layouts  5.39 us (3%)
  other arithmetic  3.93 us (2%)
    ppermute x18, waiting for transfers between devices, swap(): return lax.ppermute(array, (axis, 'c'), ring_pairs(first))  50.4 us
    ppermute x18, starting transfers between devices, swap(): return lax.ppermute(array, (axis, 'c'), ring_pairs(first))  38.3 us
    all_to_all x1, blocking collectives, per_device(): lax.all_to_all(sent, ('x', 'zl', 'zh', 'y', 'c'), 0, 0, axis_index_groups...  30.4 us
    pallas_call x1, Pallas kernels, per_device(): call(sequence_kernel, [shape(LAYERS, SENT, BLOCK)], [SMEM] + [ANY] * 18,...  25.9 us
    ppermute x2, waiting for transfers between devices, opposite(): return lax.ppermute(array, axis, [(i, i ^ 2) for i in range(4)])  5.26 us
    pallas_call x1, Pallas kernels, per_device(): call(weight_kernel, [half, half], [SMEM, ANY], [pltpu.VMEM((LAYERS, SENT,...  4.92 us
    ppermute x9, waiting for transfers between devices, other_core(): return lax.ppermute(array, 'c', [(0, 1), (1, 0)])  4.85 us
    ppermute x1, waiting for transfers between devices, per_device(): other = lax.ppermute(along, ('zl', 'zh', 'c'), pairs)  4.83 us
  transfers between devices with their start and end apart: 30, of which 18 were waited for; matrix products, arithmetic and copies ran while one was open for 1% of the time, Pallas kernels for 0%

profile of v4, /device:TPU:2, one launch (start us, length us, event | category | flops | bytes accessed | tf_op | source)
XLA Modules:
  0.0 181.0 jit_solution(7023931374994419861)
XLA Ops:
  0.6 0.7 pad_slice_fusion
  1.3 0.7 pad_slice_fusion.1
  2.0 0.8 maximum_maximum_fusion
  2.9 6.4 %collective-permute-start.1 = (bf16[112,256]{1,0:T(8,128)(2,1)S(1)}, bf16[112,256]{1,0:T(8,128)(2,1)S(1)}, u32[]{:S(2)}, u32[]{:S(2)}) collective-permute-start(bf16[112,256]{1,0:T(8,128)(2,1)S(1)} %maximum_maximum_fusion), channel_id=1, source_target_pairs={{0,24},{1,9},{8,16},{9,1},{16,8},{17,25},{24,0},{25,17},{2,26},{3,... | collective-permute-start | bytes 172040 | tf_op jit(solution)/shard_map/ppermute | solution.py:383
  9.2 1.5 collective-permute-start
  10.7 1.0 collective-permute-start.2
  11.7 0.8 fusion.15
  12.8 1.6 collective-permute-done.1
  14.4 1.1 collective-permute-done
  15.6 3.6 %collective-permute-done.2 = bf16[112,256]{1,0:T(8,128)(2,1)S(1)} collective-permute-done((bf16[112,256]{1,0:T(8,128)(2,1)S(1)}, bf16[112,256]{1,0:T(8,128)(2,1)S(1)}, u32[]{:S(2)}, u32[]{:S(2)}) %collective-permute-start.2) | collective-permute-done | bytes 57376 | tf_op jit(solution)/shard_map/ppermute | solution.py:391
  19.9 1.2 collective-permute-start.3
  21.2 4.8 %collective-permute-done.3 = bf16[4,112,256]{2,1,0:T(8,128)(2,1)S(1)} collective-permute-done((bf16[4,112,256]{2,1,0:T(8,128)(2,1)S(1)}, bf16[4,112,256]{2,1,0:T(8,128)(2,1)S(1)}, u32[]{:S(2)}, u32[]{:S(2)}) %collective-permute-start.3) | collective-permute-done | bytes 229408 | tf_op jit(solution)/shard_map/ppermute | solution.py:427
  26.2 0.6 collective-permute-start.4
  26.8 1.6 collective-permute-start.14
  28.4 2.2 %collective-permute-start.5 = (bf16[2,4,112,128]{3,2,1,0:T(8,128)(2,1)S(1)}, bf16[2,4,112,128]{3,2,1,0:T(8,128)(2,1)S(1)}, u32[]{:S(2)}, u32[]{:S(2)}) collective-permute-start(bf16[2,4,112,128]{3,2,1,0:T(8,128)(2,1)S(1)} %get-tuple-element.21), channel_id=1, source_target_pairs={{0,192},{1,65},{64,128},{65,1},{128,64},{129,193},{192,0},{193,129... | collective-permute-start | bytes 688136 | tf_op jit(solution)/shard_map/ppermute | solution.py:383
  30.5 2.3 %collective-permute-done.4 = bf16[2,4,112,128]{3,2,1,0:T(8,128)(2,1)S(1)} collective-permute-done((bf16[2,4,112,128]{3,2,1,0:T(8,128)(2,1)S(1)}, bf16[2,4,112,128]{3,2,1,0:T(8,128)(2,1)S(1)}, u32[]{:S(2)}, u32[]{:S(2)}) %collective-permute-start.4) | collective-permute-done | bytes 229408 | tf_op jit(solution)/shard_map/ppermute | solution.py:383
  32.9 2.6 %collective-permute-start.6 = (bf16[2,4,112,128]{3,2,1,0:T(8,128)(2,1)S(1)}, bf16[2,4,112,128]{3,2,1,0:T(8,128)(2,1)S(1)}, u32[]{:S(2)}, u32[]{:S(2)}) collective-permute-start(bf16[2,4,112,128]{3,2,1,0:T(8,128)(2,1)S(1)} %collective-permute-done.4), channel_id=1, source_target_pairs={{0,192},{1,65},{64,128},{65,1},{128,64},{129,193},{192,0},{193,129... | collective-permute-start | bytes 688136 | tf_op jit(solution)/shard_map/ppermute | solution.py:383
  35.5 2.3 %collective-permute-start.15 = (bf16[2,4,112,128]{3,2,1,0:T(8,128)(2,1)S(1)}, bf16[2,4,112,128]{3,2,1,0:T(8,128)(2,1)S(1)}, u32[]{:S(2)}, u32[]{:S(2)}) collective-permute-start(bf16[2,4,112,128]{3,2,1,0:T(8,128)(2,1)S(1)} %get-tuple-element.20), channel_id=1, source_target_pairs={{0,6},{1,3},{2,4},{3,1},{4,2},{5,7},{6,0},{7,5},{8,14},{9,11},{10,... | collective-permute-start | bytes 688136 | tf_op jit(solution)/shard_map/ppermute | solution.py:383
  37.8 1.0 collective-permute-start.16
  38.7 0.8 collective-permute-done.6
  39.7 4.4 %collective-permute-start.8 = (bf16[4,2,4,112,128]{4,3,2,1,0:T(8,128)(2,1)S(1)}, bf16[4,2,4,112,128]{4,3,2,1,0:T(8,128)(2,1)S(1)}, u32[]{:S(2)}, u32[]{:S(2)}) collective-permute-start(bf16[4,2,4,112,128]{4,3,2,1,0:T(8,128)(2,1)S(1)} %pad_maximum_fusion.refs_0_), channel_id=1, source_target_pairs={{0,6},{1,3},{2,4},{3,1},{4,2},{5,7},{6,0},{7,5},{8,14},{9,11},{10,... | collective-permute-start | bytes 2752520 | tf_op jit(solution)/shard_map/ppermute | solution.py:383
  44.2 1.0 collective-permute-done.16
  45.3 1.9 %collective-permute-start.17 = (bf16[4,2,4,112,128]{4,3,2,1,0:T(8,128)(2,1)S(1)}, bf16[4,2,4,112,128]{4,3,2,1,0:T(8,128)(2,1)}, u32[]{:S(2)}, u32[]{:S(2)}) collective-permute-start(bf16[4,2,4,112,128]{4,3,2,1,0:T(8,128)(2,1)S(1)} %pad_maximum_fusion.1.refs_8_), channel_id=1, source_target_pairs={{0,64},{1,193},{64,0},{65,129},{128,192},{129,65},{192,128},{193,1... | collective-permute-start | bytes 2752520 | tf_op jit(solution)/shard_map/ppermute | solution.py:383
  47.3 0.9 collective-permute-start.18
  48.2 16.5 %collective-permute-done.8.refs_2_ = bf16[4,2,4,112,128]{4,3,2,1,0:T(8,128)(2,1)S(1)} collective-permute-done((bf16[4,2,4,112,128]{4,3,2,1,0:T(8,128)(2,1)S(1)}, bf16[4,2,4,112,128]{4,3,2,1,0:T(8,128)(2,1)S(1)}, u32[]{:S(2)}, u32[]{:S(2)}) %collective-permute-start.8) | collective-permute-done | bytes 917536 | tf_op jit(solution)/shard_map/ppermute | solution.py:383
  64.7 3.8 %collective-permute-start.9 = (bf16[4,2,4,112,128]{4,3,2,1,0:T(8,128)(2,1)}, bf16[4,2,4,112,128]{4,3,2,1,0:T(8,128)(2,1)}, u32[]{:S(2)}, u32[]{:S(2)}) collective-permute-start(bf16[4,2,4,112,128]{4,3,2,1,0:T(8,128)(2,1)} %collective-permute-done.7.refs_1_), channel_id=1, source_target_pairs={{0,6},{1,3},{2,4},{3,1},{4,2},{5,7},{6,0},{7,5},{8,14},{9,11},{10,... | collective-permute-start | bytes 2752520 | tf_op jit(solution)/shard_map/ppermute | solution.py:383
  68.5 1.7 collective-permute-start.19
  71.2 1.0 copy-done.8
  72.2 8.0 %collective-permute-done.9.refs_3_ = bf16[4,2,4,112,128]{4,3,2,1,0:T(8,128)(2,1)} collective-permute-done((bf16[4,2,4,112,128]{4,3,2,1,0:T(8,128)(2,1)}, bf16[4,2,4,112,128]{4,3,2,1,0:T(8,128)(2,1)}, u32[]{:S(2)}, u32[]{:S(2)}) %collective-permute-start.9) | collective-permute-done | bytes 917536 | tf_op jit(solution)/shard_map/ppermute | solution.py:383
  80.2 2.0 %collective-permute-done.19.refs_11_ = bf16[4,2,4,112,128]{4,3,2,1,0:T(8,128)(2,1)} collective-permute-done((bf16[4,2,4,112,128]{4,3,2,1,0:T(8,128)(2,1)}, bf16[4,2,4,112,128]{4,3,2,1,0:T(8,128)(2,1)}, u32[]{:S(2)}, u32[]{:S(2)}) %collective-permute-start.19) | collective-permute-done | bytes 917536 | tf_op jit(solution)/shard_map/ppermute | solution.py:383
  82.2 0.6 stack.105.pos_ref
  83.0 2.0 %collective-permute-done.23.refs_15_ = bf16[4,2,4,112,128]{4,3,2,1,0:T(8,128)(2,1)} collective-permute-done((bf16[4,2,4,112,128]{4,3,2,1,0:T(8,128)(2,1)}, bf16[4,2,4,112,128]{4,3,2,1,0:T(8,128)(2,1)}, u32[]{:S(2)}, u32[]{:S(2)}) %collective-permute-start.23) | collective-permute-done | bytes 917536 | tf_op jit(solution)/shard_map/ppermute | solution.py:387
  85.0 25.9 %shard_map.93 = bf16[8,304,384]{2,1,0:T(8,128)(2,1)} custom-call(s32[5]{0:T(128)} %stack.105.pos_ref, bf16[4,2,4,112,128]{4,3,2,1,0:T(8,128)(2,1)} %copy-done, bf16[4,2,4,112,128]{4,3,2,1,0:T(8,128)(2,1)} %collective-permute-done.7.refs_1_, bf16[4,2,4,112,128]{4,3,2,1,0:T(8,128)(2,1)} %copy-done.6, ...), custom_call_target="tpu_custom_call" | custom-call | flops 8000000000 | bytes 30000000 | tf_op jit(solution)/shard_map/pallas_call | solution.py:437
  110.9 30.4 %all_to_all.5.got_ref = bf16[8,304,384]{2,1,0:T(8,128)(2,1)} all-to-all(bf16[8,304,384]{2,1,0:T(8,128)(2,1)} %shard_map.93), channel_id=1, replica_groups={{0,32,64,96,128,160,192,224},{1,57,65,121,129,185,193,249},{2,34,66,98,..., dimensions={0} | all-to-all | bytes 3735552 | tf_op jit(solution)/shard_map/all_to_all | solution.py:468
  141.3 4.9 %shard_map.94 = (bf16[4,4,112,256]{3,2,1,0:T(8,128)(2,1)}, bf16[4,4,112,256]{3,2,1,0:T(8,128)(2,1)}) custom-call(s32[5]{0:T(128)} %stack.105.pos_ref, bf16[8,304,384]{2,1,0:T(8,128)(2,1)} %all_to_all.5.got_ref), custom_call_target="tpu_custom_call" | custom-call | flops 600000000 | bytes 4000000 | tf_op jit(solution)/shard_map/pallas_call | solution.py:472
  146.3 2.7 %collective-permute-done.24 = bf16[4,4,112,256]{3,2,1,0:T(8,128)(2,1)S(1)} collective-permute-done((bf16[4,4,112,256]{3,2,1,0:T(8,128)(2,1)}, bf16[4,4,112,256]{3,2,1,0:T(8,128)(2,1)S(1)}, u32[]{:S(2)}, u32[]{:S(2)}) %collective-permute-start.24) | collective-permute-done | bytes 917536 | tf_op jit(solution)/shard_map/ppermute | solution.py:387
  149.0 1.4 add_convert_fusion.1
  150.4 0.7 collective-permute-start.25
  151.2 7.8 %collective-permute-done.25 = bf16[2,4,112,256]{3,2,1,0:T(8,128)(2,1)S(1)} collective-permute-done((bf16[2,4,112,256]{3,2,1,0:T(8,128)(2,1)S(1)}, bf16[2,4,112,256]{3,2,1,0:T(8,128)(2,1)S(1)}, u32[]{:S(2)}, u32[]{:S(2)}) %collective-permute-start.25) | collective-permute-done | bytes 458784 | tf_op jit(solution)/shard_map/ppermute | solution.py:383
  159.1 1.7 collective-permute-start.26
  160.8 5.6 %collective-permute-done.26 = bf16[4,112,256]{2,1,0:T(8,128)(2,1)S(1)} collective-permute-done((bf16[4,112,256]{2,1,0:T(8,128)(2,1)S(1)}, bf16[4,112,256]{2,1,0:T(8,128)(2,1)S(1)}, u32[]{:S(2)}, u32[]{:S(2)}) %collective-permute-start.26) | collective-permute-done | bytes 229408 | tf_op jit(solution)/shard_map/ppermute | solution.py:383
  166.5 0.6 slice_bitcast_fusion
  167.1 1.6 collective-permute-start.29
  168.7 4.5 %collective-permute-start.28 = (bf16[112,256]{1,0:T(8,128)(2,1)S(1)}, bf16[112,256]{1,0:T(8,128)(2,1)S(1)}, u32[]{:S(2)}, u32[]{:S(2)}) collective-permute-start(bf16[112,256]{1,0:T(8,128)(2,1)S(1)} %get-tuple-element.23), channel_id=1, source_target_pairs={{0,24},{1,9},{8,16},{9,1},{16,8},{17,25},{24,0},{25,17},{2,26},{3,... | collective-permute-start | bytes 172040 | tf_op jit(solution)/shard_map/ppermute | solution.py:383
  173.6 1.6 collective-permute-done.29.d_ref
  175.2 1.2 collective-permute-done.28.c_ref
  176.4 2.4 %collective-permute-done.27.b_ref = bf16[112,256]{1,0:T(8,128)(2,1)S(1)} collective-permute-done((bf16[112,256]{1,0:T(8,128)(2,1)S(1)}, bf16[112,256]{1,0:T(8,128)(2,1)S(1)}, u32[]{:S(2)}, u32[]{:S(2)}) %collective-permute-start.27) | collective-permute-done | bytes 57376 | tf_op jit(solution)/shard_map/ppermute | solution.py:383
  179.5 1.6 shard_map.95
  (55 shorter events, 4.0 us)
Async XLA Ops:
  2.9 11.6 %collective-permute-start.1 = (bf16[112,256]{1,0:T(8,128)(2,1)S(1)}, bf16[112,256]{1,0:T(8,128)(2,1)S(1)}, u32[]{:S(2)}, u32[]{:S(2)}) collective-permute-start(bf16[112,256]{1,0:T(8,128)(2,1)S(1)} %maximum_maximum_fusion), channel_id=1, source_target_pairs={{0,24},{1,9},{8,16},{9,1},{16,8},{17,25},{24,0},{25,17},{2,26},{3,... | collective-permute-start | bytes 172040 | tf_op jit(solution)/shard_map/ppermute | solution.py:383
  9.2 6.3 %collective-permute-start = (bf16[112,256]{1,0:T(8,128)(2,1)S(1)}, bf16[112,256]{1,0:T(8,128)(2,1)S(1)}, u32[]{:S(2)}, u32[]{:S(2)}) collective-permute-start(bf16[112,256]{1,0:T(8,128)(2,1)S(1)} %maximum_maximum_fusion), channel_id=1, source_target_pairs={{0,8},{1,25},{8,0},{9,17},{16,24},{17,9},{24,16},{25,1},{2,10},{3,... | collective-permute-start | bytes 172040 | tf_op jit(solution)/shard_map/ppermute | solution.py:383
  10.7 8.5 %collective-permute-start.2 = (bf16[112,256]{1,0:T(8,128)(2,1)S(1)}, bf16[112,256]{1,0:T(8,128)(2,1)S(1)}, u32[]{:S(2)}, u32[]{:S(2)}) collective-permute-start(bf16[112,256]{1,0:T(8,128)(2,1)S(1)} %maximum_maximum_fusion), channel_id=1, source_target_pairs={{0,16},{8,24},{16,0},{24,8},{1,17},{9,25},{17,1},{25,9},{2,18},{10... | collective-permute-start | bytes 172040 | tf_op jit(solution)/shard_map/ppermute | solution.py:391
  19.9 6.1 %collective-permute-start.3 = (bf16[4,112,256]{2,1,0:T(8,128)(2,1)S(1)}, bf16[4,112,256]{2,1,0:T(8,128)(2,1)S(1)}, u32[]{:S(2)}, u32[]{:S(2)}) collective-permute-start(bf16[4,112,256]{2,1,0:T(8,128)(2,1)S(1)} %broadcast_select_fusion), channel_id=1, source_target_pairs={{0,32},{1,57},{32,0},{33,9},{8,40},{9,33},{40,8},{41,17},{16,48},{... | collective-permute-start | bytes 688136 | tf_op jit(solution)/shard_map/ppermute | solution.py:427
  26.2 6.7 %collective-permute-start.4 = (bf16[2,4,112,128]{3,2,1,0:T(8,128)(2,1)S(1)}, bf16[2,4,112,128]{3,2,1,0:T(8,128)(2,1)S(1)}, u32[]{:S(2)}, u32[]{:S(2)}) collective-permute-start(bf16[2,4,112,128]{3,2,1,0:T(8,128)(2,1)S(1)} %get-tuple-element.21), channel_id=1, source_target_pairs={{0,64},{1,193},{64,0},{65,129},{128,192},{129,65},{192,128},{193,1... | collective-permute-start | bytes 688136 | tf_op jit(solution)/shard_map/ppermute | solution.py:383
  26.8 10.9 %collective-permute-start.14 = (bf16[2,4,112,128]{3,2,1,0:T(8,128)(2,1)S(1)}, bf16[2,4,112,128]{3,2,1,0:T(8,128)(2,1)S(1)}, u32[]{:S(2)}, u32[]{:S(2)}) collective-permute-start(bf16[2,4,112,128]{3,2,1,0:T(8,128)(2,1)S(1)} %get-tuple-element.20), channel_id=1, source_target_pairs={{0,2},{1,7},{2,0},{3,5},{4,6},{5,3},{6,4},{7,1},{8,10},{9,15},{10,... | collective-permute-start | bytes 688136 | tf_op jit(solution)/shard_map/ppermute | solution.py:383
  28.4 10.3 %collective-permute-start.5 = (bf16[2,4,112,128]{3,2,1,0:T(8,128)(2,1)S(1)}, bf16[2,4,112,128]{3,2,1,0:T(8,128)(2,1)S(1)}, u32[]{:S(2)}, u32[]{:S(2)}) collective-permute-start(bf16[2,4,112,128]{3,2,1,0:T(8,128)(2,1)S(1)} %get-tuple-element.21), channel_id=1, source_target_pairs={{0,192},{1,65},{64,128},{65,1},{128,64},{129,193},{192,0},{193,129... | collective-permute-start | bytes 688136 | tf_op jit(solution)/shard_map/ppermute | solution.py:383
  32.9 6.6 %collective-permute-start.6 = (bf16[2,4,112,128]{3,2,1,0:T(8,128)(2,1)S(1)}, bf16[2,4,112,128]{3,2,1,0:T(8,128)(2,1)S(1)}, u32[]{:S(2)}, u32[]{:S(2)}) collective-permute-start(bf16[2,4,112,128]{3,2,1,0:T(8,128)(2,1)S(1)} %collective-permute-done.4), channel_id=1, source_target_pairs={{0,192},{1,65},{64,128},{65,1},{128,64},{129,193},{192,0},{193,129... | collective-permute-start | bytes 688136 | tf_op jit(solution)/shard_map/ppermute | solution.py:383
  35.5 8.7 %collective-permute-start.15 = (bf16[2,4,112,128]{3,2,1,0:T(8,128)(2,1)S(1)}, bf16[2,4,112,128]{3,2,1,0:T(8,128)(2,1)S(1)}, u32[]{:S(2)}, u32[]{:S(2)}) collective-permute-start(bf16[2,4,112,128]{3,2,1,0:T(8,128)(2,1)S(1)} %get-tuple-element.20), channel_id=1, source_target_pairs={{0,6},{1,3},{2,4},{3,1},{4,2},{5,7},{6,0},{7,5},{8,14},{9,11},{10,... | collective-permute-start | bytes 688136 | tf_op jit(solution)/shard_map/ppermute | solution.py:383
  37.8 7.4 %collective-permute-start.16 = (bf16[2,4,112,128]{3,2,1,0:T(8,128)(2,1)S(1)}, bf16[2,4,112,128]{3,2,1,0:T(8,128)(2,1)S(1)}, u32[]{:S(2)}, u32[]{:S(2)}) collective-permute-start(bf16[2,4,112,128]{3,2,1,0:T(8,128)(2,1)S(1)} %collective-permute-done.14), channel_id=1, source_target_pairs={{0,6},{1,3},{2,4},{3,1},{4,2},{5,7},{6,0},{7,5},{8,14},{9,11},{10,... | collective-permute-start | bytes 688136 | tf_op jit(solution)/shard_map/ppermute | solution.py:383
  39.6 45.4 %copy-start = (bf16[4,2,4,112,128]{4,3,2,1,0:T(8,128)(2,1)}, bf16[4,2,4,112,128]{4,3,2,1,0:T(8,128)(2,1)S(1)}, u32[]{:S(2)}) copy-start(bf16[4,2,4,112,128]{4,3,2,1,0:T(8,128)(2,1)S(1)} %pad_maximum_fusion.refs_0_) | copy-start | bytes 2752516
  39.6 7.6 %collective-permute-start.10 = (bf16[4,2,4,112,128]{4,3,2,1,0:T(8,128)(2,1)S(1)}, bf16[4,2,4,112,128]{4,3,2,1,0:T(8,128)(2,1)S(1)}, u32[]{:S(2)}, u32[]{:S(2)}) collective-permute-start(bf16[4,2,4,112,128]{4,3,2,1,0:T(8,128)(2,1)S(1)} %pad_maximum_fusion.refs_0_), channel_id=1, source_target_pairs={{0,1},{1,0},{2,3},{3,2},{4,5},{5,4},{6,7},{7,6},{8,9},{9,8},{10,11... | collective-permute-start | bytes 2752520 | tf_op jit(solution)/shard_map/ppermute | solution.py:387
  39.7 25.0 %collective-permute-start.8 = (bf16[4,2,4,112,128]{4,3,2,1,0:T(8,128)(2,1)S(1)}, bf16[4,2,4,112,128]{4,3,2,1,0:T(8,128)(2,1)S(1)}, u32[]{:S(2)}, u32[]{:S(2)}) collective-permute-start(bf16[4,2,4,112,128]{4,3,2,1,0:T(8,128)(2,1)S(1)} %pad_maximum_fusion.refs_0_), channel_id=1, source_target_pairs={{0,6},{1,3},{2,4},{3,1},{4,2},{5,7},{6,0},{7,5},{8,14},{9,11},{10,... | collective-permute-start | bytes 2752520 | tf_op jit(solution)/shard_map/ppermute | solution.py:383
  44.1 20.6 %collective-permute-start.7 = (bf16[4,2,4,112,128]{4,3,2,1,0:T(8,128)(2,1)S(1)}, bf16[4,2,4,112,128]{4,3,2,1,0:T(8,128)(2,1)}, u32[]{:S(2)}, u32[]{:S(2)}) collective-permute-start(bf16[4,2,4,112,128]{4,3,2,1,0:T(8,128)(2,1)S(1)} %pad_maximum_fusion.refs_0_), channel_id=1, source_target_pairs={{0,2},{1,7},{2,0},{3,5},{4,6},{5,3},{6,4},{7,1},{8,10},{9,15},{10,... | collective-permute-start | bytes 2752520 | tf_op jit(solution)/shard_map/ppermute | solution.py:383
  45.3 39.8 %copy-start.1 = (bf16[4,2,4,112,128]{4,3,2,1,0:T(8,128)(2,1)}, bf16[4,2,4,112,128]{4,3,2,1,0:T(8,128)(2,1)S(1)}, u32[]{:S(2)}) copy-start(bf16[4,2,4,112,128]{4,3,2,1,0:T(8,128)(2,1)S(1)} %pad_maximum_fusion.1.refs_8_) | copy-start | bytes 2752516
  45.3 23.2 %collective-permute-start.17 = (bf16[4,2,4,112,128]{4,3,2,1,0:T(8,128)(2,1)S(1)}, bf16[4,2,4,112,128]{4,3,2,1,0:T(8,128)(2,1)}, u32[]{:S(2)}, u32[]{:S(2)}) collective-permute-start(bf16[4,2,4,112,128]{4,3,2,1,0:T(8,128)(2,1)S(1)} %pad_maximum_fusion.1.refs_8_), channel_id=1, source_target_pairs={{0,64},{1,193},{64,0},{65,129},{128,192},{129,65},{192,128},{193,1... | collective-permute-start | bytes 2752520 | tf_op jit(solution)/shard_map/ppermute | solution.py:383
  47.2 23.0 %collective-permute-start.20 = (bf16[4,2,4,112,128]{4,3,2,1,0:T(8,128)(2,1)S(1)}, bf16[4,2,4,112,128]{4,3,2,1,0:T(8,128)(2,1)S(1)}, u32[]{:S(2)}, u32[]{:S(2)}) collective-permute-start(bf16[4,2,4,112,128]{4,3,2,1,0:T(8,128)(2,1)S(1)} %pad_maximum_fusion.1.refs_8_), channel_id=1, source_target_pairs={{0,1},{1,0},{2,3},{3,2},{4,5},{5,4},{6,7},{7,6},{8,9},{9,8},{10,11... | collective-permute-start | bytes 2752520 | tf_op jit(solution)/shard_map/ppermute | solution.py:387
  47.3 37.8 %copy-start.5 = (bf16[4,2,4,112,128]{4,3,2,1,0:T(8,128)(2,1)}, bf16[4,2,4,112,128]{4,3,2,1,0:T(8,128)(2,1)S(1)}, u32[]{:S(2)}) copy-start(bf16[4,2,4,112,128]{4,3,2,1,0:T(8,128)(2,1)S(1)} %collective-permute-done.10.refs_4_) | copy-start | bytes 2752516
  47.3 23.0 %collective-permute-start.18 = (bf16[4,2,4,112,128]{4,3,2,1,0:T(8,128)(2,1)S(1)}, bf16[4,2,4,112,128]{4,3,2,1,0:T(8,128)(2,1)}, u32[]{:S(2)}, u32[]{:S(2)}) collective-permute-start(bf16[4,2,4,112,128]{4,3,2,1,0:T(8,128)(2,1)S(1)} %pad_maximum_fusion.1.refs_8_), channel_id=1, source_target_pairs={{0,192},{1,65},{64,128},{65,1},{128,64},{129,193},{192,0},{193,129... | collective-permute-start | bytes 2752520 | tf_op jit(solution)/shard_map/ppermute | solution.py:383
  64.7 5.5 %copy-start.6 = (bf16[4,2,4,112,128]{4,3,2,1,0:T(8,128)(2,1)}, bf16[4,2,4,112,128]{4,3,2,1,0:T(8,128)(2,1)S(1)}, u32[]{:S(2)}) copy-start(bf16[4,2,4,112,128]{4,3,2,1,0:T(8,128)(2,1)S(1)} %collective-permute-done.8.refs_2_) | copy-start | bytes 2752516
  64.7 6.0 %collective-permute-start.12 = (bf16[4,2,4,112,128]{4,3,2,1,0:T(8,128)(2,1)S(1)}, bf16[4,2,4,112,128]{4,3,2,1,0:T(8,128)(2,1)S(1)}, u32[]{:S(2)}, u32[]{:S(2)}) collective-permute-start(bf16[4,2,4,112,128]{4,3,2,1,0:T(8,128)(2,1)S(1)} %collective-permute-done.8.refs_2_), channel_id=1, source_target_pairs={{0,1},{1,0},{2,3},{3,2},{4,5},{5,4},{6,7},{7,6},{8,9},{9,8},{10,11... | collective-permute-start | bytes 2752520 | tf_op jit(solution)/shard_map/ppermute | solution.py:387
  64.7 15.5 %collective-permute-start.9 = (bf16[4,2,4,112,128]{4,3,2,1,0:T(8,128)(2,1)}, bf16[4,2,4,112,128]{4,3,2,1,0:T(8,128)(2,1)}, u32[]{:S(2)}, u32[]{:S(2)}) collective-permute-start(bf16[4,2,4,112,128]{4,3,2,1,0:T(8,128)(2,1)} %collective-permute-done.7.refs_1_), channel_id=1, source_target_pairs={{0,6},{1,3},{2,4},{3,1},{4,2},{5,7},{6,0},{7,5},{8,14},{9,11},{10,... | collective-permute-start | bytes 2752520 | tf_op jit(solution)/shard_map/ppermute | solution.py:383
  68.5 13.7 %collective-permute-start.19 = (bf16[4,2,4,112,128]{4,3,2,1,0:T(8,128)(2,1)}, bf16[4,2,4,112,128]{4,3,2,1,0:T(8,128)(2,1)}, u32[]{:S(2)}, u32[]{:S(2)}) collective-permute-start(bf16[4,2,4,112,128]{4,3,2,1,0:T(8,128)(2,1)} %collective-permute-done.17.refs_9_), channel_id=1, source_target_pairs={{0,192},{1,65},{64,128},{65,1},{128,64},{129,193},{192,0},{193,129... | collective-permute-start | bytes 2752520 | tf_op jit(solution)/shard_map/ppermute | solution.py:383
  70.2 0.9 copy-start.7
  70.2 12.6 %collective-permute-start.11 = (bf16[4,2,4,112,128]{4,3,2,1,0:T(8,128)(2,1)}, bf16[4,2,4,112,128]{4,3,2,1,0:T(8,128)(2,1)}, u32[]{:S(2)}, u32[]{:S(2)}) collective-permute-start(bf16[4,2,4,112,128]{4,3,2,1,0:T(8,128)(2,1)} %collective-permute-done.7.refs_1_), channel_id=1, source_target_pairs={{0,1},{1,0},{2,3},{3,2},{4,5},{5,4},{6,7},{7,6},{8,9},{9,8},{10,11... | collective-permute-start | bytes 2752520 | tf_op jit(solution)/shard_map/ppermute | solution.py:387
  70.3 12.6 %collective-permute-start.21 = (bf16[4,2,4,112,128]{4,3,2,1,0:T(8,128)(2,1)}, bf16[4,2,4,112,128]{4,3,2,1,0:T(8,128)(2,1)}, u32[]{:S(2)}, u32[]{:S(2)}) collective-permute-start(bf16[4,2,4,112,128]{4,3,2,1,0:T(8,128)(2,1)} %collective-permute-done.17.refs_9_), channel_id=1, source_target_pairs={{0,1},{1,0},{2,3},{3,2},{4,5},{5,4},{6,7},{7,6},{8,9},{9,8},{10,11... | collective-permute-start | bytes 2752520 | tf_op jit(solution)/shard_map/ppermute | solution.py:387
  71.2 1.0 copy-start.8
  71.2 11.7 %collective-permute-start.22 = (bf16[4,2,4,112,128]{4,3,2,1,0:T(8,128)(2,1)}, bf16[4,2,4,112,128]{4,3,2,1,0:T(8,128)(2,1)}, u32[]{:S(2)}, u32[]{:S(2)}) collective-permute-start(bf16[4,2,4,112,128]{4,3,2,1,0:T(8,128)(2,1)} %collective-permute-done.18.refs_10_), channel_id=1, source_target_pairs={{0,1},{1,0},{2,3},{3,2},{4,5},{5,4},{6,7},{7,6},{8,9},{9,8},{10,11... | collective-permute-start | bytes 2752520 | tf_op jit(solution)/shard_map/ppermute | solution.py:387
  80.2 2.8 %collective-permute-start.13 = (bf16[4,2,4,112,128]{4,3,2,1,0:T(8,128)(2,1)}, bf16[4,2,4,112,128]{4,3,2,1,0:T(8,128)(2,1)}, u32[]{:S(2)}, u32[]{:S(2)}) collective-permute-start(bf16[4,2,4,112,128]{4,3,2,1,0:T(8,128)(2,1)} %collective-permute-done.9.refs_3_), channel_id=1, source_target_pairs={{0,1},{1,0},{2,3},{3,2},{4,5},{5,4},{6,7},{7,6},{8,9},{9,8},{10,11... | collective-permute-start | bytes 2752520 | tf_op jit(solution)/shard_map/ppermute | solution.py:387
  82.2 2.8 %collective-permute-start.23 = (bf16[4,2,4,112,128]{4,3,2,1,0:T(8,128)(2,1)}, bf16[4,2,4,112,128]{4,3,2,1,0:T(8,128)(2,1)}, u32[]{:S(2)}, u32[]{:S(2)}) collective-permute-start(bf16[4,2,4,112,128]{4,3,2,1,0:T(8,128)(2,1)} %collective-permute-done.19.refs_11_), channel_id=1, source_target_pairs={{0,1},{1,0},{2,3},{3,2},{4,5},{5,4},{6,7},{7,6},{8,9},{9,8},{10,11... | collective-permute-start | bytes 2752520 | tf_op jit(solution)/shard_map/ppermute | solution.py:387
  146.2 2.8 %collective-permute-start.24 = (bf16[4,4,112,256]{3,2,1,0:T(8,128)(2,1)}, bf16[4,4,112,256]{3,2,1,0:T(8,128)(2,1)S(1)}, u32[]{:S(2)}, u32[]{:S(2)}) collective-permute-start(bf16[4,4,112,256]{3,2,1,0:T(8,128)(2,1)} %get-tuple-element.11), channel_id=1, source_target_pairs={{0,1},{1,0},{2,3},{3,2},{4,5},{5,4},{6,7},{7,6},{8,9},{9,8},{10,11... | collective-permute-start | bytes 2752520 | tf_op jit(solution)/shard_map/ppermute | solution.py:387
  150.4 8.6 %collective-permute-start.25 = (bf16[2,4,112,256]{3,2,1,0:T(8,128)(2,1)S(1)}, bf16[2,4,112,256]{3,2,1,0:T(8,128)(2,1)S(1)}, u32[]{:S(2)}, u32[]{:S(2)}) collective-permute-start(bf16[2,4,112,256]{3,2,1,0:T(8,128)(2,1)S(1)} %get-tuple-element.17), channel_id=1, source_target_pairs={{0,2},{1,7},{2,0},{3,5},{4,6},{5,3},{6,4},{7,1},{8,10},{9,15},{10,... | collective-permute-start | bytes 1376264 | tf_op jit(solution)/shard_map/ppermute | solution.py:383
  159.1 7.3 %collective-permute-start.26 = (bf16[4,112,256]{2,1,0:T(8,128)(2,1)S(1)}, bf16[4,112,256]{2,1,0:T(8,128)(2,1)S(1)}, u32[]{:S(2)}, u32[]{:S(2)}) collective-permute-start(bf16[4,112,256]{2,1,0:T(8,128)(2,1)S(1)} %fusion.2), channel_id=1, source_target_pairs={{0,6},{1,3},{2,4},{3,1},{4,2},{5,7},{6,0},{7,5},{8,14},{9,11},{10,... | collective-permute-start | bytes 688136 | tf_op jit(solution)/shard_map/ppermute | solution.py:383
  167.1 8.1 %collective-permute-start.29 = (bf16[112,256]{1,0:T(8,128)(2,1)S(1)}, bf16[112,256]{1,0:T(8,128)(2,1)S(1)}, u32[]{:S(2)}, u32[]{:S(2)}) collective-permute-start(bf16[112,256]{1,0:T(8,128)(2,1)S(1)} %get-tuple-element.22), channel_id=1, source_target_pairs={{0,16},{8,24},{16,0},{24,8},{1,17},{9,25},{17,1},{25,9},{2,18},{10... | collective-permute-start | bytes 172040 | tf_op jit(solution)/shard_map/ppermute | solution.py:391
  168.7 7.7 %collective-permute-start.28 = (bf16[112,256]{1,0:T(8,128)(2,1)S(1)}, bf16[112,256]{1,0:T(8,128)(2,1)S(1)}, u32[]{:S(2)}, u32[]{:S(2)}) collective-permute-start(bf16[112,256]{1,0:T(8,128)(2,1)S(1)} %get-tuple-element.23), channel_id=1, source_target_pairs={{0,24},{1,9},{8,16},{9,1},{16,8},{17,25},{24,0},{25,17},{2,26},{3,... | collective-permute-start | bytes 172040 | tf_op jit(solution)/shard_map/ppermute | solution.py:383
  173.2 5.7 %collective-permute-start.27 = (bf16[112,256]{1,0:T(8,128)(2,1)S(1)}, bf16[112,256]{1,0:T(8,128)(2,1)S(1)}, u32[]{:S(2)}, u32[]{:S(2)}) collective-permute-start(bf16[112,256]{1,0:T(8,128)(2,1)S(1)} %get-tuple-element.24), channel_id=1, source_target_pairs={{0,8},{1,25},{8,0},{9,17},{16,24},{17,9},{24,16},{25,1},{2,10},{3,... | collective-permute-start | bytes 172040 | tf_op jit(solution)/shard_map/ppermute | solution.py:383
  175.2 3.6 %copy-start.2 = (bf16[112,256]{1,0:T(8,128)(2,1)}, bf16[112,256]{1,0:T(8,128)(2,1)S(1)}, u32[]{:S(2)}) copy-start(bf16[112,256]{1,0:T(8,128)(2,1)S(1)} %collective-permute-done.29.d_ref) | copy-start | bytes 172036
  176.4 2.4 %copy-start.3 = (bf16[112,256]{1,0:T(8,128)(2,1)}, bf16[112,256]{1,0:T(8,128)(2,1)S(1)}, u32[]{:S(2)}) copy-start(bf16[112,256]{1,0:T(8,128)(2,1)S(1)} %collective-permute-done.28.c_ref) | copy-start | bytes 172036
  178.8 0.6 copy-start.4

commit v5 on v4

--- a/solution.py
+++ b/solution.py
@@ -110,15 +110,15 @@
     return jnp.where(i >= 2, 5 - i, i)
 
 
-def partner(i, c, first):
-    return jnp.where((c == 0) == first, i ^ 1, 3 - i)
+def ring(i):
+    return [i, i ^ 1, 3 - i, (3 - i) ^ 1]
 
 
 def sequence_kernel(pos_ref, *refs):
-    left, right = refs[:8], refs[8:16]
-    entry_ref, cot_ref, sent_ref = refs[16:19]
-    w_scr, rows_scr, xs, ns, mixed_scr, decay_scr, write_scr, small_scr, proj_scr = refs[19:28]
-    first_scr, sem_a, sem_b, sem_c = refs[28:]
+    sets = refs[:5], refs[5:10]
+    entry_ref, cot_ref, sent_ref = refs[10:13]
+    w_scr, rows_scr, xs, ns, mixed_scr, decay_scr, write_scr, small_scr, proj_scr = refs[13:22]
+    first_scr, sem_w, sem_c = refs[22:]
     x, y, c, zh, section = (pos_ref[i] for i in range(5))
     mine = jnp.minimum(section, SEQS - 1)
     loads = []
@@ -129,37 +129,30 @@
         copy.start()
         loads.append(copy)
 
-    def ring(i, core):
-        one, two = partner(i, core, True), partner(i, core, False)
-        return [i, one, two, partner(two, core, True)]
-
-    for target in range(4):
-        for kc in range(2):
-            cc = (c + kc) % 2
-            ys, xx = ring(y, cc), ring(x, cc)
-            slot = sum(jnp.where(xx[j] == target, j, 0) for j in range(4))
-            for i in range(4):
-                pltpu.make_async_copy(
-                    left[kc * 4 + i].at[slot],
-                    w_scr.at[2 * target : 2 * target + 2, :, ys[i], cc, :, :C],
-                    sem_a.at[target],
-                ).start()
-
-                @pl.when(xx[i] == target)
-                def _(i=i, kc=kc, cc=cc, ys=ys, target=target):
-                    for j in range(4):
-                        pltpu.make_async_copy(
-                            right[kc * 4 + i].at[j],
-                            w_scr.at[2 * target : 2 * target + 2, :, ys[j], cc, :, C:],
-                            sem_b.at[target],
-                        ).start()
+    def place(at):
+        side = (c + at) % 2
+        ys, xs_ = ring(y), ring(x)
+        for i in range(4):
+            for j in range(4):
+                src = sets[at][i].at[j] if i < 3 else sets[at][3 + j // 2].at[j % 2]
+                yy = jnp.where(side == 0, ys[i], ys[j])
+                xx = jnp.where(side == 0, xs_[j], xs_[i])
+                lanes = pl.ds(pl.multiple_of(side * C, C), C)
+                yield src, w_scr.at[pl.ds(2 * xx, 2), :, yy, :, :, lanes], xx
+
+    for low, high in ((0, 0), (1, 1), (2, 3)):
+        for at in range(2):
+            for src, dst, xx in place(at):
+
+                @pl.when((xx >= low) & (xx <= high))
+                def _(src=src, dst=dst, xx=xx):
+                    pltpu.make_async_copy(src, dst, sem_w.at[xx]).start()
 
     def wait_layers(at):
-        for sem, src in ((sem_a, left[0]), (sem_b, right[0])):
-            for _ in range(8):
-                pltpu.make_async_copy(
-                    src.at[0], w_scr.at[0:2, :, 0, 0, :, :C], sem.at[at]
-                ).wait()
+        for _ in range(8):
+            pltpu.make_async_copy(
+                sets[0][0].at[0], w_scr.at[0:2, :, 0, :, :, :C], sem_w.at[at]
+            ).wait()
 
     causal, diag, spread, block, tri = masks()
 
@@ -391,10 +384,23 @@
     return lax.ppermute(array, axis, [(i, i ^ 2) for i in range(4)])
 
 
-def gather_ring(array, axis, direct=False):
-    one = swap(array, axis, True)
-    two = swap(array, axis, False)
-    return [array, one, two, opposite(array, axis) if direct else swap(one, axis, False)]
+def cross(array, of_core, first):
+    pairs = []
+    for x in range(4):
+        for y in range(4):
+            for c in range(2):
+                to = [x, y]
+                axis = of_core[c]
+                to[axis] = to[axis] ^ 1 if first else 3 - to[axis]
+                pairs.append(((x * 4 + y) * 2 + c, (to[0] * 4 + to[1]) * 2 + c))
+    return lax.ppermute(array, ("x", "y", "c"), pairs)
+
+
+def gather_cross(array, of_core):
+    one = cross(array, of_core, True)
+    two = cross(array, of_core, False)
+    half = array.shape[0] // 2
+    return [array, one, two, cross(one[:half], of_core, False), cross(two[half:], of_core, True)]
 
 
 def add(a, b):
@@ -414,11 +420,15 @@
         [key_weight[0], jnp.concatenate([wide[:16], right], axis=1)], axis=0
     )
 
-    along = jnp.stack(gather_ring(packed, "zh", direct=True))
-    first, second = partner(zh, c, True), partner(zh, c, False)
-    across = partner(second, c, True)
-    order = [jnp.where(j == first, 1, jnp.where(j == second, 2, jnp.where(j == across, 3, 0))) for j in range(4)]
-    along = jnp.take(along, jnp.stack(order), axis=0)
+    left, right = packed[:, :C], packed[:, C:]
+    mine = jnp.where(c == 0, left, right)
+    theirs = other_core(jnp.where(c == 0, right, left))
+    half = jnp.where(c == 0, jnp.stack([mine, theirs]), jnp.stack([theirs, mine]))
+
+    along = [half, swap(half, "zh", True), swap(half, "zh", False), opposite(half, "zh")]
+    bits = gray(jnp.arange(4)) ^ gray(zh)
+    order = jnp.where(c == 0, bits, jnp.array([0, 2, 1, 3])[bits])
+    along = jnp.take(jnp.stack(along), order, axis=0)
     pairs = []
     for z in range(8):
         for core in range(2):
@@ -427,17 +437,14 @@
     other = lax.ppermute(along, ("zl", "zh", "c"), pairs)
     both = jnp.where(zl == 0, jnp.stack([along, other]), jnp.stack([other, along]))
 
-    left = jnp.stack(gather_ring(both[..., :C], "x"))
-    right = jnp.stack(gather_ring(both[..., C:], "y"))
-    left = gather_ring(left, "y")
-    right = gather_ring(right, "x")
-    left = left + [other_core(a) for a in left]
-    right = right + [other_core(a) for a in right]
+    *three, low, high = gather_cross(both, (0, 1))
+    sets = gather_cross(jnp.stack(three + [jnp.concatenate([low, high])]), (1, 0))
+    sets = sets + [other_core(a) for a in sets]
 
     sent = call(
         sequence_kernel,
         [shape(LAYERS, SENT, BLOCK)],
-        [SMEM] + [ANY] * 18,
+        [SMEM] + [ANY] * 12,
         [
             pltpu.VMEM((LAYERS, 4, 4, 2, PIECE, 256), BF16),
             pltpu.VMEM((LAYERS, T, D), BF16),
@@ -450,11 +457,10 @@
             pltpu.VMEM((LAYERS, T, 256), F32),
             pltpu.VMEM((2, T, D), BF16),
             pltpu.SemaphoreType.DMA((4,)),
-            pltpu.SemaphoreType.DMA((4,)),
             pltpu.SemaphoreType.DMA((2,)),
         ],
         cost=(8_000_000_000, 30_000_000),
-    )(pos, *left, *right, entries, cotangents)[0]
+    )(pos, *sets, entries, cotangents)[0]
 
     groups = [
         [

time: 181 us -> 184 us (1.017)
  starting transfers between devices: 42.8 us -> 35.3 us
  waiting for transfers between devices: 65.3 us -> 72.7 us
  local copies, waits for them, and re-layouts: 5.39 us -> 7.65 us
    ppermute x0 -> x8, waiting for transfers between devices: none -> 42.1 us  [cross(): return lax.ppermute(array, ('x', 'y', 'c'), pairs)]
    ppermute x18 -> x6, waiting for transfers between devices: 50.4 us -> 18.6 us  [swap(): return lax.ppermute(array, (axis, 'c'), ring_pairs(first))]
    ppermute x18 -> x6, starting transfers between devices: 38.3 us -> 8.35 us  [swap(): return lax.ppermute(array, (axis, 'c'), ring_pairs(first))]
    ppermute x0 -> x8, starting transfers between devices: none -> 13.8 us  [cross(): return lax.ppermute(array, ('x', 'y', 'c'), pairs)]
    ppermute x2, starting transfers between devices: 2.58 us -> 10.4 us  [opposite(): return lax.ppermute(array, axis, [(i, i ^ 2) for i in range(4)])]
    slice x0 -> x4, local copies, waits for them, and re-layouts: none -> 2.51 us  [the longest x2 1.26 us: gather_cross(): two[half:]]
    ppermute x2, waiting for transfers between devices: 5.26 us -> 3.13 us  [opposite(): return lax.ppermute(array, axis, [(i, i ^ 2) for i in range(4)])]
    ppermute x9 -> x7, waiting for transfers between devices: 4.85 us -> 4.88 us  [other_core(): return lax.ppermute(array, 'c', [(0, 1), (1, 0)])]
  transfers between devices with their start and end apart: 30 -> 24, of which waited for: 18 -> 18; matrix products, arithmetic and copies ran while one was open for 1% -> 3% of each run, Pallas kernels for 0% -> 0%
where the time goes in v5:
time: 184 us; the launch traced here: 182 us
  waiting for transfers between devices  72.7 us (40%)
  starting transfers between devices  35.3 us (19%)
  Pallas kernels  32.3 us (18%)
  blocking collectives  30.5 us (17%)
  local copies, waits for them, and re-layouts  7.65 us (4%)
  other arithmetic  3.18 us (2%)
    ppermute x8, waiting for transfers between devices, cross(): return lax.ppermute(array, ('x', 'y', 'c'), pairs)  42.1 us
    all_to_all x1, blocking collectives, per_device(): lax.all_to_all(sent, ('x', 'zl', 'zh', 'y', 'c'), 0, 0, axis_index_groups...  30.5 us
    pallas_call x1, Pallas kernels, per_device(): call(sequence_kernel, [shape(LAYERS, SENT, BLOCK)], [SMEM] + [ANY] * 12,...  25.8 us
    ppermute x6, waiting for transfers between devices, swap(): return lax.ppermute(array, (axis, 'c'), ring_pairs(first))  18.6 us
    ppermute x8, starting transfers between devices, cross(): return lax.ppermute(array, ('x', 'y', 'c'), pairs)  13.8 us
    ppermute x2, starting transfers between devices, opposite(): return lax.ppermute(array, axis, [(i, i ^ 2) for i in range(4)])  10.4 us
    ppermute x6, starting transfers between devices, swap(): return lax.ppermute(array, (axis, 'c'), ring_pairs(first))  8.35 us
    pallas_call x1, Pallas kernels, per_device(): call(weight_kernel, [half, half], [SMEM, ANY], [pltpu.VMEM((LAYERS, SENT,...  4.92 us
  transfers between devices with their start and end apart: 24, of which 18 were waited for; matrix products, arithmetic and copies ran while one was open for 3% of the time, Pallas kernels for 0%

profile of v5, /device:TPU:2, one launch (start us, length us, event | category | flops | bytes accessed | tf_op | source)
XLA Modules:
  0.0 182.4 jit_solution(10102531991090960113)
XLA Ops:
  0.6 0.7 pad_slice_fusion
  1.3 0.7 pad_slice_fusion.1
  2.0 0.8 maximum_maximum_fusion
  3.0 1.3 gather_fusion
  4.4 7.3 %collective-permute-start.3 = (bf16[2,112,128]{2,1,0:T(8,128)(2,1)S(1)}, bf16[2,112,128]{2,1,0:T(8,128)(2,1)S(1)}, u32[]{:S(2)}, u32[]{:S(2)}) collective-permute-start(bf16[2,112,128]{2,1,0:T(8,128)(2,1)S(1)} %maximum_select_fusion.3), channel_id=1, source_target_pairs={{0,16},{8,24},{16,0},{24,8},{1,17},{9,25},{17,1},{25,9},{2,18},{10... | collective-permute-start | bytes 172040 | tf_op jit(solution)/shard_map/ppermute | solution.py:384
  11.7 1.5 collective-permute-start.1
  13.2 1.2 collective-permute-done.3
  14.3 4.0 %collective-permute-done.2 = bf16[2,112,128]{2,1,0:T(8,128)(2,1)S(1)} collective-permute-done((bf16[2,112,128]{2,1,0:T(8,128)(2,1)S(1)}, bf16[2,112,128]{2,1,0:T(8,128)(2,1)S(1)}, u32[]{:S(2)}, u32[]{:S(2)}) %collective-permute-start.2) | collective-permute-done | bytes 57376 | tf_op jit(solution)/shard_map/ppermute | solution.py:376
  18.6 0.6 gather_fusion.1
  19.2 2.1 %collective-permute-start.4 = (bf16[4,2,112,128]{3,2,1,0:T(8,128)(2,1)S(1)}, bf16[4,2,112,128]{3,2,1,0:T(8,128)(2,1)S(1)}, u32[]{:S(2)}, u32[]{:S(2)}) collective-permute-start(bf16[4,2,112,128]{3,2,1,0:T(8,128)(2,1)S(1)} %broadcast_select_fusion), channel_id=1, source_target_pairs={{0,32},{1,57},{32,0},{33,9},{8,40},{9,33},{40,8},{41,17},{16,48},{... | collective-permute-start | bytes 688136 | tf_op jit(solution)/shard_map/ppermute | solution.py:437
  21.4 4.0 %collective-permute-done.4 = bf16[4,2,112,128]{3,2,1,0:T(8,128)(2,1)S(1)} collective-permute-done((bf16[4,2,112,128]{3,2,1,0:T(8,128)(2,1)S(1)}, bf16[4,2,112,128]{3,2,1,0:T(8,128)(2,1)S(1)}, u32[]{:S(2)}, u32[]{:S(2)}) %collective-permute-start.4) | collective-permute-done | bytes 229408 | tf_op jit(solution)/shard_map/ppermute | solution.py:437
  25.4 1.6 collective-permute-start.6
  27.0 1.8 collective-permute-start.5
  28.8 5.2 %collective-permute-done.6 = bf16[2,4,2,112,128]{4,3,2,1,0:T(8,128)(2,1)S(1)} collective-permute-done((bf16[2,4,2,112,128]{4,3,2,1,0:T(8,128)(2,1)S(1)}, bf16[2,4,2,112,128]{4,3,2,1,0:T(8,128)(2,1)S(1)}, u32[]{:S(2)}, u32[]{:S(2)}) %collective-permute-start.6) | collective-permute-done | bytes 458784 | tf_op jit(solution)/shard_map/ppermute | solution.py:396
  34.0 1.8 %collective-permute-start.8 = (bf16[1,4,2,112,128]{4,3,2,1,0:T(8,128)(2,1)S(1)}, bf16[1,4,2,112,128]{4,3,2,1,0:T(8,128)(2,1)S(1)}, u32[]{:S(2)}, u32[]{:S(2)}) collective-permute-start(bf16[1,4,2,112,128]{4,3,2,1,0:T(8,128)(2,1)S(1)} %slice.87), channel_id=1, source_target_pairs={{0,64},{1,3},{2,66},{3,1},{4,68},{5,7},{6,70},{7,5},{64,0},{65,67}... | collective-permute-start | bytes 688136 | tf_op jit(solution)/shard_map/ppermute | solution.py:396
  35.9 2.2 %collective-permute-start.7 = (bf16[1,4,2,112,128]{4,3,2,1,0:T(8,128)(2,1)S(1)}, bf16[1,4,2,112,128]{4,3,2,1,0:T(8,128)(2,1)S(1)}, u32[]{:S(2)}, u32[]{:S(2)}) collective-permute-start(bf16[1,4,2,112,128]{4,3,2,1,0:T(8,128)(2,1)S(1)} %slice.86), channel_id=1, source_target_pairs={{0,192},{1,7},{2,194},{3,5},{4,196},{5,3},{6,198},{7,1},{64,128},{... | collective-permute-start | bytes 688136 | tf_op jit(solution)/shard_map/ppermute | solution.py:396
  38.3 1.8 %collective-permute-done.8 = bf16[1,4,2,112,128]{4,3,2,1,0:T(8,128)(2,1)S(1)} collective-permute-done((bf16[1,4,2,112,128]{4,3,2,1,0:T(8,128)(2,1)S(1)}, bf16[1,4,2,112,128]{4,3,2,1,0:T(8,128)(2,1)S(1)}, u32[]{:S(2)}, u32[]{:S(2)}) %collective-permute-start.8) | collective-permute-done | bytes 229408 | tf_op jit(solution)/shard_map/ppermute | solution.py:396
  40.1 2.0 %collective-permute-done.7 = bf16[1,4,2,112,128]{4,3,2,1,0:T(8,128)(2,1)S(1)} collective-permute-done((bf16[1,4,2,112,128]{4,3,2,1,0:T(8,128)(2,1)S(1)}, bf16[1,4,2,112,128]{4,3,2,1,0:T(8,128)(2,1)S(1)}, u32[]{:S(2)}, u32[]{:S(2)}) %collective-permute-start.7) | collective-permute-done | bytes 229408 | tf_op jit(solution)/shard_map/ppermute | solution.py:396
  42.2 0.2 pad_maximum_fusion.refs_0_
  42.4 3.1 %collective-permute-start.10 = (bf16[4,2,4,2,112,128]{5,4,3,2,1,0:T(8,128)(2,1)S(1)}, bf16[4,2,4,2,112,128]{5,4,3,2,1,0:T(8,128)(2,1)}, u32[]{:S(2)}, u32[]{:S(2)}) collective-permute-start(bf16[4,2,4,2,112,128]{5,4,3,2,1,0:T(8,128)(2,1)S(1)} %pad_maximum_fusion.refs_0_), channel_id=1, source_target_pairs={{0,6},{1,193},{2,4},{3,195},{4,2},{5,197},{6,0},{7,199},{64,70},{6... | collective-permute-start | bytes 5505032 | tf_op jit(solution)/shard_map/ppermute | solution.py:396
  45.6 21.4 %collective-permute-done.10.refs_2_ = bf16[4,2,4,2,112,128]{5,4,3,2,1,0:T(8,128)(2,1)} collective-permute-done((bf16[4,2,4,2,112,128]{5,4,3,2,1,0:T(8,128)(2,1)S(1)}, bf16[4,2,4,2,112,128]{5,4,3,2,1,0:T(8,128)(2,1)}, u32[]{:S(2)}, u32[]{:S(2)}) %collective-permute-start.10) | collective-permute-done | bytes 1835040 | tf_op jit(solution)/shard_map/ppermute | solution.py:396
  67.0 1.2 slice.89
  68.3 0.5 collective-permute-start.12
  68.8 1.2 slice.88
  70.1 2.7 %collective-permute-start.11 = (bf16[2,2,4,2,112,128]{5,4,3,2,1,0:T(8,128)(2,1)S(1)}, bf16[2,2,4,2,112,128]{5,4,3,2,1,0:T(8,128)(2,1)}, u32[]{:S(2)}, u32[]{:S(2)}) collective-permute-start(bf16[2,2,4,2,112,128]{5,4,3,2,1,0:T(8,128)(2,1)S(1)} %slice.88), channel_id=1, source_target_pairs={{0,6},{1,193},{2,4},{3,195},{4,2},{5,197},{6,0},{7,199},{64,70},{6... | collective-permute-start | bytes 2752520 | tf_op jit(solution)/shard_map/ppermute | solution.py:396
  72.8 0.5 collective-permute-start.14
  73.3 8.5 %collective-permute-done.12.refs_4_ = bf16[2,2,4,2,112,128]{5,4,3,2,1,0:T(8,128)(2,1)S(1)} collective-permute-done((bf16[2,2,4,2,112,128]{5,4,3,2,1,0:T(8,128)(2,1)S(1)}, bf16[2,2,4,2,112,128]{5,4,3,2,1,0:T(8,128)(2,1)S(1)}, u32[]{:S(2)}, u32[]{:S(2)}) %collective-permute-start.12) | collective-permute-done | bytes 917536 | tf_op jit(solution)/shard_map/ppermute | solution.py:396
  81.8 3.1 %collective-permute-done.11.refs_3_ = bf16[2,2,4,2,112,128]{5,4,3,2,1,0:T(8,128)(2,1)} collective-permute-done((bf16[2,2,4,2,112,128]{5,4,3,2,1,0:T(8,128)(2,1)S(1)}, bf16[2,2,4,2,112,128]{5,4,3,2,1,0:T(8,128)(2,1)}, u32[]{:S(2)}, u32[]{:S(2)}) %collective-permute-start.11) | collective-permute-done | bytes 917536 | tf_op jit(solution)/shard_map/ppermute | solution.py:396
  84.9 0.6 stack.91.pos_ref
  85.5 2.2 %collective-permute-done.16.refs_8_ = bf16[2,2,4,2,112,128]{5,4,3,2,1,0:T(8,128)(2,1)} collective-permute-done((bf16[2,2,4,2,112,128]{5,4,3,2,1,0:T(8,128)(2,1)}, bf16[2,2,4,2,112,128]{5,4,3,2,1,0:T(8,128)(2,1)}, u32[]{:S(2)}, u32[]{:S(2)}) %collective-permute-start.16) | collective-permute-done | bytes 917536 | tf_op jit(solution)/shard_map/ppermute | solution.py:380
  87.7 25.8 %shard_map.102 = bf16[8,304,384]{2,1,0:T(8,128)(2,1)} custom-call(s32[5]{0:T(128)} %stack.91.pos_ref, bf16[4,2,4,2,112,128]{5,4,3,2,1,0:T(8,128)(2,1)} %copy-done, bf16[4,2,4,2,112,128]{5,4,3,2,1,0:T(8,128)(2,1)} %collective-permute-done.9.refs_1_, bf16[4,2,4,2,112,128]{5,4,3,2,1,0:T(8,128)(2,1)} %collective-permute-done.10.refs_2_, ...), custom_call_target="tpu_custom_call" | custom-call | flops 8000000000 | bytes 30000000 | tf_op jit(solution)/shard_map/pallas_call | solution.py:444
  113.5 30.5 %all_to_all.5.got_ref = bf16[8,304,384]{2,1,0:T(8,128)(2,1)} all-to-all(bf16[8,304,384]{2,1,0:T(8,128)(2,1)} %shard_map.102), channel_id=1, replica_groups={{0,32,64,96,128,160,192,224},{1,57,65,121,129,185,193,249},{2,34,66,98,..., dimensions={0} | all-to-all | bytes 3735552 | tf_op jit(solution)/shard_map/all_to_all | solution.py:474
  144.0 4.9 %shard_map.103 = (bf16[4,4,112,256]{3,2,1,0:T(8,128)(2,1)}, bf16[4,4,112,256]{3,2,1,0:T(8,128)(2,1)}) custom-call(s32[5]{0:T(128)} %stack.91.pos_ref, bf16[8,304,384]{2,1,0:T(8,128)(2,1)} %all_to_all.5.got_ref), custom_call_target="tpu_custom_call" | custom-call | flops 600000000 | bytes 4000000 | tf_op jit(solution)/shard_map/pallas_call | solution.py:478
  149.0 2.7 %collective-permute-done.18 = bf16[4,4,112,256]{3,2,1,0:T(8,128)(2,1)S(1)} collective-permute-done((bf16[4,4,112,256]{3,2,1,0:T(8,128)(2,1)}, bf16[4,4,112,256]{3,2,1,0:T(8,128)(2,1)S(1)}, u32[]{:S(2)}, u32[]{:S(2)}) %collective-permute-start.18) | collective-permute-done | bytes 917536 | tf_op jit(solution)/shard_map/ppermute | solution.py:380
  151.7 1.4 add_convert_fusion.1
  153.1 0.8 collective-permute-start.19
  153.9 7.7 %collective-permute-done.19 = bf16[2,4,112,256]{3,2,1,0:T(8,128)(2,1)S(1)} collective-permute-done((bf16[2,4,112,256]{3,2,1,0:T(8,128)(2,1)S(1)}, bf16[2,4,112,256]{3,2,1,0:T(8,128)(2,1)S(1)}, u32[]{:S(2)}, u32[]{:S(2)}) %collective-permute-start.19) | collective-permute-done | bytes 458784 | tf_op jit(solution)/shard_map/ppermute | solution.py:376
  161.7 2.7 %collective-permute-start.20 = (bf16[4,112,256]{2,1,0:T(8,128)(2,1)S(1)}, bf16[4,112,256]{2,1,0:T(8,128)(2,1)S(1)}, u32[]{:S(2)}, u32[]{:S(2)}) collective-permute-start(bf16[4,112,256]{2,1,0:T(8,128)(2,1)S(1)} %fusion.2), channel_id=1, source_target_pairs={{0,6},{1,3},{2,4},{3,1},{4,2},{5,7},{6,0},{7,5},{8,14},{9,11},{10,... | collective-permute-start | bytes 688136 | tf_op jit(solution)/shard_map/ppermute | solution.py:376
  164.4 4.7 %collective-permute-done.20 = bf16[4,112,256]{2,1,0:T(8,128)(2,1)S(1)} collective-permute-done((bf16[4,112,256]{2,1,0:T(8,128)(2,1)S(1)}, bf16[4,112,256]{2,1,0:T(8,128)(2,1)S(1)}, u32[]{:S(2)}, u32[]{:S(2)}) %collective-permute-start.20) | collective-permute-done | bytes 229408 | tf_op jit(solution)/shard_map/ppermute | solution.py:376
  169.1 0.6 slice_bitcast_fusion
  169.7 3.1 %collective-permute-start.23 = (bf16[112,256]{1,0:T(8,128)(2,1)S(1)}, bf16[112,256]{1,0:T(8,128)(2,1)S(1)}, u32[]{:S(2)}, u32[]{:S(2)}) collective-permute-start(bf16[112,256]{1,0:T(8,128)(2,1)S(1)} %get-tuple-element.18), channel_id=1, source_target_pairs={{0,16},{8,24},{16,0},{24,8},{1,17},{9,25},{17,1},{25,9},{2,18},{10... | collective-permute-start | bytes 172040 | tf_op jit(solution)/shard_map/ppermute | solution.py:384
  172.9 2.3 %collective-permute-start.22 = (bf16[112,256]{1,0:T(8,128)(2,1)S(1)}, bf16[112,256]{1,0:T(8,128)(2,1)S(1)}, u32[]{:S(2)}, u32[]{:S(2)}) collective-permute-start(bf16[112,256]{1,0:T(8,128)(2,1)S(1)} %get-tuple-element.19), channel_id=1, source_target_pairs={{0,24},{1,9},{8,16},{9,1},{16,8},{17,25},{24,0},{25,17},{2,26},{3,... | collective-permute-start | bytes 172040 | tf_op jit(solution)/shard_map/ppermute | solution.py:376
  175.1 1.1 collective-permute-start.21
  176.2 2.0 %collective-permute-done.23.d_ref = bf16[112,256]{1,0:T(8,128)(2,1)S(1)} collective-permute-done((bf16[112,256]{1,0:T(8,128)(2,1)S(1)}, bf16[112,256]{1,0:T(8,128)(2,1)S(1)}, u32[]{:S(2)}, u32[]{:S(2)}) %collective-permute-start.23) | collective-permute-done | bytes 57376 | tf_op jit(solution)/shard_map/ppermute | solution.py:384
  178.2 1.4 collective-permute-done.22.c_ref
  179.6 0.6 collective-permute-done.21.b_ref
  180.2 0.6 copy-done.3
  180.8 1.6 shard_map.104
  (45 shorter events, 1.4 us)
Async XLA Ops:
  2.9 1.5 collective-permute-start
  4.4 9.9 %collective-permute-start.3 = (bf16[2,112,128]{2,1,0:T(8,128)(2,1)S(1)}, bf16[2,112,128]{2,1,0:T(8,128)(2,1)S(1)}, u32[]{:S(2)}, u32[]{:S(2)}) collective-permute-start(bf16[2,112,128]{2,1,0:T(8,128)(2,1)S(1)} %maximum_select_fusion.3), channel_id=1, source_target_pairs={{0,16},{8,24},{16,0},{24,8},{1,17},{9,25},{17,1},{25,9},{2,18},{10... | collective-permute-start | bytes 172040 | tf_op jit(solution)/shard_map/ppermute | solution.py:384
  11.7 6.7 %collective-permute-start.2 = (bf16[2,112,128]{2,1,0:T(8,128)(2,1)S(1)}, bf16[2,112,128]{2,1,0:T(8,128)(2,1)S(1)}, u32[]{:S(2)}, u32[]{:S(2)}) collective-permute-start(bf16[2,112,128]{2,1,0:T(8,128)(2,1)S(1)} %maximum_select_fusion.3), channel_id=1, source_target_pairs={{0,24},{1,9},{8,16},{9,1},{16,8},{17,25},{24,0},{25,17},{2,26},{3,... | collective-permute-start | bytes 172040 | tf_op jit(solution)/shard_map/ppermute | solution.py:376
  11.7 6.8 %collective-permute-start.1 = (bf16[2,112,128]{2,1,0:T(8,128)(2,1)S(1)}, bf16[2,112,128]{2,1,0:T(8,128)(2,1)S(1)}, u32[]{:S(2)}, u32[]{:S(2)}) collective-permute-start(bf16[2,112,128]{2,1,0:T(8,128)(2,1)S(1)} %maximum_select_fusion.3), channel_id=1, source_target_pairs={{0,8},{1,25},{8,0},{9,17},{16,24},{17,9},{24,16},{25,1},{2,10},{3,... | collective-permute-start | bytes 172040 | tf_op jit(solution)/shard_map/ppermute | solution.py:376
  19.2 6.1 %collective-permute-start.4 = (bf16[4,2,112,128]{3,2,1,0:T(8,128)(2,1)S(1)}, bf16[4,2,112,128]{3,2,1,0:T(8,128)(2,1)S(1)}, u32[]{:S(2)}, u32[]{:S(2)}) collective-permute-start(bf16[4,2,112,128]{3,2,1,0:T(8,128)(2,1)S(1)} %broadcast_select_fusion), channel_id=1, source_target_pairs={{0,32},{1,57},{32,0},{33,9},{8,40},{9,33},{40,8},{41,17},{16,48},{... | collective-permute-start | bytes 688136 | tf_op jit(solution)/shard_map/ppermute | solution.py:437
  25.4 8.6 %collective-permute-start.6 = (bf16[2,4,2,112,128]{4,3,2,1,0:T(8,128)(2,1)S(1)}, bf16[2,4,2,112,128]{4,3,2,1,0:T(8,128)(2,1)S(1)}, u32[]{:S(2)}, u32[]{:S(2)}) collective-permute-start(bf16[2,4,2,112,128]{4,3,2,1,0:T(8,128)(2,1)S(1)} %maximum_select_fusion.1), channel_id=1, source_target_pairs={{0,192},{1,7},{2,194},{3,5},{4,196},{5,3},{6,198},{7,1},{64,128},{... | collective-permute-start | bytes 1376264 | tf_op jit(solution)/shard_map/ppermute | solution.py:396
  27.0 8.8 %collective-permute-start.5 = (bf16[2,4,2,112,128]{4,3,2,1,0:T(8,128)(2,1)S(1)}, bf16[2,4,2,112,128]{4,3,2,1,0:T(8,128)(2,1)S(1)}, u32[]{:S(2)}, u32[]{:S(2)}) collective-permute-start(bf16[2,4,2,112,128]{4,3,2,1,0:T(8,128)(2,1)S(1)} %maximum_select_fusion.1), channel_id=1, source_target_pairs={{0,64},{1,3},{2,66},{3,1},{4,68},{5,7},{6,70},{7,5},{64,0},{65,67}... | collective-permute-start | bytes 1376264 | tf_op jit(solution)/shard_map/ppermute | solution.py:396
  34.0 6.1 %collective-permute-start.8 = (bf16[1,4,2,112,128]{4,3,2,1,0:T(8,128)(2,1)S(1)}, bf16[1,4,2,112,128]{4,3,2,1,0:T(8,128)(2,1)S(1)}, u32[]{:S(2)}, u32[]{:S(2)}) collective-permute-start(bf16[1,4,2,112,128]{4,3,2,1,0:T(8,128)(2,1)S(1)} %slice.87), channel_id=1, source_target_pairs={{0,64},{1,3},{2,66},{3,1},{4,68},{5,7},{6,70},{7,5},{64,0},{65,67}... | collective-permute-start | bytes 688136 | tf_op jit(solution)/shard_map/ppermute | solution.py:396
  35.9 6.2 %collective-permute-start.7 = (bf16[1,4,2,112,128]{4,3,2,1,0:T(8,128)(2,1)S(1)}, bf16[1,4,2,112,128]{4,3,2,1,0:T(8,128)(2,1)S(1)}, u32[]{:S(2)}, u32[]{:S(2)}) collective-permute-start(bf16[1,4,2,112,128]{4,3,2,1,0:T(8,128)(2,1)S(1)} %slice.86), channel_id=1, source_target_pairs={{0,192},{1,7},{2,194},{3,5},{4,196},{5,3},{6,198},{7,1},{64,128},{... | collective-permute-start | bytes 688136 | tf_op jit(solution)/shard_map/ppermute | solution.py:396
  42.4 27.7 %copy-start = (bf16[4,2,4,2,112,128]{5,4,3,2,1,0:T(8,128)(2,1)}, bf16[4,2,4,2,112,128]{5,4,3,2,1,0:T(8,128)(2,1)S(1)}, u32[]{:S(2)}) copy-start(bf16[4,2,4,2,112,128]{5,4,3,2,1,0:T(8,128)(2,1)S(1)} %pad_maximum_fusion.refs_0_) | copy-start | bytes 5505028
  42.4 24.6 %collective-permute-start.10 = (bf16[4,2,4,2,112,128]{5,4,3,2,1,0:T(8,128)(2,1)S(1)}, bf16[4,2,4,2,112,128]{5,4,3,2,1,0:T(8,128)(2,1)}, u32[]{:S(2)}, u32[]{:S(2)}) collective-permute-start(bf16[4,2,4,2,112,128]{5,4,3,2,1,0:T(8,128)(2,1)S(1)} %pad_maximum_fusion.refs_0_), channel_id=1, source_target_pairs={{0,6},{1,193},{2,4},{3,195},{4,2},{5,197},{6,0},{7,199},{64,70},{6... | collective-permute-start | bytes 5505032 | tf_op jit(solution)/shard_map/ppermute | solution.py:396
  45.5 23.3 %collective-permute-start.9 = (bf16[4,2,4,2,112,128]{5,4,3,2,1,0:T(8,128)(2,1)S(1)}, bf16[4,2,4,2,112,128]{5,4,3,2,1,0:T(8,128)(2,1)}, u32[]{:S(2)}, u32[]{:S(2)}) collective-permute-start(bf16[4,2,4,2,112,128]{5,4,3,2,1,0:T(8,128)(2,1)S(1)} %pad_maximum_fusion.refs_0_), channel_id=1, source_target_pairs={{0,2},{1,65},{2,0},{3,67},{4,6},{5,69},{6,4},{7,71},{64,66},{65,1}... | collective-permute-start | bytes 5505032 | tf_op jit(solution)/shard_map/ppermute | solution.py:396
  45.6 39.9 %collective-permute-start.13 = (bf16[4,2,4,2,112,128]{5,4,3,2,1,0:T(8,128)(2,1)S(1)}, bf16[4,2,4,2,112,128]{5,4,3,2,1,0:T(8,128)(2,1)}, u32[]{:S(2)}, u32[]{:S(2)}) collective-permute-start(bf16[4,2,4,2,112,128]{5,4,3,2,1,0:T(8,128)(2,1)S(1)} %pad_maximum_fusion.refs_0_), channel_id=1, source_target_pairs={{0,1},{1,0},{2,3},{3,2},{4,5},{5,4},{6,7},{7,6},{8,9},{9,8},{10,11... | collective-permute-start | bytes 5505032 | tf_op jit(solution)/shard_map/ppermute | solution.py:380
  68.3 13.5 %collective-permute-start.12 = (bf16[2,2,4,2,112,128]{5,4,3,2,1,0:T(8,128)(2,1)S(1)}, bf16[2,2,4,2,112,128]{5,4,3,2,1,0:T(8,128)(2,1)S(1)}, u32[]{:S(2)}, u32[]{:S(2)}) collective-permute-start(bf16[2,2,4,2,112,128]{5,4,3,2,1,0:T(8,128)(2,1)S(1)} %slice.89), channel_id=1, source_target_pairs={{0,2},{1,65},{2,0},{3,67},{4,6},{5,69},{6,4},{7,71},{64,66},{65,1}... | collective-permute-start | bytes 2752520 | tf_op jit(solution)/shard_map/ppermute | solution.py:396
  70.1 14.8 %collective-permute-start.11 = (bf16[2,2,4,2,112,128]{5,4,3,2,1,0:T(8,128)(2,1)S(1)}, bf16[2,2,4,2,112,128]{5,4,3,2,1,0:T(8,128)(2,1)}, u32[]{:S(2)}, u32[]{:S(2)}) collective-permute-start(bf16[2,2,4,2,112,128]{5,4,3,2,1,0:T(8,128)(2,1)S(1)} %slice.88), channel_id=1, source_target_pairs={{0,6},{1,193},{2,4},{3,195},{4,2},{5,197},{6,0},{7,199},{64,70},{6... | collective-permute-start | bytes 2752520 | tf_op jit(solution)/shard_map/ppermute | solution.py:396
  72.8 12.8 %collective-permute-start.15 = (bf16[4,2,4,2,112,128]{5,4,3,2,1,0:T(8,128)(2,1)}, bf16[4,2,4,2,112,128]{5,4,3,2,1,0:T(8,128)(2,1)}, u32[]{:S(2)}, u32[]{:S(2)}) collective-permute-start(bf16[4,2,4,2,112,128]{5,4,3,2,1,0:T(8,128)(2,1)} %collective-permute-done.10.refs_2_), channel_id=1, source_target_pairs={{0,1},{1,0},{2,3},{3,2},{4,5},{5,4},{6,7},{7,6},{8,9},{9,8},{10,11... | collective-permute-start | bytes 5505032 | tf_op jit(solution)/shard_map/ppermute | solution.py:380
  72.8 15.0 %collective-permute-start.14 = (bf16[4,2,4,2,112,128]{5,4,3,2,1,0:T(8,128)(2,1)}, bf16[4,2,4,2,112,128]{5,4,3,2,1,0:T(8,128)(2,1)}, u32[]{:S(2)}, u32[]{:S(2)}) collective-permute-start(bf16[4,2,4,2,112,128]{5,4,3,2,1,0:T(8,128)(2,1)} %collective-permute-done.9.refs_1_), channel_id=1, source_target_pairs={{0,1},{1,0},{2,3},{3,2},{4,5},{5,4},{6,7},{7,6},{8,9},{9,8},{10,11... | collective-permute-start | bytes 5505032 | tf_op jit(solution)/shard_map/ppermute | solution.py:380
  81.8 6.0 %copy-start.4 = (bf16[2,2,4,2,112,128]{5,4,3,2,1,0:T(8,128)(2,1)}, bf16[2,2,4,2,112,128]{5,4,3,2,1,0:T(8,128)(2,1)S(1)}, u32[]{:S(2)}) copy-start(bf16[2,2,4,2,112,128]{5,4,3,2,1,0:T(8,128)(2,1)S(1)} %collective-permute-done.12.refs_4_) | copy-start | bytes 2752516
  81.8 3.7 %collective-permute-start.17 = (bf16[2,2,4,2,112,128]{5,4,3,2,1,0:T(8,128)(2,1)S(1)}, bf16[2,2,4,2,112,128]{5,4,3,2,1,0:T(8,128)(2,1)}, u32[]{:S(2)}, u32[]{:S(2)}) collective-permute-start(bf16[2,2,4,2,112,128]{5,4,3,2,1,0:T(8,128)(2,1)S(1)} %collective-permute-done.12.refs_4_), channel_id=1, source_target_pairs={{0,1},{1,0},{2,3},{3,2},{4,5},{5,4},{6,7},{7,6},{8,9},{9,8},{10,11... | collective-permute-start | bytes 2752520 | tf_op jit(solution)/shard_map/ppermute | solution.py:380
  84.9 2.8 %collective-permute-start.16 = (bf16[2,2,4,2,112,128]{5,4,3,2,1,0:T(8,128)(2,1)}, bf16[2,2,4,2,112,128]{5,4,3,2,1,0:T(8,128)(2,1)}, u32[]{:S(2)}, u32[]{:S(2)}) collective-permute-start(bf16[2,2,4,2,112,128]{5,4,3,2,1,0:T(8,128)(2,1)} %collective-permute-done.11.refs_3_), channel_id=1, source_target_pairs={{0,1},{1,0},{2,3},{3,2},{4,5},{5,4},{6,7},{7,6},{8,9},{9,8},{10,11... | collective-permute-start | bytes 2752520 | tf_op jit(solution)/shard_map/ppermute | solution.py:380
  148.9 2.8 %collective-permute-start.18 = (bf16[4,4,112,256]{3,2,1,0:T(8,128)(2,1)}, bf16[4,4,112,256]{3,2,1,0:T(8,128)(2,1)S(1)}, u32[]{:S(2)}, u32[]{:S(2)}) collective-permute-start(bf16[4,4,112,256]{3,2,1,0:T(8,128)(2,1)} %get-tuple-element.11), channel_id=1, source_target_pairs={{0,1},{1,0},{2,3},{3,2},{4,5},{5,4},{6,7},{7,6},{8,9},{9,8},{10,11... | collective-permute-start | bytes 2752520 | tf_op jit(solution)/shard_map/ppermute | solution.py:380
  153.1 8.6 %collective-permute-start.19 = (bf16[2,4,112,256]{3,2,1,0:T(8,128)(2,1)S(1)}, bf16[2,4,112,256]{3,2,1,0:T(8,128)(2,1)S(1)}, u32[]{:S(2)}, u32[]{:S(2)}) collective-permute-start(bf16[2,4,112,256]{3,2,1,0:T(8,128)(2,1)S(1)} %get-tuple-element.17), channel_id=1, source_target_pairs={{0,2},{1,7},{2,0},{3,5},{4,6},{5,3},{6,4},{7,1},{8,10},{9,15},{10,... | collective-permute-start | bytes 1376264 | tf_op jit(solution)/shard_map/ppermute | solution.py:376
  161.7 7.3 %collective-permute-start.20 = (bf16[4,112,256]{2,1,0:T(8,128)(2,1)S(1)}, bf16[4,112,256]{2,1,0:T(8,128)(2,1)S(1)}, u32[]{:S(2)}, u32[]{:S(2)}) collective-permute-start(bf16[4,112,256]{2,1,0:T(8,128)(2,1)S(1)} %fusion.2), channel_id=1, source_target_pairs={{0,6},{1,3},{2,4},{3,1},{4,2},{5,7},{6,0},{7,5},{8,14},{9,11},{10,... | collective-permute-start | bytes 688136 | tf_op jit(solution)/shard_map/ppermute | solution.py:376
  169.7 8.5 %collective-permute-start.23 = (bf16[112,256]{1,0:T(8,128)(2,1)S(1)}, bf16[112,256]{1,0:T(8,128)(2,1)S(1)}, u32[]{:S(2)}, u32[]{:S(2)}) collective-permute-start(bf16[112,256]{1,0:T(8,128)(2,1)S(1)} %get-tuple-element.18), channel_id=1, source_target_pairs={{0,16},{8,24},{16,0},{24,8},{1,17},{9,25},{17,1},{25,9},{2,18},{10... | collective-permute-start | bytes 172040 | tf_op jit(solution)/shard_map/ppermute | solution.py:384
  172.9 6.7 %collective-permute-start.22 = (bf16[112,256]{1,0:T(8,128)(2,1)S(1)}, bf16[112,256]{1,0:T(8,128)(2,1)S(1)}, u32[]{:S(2)}, u32[]{:S(2)}) collective-permute-start(bf16[112,256]{1,0:T(8,128)(2,1)S(1)} %get-tuple-element.19), channel_id=1, source_target_pairs={{0,24},{1,9},{8,16},{9,1},{16,8},{17,25},{24,0},{25,17},{2,26},{3,... | collective-permute-start | bytes 172040 | tf_op jit(solution)/shard_map/ppermute | solution.py:376
  175.1 5.1 %collective-permute-start.21 = (bf16[112,256]{1,0:T(8,128)(2,1)S(1)}, bf16[112,256]{1,0:T(8,128)(2,1)S(1)}, u32[]{:S(2)}, u32[]{:S(2)}) collective-permute-start(bf16[112,256]{1,0:T(8,128)(2,1)S(1)} %get-tuple-element.20), channel_id=1, source_target_pairs={{0,8},{1,25},{8,0},{9,17},{16,24},{17,9},{24,16},{25,1},{2,10},{3,... | collective-permute-start | bytes 172040 | tf_op jit(solution)/shard_map/ppermute | solution.py:376
  178.2 2.0 %copy-start.1 = (bf16[112,256]{1,0:T(8,128)(2,1)}, bf16[112,256]{1,0:T(8,128)(2,1)S(1)}, u32[]{:S(2)}) copy-start(bf16[112,256]{1,0:T(8,128)(2,1)S(1)} %collective-permute-done.23.d_ref) | copy-start | bytes 172036
  179.6 0.6 copy-start.2
  180.2 0.6 copy-start.3

commit v6 on v4

--- a/solution.py
+++ b/solution.py
@@ -61,7 +61,8 @@
     spread = jnp.where(spread, 1.0, 0.0).astype(BF16)
     block = iota((C, C), 0) // T == iota((C, C), 1) // T
     tri = jnp.where(iota((T, T), 0) >= iota((T, T), 1), 1.0, 0.0).astype(BF16)
-    return row >= col, row == col, spread, block, tri
+    tri_back = jnp.where(iota((T, T), 0) <= iota((T, T), 1), 1.0, 0.0).astype(BF16)
+    return row >= col, row == col, spread, block, tri, tri_back
 
 
 def tile4(a):
@@ -114,12 +115,17 @@
     return jnp.where((c == 0) == first, i ^ 1, 3 - i)
 
 
-def sequence_kernel(pos_ref, *refs):
+def sequence_kernel(*refs):
     left, right = refs[:8], refs[8:16]
-    entry_ref, cot_ref, sent_ref = refs[16:19]
+    entry_ref, cot_ref, out_ref = refs[16:19]
     w_scr, rows_scr, xs, ns, mixed_scr, decay_scr, write_scr, small_scr, proj_scr = refs[19:28]
-    first_scr, sem_a, sem_b, sem_c = refs[28:]
-    x, y, c, zh, section = (pos_ref[i] for i in range(5))
+    first_scr, sent_ref, sem_a, sem_b, sem_c, sem_out = refs[28:]
+
+    def send(layer, rows):
+        pltpu.make_async_copy(sent_ref.at[layer, rows], out_ref.at[layer, rows], sem_out).start()
+
+    x, y, c = (lax.axis_index(a) for a in ("x", "y", "c"))
+    section = x * 2 + lax.axis_index("zl")
     mine = jnp.minimum(section, SEQS - 1)
     loads = []
     for i, ref in enumerate((entry_ref, cot_ref)):
@@ -161,7 +167,7 @@
                     src.at[0], w_scr.at[0:2, :, 0, 0, :, :C], sem.at[at]
                 ).wait()
 
-    causal, diag, spread, block, tri = masks()
+    causal, diag, spread, block, tri, tri_back = masks()
 
     def keys_of(layer, m):
         parts = [w_scr[layer, m // 2, (m % 2) * 2 + i // 2, i % 2, :ROWS] for i in range(4)]
@@ -183,6 +189,7 @@
         ns[layer] = normed
         for m in range(BLOCKS):
             sent_ref[layer, T * m : T * (m + 1)] = normed[:, BLOCK * m : BLOCK * (m + 1)]
+        send(layer, pl.ds(0, TOK))
         logits = nt(normed, rows_low) + bias
         key_query = sum(
             nn(normed[:, BLOCK * m : BLOCK * (m + 1)], keys_of(layer, m)) for m in range(BLOCKS)
@@ -248,16 +255,10 @@
         d_write_s = jnp.sum(scored, axis=0, keepdims=True)
         weighted = near * write_s
         d_scores = sum(weighted[:, C * g : C * (g + 1)] for g in range(GROUPS)).astype(BF16)
-        d_total = scored * write_s - jnp.where(diag, d_write_s * write_s, 0.0)
-        gathered = []
-        for part in (d_total, jnp.where(diag, d_write_s, 0.0)):
-            hi = part.astype(BF16)
-            gathered += [hi, (part - hi.astype(F32)).astype(BF16)]
-        summed = nt(jnp.concatenate(gathered, axis=0), spread[:T])
-        d_total = summed[:T] + summed[T : 2 * T]
-        d_write = summed[2 * T : 3 * T] + summed[3 * T :]
-        d_log = tn(tri, split3(d_total))
-        d_log = d_log[:, :T] + d_log[:, T : 2 * T] + d_log[:, 2 * T : 3 * T]
+        later = jnp.where(causal & ~diag, nn(tri_back, (scored * write_s).astype(BF16)), 0.0)
+        own = jnp.where(diag, d_write_s, 0.0)
+        summed = nt(jnp.concatenate([later.astype(BF16), own.astype(BF16)], axis=0), spread[:T])
+        d_log, d_write = summed[:T], summed[T:]
         d_rate = keep * (d_write * keep - d_log)
         d_logits = d_rate / (1.0 + jnp.exp(-logits))
         d_low = jnp.where(iota((T, T), 1) < H, d_logits, 0.0).astype(BF16)
@@ -283,14 +284,16 @@
         sent_ref[layer, TOK + T :] = jnp.concatenate(
             [d[:, BLOCK * i : BLOCK * (i + 1)] for d in (d_gain, d_scale) for i in range(8)], axis=0
         ).astype(BF16)
+        send(layer, pl.ds(TOK, T + 16))
         return (dy + inv_rms * (d_hat - x_hat * mean)).astype(BF16)
 
     cot = jnp.where(section < SEQS, first_scr[1].astype(F32), 0.0).astype(BF16)
     lax.fori_loop(0, LAYERS, backward, cot, unroll=2)
-
-
-def weight_kernel(pos_ref, got_ref, keep_ref, send_ref, got, scr, sem_in, sem):
-    y, c, zh = pos_ref[1], pos_ref[2], pos_ref[3]
+    pltpu.make_async_copy(sent_ref, out_ref, sem_out).wait()
+
+
+def weight_kernel(got_ref, keep_ref, send_ref, got, scr, sem_in, sem):
+    y, c, zh = (lax.axis_index(a) for a in ("y", "c", "zh"))
     loads = []
     for m in list(range(BLOCKS)) + [BLOCKS]:
         at = pl.ds(T * m, T if m < BLOCKS else T + 16)
@@ -349,7 +352,6 @@
 
 ANY = pl.BlockSpec(memory_space=pl.ANY)
 VMEM = pl.BlockSpec(memory_space=pltpu.VMEM)
-SMEM = pl.BlockSpec(memory_space=pltpu.SMEM)
 PARAMS = pltpu.CompilerParams(vmem_limit_bytes=56 * 1024 * 1024)
 
 
@@ -403,15 +405,16 @@
 
 def per_device(entries, cotangents, scales, key_weight, rate_weight, rate_bias):
     x, zl, zh, y, c = (lax.axis_index(a) for a in ("x", "zl", "zh", "y", "c"))
-    section = x * 2 + zl
-    pos = jnp.stack([x, y, c, zh, section]).astype(jnp.int32)
-
-    wide = jnp.pad(rate_weight[0].T, ((0, 0), (0, C - ROWS)))
-    small = jnp.pad(scales[0], ((0, 0), (0, C - ROWS)))
-    line = jnp.pad(rate_bias, ((0, 0), (0, C - H)))
-    right = jnp.concatenate([wide[16:], small, line, jnp.zeros((5, C), BF16)], axis=0)
-    packed = jnp.concatenate(
-        [key_weight[0], jnp.concatenate([wide[:16], right], axis=1)], axis=0
+    rates = rate_weight[0].T
+    packed = sum(
+        jnp.pad(a, ((row, PIECE - row - a.shape[0]), (lane, 256 - lane - a.shape[1])))
+        for a, row, lane in (
+            (key_weight[0], 0, 0),
+            (rates[:16], ROWS, 0),
+            (rates[16:], ROWS, C),
+            (scales[0], ROWS + 8, C),
+            (rate_bias, ROWS + 10, C),
+        )
     )
 
     along = jnp.stack(gather_ring(packed, "zh", direct=True))
@@ -437,7 +440,7 @@
     sent = call(
         sequence_kernel,
         [shape(LAYERS, SENT, BLOCK)],
-        [SMEM] + [ANY] * 18,
+        [ANY] * 18,
         [
             pltpu.VMEM((LAYERS, 4, 4, 2, PIECE, 256), BF16),
             pltpu.VMEM((LAYERS, T, D), BF16),
@@ -449,12 +452,15 @@
             pltpu.VMEM((LAYERS, T, 256), F32),
             pltpu.VMEM((LAYERS, T, 256), F32),
             pltpu.VMEM((2, T, D), BF16),
+            pltpu.VMEM((LAYERS, SENT, BLOCK), BF16),
             pltpu.SemaphoreType.DMA((4,)),
             pltpu.SemaphoreType.DMA((4,)),
             pltpu.SemaphoreType.DMA((2,)),
+            pltpu.SemaphoreType.DMA,
         ],
+        [ANY],
         cost=(8_000_000_000, 30_000_000),
-    )(pos, *left, *right, entries, cotangents)[0]
+    )(*left, *right, entries, cotangents)[0]
 
     groups = [
         [
@@ -472,7 +478,7 @@
     keep, send = call(
         weight_kernel,
         [half, half],
-        [SMEM, ANY],
+        [ANY],
         [
             pltpu.VMEM((LAYERS, SENT, BLOCK), BF16),
             pltpu.VMEM((2, 4, 4, PIECE, 256), BF16),
@@ -481,7 +487,7 @@
         ],
         [ANY] * 2,
         cost=(600_000_000, 4_000_000),
-    )(pos, got)
+    )(got)
     got = other_core(send)
     got = swap(add(keep[2:], got[2:]), "y", True), keep[:2], got[:2]
     keep = add(got[1], got[2])

time: 181 us -> 178 us (0.983)
  Pallas kernels: 32.3 us -> 29 us
    pallas_call x2, Pallas kernels: 30.8 us -> 27.4 us  [the longest x1 23.1 us: per_device(): call(sequence_kernel, [shape(LAYERS, SENT, BLOCK)], [ANY] * 18, [pltpu.VM...]
  transfers between devices with their start and end apart: 30 -> 30, of which waited for: 18 -> 17; matrix products, arithmetic and copies ran while one was open for 1% -> 1% of each run, Pallas kernels for 0% -> 0%
where the time goes in v6:
time: 178 us; the launch traced here: 177 us
  waiting for transfers between devices  64.8 us (36%)
  starting transfers between devices  42.5 us (24%)
  blocking collectives  30.5 us (17%)
  Pallas kernels  29 us (16%)
  local copies, waits for them, and re-layouts  5.69 us (3%)
  other arithmetic  3.92 us (2%)
    ppermute x18, waiting for transfers between devices, swap(): return lax.ppermute(array, (axis, 'c'), ring_pairs(first))  51.5 us
    ppermute x18, starting transfers between devices, swap(): return lax.ppermute(array, (axis, 'c'), ring_pairs(first))  37.9 us
    all_to_all x1, blocking collectives, per_device(): lax.all_to_all(sent, ('x', 'zl', 'zh', 'y', 'c'), 0, 0, axis_index_groups...  30.5 us
    pallas_call x1, Pallas kernels, per_device(): call(sequence_kernel, [shape(LAYERS, SENT, BLOCK)], [ANY] * 18, [pltpu.VM...  23.1 us
    ppermute x2, waiting for transfers between devices, opposite(): return lax.ppermute(array, axis, [(i, i ^ 2) for i in range(4)])  5.33 us
    ppermute x1, waiting for transfers between devices, per_device(): other = lax.ppermute(along, ('zl', 'zh', 'c'), pairs)  4.84 us
    pallas_call x1, Pallas kernels, per_device(): call(weight_kernel, [half, half], [ANY], [pltpu.VMEM((LAYERS, SENT, BLOCK...  4.29 us
  transfers between devices with their start and end apart: 30, of which 17 were waited for; matrix products, arithmetic and copies ran while one was open for 1% of the time, Pallas kernels for 0%

profile of v6, /device:TPU:2, one launch (start us, length us, event | category | flops | bytes accessed | tf_op | source)
XLA Modules:
  0.0 177.3 jit_solution(12385590546616137544)
XLA Ops:
  0.6 0.7 slice.67
  1.3 0.7 slice.66
  2.0 0.8 pad_add_fusion
  2.8 6.3 %collective-permute-start.1 = (bf16[112,256]{1,0:T(8,128)(2,1)S(1)}, bf16[112,256]{1,0:T(8,128)(2,1)S(1)}, u32[]{:S(2)}, u32[]{:S(2)}) collective-permute-start(bf16[112,256]{1,0:T(8,128)(2,1)S(1)} %pad_add_fusion), channel_id=1, source_target_pairs={{0,24},{1,9},{8,16},{9,1},{16,8},{17,25},{24,0},{25,17},{2,26},{3,... | collective-permute-start | bytes 172040 | tf_op jit(solution)/shard_map/ppermute | solution.py:385
  9.2 1.5 collective-permute-start
  10.6 1.0 collective-permute-start.2
  11.6 0.8 fusion.4
  12.7 1.7 collective-permute-done.1
  14.4 1.1 collective-permute-done
  15.5 3.6 %collective-permute-done.2 = bf16[112,256]{1,0:T(8,128)(2,1)S(1)} collective-permute-done((bf16[112,256]{1,0:T(8,128)(2,1)S(1)}, bf16[112,256]{1,0:T(8,128)(2,1)S(1)}, u32[]{:S(2)}, u32[]{:S(2)}) %collective-permute-start.2) | collective-permute-done | bytes 57376 | tf_op jit(solution)/shard_map/ppermute | solution.py:393
  19.8 1.2 collective-permute-start.3
  21.1 4.8 %collective-permute-done.3 = bf16[4,112,256]{2,1,0:T(8,128)(2,1)S(1)} collective-permute-done((bf16[4,112,256]{2,1,0:T(8,128)(2,1)S(1)}, bf16[4,112,256]{2,1,0:T(8,128)(2,1)S(1)}, u32[]{:S(2)}, u32[]{:S(2)}) %collective-permute-start.3) | collective-permute-done | bytes 229408 | tf_op jit(solution)/shard_map/ppermute | solution.py:430
  26.1 0.6 collective-permute-start.4
  26.8 1.6 collective-permute-start.14
  28.3 2.2 %collective-permute-start.5 = (bf16[2,4,112,128]{3,2,1,0:T(8,128)(2,1)S(1)}, bf16[2,4,112,128]{3,2,1,0:T(8,128)(2,1)S(1)}, u32[]{:S(2)}, u32[]{:S(2)}) collective-permute-start(bf16[2,4,112,128]{3,2,1,0:T(8,128)(2,1)S(1)} %get-tuple-element.21), channel_id=1, source_target_pairs={{0,192},{1,65},{64,128},{65,1},{128,64},{129,193},{192,0},{193,129... | collective-permute-start | bytes 688136 | tf_op jit(solution)/shard_map/ppermute | solution.py:385
  30.5 2.4 %collective-permute-done.4 = bf16[2,4,112,128]{3,2,1,0:T(8,128)(2,1)S(1)} collective-permute-done((bf16[2,4,112,128]{3,2,1,0:T(8,128)(2,1)S(1)}, bf16[2,4,112,128]{3,2,1,0:T(8,128)(2,1)S(1)}, u32[]{:S(2)}, u32[]{:S(2)}) %collective-permute-start.4) | collective-permute-done | bytes 229408 | tf_op jit(solution)/shard_map/ppermute | solution.py:385
  32.8 2.6 %collective-permute-start.6 = (bf16[2,4,112,128]{3,2,1,0:T(8,128)(2,1)S(1)}, bf16[2,4,112,128]{3,2,1,0:T(8,128)(2,1)S(1)}, u32[]{:S(2)}, u32[]{:S(2)}) collective-permute-start(bf16[2,4,112,128]{3,2,1,0:T(8,128)(2,1)S(1)} %collective-permute-done.4), channel_id=1, source_target_pairs={{0,192},{1,65},{64,128},{65,1},{128,64},{129,193},{192,0},{193,129... | collective-permute-start | bytes 688136 | tf_op jit(solution)/shard_map/ppermute | solution.py:385
  35.5 2.2 %collective-permute-start.15 = (bf16[2,4,112,128]{3,2,1,0:T(8,128)(2,1)S(1)}, bf16[2,4,112,128]{3,2,1,0:T(8,128)(2,1)S(1)}, u32[]{:S(2)}, u32[]{:S(2)}) collective-permute-start(bf16[2,4,112,128]{3,2,1,0:T(8,128)(2,1)S(1)} %get-tuple-element.20), channel_id=1, source_target_pairs={{0,6},{1,3},{2,4},{3,1},{4,2},{5,7},{6,0},{7,5},{8,14},{9,11},{10,... | collective-permute-start | bytes 688136 | tf_op jit(solution)/shard_map/ppermute | solution.py:385
  37.7 1.0 collective-permute-start.16
  38.7 0.8 collective-permute-done.6
  39.7 4.4 %collective-permute-start.8 = (bf16[4,2,4,112,128]{4,3,2,1,0:T(8,128)(2,1)S(1)}, bf16[4,2,4,112,128]{4,3,2,1,0:T(8,128)(2,1)S(1)}, u32[]{:S(2)}, u32[]{:S(2)}) collective-permute-start(bf16[4,2,4,112,128]{4,3,2,1,0:T(8,128)(2,1)S(1)} %pad_maximum_fusion.refs_0_), channel_id=1, source_target_pairs={{0,6},{1,3},{2,4},{3,1},{4,2},{5,7},{6,0},{7,5},{8,14},{9,11},{10,... | collective-permute-start | bytes 2752520 | tf_op jit(solution)/shard_map/ppermute | solution.py:385
  44.2 1.0 collective-permute-done.16
  45.3 2.0 %collective-permute-start.17 = (bf16[4,2,4,112,128]{4,3,2,1,0:T(8,128)(2,1)S(1)}, bf16[4,2,4,112,128]{4,3,2,1,0:T(8,128)(2,1)S(1)}, u32[]{:S(2)}, u32[]{:S(2)}) collective-permute-start(bf16[4,2,4,112,128]{4,3,2,1,0:T(8,128)(2,1)S(1)} %pad_maximum_fusion.1.refs_8_), channel_id=1, source_target_pairs={{0,64},{1,193},{64,0},{65,129},{128,192},{129,65},{192,128},{193,1... | collective-permute-start | bytes 2752520 | tf_op jit(solution)/shard_map/ppermute | solution.py:385
  47.2 0.9 collective-permute-start.18
  48.2 16.5 %collective-permute-done.8.refs_2_ = bf16[4,2,4,112,128]{4,3,2,1,0:T(8,128)(2,1)S(1)} collective-permute-done((bf16[4,2,4,112,128]{4,3,2,1,0:T(8,128)(2,1)S(1)}, bf16[4,2,4,112,128]{4,3,2,1,0:T(8,128)(2,1)S(1)}, u32[]{:S(2)}, u32[]{:S(2)}) %collective-permute-start.8) | collective-permute-done | bytes 917536 | tf_op jit(solution)/shard_map/ppermute | solution.py:385
  64.7 3.8 %collective-permute-start.9 = (bf16[4,2,4,112,128]{4,3,2,1,0:T(8,128)(2,1)S(1)}, bf16[4,2,4,112,128]{4,3,2,1,0:T(8,128)(2,1)S(1)}, u32[]{:S(2)}, u32[]{:S(2)}) collective-permute-start(bf16[4,2,4,112,128]{4,3,2,1,0:T(8,128)(2,1)S(1)} %collective-permute-done.7.refs_1_), channel_id=1, source_target_pairs={{0,6},{1,3},{2,4},{3,1},{4,2},{5,7},{6,0},{7,5},{8,14},{9,11},{10,... | collective-permute-start | bytes 2752520 | tf_op jit(solution)/shard_map/ppermute | solution.py:385
  68.5 1.6 collective-permute-start.19
  70.9 9.0 %collective-permute-done.9.refs_3_ = bf16[4,2,4,112,128]{4,3,2,1,0:T(8,128)(2,1)S(1)} collective-permute-done((bf16[4,2,4,112,128]{4,3,2,1,0:T(8,128)(2,1)S(1)}, bf16[4,2,4,112,128]{4,3,2,1,0:T(8,128)(2,1)S(1)}, u32[]{:S(2)}, u32[]{:S(2)}) %collective-permute-start.9) | collective-permute-done | bytes 917536 | tf_op jit(solution)/shard_map/ppermute | solution.py:385
  79.8 2.0 %collective-permute-done.19.refs_11_ = bf16[4,2,4,112,128]{4,3,2,1,0:T(8,128)(2,1)S(1)} collective-permute-done((bf16[4,2,4,112,128]{4,3,2,1,0:T(8,128)(2,1)S(1)}, bf16[4,2,4,112,128]{4,3,2,1,0:T(8,128)(2,1)S(1)}, u32[]{:S(2)}, u32[]{:S(2)}) %collective-permute-start.19) | collective-permute-done | bytes 917536 | tf_op jit(solution)/shard_map/ppermute | solution.py:385
  83.7 0.9 copy-done.17
  84.7 23.1 %shard_map.93 = bf16[8,304,384]{2,1,0:T(8,128)(2,1)} custom-call(bf16[4,2,4,112,128]{4,3,2,1,0:T(8,128)(2,1)} %copy-done, bf16[4,2,4,112,128]{4,3,2,1,0:T(8,128)(2,1)} %copy-done.7, bf16[4,2,4,112,128]{4,3,2,1,0:T(8,128)(2,1)} %copy-done.6, bf16[4,2,4,112,128]{4,3,2,1,0:T(8,128)(2,1)} %copy-done.12, bf16[4,2,4,112,128]{4,3,2,1,0:T(8,128)(2,1)} %copy-done.5, ...), custom_call_target="tpu_custom_call" | custom-call | flops 8000000000 | bytes 30000000 | tf_op jit(solution)/shard_map/pallas_call | solution.py:440
  107.8 30.5 %all_to_all.5.got_ref = bf16[8,304,384]{2,1,0:T(8,128)(2,1)} all-to-all(bf16[8,304,384]{2,1,0:T(8,128)(2,1)} %shard_map.93), channel_id=1, replica_groups={{0,32,64,96,128,160,192,224},{1,57,65,121,129,185,193,249},{2,34,66,98,..., dimensions={0} | all-to-all | bytes 3735552 | tf_op jit(solution)/shard_map/all_to_all | solution.py:474
  138.3 4.3 %shard_map.94 = (bf16[4,4,112,256]{3,2,1,0:T(8,128)(2,1)}, bf16[4,4,112,256]{3,2,1,0:T(8,128)(2,1)}) custom-call(bf16[8,304,384]{2,1,0:T(8,128)(2,1)} %all_to_all.5.got_ref), custom_call_target="tpu_custom_call" | custom-call | flops 600000000 | bytes 4000000 | tf_op jit(solution)/shard_map/pallas_call | solution.py:478
  142.7 2.7 %collective-permute-done.24 = bf16[4,4,112,256]{3,2,1,0:T(8,128)(2,1)S(1)} collective-permute-done((bf16[4,4,112,256]{3,2,1,0:T(8,128)(2,1)}, bf16[4,4,112,256]{3,2,1,0:T(8,128)(2,1)S(1)}, u32[]{:S(2)}, u32[]{:S(2)}) %collective-permute-start.24) | collective-permute-done | bytes 917536 | tf_op jit(solution)/shard_map/ppermute | solution.py:389
  145.4 1.4 add_convert_fusion.1
  146.8 0.6 collective-permute-start.25
  147.4 8.0 %collective-permute-done.25 = bf16[2,4,112,256]{3,2,1,0:T(8,128)(2,1)S(1)} collective-permute-done((bf16[2,4,112,256]{3,2,1,0:T(8,128)(2,1)S(1)}, bf16[2,4,112,256]{3,2,1,0:T(8,128)(2,1)S(1)}, u32[]{:S(2)}, u32[]{:S(2)}) %collective-permute-start.25) | collective-permute-done | bytes 458784 | tf_op jit(solution)/shard_map/ppermute | solution.py:385
  155.4 1.6 collective-permute-start.26
  157.0 5.7 %collective-permute-done.26 = bf16[4,112,256]{2,1,0:T(8,128)(2,1)S(1)} collective-permute-done((bf16[4,112,256]{2,1,0:T(8,128)(2,1)S(1)}, bf16[4,112,256]{2,1,0:T(8,128)(2,1)S(1)}, u32[]{:S(2)}, u32[]{:S(2)}) %collective-permute-start.26) | collective-permute-done | bytes 229408 | tf_op jit(solution)/shard_map/ppermute | solution.py:385
  162.8 0.6 slice_bitcast_fusion
  163.5 1.4 collective-permute-start.29
  164.9 4.5 %collective-permute-start.28 = (bf16[112,256]{1,0:T(8,128)(2,1)S(1)}, bf16[112,256]{1,0:T(8,128)(2,1)S(1)}, u32[]{:S(2)}, u32[]{:S(2)}) collective-permute-start(bf16[112,256]{1,0:T(8,128)(2,1)S(1)} %get-tuple-element.23), channel_id=1, source_target_pairs={{0,24},{1,9},{8,16},{9,1},{16,8},{17,25},{24,0},{25,17},{2,26},{3,... | collective-permute-start | bytes 172040 | tf_op jit(solution)/shard_map/ppermute | solution.py:385
  169.4 0.6 collective-permute-start.27
  170.0 1.7 collective-permute-done.29.d_ref
  171.7 1.1 collective-permute-done.28.c_ref
  172.8 2.3 %collective-permute-done.27.b_ref = bf16[112,256]{1,0:T(8,128)(2,1)S(1)} collective-permute-done((bf16[112,256]{1,0:T(8,128)(2,1)S(1)}, bf16[112,256]{1,0:T(8,128)(2,1)S(1)}, u32[]{:S(2)}, u32[]{:S(2)}) %collective-permute-start.27) | collective-permute-done | bytes 57376 | tf_op jit(solution)/shard_map/ppermute | solution.py:385
  175.1 0.6 copy-done.4
  175.7 1.6 shard_map.95
  (71 shorter events, 4.4 us)
Async XLA Ops:
  2.8 11.5 %collective-permute-start.1 = (bf16[112,256]{1,0:T(8,128)(2,1)S(1)}, bf16[112,256]{1,0:T(8,128)(2,1)S(1)}, u32[]{:S(2)}, u32[]{:S(2)}) collective-permute-start(bf16[112,256]{1,0:T(8,128)(2,1)S(1)} %pad_add_fusion), channel_id=1, source_target_pairs={{0,24},{1,9},{8,16},{9,1},{16,8},{17,25},{24,0},{25,17},{2,26},{3,... | collective-permute-start | bytes 172040 | tf_op jit(solution)/shard_map/ppermute | solution.py:385
  9.2 6.3 %collective-permute-start = (bf16[112,256]{1,0:T(8,128)(2,1)S(1)}, bf16[112,256]{1,0:T(8,128)(2,1)S(1)}, u32[]{:S(2)}, u32[]{:S(2)}) collective-permute-start(bf16[112,256]{1,0:T(8,128)(2,1)S(1)} %pad_add_fusion), channel_id=1, source_target_pairs={{0,8},{1,25},{8,0},{9,17},{16,24},{17,9},{24,16},{25,1},{2,10},{3,... | collective-permute-start | bytes 172040 | tf_op jit(solution)/shard_map/ppermute | solution.py:385
  10.6 8.5 %collective-permute-start.2 = (bf16[112,256]{1,0:T(8,128)(2,1)S(1)}, bf16[112,256]{1,0:T(8,128)(2,1)S(1)}, u32[]{:S(2)}, u32[]{:S(2)}) collective-permute-start(bf16[112,256]{1,0:T(8,128)(2,1)S(1)} %pad_add_fusion), channel_id=1, source_target_pairs={{0,16},{8,24},{16,0},{24,8},{1,17},{9,25},{17,1},{25,9},{2,18},{10... | collective-permute-start | bytes 172040 | tf_op jit(solution)/shard_map/ppermute | solution.py:393
  19.8 6.1 %collective-permute-start.3 = (bf16[4,112,256]{2,1,0:T(8,128)(2,1)S(1)}, bf16[4,112,256]{2,1,0:T(8,128)(2,1)S(1)}, u32[]{:S(2)}, u32[]{:S(2)}) collective-permute-start(bf16[4,112,256]{2,1,0:T(8,128)(2,1)S(1)} %broadcast_select_fusion), channel_id=1, source_target_pairs={{0,32},{1,57},{32,0},{33,9},{8,40},{9,33},{40,8},{41,17},{16,48},{... | collective-permute-start | bytes 688136 | tf_op jit(solution)/shard_map/ppermute | solution.py:430
  26.1 6.7 %collective-permute-start.4 = (bf16[2,4,112,128]{3,2,1,0:T(8,128)(2,1)S(1)}, bf16[2,4,112,128]{3,2,1,0:T(8,128)(2,1)S(1)}, u32[]{:S(2)}, u32[]{:S(2)}) collective-permute-start(bf16[2,4,112,128]{3,2,1,0:T(8,128)(2,1)S(1)} %get-tuple-element.21), channel_id=1, source_target_pairs={{0,64},{1,193},{64,0},{65,129},{128,192},{129,65},{192,128},{193,1... | collective-permute-start | bytes 688136 | tf_op jit(solution)/shard_map/ppermute | solution.py:385
  26.8 10.9 %collective-permute-start.14 = (bf16[2,4,112,128]{3,2,1,0:T(8,128)(2,1)S(1)}, bf16[2,4,112,128]{3,2,1,0:T(8,128)(2,1)S(1)}, u32[]{:S(2)}, u32[]{:S(2)}) collective-permute-start(bf16[2,4,112,128]{3,2,1,0:T(8,128)(2,1)S(1)} %get-tuple-element.20), channel_id=1, source_target_pairs={{0,2},{1,7},{2,0},{3,5},{4,6},{5,3},{6,4},{7,1},{8,10},{9,15},{10,... | collective-permute-start | bytes 688136 | tf_op jit(solution)/shard_map/ppermute | solution.py:385
  28.3 10.4 %collective-permute-start.5 = (bf16[2,4,112,128]{3,2,1,0:T(8,128)(2,1)S(1)}, bf16[2,4,112,128]{3,2,1,0:T(8,128)(2,1)S(1)}, u32[]{:S(2)}, u32[]{:S(2)}) collective-permute-start(bf16[2,4,112,128]{3,2,1,0:T(8,128)(2,1)S(1)} %get-tuple-element.21), channel_id=1, source_target_pairs={{0,192},{1,65},{64,128},{65,1},{128,64},{129,193},{192,0},{193,129... | collective-permute-start | bytes 688136 | tf_op jit(solution)/shard_map/ppermute | solution.py:385
  32.8 6.6 %collective-permute-start.6 = (bf16[2,4,112,128]{3,2,1,0:T(8,128)(2,1)S(1)}, bf16[2,4,112,128]{3,2,1,0:T(8,128)(2,1)S(1)}, u32[]{:S(2)}, u32[]{:S(2)}) collective-permute-start(bf16[2,4,112,128]{3,2,1,0:T(8,128)(2,1)S(1)} %collective-permute-done.4), channel_id=1, source_target_pairs={{0,192},{1,65},{64,128},{65,1},{128,64},{129,193},{192,0},{193,129... | collective-permute-start | bytes 688136 | tf_op jit(solution)/shard_map/ppermute | solution.py:385
  35.5 8.7 %collective-permute-start.15 = (bf16[2,4,112,128]{3,2,1,0:T(8,128)(2,1)S(1)}, bf16[2,4,112,128]{3,2,1,0:T(8,128)(2,1)S(1)}, u32[]{:S(2)}, u32[]{:S(2)}) collective-permute-start(bf16[2,4,112,128]{3,2,1,0:T(8,128)(2,1)S(1)} %get-tuple-element.20), channel_id=1, source_target_pairs={{0,6},{1,3},{2,4},{3,1},{4,2},{5,7},{6,0},{7,5},{8,14},{9,11},{10,... | collective-permute-start | bytes 688136 | tf_op jit(solution)/shard_map/ppermute | solution.py:385
  37.7 7.4 %collective-permute-start.16 = (bf16[2,4,112,128]{3,2,1,0:T(8,128)(2,1)S(1)}, bf16[2,4,112,128]{3,2,1,0:T(8,128)(2,1)S(1)}, u32[]{:S(2)}, u32[]{:S(2)}) collective-permute-start(bf16[2,4,112,128]{3,2,1,0:T(8,128)(2,1)S(1)} %collective-permute-done.14), channel_id=1, source_target_pairs={{0,6},{1,3},{2,4},{3,1},{4,2},{5,7},{6,0},{7,5},{8,14},{9,11},{10,... | collective-permute-start | bytes 688136 | tf_op jit(solution)/shard_map/ppermute | solution.py:385
  39.6 45.1 %copy-start = (bf16[4,2,4,112,128]{4,3,2,1,0:T(8,128)(2,1)}, bf16[4,2,4,112,128]{4,3,2,1,0:T(8,128)(2,1)S(1)}, u32[]{:S(2)}) copy-start(bf16[4,2,4,112,128]{4,3,2,1,0:T(8,128)(2,1)S(1)} %pad_maximum_fusion.refs_0_) | copy-start | bytes 2752516
  39.6 7.7 %collective-permute-start.10 = (bf16[4,2,4,112,128]{4,3,2,1,0:T(8,128)(2,1)S(1)}, bf16[4,2,4,112,128]{4,3,2,1,0:T(8,128)(2,1)S(1)}, u32[]{:S(2)}, u32[]{:S(2)}) collective-permute-start(bf16[4,2,4,112,128]{4,3,2,1,0:T(8,128)(2,1)S(1)} %pad_maximum_fusion.refs_0_), channel_id=1, source_target_pairs={{0,1},{1,0},{2,3},{3,2},{4,5},{5,4},{6,7},{7,6},{8,9},{9,8},{10,11... | collective-permute-start | bytes 2752520 | tf_op jit(solution)/shard_map/ppermute | solution.py:389
  39.7 25.0 %collective-permute-start.8 = (bf16[4,2,4,112,128]{4,3,2,1,0:T(8,128)(2,1)S(1)}, bf16[4,2,4,112,128]{4,3,2,1,0:T(8,128)(2,1)S(1)}, u32[]{:S(2)}, u32[]{:S(2)}) collective-permute-start(bf16[4,2,4,112,128]{4,3,2,1,0:T(8,128)(2,1)S(1)} %pad_maximum_fusion.refs_0_), channel_id=1, source_target_pairs={{0,6},{1,3},{2,4},{3,1},{4,2},{5,7},{6,0},{7,5},{8,14},{9,11},{10,... | collective-permute-start | bytes 2752520 | tf_op jit(solution)/shard_map/ppermute | solution.py:385
  44.0 20.6 %collective-permute-start.7 = (bf16[4,2,4,112,128]{4,3,2,1,0:T(8,128)(2,1)S(1)}, bf16[4,2,4,112,128]{4,3,2,1,0:T(8,128)(2,1)S(1)}, u32[]{:S(2)}, u32[]{:S(2)}) collective-permute-start(bf16[4,2,4,112,128]{4,3,2,1,0:T(8,128)(2,1)S(1)} %pad_maximum_fusion.refs_0_), channel_id=1, source_target_pairs={{0,2},{1,7},{2,0},{3,5},{4,6},{5,3},{6,4},{7,1},{8,10},{9,15},{10,... | collective-permute-start | bytes 2752520 | tf_op jit(solution)/shard_map/ppermute | solution.py:385
  45.3 39.4 %copy-start.1 = (bf16[4,2,4,112,128]{4,3,2,1,0:T(8,128)(2,1)}, bf16[4,2,4,112,128]{4,3,2,1,0:T(8,128)(2,1)S(1)}, u32[]{:S(2)}) copy-start(bf16[4,2,4,112,128]{4,3,2,1,0:T(8,128)(2,1)S(1)} %pad_maximum_fusion.1.refs_8_) | copy-start | bytes 2752516
  45.3 23.2 %collective-permute-start.17 = (bf16[4,2,4,112,128]{4,3,2,1,0:T(8,128)(2,1)S(1)}, bf16[4,2,4,112,128]{4,3,2,1,0:T(8,128)(2,1)S(1)}, u32[]{:S(2)}, u32[]{:S(2)}) collective-permute-start(bf16[4,2,4,112,128]{4,3,2,1,0:T(8,128)(2,1)S(1)} %pad_maximum_fusion.1.refs_8_), channel_id=1, source_target_pairs={{0,64},{1,193},{64,0},{65,129},{128,192},{129,65},{192,128},{193,1... | collective-permute-start | bytes 2752520 | tf_op jit(solution)/shard_map/ppermute | solution.py:385
  47.2 22.8 %collective-permute-start.20 = (bf16[4,2,4,112,128]{4,3,2,1,0:T(8,128)(2,1)S(1)}, bf16[4,2,4,112,128]{4,3,2,1,0:T(8,128)(2,1)S(1)}, u32[]{:S(2)}, u32[]{:S(2)}) collective-permute-start(bf16[4,2,4,112,128]{4,3,2,1,0:T(8,128)(2,1)S(1)} %pad_maximum_fusion.1.refs_8_), channel_id=1, source_target_pairs={{0,1},{1,0},{2,3},{3,2},{4,5},{5,4},{6,7},{7,6},{8,9},{9,8},{10,11... | collective-permute-start | bytes 2752520 | tf_op jit(solution)/shard_map/ppermute | solution.py:389
  47.2 37.4 %copy-start.5 = (bf16[4,2,4,112,128]{4,3,2,1,0:T(8,128)(2,1)}, bf16[4,2,4,112,128]{4,3,2,1,0:T(8,128)(2,1)S(1)}, u32[]{:S(2)}) copy-start(bf16[4,2,4,112,128]{4,3,2,1,0:T(8,128)(2,1)S(1)} %collective-permute-done.10.refs_4_) | copy-start | bytes 2752516
  47.2 22.8 %collective-permute-start.18 = (bf16[4,2,4,112,128]{4,3,2,1,0:T(8,128)(2,1)S(1)}, bf16[4,2,4,112,128]{4,3,2,1,0:T(8,128)(2,1)S(1)}, u32[]{:S(2)}, u32[]{:S(2)}) collective-permute-start(bf16[4,2,4,112,128]{4,3,2,1,0:T(8,128)(2,1)S(1)} %pad_maximum_fusion.1.refs_8_), channel_id=1, source_target_pairs={{0,192},{1,65},{64,128},{65,1},{128,64},{129,193},{192,0},{193,129... | collective-permute-start | bytes 2752520 | tf_op jit(solution)/shard_map/ppermute | solution.py:385
  64.7 20.0 %copy-start.6 = (bf16[4,2,4,112,128]{4,3,2,1,0:T(8,128)(2,1)}, bf16[4,2,4,112,128]{4,3,2,1,0:T(8,128)(2,1)S(1)}, u32[]{:S(2)}) copy-start(bf16[4,2,4,112,128]{4,3,2,1,0:T(8,128)(2,1)S(1)} %collective-permute-done.8.refs_2_) | copy-start | bytes 2752516
  64.7 5.9 %collective-permute-start.12 = (bf16[4,2,4,112,128]{4,3,2,1,0:T(8,128)(2,1)S(1)}, bf16[4,2,4,112,128]{4,3,2,1,0:T(8,128)(2,1)S(1)}, u32[]{:S(2)}, u32[]{:S(2)}) collective-permute-start(bf16[4,2,4,112,128]{4,3,2,1,0:T(8,128)(2,1)S(1)} %collective-permute-done.8.refs_2_), channel_id=1, source_target_pairs={{0,1},{1,0},{2,3},{3,2},{4,5},{5,4},{6,7},{7,6},{8,9},{9,8},{10,11... | collective-permute-start | bytes 2752520 | tf_op jit(solution)/shard_map/ppermute | solution.py:389
  64.7 20.0 %copy-start.7 = (bf16[4,2,4,112,128]{4,3,2,1,0:T(8,128)(2,1)}, bf16[4,2,4,112,128]{4,3,2,1,0:T(8,128)(2,1)S(1)}, u32[]{:S(2)}) copy-start(bf16[4,2,4,112,128]{4,3,2,1,0:T(8,128)(2,1)S(1)} %collective-permute-done.7.refs_1_) | copy-start | bytes 2752516
  64.7 15.1 %collective-permute-start.9 = (bf16[4,2,4,112,128]{4,3,2,1,0:T(8,128)(2,1)S(1)}, bf16[4,2,4,112,128]{4,3,2,1,0:T(8,128)(2,1)S(1)}, u32[]{:S(2)}, u32[]{:S(2)}) collective-permute-start(bf16[4,2,4,112,128]{4,3,2,1,0:T(8,128)(2,1)S(1)} %collective-permute-done.7.refs_1_), channel_id=1, source_target_pairs={{0,6},{1,3},{2,4},{3,1},{4,2},{5,7},{6,0},{7,5},{8,14},{9,11},{10,... | collective-permute-start | bytes 2752520 | tf_op jit(solution)/shard_map/ppermute | solution.py:385
  68.5 16.2 %copy-start.8 = (bf16[4,2,4,112,128]{4,3,2,1,0:T(8,128)(2,1)}, bf16[4,2,4,112,128]{4,3,2,1,0:T(8,128)(2,1)S(1)}, u32[]{:S(2)}) copy-start(bf16[4,2,4,112,128]{4,3,2,1,0:T(8,128)(2,1)S(1)} %collective-permute-done.17.refs_9_) | copy-start | bytes 2752516
  68.5 13.4 %collective-permute-start.19 = (bf16[4,2,4,112,128]{4,3,2,1,0:T(8,128)(2,1)S(1)}, bf16[4,2,4,112,128]{4,3,2,1,0:T(8,128)(2,1)S(1)}, u32[]{:S(2)}, u32[]{:S(2)}) collective-permute-start(bf16[4,2,4,112,128]{4,3,2,1,0:T(8,128)(2,1)S(1)} %collective-permute-done.17.refs_9_), channel_id=1, source_target_pairs={{0,192},{1,65},{64,128},{65,1},{128,64},{129,193},{192,0},{193,129... | collective-permute-start | bytes 2752520 | tf_op jit(solution)/shard_map/ppermute | solution.py:385
  70.0 14.6 %copy-start.9 = (bf16[4,2,4,112,128]{4,3,2,1,0:T(8,128)(2,1)}, bf16[4,2,4,112,128]{4,3,2,1,0:T(8,128)(2,1)S(1)}, u32[]{:S(2)}) copy-start(bf16[4,2,4,112,128]{4,3,2,1,0:T(8,128)(2,1)S(1)} %collective-permute-done.20.refs_12_) | copy-start | bytes 2752516
  70.0 11.8 %collective-permute-start.11 = (bf16[4,2,4,112,128]{4,3,2,1,0:T(8,128)(2,1)S(1)}, bf16[4,2,4,112,128]{4,3,2,1,0:T(8,128)(2,1)S(1)}, u32[]{:S(2)}, u32[]{:S(2)}) collective-permute-start(bf16[4,2,4,112,128]{4,3,2,1,0:T(8,128)(2,1)S(1)} %collective-permute-done.7.refs_1_), channel_id=1, source_target_pairs={{0,1},{1,0},{2,3},{3,2},{4,5},{5,4},{6,7},{7,6},{8,9},{9,8},{10,11... | collective-permute-start | bytes 2752520 | tf_op jit(solution)/shard_map/ppermute | solution.py:389
  70.1 14.6 %copy-start.10 = (bf16[4,2,4,112,128]{4,3,2,1,0:T(8,128)(2,1)}, bf16[4,2,4,112,128]{4,3,2,1,0:T(8,128)(2,1)S(1)}, u32[]{:S(2)}) copy-start(bf16[4,2,4,112,128]{4,3,2,1,0:T(8,128)(2,1)S(1)} %collective-permute-done.18.refs_10_) | copy-start | bytes 2752516
  70.1 11.8 %collective-permute-start.21 = (bf16[4,2,4,112,128]{4,3,2,1,0:T(8,128)(2,1)S(1)}, bf16[4,2,4,112,128]{4,3,2,1,0:T(8,128)(2,1)S(1)}, u32[]{:S(2)}, u32[]{:S(2)}) collective-permute-start(bf16[4,2,4,112,128]{4,3,2,1,0:T(8,128)(2,1)S(1)} %collective-permute-done.17.refs_9_), channel_id=1, source_target_pairs={{0,1},{1,0},{2,3},{3,2},{4,5},{5,4},{6,7},{7,6},{8,9},{9,8},{10,11... | collective-permute-start | bytes 2752520 | tf_op jit(solution)/shard_map/ppermute | solution.py:389
  70.6 14.1 %copy-start.11 = (bf16[4,2,4,112,128]{4,3,2,1,0:T(8,128)(2,1)}, bf16[4,2,4,112,128]{4,3,2,1,0:T(8,128)(2,1)S(1)}, u32[]{:S(2)}) copy-start(bf16[4,2,4,112,128]{4,3,2,1,0:T(8,128)(2,1)S(1)} %collective-permute-done.12.refs_6_) | copy-start | bytes 2752516
  70.6 11.3 %collective-permute-start.22 = (bf16[4,2,4,112,128]{4,3,2,1,0:T(8,128)(2,1)S(1)}, bf16[4,2,4,112,128]{4,3,2,1,0:T(8,128)(2,1)S(1)}, u32[]{:S(2)}, u32[]{:S(2)}) collective-permute-start(bf16[4,2,4,112,128]{4,3,2,1,0:T(8,128)(2,1)S(1)} %collective-permute-done.18.refs_10_), channel_id=1, source_target_pairs={{0,1},{1,0},{2,3},{3,2},{4,5},{5,4},{6,7},{7,6},{8,9},{9,8},{10,11... | collective-permute-start | bytes 2752520 | tf_op jit(solution)/shard_map/ppermute | solution.py:389
  79.8 2.1 %copy-start.12 = (bf16[4,2,4,112,128]{4,3,2,1,0:T(8,128)(2,1)}, bf16[4,2,4,112,128]{4,3,2,1,0:T(8,128)(2,1)S(1)}, u32[]{:S(2)}) copy-start(bf16[4,2,4,112,128]{4,3,2,1,0:T(8,128)(2,1)S(1)} %collective-permute-done.9.refs_3_) | copy-start | bytes 2752516
  79.8 2.5 %collective-permute-start.13 = (bf16[4,2,4,112,128]{4,3,2,1,0:T(8,128)(2,1)S(1)}, bf16[4,2,4,112,128]{4,3,2,1,0:T(8,128)(2,1)S(1)}, u32[]{:S(2)}, u32[]{:S(2)}) collective-permute-start(bf16[4,2,4,112,128]{4,3,2,1,0:T(8,128)(2,1)S(1)} %collective-permute-done.9.refs_3_), channel_id=1, source_target_pairs={{0,1},{1,0},{2,3},{3,2},{4,5},{5,4},{6,7},{7,6},{8,9},{9,8},{10,11... | collective-permute-start | bytes 2752520 | tf_op jit(solution)/shard_map/ppermute | solution.py:389
  81.9 1.0 copy-start.13
  81.9 2.8 %collective-permute-start.23 = (bf16[4,2,4,112,128]{4,3,2,1,0:T(8,128)(2,1)S(1)}, bf16[4,2,4,112,128]{4,3,2,1,0:T(8,128)(2,1)}, u32[]{:S(2)}, u32[]{:S(2)}) collective-permute-start(bf16[4,2,4,112,128]{4,3,2,1,0:T(8,128)(2,1)S(1)} %collective-permute-done.19.refs_11_), channel_id=1, source_target_pairs={{0,1},{1,0},{2,3},{3,2},{4,5},{5,4},{6,7},{7,6},{8,9},{9,8},{10,11... | collective-permute-start | bytes 2752520 | tf_op jit(solution)/shard_map/ppermute | solution.py:389
  81.9 1.3 copy-start.14
  81.9 1.5 copy-start.16
  81.9 1.8 copy-start.15
  83.7 0.9 copy-start.17
  142.6 2.8 %collective-permute-start.24 = (bf16[4,4,112,256]{3,2,1,0:T(8,128)(2,1)}, bf16[4,4,112,256]{3,2,1,0:T(8,128)(2,1)S(1)}, u32[]{:S(2)}, u32[]{:S(2)}) collective-permute-start(bf16[4,4,112,256]{3,2,1,0:T(8,128)(2,1)} %get-tuple-element.11), channel_id=1, source_target_pairs={{0,1},{1,0},{2,3},{3,2},{4,5},{5,4},{6,7},{7,6},{8,9},{9,8},{10,11... | collective-permute-start | bytes 2752520 | tf_op jit(solution)/shard_map/ppermute | solution.py:389
  146.8 8.6 %collective-permute-start.25 = (bf16[2,4,112,256]{3,2,1,0:T(8,128)(2,1)S(1)}, bf16[2,4,112,256]{3,2,1,0:T(8,128)(2,1)S(1)}, u32[]{:S(2)}, u32[]{:S(2)}) collective-permute-start(bf16[2,4,112,256]{3,2,1,0:T(8,128)(2,1)S(1)} %get-tuple-element.17), channel_id=1, source_target_pairs={{0,2},{1,7},{2,0},{3,5},{4,6},{5,3},{6,4},{7,1},{8,10},{9,15},{10,... | collective-permute-start | bytes 1376264 | tf_op jit(solution)/shard_map/ppermute | solution.py:385
  155.4 7.3 %collective-permute-start.26 = (bf16[4,112,256]{2,1,0:T(8,128)(2,1)S(1)}, bf16[4,112,256]{2,1,0:T(8,128)(2,1)S(1)}, u32[]{:S(2)}, u32[]{:S(2)}) collective-permute-start(bf16[4,112,256]{2,1,0:T(8,128)(2,1)S(1)} %fusion.2), channel_id=1, source_target_pairs={{0,6},{1,3},{2,4},{3,1},{4,2},{5,7},{6,0},{7,5},{8,14},{9,11},{10,... | collective-permute-start | bytes 688136 | tf_op jit(solution)/shard_map/ppermute | solution.py:385
  163.5 8.2 %collective-permute-start.29 = (bf16[112,256]{1,0:T(8,128)(2,1)S(1)}, bf16[112,256]{1,0:T(8,128)(2,1)S(1)}, u32[]{:S(2)}, u32[]{:S(2)}) collective-permute-start(bf16[112,256]{1,0:T(8,128)(2,1)S(1)} %get-tuple-element.22), channel_id=1, source_target_pairs={{0,16},{8,24},{16,0},{24,8},{1,17},{9,25},{17,1},{25,9},{2,18},{10... | collective-permute-start | bytes 172040 | tf_op jit(solution)/shard_map/ppermute | solution.py:393
  164.9 7.8 %collective-permute-start.28 = (bf16[112,256]{1,0:T(8,128)(2,1)S(1)}, bf16[112,256]{1,0:T(8,128)(2,1)S(1)}, u32[]{:S(2)}, u32[]{:S(2)}) collective-permute-start(bf16[112,256]{1,0:T(8,128)(2,1)S(1)} %get-tuple-element.23), channel_id=1, source_target_pairs={{0,24},{1,9},{8,16},{9,1},{16,8},{17,25},{24,0},{25,17},{2,26},{3,... | collective-permute-start | bytes 172040 | tf_op jit(solution)/shard_map/ppermute | solution.py:385
  169.4 5.7 %collective-permute-start.27 = (bf16[112,256]{1,0:T(8,128)(2,1)S(1)}, bf16[112,256]{1,0:T(8,128)(2,1)S(1)}, u32[]{:S(2)}, u32[]{:S(2)}) collective-permute-start(bf16[112,256]{1,0:T(8,128)(2,1)S(1)} %get-tuple-element.24), channel_id=1, source_target_pairs={{0,8},{1,25},{8,0},{9,17},{16,24},{17,9},{24,16},{25,1},{2,10},{3,... | collective-permute-start | bytes 172040 | tf_op jit(solution)/shard_map/ppermute | solution.py:385
  171.7 3.4 %copy-start.2 = (bf16[112,256]{1,0:T(8,128)(2,1)}, bf16[112,256]{1,0:T(8,128)(2,1)S(1)}, u32[]{:S(2)}) copy-start(bf16[112,256]{1,0:T(8,128)(2,1)S(1)} %collective-permute-done.29.d_ref) | copy-start | bytes 172036
  172.8 2.3 %copy-start.3 = (bf16[112,256]{1,0:T(8,128)(2,1)}, bf16[112,256]{1,0:T(8,128)(2,1)S(1)}, u32[]{:S(2)}) copy-start(bf16[112,256]{1,0:T(8,128)(2,1)S(1)} %collective-permute-done.28.c_ref) | copy-start | bytes 172036
  175.1 0.6 copy-start.4

commit v7 on v6

--- a/solution.py
+++ b/solution.py
@@ -352,7 +352,7 @@
 
 ANY = pl.BlockSpec(memory_space=pl.ANY)
 VMEM = pl.BlockSpec(memory_space=pltpu.VMEM)
-PARAMS = pltpu.CompilerParams(vmem_limit_bytes=56 * 1024 * 1024)
+PARAMS = pltpu.CompilerParams(vmem_limit_bytes=30 * 1024 * 1024)
 
 
 def shape(*dims, dtype=BF16):
@@ -406,16 +406,15 @@
 def per_device(entries, cotangents, scales, key_weight, rate_weight, rate_bias):
     x, zl, zh, y, c = (lax.axis_index(a) for a in ("x", "zl", "zh", "y", "c"))
     rates = rate_weight[0].T
-    packed = sum(
-        jnp.pad(a, ((row, PIECE - row - a.shape[0]), (lane, 256 - lane - a.shape[1])))
-        for a, row, lane in (
-            (key_weight[0], 0, 0),
-            (rates[:16], ROWS, 0),
-            (rates[16:], ROWS, C),
-            (scales[0], ROWS + 8, C),
-            (rate_bias, ROWS + 10, C),
-        )
-    )
+
+    def put(a, row, lane):
+        pads = (row, PIECE - row - a.shape[0], 0), (lane, 256 - lane - a.shape[1], 0)
+        return lax.pad(a, jnp.zeros((), BF16), pads)
+
+    shifted = put(rates, ROWS - 16, C)
+    shifted = jnp.where(iota((PIECE, 256), 0) >= ROWS, shifted, jnp.zeros_like(shifted))
+    packed = put(key_weight[0], 0, 0) + put(rates, ROWS, 0) + shifted
+    packed = packed + put(scales[0], ROWS + 8, C) + put(rate_bias, ROWS + 10, C)
 
     along = jnp.stack(gather_ring(packed, "zh", direct=True))
     first, second = partner(zh, c, True), partner(zh, c, False)

time: 178 us -> 174 us (0.978)
  local copies, waits for them, and re-layouts: 5.69 us -> 0.71 us
  Pallas kernels: 29 us -> 31.1 us
  blocking collectives: 30.5 us -> 28.5 us
    pallas_call x1, Pallas kernels: 23.1 us -> 26.9 us  [per_device(): call(sequence_kernel, [shape(LAYERS, SENT, BLOCK)], [ANY] * 18, [pltpu.VM...]
    unnamed x36 -> x4, local copies, waits for them, and re-layouts: 2.99 us -> 0.01 us
    all_to_all x1, blocking collectives: 30.5 us -> 28.5 us  [per_device(): lax.all_to_all(sent, ('x', 'zl', 'zh', 'y', 'c'), 0, 0, axis_index_groups...]
    ppermute x9, waiting for transfers between devices: 3.07 us -> 4.92 us  [other_core(): return lax.ppermute(array, 'c', [(0, 1), (1, 0)])]
  transfers between devices with their start and end apart: 30 -> 30, of which waited for: 17 -> 18; matrix products, arithmetic and copies ran while one was open for 1% -> 1% of each run, Pallas kernels for 0% -> 0%
where the time goes in v7:
time: 174 us; the launch traced here: 173 us
  waiting for transfers between devices  64.9 us (37%)
  starting transfers between devices  43.8 us (25%)
  Pallas kernels  31.1 us (18%)
  blocking collectives  28.5 us (16%)
  other arithmetic  2.97 us (2%)
    ppermute x18, waiting for transfers between devices, swap(): return lax.ppermute(array, (axis, 'c'), ring_pairs(first))  49.8 us
    ppermute x18, starting transfers between devices, swap(): return lax.ppermute(array, (axis, 'c'), ring_pairs(first))  38.5 us
    all_to_all x1, blocking collectives, per_device(): lax.all_to_all(sent, ('x', 'zl', 'zh', 'y', 'c'), 0, 0, axis_index_groups...  28.5 us
    pallas_call x1, Pallas kernels, per_device(): call(sequence_kernel, [shape(LAYERS, SENT, BLOCK)], [ANY] * 18, [pltpu.VM...  26.9 us
    ppermute x2, waiting for transfers between devices, opposite(): return lax.ppermute(array, axis, [(i, i ^ 2) for i in range(4)])  5.31 us
    ppermute x9, waiting for transfers between devices, other_core(): return lax.ppermute(array, 'c', [(0, 1), (1, 0)])  4.92 us
    ppermute x1, waiting for transfers between devices, per_device(): other = lax.ppermute(along, ('zl', 'zh', 'c'), pairs)  4.83 us
  transfers between devices with their start and end apart: 30, of which 18 were waited for; matrix products, arithmetic and copies ran while one was open for 1% of the time, Pallas kernels for 0%

profile of v7, /device:TPU:2, one launch (start us, length us, event | category | flops | bytes accessed | tf_op | source)
XLA Modules:
  0.0 172.7 jit_solution(2963805833280898478)
XLA Ops:
  0.6 0.9 fusion.6
  1.6 6.3 %collective-permute-start.1 = (bf16[112,256]{1,0:T(8,128)(2,1)S(1)}, bf16[112,256]{1,0:T(8,128)(2,1)S(1)}, u32[]{:S(2)}, u32[]{:S(2)}) collective-permute-start(bf16[112,256]{1,0:T(8,128)(2,1)S(1)} %fusion.6), channel_id=1, source_target_pairs={{0,24},{1,9},{8,16},{9,1},{16,8},{17,25},{24,0},{25,17},{2,26},{3,... | collective-permute-start | bytes 172040 | tf_op jit(solution)/shard_map/ppermute | solution.py:385
  7.9 1.5 collective-permute-start
  9.4 1.0 collective-permute-start.2
  10.4 0.9 fusion.8
  11.5 1.6 collective-permute-done.1
  13.1 1.1 collective-permute-done
  14.2 3.6 %collective-permute-done.2 = bf16[112,256]{1,0:T(8,128)(2,1)S(1)} collective-permute-done((bf16[112,256]{1,0:T(8,128)(2,1)S(1)}, bf16[112,256]{1,0:T(8,128)(2,1)S(1)}, u32[]{:S(2)}, u32[]{:S(2)}) %collective-permute-start.2) | collective-permute-done | bytes 57376 | tf_op jit(solution)/shard_map/ppermute | solution.py:393
  17.9 0.6 gather_fusion
  18.5 1.2 collective-permute-start.3
  19.8 4.8 %collective-permute-done.3 = bf16[4,112,256]{2,1,0:T(8,128)(2,1)S(1)} collective-permute-done((bf16[4,112,256]{2,1,0:T(8,128)(2,1)S(1)}, bf16[4,112,256]{2,1,0:T(8,128)(2,1)S(1)}, u32[]{:S(2)}, u32[]{:S(2)}) %collective-permute-start.3) | collective-permute-done | bytes 229408 | tf_op jit(solution)/shard_map/ppermute | solution.py:429
  24.9 0.6 collective-permute-start.4
  25.5 1.6 collective-permute-start.14
  27.1 2.2 %collective-permute-start.5 = (bf16[2,4,112,128]{3,2,1,0:T(8,128)(2,1)S(1)}, bf16[2,4,112,128]{3,2,1,0:T(8,128)(2,1)S(1)}, u32[]{:S(2)}, u32[]{:S(2)}) collective-permute-start(bf16[2,4,112,128]{3,2,1,0:T(8,128)(2,1)S(1)} %get-tuple-element.21), channel_id=1, source_target_pairs={{0,192},{1,65},{64,128},{65,1},{128,64},{129,193},{192,0},{193,129... | collective-permute-start | bytes 688136 | tf_op jit(solution)/shard_map/ppermute | solution.py:385
  29.2 2.3 %collective-permute-done.4 = bf16[2,4,112,128]{3,2,1,0:T(8,128)(2,1)S(1)} collective-permute-done((bf16[2,4,112,128]{3,2,1,0:T(8,128)(2,1)S(1)}, bf16[2,4,112,128]{3,2,1,0:T(8,128)(2,1)S(1)}, u32[]{:S(2)}, u32[]{:S(2)}) %collective-permute-start.4) | collective-permute-done | bytes 229408 | tf_op jit(solution)/shard_map/ppermute | solution.py:385
  31.6 2.6 %collective-permute-start.6 = (bf16[2,4,112,128]{3,2,1,0:T(8,128)(2,1)S(1)}, bf16[2,4,112,128]{3,2,1,0:T(8,128)(2,1)S(1)}, u32[]{:S(2)}, u32[]{:S(2)}) collective-permute-start(bf16[2,4,112,128]{3,2,1,0:T(8,128)(2,1)S(1)} %collective-permute-done.4), channel_id=1, source_target_pairs={{0,192},{1,65},{64,128},{65,1},{128,64},{129,193},{192,0},{193,129... | collective-permute-start | bytes 688136 | tf_op jit(solution)/shard_map/ppermute | solution.py:385
  34.2 2.3 %collective-permute-start.15 = (bf16[2,4,112,128]{3,2,1,0:T(8,128)(2,1)S(1)}, bf16[2,4,112,128]{3,2,1,0:T(8,128)(2,1)S(1)}, u32[]{:S(2)}, u32[]{:S(2)}) collective-permute-start(bf16[2,4,112,128]{3,2,1,0:T(8,128)(2,1)S(1)} %get-tuple-element.20), channel_id=1, source_target_pairs={{0,6},{1,3},{2,4},{3,1},{4,2},{5,7},{6,0},{7,5},{8,14},{9,11},{10,... | collective-permute-start | bytes 688136 | tf_op jit(solution)/shard_map/ppermute | solution.py:385
  36.4 1.0 collective-permute-start.16
  37.4 0.8 collective-permute-done.6
  38.4 4.4 %collective-permute-start.8 = (bf16[4,2,4,112,128]{4,3,2,1,0:T(8,128)(2,1)S(1)}, bf16[4,2,4,112,128]{4,3,2,1,0:T(8,128)(2,1)S(1)}, u32[]{:S(2)}, u32[]{:S(2)}) collective-permute-start(bf16[4,2,4,112,128]{4,3,2,1,0:T(8,128)(2,1)S(1)} %pad_maximum_fusion.refs_0_), channel_id=1, source_target_pairs={{0,6},{1,3},{2,4},{3,1},{4,2},{5,7},{6,0},{7,5},{8,14},{9,11},{10,... | collective-permute-start | bytes 2752520 | tf_op jit(solution)/shard_map/ppermute | solution.py:385
  42.9 1.0 collective-permute-done.16
  44.0 1.9 %collective-permute-start.17 = (bf16[4,2,4,112,128]{4,3,2,1,0:T(8,128)(2,1)S(1)}, bf16[4,2,4,112,128]{4,3,2,1,0:T(8,128)(2,1)S(1)}, u32[]{:S(2)}, u32[]{:S(2)}) collective-permute-start(bf16[4,2,4,112,128]{4,3,2,1,0:T(8,128)(2,1)S(1)} %pad_maximum_fusion.1.refs_8_), channel_id=1, source_target_pairs={{0,64},{1,193},{64,0},{65,129},{128,192},{129,65},{192,128},{193,1... | collective-permute-start | bytes 2752520 | tf_op jit(solution)/shard_map/ppermute | solution.py:385
  45.9 0.8 collective-permute-start.18
  46.8 16.6 %collective-permute-done.8.refs_2_ = bf16[4,2,4,112,128]{4,3,2,1,0:T(8,128)(2,1)S(1)} collective-permute-done((bf16[4,2,4,112,128]{4,3,2,1,0:T(8,128)(2,1)S(1)}, bf16[4,2,4,112,128]{4,3,2,1,0:T(8,128)(2,1)S(1)}, u32[]{:S(2)}, u32[]{:S(2)}) %collective-permute-start.8) | collective-permute-done | bytes 917536 | tf_op jit(solution)/shard_map/ppermute | solution.py:385
  63.4 3.7 %collective-permute-start.9 = (bf16[4,2,4,112,128]{4,3,2,1,0:T(8,128)(2,1)S(1)}, bf16[4,2,4,112,128]{4,3,2,1,0:T(8,128)(2,1)S(1)}, u32[]{:S(2)}, u32[]{:S(2)}) collective-permute-start(bf16[4,2,4,112,128]{4,3,2,1,0:T(8,128)(2,1)S(1)} %collective-permute-done.7.refs_1_), channel_id=1, source_target_pairs={{0,6},{1,3},{2,4},{3,1},{4,2},{5,7},{6,0},{7,5},{8,14},{9,11},{10,... | collective-permute-start | bytes 2752520 | tf_op jit(solution)/shard_map/ppermute | solution.py:385
  67.1 1.7 collective-permute-start.19
  68.8 0.5 collective-permute-start.21
  69.3 0.3 collective-permute-start.22
  69.6 8.9 %collective-permute-done.9.refs_3_ = bf16[4,2,4,112,128]{4,3,2,1,0:T(8,128)(2,1)S(1)} collective-permute-done((bf16[4,2,4,112,128]{4,3,2,1,0:T(8,128)(2,1)S(1)}, bf16[4,2,4,112,128]{4,3,2,1,0:T(8,128)(2,1)S(1)}, u32[]{:S(2)}, u32[]{:S(2)}) %collective-permute-start.9) | collective-permute-done | bytes 917536 | tf_op jit(solution)/shard_map/ppermute | solution.py:385
  78.5 2.0 %collective-permute-done.19.refs_11_ = bf16[4,2,4,112,128]{4,3,2,1,0:T(8,128)(2,1)S(1)} collective-permute-done((bf16[4,2,4,112,128]{4,3,2,1,0:T(8,128)(2,1)S(1)}, bf16[4,2,4,112,128]{4,3,2,1,0:T(8,128)(2,1)S(1)}, u32[]{:S(2)}, u32[]{:S(2)}) %collective-permute-start.19) | collective-permute-done | bytes 917536 | tf_op jit(solution)/shard_map/ppermute | solution.py:385
  80.5 0.4 collective-permute-done.13.refs_7_
  80.9 2.0 %collective-permute-done.23.refs_15_ = bf16[4,2,4,112,128]{4,3,2,1,0:T(8,128)(2,1)S(1)} collective-permute-done((bf16[4,2,4,112,128]{4,3,2,1,0:T(8,128)(2,1)S(1)}, bf16[4,2,4,112,128]{4,3,2,1,0:T(8,128)(2,1)S(1)}, u32[]{:S(2)}, u32[]{:S(2)}) %collective-permute-start.23) | collective-permute-done | bytes 917536 | tf_op jit(solution)/shard_map/ppermute | solution.py:389
  83.0 26.9 %shard_map.93 = bf16[8,304,384]{2,1,0:T(8,128)(2,1)S(1)} custom-call(bf16[4,2,4,112,128]{4,3,2,1,0:T(8,128)(2,1)S(1)} %pad_maximum_fusion.refs_0_, bf16[4,2,4,112,128]{4,3,2,1,0:T(8,128)(2,1)S(1)} %collective-permute-done.7.refs_1_, bf16[4,2,4,112,128]{4,3,2,1,0:T(8,128)(2,1)S(1)} %collective-permute-done.8.refs_2_, ...), custom_call_target="tpu_custom_call" | custom-call | flops 8000000000 | bytes 30000000 | tf_op jit(solution)/shard_map/pallas_call | solution.py:439
  109.9 28.5 %all_to_all.5.got_ref = bf16[8,304,384]{2,1,0:T(8,128)(2,1)S(1)} all-to-all(bf16[8,304,384]{2,1,0:T(8,128)(2,1)S(1)} %shard_map.93), channel_id=1, replica_groups={{0,32,64,96,128,160,192,224},{1,57,65,121,129,185,193,249},{2,34,66,98,..., dimensions={0} | all-to-all | bytes 3735552 | tf_op jit(solution)/shard_map/all_to_all | solution.py:473
  138.4 3.5 %shard_map.94 = (bf16[4,4,112,256]{3,2,1,0:T(8,128)(2,1)S(1)}, bf16[4,4,112,256]{3,2,1,0:T(8,128)(2,1)S(1)}) custom-call(bf16[8,304,384]{2,1,0:T(8,128)(2,1)S(1)} %all_to_all.5.got_ref), custom_call_target="tpu_custom_call" | custom-call | flops 600000000 | bytes 4000000 | tf_op jit(solution)/shard_map/pallas_call | solution.py:477
  142.0 2.5 %collective-permute-done.24 = bf16[4,4,112,256]{3,2,1,0:T(8,128)(2,1)S(1)} collective-permute-done((bf16[4,4,112,256]{3,2,1,0:T(8,128)(2,1)S(1)}, bf16[4,4,112,256]{3,2,1,0:T(8,128)(2,1)S(1)}, u32[]{:S(2)}, u32[]{:S(2)}) %collective-permute-start.24) | collective-permute-done | bytes 917536 | tf_op jit(solution)/shard_map/ppermute | solution.py:389
  144.4 0.3 add_convert_fusion.1
  144.7 0.8 collective-permute-start.25
  145.5 7.8 %collective-permute-done.25 = bf16[2,4,112,256]{3,2,1,0:T(8,128)(2,1)S(1)} collective-permute-done((bf16[2,4,112,256]{3,2,1,0:T(8,128)(2,1)S(1)}, bf16[2,4,112,256]{3,2,1,0:T(8,128)(2,1)S(1)}, u32[]{:S(2)}, u32[]{:S(2)}) %collective-permute-start.25) | collective-permute-done | bytes 458784 | tf_op jit(solution)/shard_map/ppermute | solution.py:385
  153.3 2.6 %collective-permute-start.26 = (bf16[4,112,256]{2,1,0:T(8,128)(2,1)S(1)}, bf16[4,112,256]{2,1,0:T(8,128)(2,1)S(1)}, u32[]{:S(2)}, u32[]{:S(2)}) collective-permute-start(bf16[4,112,256]{2,1,0:T(8,128)(2,1)S(1)} %fusion.2), channel_id=1, source_target_pairs={{0,6},{1,3},{2,4},{3,1},{4,2},{5,7},{6,0},{7,5},{8,14},{9,11},{10,... | collective-permute-start | bytes 688136 | tf_op jit(solution)/shard_map/ppermute | solution.py:385
  155.9 4.7 %collective-permute-done.26 = bf16[4,112,256]{2,1,0:T(8,128)(2,1)S(1)} collective-permute-done((bf16[4,112,256]{2,1,0:T(8,128)(2,1)S(1)}, bf16[4,112,256]{2,1,0:T(8,128)(2,1)S(1)}, u32[]{:S(2)}, u32[]{:S(2)}) %collective-permute-start.26) | collective-permute-done | bytes 229408 | tf_op jit(solution)/shard_map/ppermute | solution.py:385
  160.8 2.1 %collective-permute-start.29 = (bf16[112,256]{1,0:T(8,128)(2,1)S(1)}, bf16[112,256]{1,0:T(8,128)(2,1)S(1)}, u32[]{:S(2)}, u32[]{:S(2)}) collective-permute-start(bf16[112,256]{1,0:T(8,128)(2,1)S(1)} %get-tuple-element.22), channel_id=1, source_target_pairs={{0,16},{8,24},{16,0},{24,8},{1,17},{9,25},{17,1},{25,9},{2,18},{10... | collective-permute-start | bytes 172040 | tf_op jit(solution)/shard_map/ppermute | solution.py:393
  162.8 4.1 %collective-permute-start.28 = (bf16[112,256]{1,0:T(8,128)(2,1)S(1)}, bf16[112,256]{1,0:T(8,128)(2,1)S(1)}, u32[]{:S(2)}, u32[]{:S(2)}) collective-permute-start(bf16[112,256]{1,0:T(8,128)(2,1)S(1)} %get-tuple-element.23), channel_id=1, source_target_pairs={{0,24},{1,9},{8,16},{9,1},{16,8},{17,25},{24,0},{25,17},{2,26},{3,... | collective-permute-start | bytes 172040 | tf_op jit(solution)/shard_map/ppermute | solution.py:385
  166.9 0.4 collective-permute-start.27
  167.4 1.7 collective-permute-done.29.d_ref
  169.0 1.7 %collective-permute-done.28.c_ref = bf16[112,256]{1,0:T(8,128)(2,1)S(1)} collective-permute-done((bf16[112,256]{1,0:T(8,128)(2,1)S(1)}, bf16[112,256]{1,0:T(8,128)(2,1)S(1)}, u32[]{:S(2)}, u32[]{:S(2)}) %collective-permute-start.28) | collective-permute-done | bytes 57376 | tf_op jit(solution)/shard_map/ppermute | solution.py:385
  170.8 1.2 collective-permute-done.27.b_ref
  172.0 0.7 shard_map.95
  (38 shorter events, 1.3 us)
Async XLA Ops:
  1.6 11.5 %collective-permute-start.1 = (bf16[112,256]{1,0:T(8,128)(2,1)S(1)}, bf16[112,256]{1,0:T(8,128)(2,1)S(1)}, u32[]{:S(2)}, u32[]{:S(2)}) collective-permute-start(bf16[112,256]{1,0:T(8,128)(2,1)S(1)} %fusion.6), channel_id=1, source_target_pairs={{0,24},{1,9},{8,16},{9,1},{16,8},{17,25},{24,0},{25,17},{2,26},{3,... | collective-permute-start | bytes 172040 | tf_op jit(solution)/shard_map/ppermute | solution.py:385
  7.9 6.3 %collective-permute-start = (bf16[112,256]{1,0:T(8,128)(2,1)S(1)}, bf16[112,256]{1,0:T(8,128)(2,1)S(1)}, u32[]{:S(2)}, u32[]{:S(2)}) collective-permute-start(bf16[112,256]{1,0:T(8,128)(2,1)S(1)} %fusion.6), channel_id=1, source_target_pairs={{0,8},{1,25},{8,0},{9,17},{16,24},{17,9},{24,16},{25,1},{2,10},{3,... | collective-permute-start | bytes 172040 | tf_op jit(solution)/shard_map/ppermute | solution.py:385
  9.4 8.5 %collective-permute-start.2 = (bf16[112,256]{1,0:T(8,128)(2,1)S(1)}, bf16[112,256]{1,0:T(8,128)(2,1)S(1)}, u32[]{:S(2)}, u32[]{:S(2)}) collective-permute-start(bf16[112,256]{1,0:T(8,128)(2,1)S(1)} %fusion.6), channel_id=1, source_target_pairs={{0,16},{8,24},{16,0},{24,8},{1,17},{9,25},{17,1},{25,9},{2,18},{10... | collective-permute-start | bytes 172040 | tf_op jit(solution)/shard_map/ppermute | solution.py:393
  18.5 6.1 %collective-permute-start.3 = (bf16[4,112,256]{2,1,0:T(8,128)(2,1)S(1)}, bf16[4,112,256]{2,1,0:T(8,128)(2,1)S(1)}, u32[]{:S(2)}, u32[]{:S(2)}) collective-permute-start(bf16[4,112,256]{2,1,0:T(8,128)(2,1)S(1)} %broadcast_select_fusion), channel_id=1, source_target_pairs={{0,32},{1,57},{32,0},{33,9},{8,40},{9,33},{40,8},{41,17},{16,48},{... | collective-permute-start | bytes 688136 | tf_op jit(solution)/shard_map/ppermute | solution.py:429
  24.9 58.1 %copy-start = (bf16[2,3,32,3072]{3,2,1,0:T(8,128)(2,1)S(1)}, bf16[2,3,32,3072]{3,2,1,0:T(8,128)(2,1)}, u32[]{:S(2)}) copy-start(bf16[2,3,32,3072]{3,2,1,0:T(8,128)(2,1)} %refs_16_.1) | copy-start | bytes 3538948
  24.9 58.1 %copy-start.1 = (bf16[2,3,32,3072]{3,2,1,0:T(8,128)(2,1)S(1)}, bf16[2,3,32,3072]{3,2,1,0:T(8,128)(2,1)}, u32[]{:S(2)}) copy-start(bf16[2,3,32,3072]{3,2,1,0:T(8,128)(2,1)} %refs_17_.1) | copy-start | bytes 3538948
  24.9 6.7 %collective-permute-start.4 = (bf16[2,4,112,128]{3,2,1,0:T(8,128)(2,1)S(1)}, bf16[2,4,112,128]{3,2,1,0:T(8,128)(2,1)S(1)}, u32[]{:S(2)}, u32[]{:S(2)}) collective-permute-start(bf16[2,4,112,128]{3,2,1,0:T(8,128)(2,1)S(1)} %get-tuple-element.21), channel_id=1, source_target_pairs={{0,64},{1,193},{64,0},{65,129},{128,192},{129,65},{192,128},{193,1... | collective-permute-start | bytes 688136 | tf_op jit(solution)/shard_map/ppermute | solution.py:385
  25.5 10.9 %collective-permute-start.14 = (bf16[2,4,112,128]{3,2,1,0:T(8,128)(2,1)S(1)}, bf16[2,4,112,128]{3,2,1,0:T(8,128)(2,1)S(1)}, u32[]{:S(2)}, u32[]{:S(2)}) collective-permute-start(bf16[2,4,112,128]{3,2,1,0:T(8,128)(2,1)S(1)} %get-tuple-element.20), channel_id=1, source_target_pairs={{0,2},{1,7},{2,0},{3,5},{4,6},{5,3},{6,4},{7,1},{8,10},{9,15},{10,... | collective-permute-start | bytes 688136 | tf_op jit(solution)/shard_map/ppermute | solution.py:385
  27.1 10.3 %collective-permute-start.5 = (bf16[2,4,112,128]{3,2,1,0:T(8,128)(2,1)S(1)}, bf16[2,4,112,128]{3,2,1,0:T(8,128)(2,1)S(1)}, u32[]{:S(2)}, u32[]{:S(2)}) collective-permute-start(bf16[2,4,112,128]{3,2,1,0:T(8,128)(2,1)S(1)} %get-tuple-element.21), channel_id=1, source_target_pairs={{0,192},{1,65},{64,128},{65,1},{128,64},{129,193},{192,0},{193,129... | collective-permute-start | bytes 688136 | tf_op jit(solution)/shard_map/ppermute | solution.py:385
  31.6 6.6 %collective-permute-start.6 = (bf16[2,4,112,128]{3,2,1,0:T(8,128)(2,1)S(1)}, bf16[2,4,112,128]{3,2,1,0:T(8,128)(2,1)S(1)}, u32[]{:S(2)}, u32[]{:S(2)}) collective-permute-start(bf16[2,4,112,128]{3,2,1,0:T(8,128)(2,1)S(1)} %collective-permute-done.4), channel_id=1, source_target_pairs={{0,192},{1,65},{64,128},{65,1},{128,64},{129,193},{192,0},{193,129... | collective-permute-start | bytes 688136 | tf_op jit(solution)/shard_map/ppermute | solution.py:385
  34.2 8.7 %collective-permute-start.15 = (bf16[2,4,112,128]{3,2,1,0:T(8,128)(2,1)S(1)}, bf16[2,4,112,128]{3,2,1,0:T(8,128)(2,1)S(1)}, u32[]{:S(2)}, u32[]{:S(2)}) collective-permute-start(bf16[2,4,112,128]{3,2,1,0:T(8,128)(2,1)S(1)} %get-tuple-element.20), channel_id=1, source_target_pairs={{0,6},{1,3},{2,4},{3,1},{4,2},{5,7},{6,0},{7,5},{8,14},{9,11},{10,... | collective-permute-start | bytes 688136 | tf_op jit(solution)/shard_map/ppermute | solution.py:385
  36.4 7.4 %collective-permute-start.16 = (bf16[2,4,112,128]{3,2,1,0:T(8,128)(2,1)S(1)}, bf16[2,4,112,128]{3,2,1,0:T(8,128)(2,1)S(1)}, u32[]{:S(2)}, u32[]{:S(2)}) collective-permute-start(bf16[2,4,112,128]{3,2,1,0:T(8,128)(2,1)S(1)} %collective-permute-done.14), channel_id=1, source_target_pairs={{0,6},{1,3},{2,4},{3,1},{4,2},{5,7},{6,0},{7,5},{8,14},{9,11},{10,... | collective-permute-start | bytes 688136 | tf_op jit(solution)/shard_map/ppermute | solution.py:385
  38.3 7.6 %collective-permute-start.10 = (bf16[4,2,4,112,128]{4,3,2,1,0:T(8,128)(2,1)S(1)}, bf16[4,2,4,112,128]{4,3,2,1,0:T(8,128)(2,1)S(1)}, u32[]{:S(2)}, u32[]{:S(2)}) collective-permute-start(bf16[4,2,4,112,128]{4,3,2,1,0:T(8,128)(2,1)S(1)} %pad_maximum_fusion.refs_0_), channel_id=1, source_target_pairs={{0,1},{1,0},{2,3},{3,2},{4,5},{5,4},{6,7},{7,6},{8,9},{9,8},{10,11... | collective-permute-start | bytes 2752520 | tf_op jit(solution)/shard_map/ppermute | solution.py:389
  38.4 25.0 %collective-permute-start.8 = (bf16[4,2,4,112,128]{4,3,2,1,0:T(8,128)(2,1)S(1)}, bf16[4,2,4,112,128]{4,3,2,1,0:T(8,128)(2,1)S(1)}, u32[]{:S(2)}, u32[]{:S(2)}) collective-permute-start(bf16[4,2,4,112,128]{4,3,2,1,0:T(8,128)(2,1)S(1)} %pad_maximum_fusion.refs_0_), channel_id=1, source_target_pairs={{0,6},{1,3},{2,4},{3,1},{4,2},{5,7},{6,0},{7,5},{8,14},{9,11},{10,... | collective-permute-start | bytes 2752520 | tf_op jit(solution)/shard_map/ppermute | solution.py:385
  42.8 20.6 %collective-permute-start.7 = (bf16[4,2,4,112,128]{4,3,2,1,0:T(8,128)(2,1)S(1)}, bf16[4,2,4,112,128]{4,3,2,1,0:T(8,128)(2,1)S(1)}, u32[]{:S(2)}, u32[]{:S(2)}) collective-permute-start(bf16[4,2,4,112,128]{4,3,2,1,0:T(8,128)(2,1)S(1)} %pad_maximum_fusion.refs_0_), channel_id=1, source_target_pairs={{0,2},{1,7},{2,0},{3,5},{4,6},{5,3},{6,4},{7,1},{8,10},{9,15},{10,... | collective-permute-start | bytes 2752520 | tf_op jit(solution)/shard_map/ppermute | solution.py:385
  44.0 23.1 %collective-permute-start.17 = (bf16[4,2,4,112,128]{4,3,2,1,0:T(8,128)(2,1)S(1)}, bf16[4,2,4,112,128]{4,3,2,1,0:T(8,128)(2,1)S(1)}, u32[]{:S(2)}, u32[]{:S(2)}) collective-permute-start(bf16[4,2,4,112,128]{4,3,2,1,0:T(8,128)(2,1)S(1)} %pad_maximum_fusion.1.refs_8_), channel_id=1, source_target_pairs={{0,64},{1,193},{64,0},{65,129},{128,192},{129,65},{192,128},{193,1... | collective-permute-start | bytes 2752520 | tf_op jit(solution)/shard_map/ppermute | solution.py:385
  45.9 22.9 %collective-permute-start.20 = (bf16[4,2,4,112,128]{4,3,2,1,0:T(8,128)(2,1)S(1)}, bf16[4,2,4,112,128]{4,3,2,1,0:T(8,128)(2,1)S(1)}, u32[]{:S(2)}, u32[]{:S(2)}) collective-permute-start(bf16[4,2,4,112,128]{4,3,2,1,0:T(8,128)(2,1)S(1)} %pad_maximum_fusion.1.refs_8_), channel_id=1, source_target_pairs={{0,1},{1,0},{2,3},{3,2},{4,5},{5,4},{6,7},{7,6},{8,9},{9,8},{10,11... | collective-permute-start | bytes 2752520 | tf_op jit(solution)/shard_map/ppermute | solution.py:389
  45.9 22.9 %collective-permute-start.18 = (bf16[4,2,4,112,128]{4,3,2,1,0:T(8,128)(2,1)S(1)}, bf16[4,2,4,112,128]{4,3,2,1,0:T(8,128)(2,1)S(1)}, u32[]{:S(2)}, u32[]{:S(2)}) collective-permute-start(bf16[4,2,4,112,128]{4,3,2,1,0:T(8,128)(2,1)S(1)} %pad_maximum_fusion.1.refs_8_), channel_id=1, source_target_pairs={{0,192},{1,65},{64,128},{65,1},{128,64},{129,193},{192,0},{193,129... | collective-permute-start | bytes 2752520 | tf_op jit(solution)/shard_map/ppermute | solution.py:385
  63.4 5.9 %collective-permute-start.12 = (bf16[4,2,4,112,128]{4,3,2,1,0:T(8,128)(2,1)S(1)}, bf16[4,2,4,112,128]{4,3,2,1,0:T(8,128)(2,1)S(1)}, u32[]{:S(2)}, u32[]{:S(2)}) collective-permute-start(bf16[4,2,4,112,128]{4,3,2,1,0:T(8,128)(2,1)S(1)} %collective-permute-done.8.refs_2_), channel_id=1, source_target_pairs={{0,1},{1,0},{2,3},{3,2},{4,5},{5,4},{6,7},{7,6},{8,9},{9,8},{10,11... | collective-permute-start | bytes 2752520 | tf_op jit(solution)/shard_map/ppermute | solution.py:389
  63.4 15.1 %collective-permute-start.9 = (bf16[4,2,4,112,128]{4,3,2,1,0:T(8,128)(2,1)S(1)}, bf16[4,2,4,112,128]{4,3,2,1,0:T(8,128)(2,1)S(1)}, u32[]{:S(2)}, u32[]{:S(2)}) collective-permute-start(bf16[4,2,4,112,128]{4,3,2,1,0:T(8,128)(2,1)S(1)} %collective-permute-done.7.refs_1_), channel_id=1, source_target_pairs={{0,6},{1,3},{2,4},{3,1},{4,2},{5,7},{6,0},{7,5},{8,14},{9,11},{10,... | collective-permute-start | bytes 2752520 | tf_op jit(solution)/shard_map/ppermute | solution.py:385
  67.1 13.4 %collective-permute-start.19 = (bf16[4,2,4,112,128]{4,3,2,1,0:T(8,128)(2,1)S(1)}, bf16[4,2,4,112,128]{4,3,2,1,0:T(8,128)(2,1)S(1)}, u32[]{:S(2)}, u32[]{:S(2)}) collective-permute-start(bf16[4,2,4,112,128]{4,3,2,1,0:T(8,128)(2,1)S(1)} %collective-permute-done.17.refs_9_), channel_id=1, source_target_pairs={{0,192},{1,65},{64,128},{65,1},{128,64},{129,193},{192,0},{193,129... | collective-permute-start | bytes 2752520 | tf_op jit(solution)/shard_map/ppermute | solution.py:385
  68.8 11.7 %collective-permute-start.11 = (bf16[4,2,4,112,128]{4,3,2,1,0:T(8,128)(2,1)S(1)}, bf16[4,2,4,112,128]{4,3,2,1,0:T(8,128)(2,1)S(1)}, u32[]{:S(2)}, u32[]{:S(2)}) collective-permute-start(bf16[4,2,4,112,128]{4,3,2,1,0:T(8,128)(2,1)S(1)} %collective-permute-done.7.refs_1_), channel_id=1, source_target_pairs={{0,1},{1,0},{2,3},{3,2},{4,5},{5,4},{6,7},{7,6},{8,9},{9,8},{10,11... | collective-permute-start | bytes 2752520 | tf_op jit(solution)/shard_map/ppermute | solution.py:389
  68.8 11.7 %collective-permute-start.21 = (bf16[4,2,4,112,128]{4,3,2,1,0:T(8,128)(2,1)S(1)}, bf16[4,2,4,112,128]{4,3,2,1,0:T(8,128)(2,1)S(1)}, u32[]{:S(2)}, u32[]{:S(2)}) collective-permute-start(bf16[4,2,4,112,128]{4,3,2,1,0:T(8,128)(2,1)S(1)} %collective-permute-done.17.refs_9_), channel_id=1, source_target_pairs={{0,1},{1,0},{2,3},{3,2},{4,5},{5,4},{6,7},{7,6},{8,9},{9,8},{10,11... | collective-permute-start | bytes 2752520 | tf_op jit(solution)/shard_map/ppermute | solution.py:389
  69.3 11.2 %collective-permute-start.22 = (bf16[4,2,4,112,128]{4,3,2,1,0:T(8,128)(2,1)S(1)}, bf16[4,2,4,112,128]{4,3,2,1,0:T(8,128)(2,1)S(1)}, u32[]{:S(2)}, u32[]{:S(2)}) collective-permute-start(bf16[4,2,4,112,128]{4,3,2,1,0:T(8,128)(2,1)S(1)} %collective-permute-done.18.refs_10_), channel_id=1, source_target_pairs={{0,1},{1,0},{2,3},{3,2},{4,5},{5,4},{6,7},{7,6},{8,9},{9,8},{10,11... | collective-permute-start | bytes 2752520 | tf_op jit(solution)/shard_map/ppermute | solution.py:389
  78.5 2.5 %collective-permute-start.13 = (bf16[4,2,4,112,128]{4,3,2,1,0:T(8,128)(2,1)S(1)}, bf16[4,2,4,112,128]{4,3,2,1,0:T(8,128)(2,1)S(1)}, u32[]{:S(2)}, u32[]{:S(2)}) collective-permute-start(bf16[4,2,4,112,128]{4,3,2,1,0:T(8,128)(2,1)S(1)} %collective-permute-done.9.refs_3_), channel_id=1, source_target_pairs={{0,1},{1,0},{2,3},{3,2},{4,5},{5,4},{6,7},{7,6},{8,9},{9,8},{10,11... | collective-permute-start | bytes 2752520 | tf_op jit(solution)/shard_map/ppermute | solution.py:389
  80.5 2.5 %collective-permute-start.23 = (bf16[4,2,4,112,128]{4,3,2,1,0:T(8,128)(2,1)S(1)}, bf16[4,2,4,112,128]{4,3,2,1,0:T(8,128)(2,1)S(1)}, u32[]{:S(2)}, u32[]{:S(2)}) collective-permute-start(bf16[4,2,4,112,128]{4,3,2,1,0:T(8,128)(2,1)S(1)} %collective-permute-done.19.refs_11_), channel_id=1, source_target_pairs={{0,1},{1,0},{2,3},{3,2},{4,5},{5,4},{6,7},{7,6},{8,9},{9,8},{10,11... | collective-permute-start | bytes 2752520 | tf_op jit(solution)/shard_map/ppermute | solution.py:389
  141.9 2.6 %collective-permute-start.24 = (bf16[4,4,112,256]{3,2,1,0:T(8,128)(2,1)S(1)}, bf16[4,4,112,256]{3,2,1,0:T(8,128)(2,1)S(1)}, u32[]{:S(2)}, u32[]{:S(2)}) collective-permute-start(bf16[4,4,112,256]{3,2,1,0:T(8,128)(2,1)S(1)} %get-tuple-element.11), channel_id=1, source_target_pairs={{0,1},{1,0},{2,3},{3,2},{4,5},{5,4},{6,7},{7,6},{8,9},{9,8},{10,11... | collective-permute-start | bytes 2752520 | tf_op jit(solution)/shard_map/ppermute | solution.py:389
  144.7 8.6 %collective-permute-start.25 = (bf16[2,4,112,256]{3,2,1,0:T(8,128)(2,1)S(1)}, bf16[2,4,112,256]{3,2,1,0:T(8,128)(2,1)S(1)}, u32[]{:S(2)}, u32[]{:S(2)}) collective-permute-start(bf16[2,4,112,256]{3,2,1,0:T(8,128)(2,1)S(1)} %get-tuple-element.17), channel_id=1, source_target_pairs={{0,2},{1,7},{2,0},{3,5},{4,6},{5,3},{6,4},{7,1},{8,10},{9,15},{10,... | collective-permute-start | bytes 1376264 | tf_op jit(solution)/shard_map/ppermute | solution.py:385
  153.3 7.3 %collective-permute-start.26 = (bf16[4,112,256]{2,1,0:T(8,128)(2,1)S(1)}, bf16[4,112,256]{2,1,0:T(8,128)(2,1)S(1)}, u32[]{:S(2)}, u32[]{:S(2)}) collective-permute-start(bf16[4,112,256]{2,1,0:T(8,128)(2,1)S(1)} %fusion.2), channel_id=1, source_target_pairs={{0,6},{1,3},{2,4},{3,1},{4,2},{5,7},{6,0},{7,5},{8,14},{9,11},{10,... | collective-permute-start | bytes 688136 | tf_op jit(solution)/shard_map/ppermute | solution.py:385
  160.8 8.3 %collective-permute-start.29 = (bf16[112,256]{1,0:T(8,128)(2,1)S(1)}, bf16[112,256]{1,0:T(8,128)(2,1)S(1)}, u32[]{:S(2)}, u32[]{:S(2)}) collective-permute-start(bf16[112,256]{1,0:T(8,128)(2,1)S(1)} %get-tuple-element.22), channel_id=1, source_target_pairs={{0,16},{8,24},{16,0},{24,8},{1,17},{9,25},{17,1},{25,9},{2,18},{10... | collective-permute-start | bytes 172040 | tf_op jit(solution)/shard_map/ppermute | solution.py:393
  162.8 7.9 %collective-permute-start.28 = (bf16[112,256]{1,0:T(8,128)(2,1)S(1)}, bf16[112,256]{1,0:T(8,128)(2,1)S(1)}, u32[]{:S(2)}, u32[]{:S(2)}) collective-permute-start(bf16[112,256]{1,0:T(8,128)(2,1)S(1)} %get-tuple-element.23), channel_id=1, source_target_pairs={{0,24},{1,9},{8,16},{9,1},{16,8},{17,25},{24,0},{25,17},{2,26},{3,... | collective-permute-start | bytes 172040 | tf_op jit(solution)/shard_map/ppermute | solution.py:385
  166.9 5.1 %collective-permute-start.27 = (bf16[112,256]{1,0:T(8,128)(2,1)S(1)}, bf16[112,256]{1,0:T(8,128)(2,1)S(1)}, u32[]{:S(2)}, u32[]{:S(2)}) collective-permute-start(bf16[112,256]{1,0:T(8,128)(2,1)S(1)} %get-tuple-element.24), channel_id=1, source_target_pairs={{0,8},{1,25},{8,0},{9,17},{16,24},{17,9},{24,16},{25,1},{2,10},{3,... | collective-permute-start | bytes 172040 | tf_op jit(solution)/shard_map/ppermute | solution.py:385

commit v8 on v7

--- a/solution.py
+++ b/solution.py
@@ -117,12 +117,9 @@
 
 def sequence_kernel(*refs):
     left, right = refs[:8], refs[8:16]
-    entry_ref, cot_ref, out_ref = refs[16:19]
+    entry_ref, cot_ref, sent_ref = refs[16:19]
     w_scr, rows_scr, xs, ns, mixed_scr, decay_scr, write_scr, small_scr, proj_scr = refs[19:28]
-    first_scr, sent_ref, sem_a, sem_b, sem_c, sem_out = refs[28:]
-
-    def send(layer, rows):
-        pltpu.make_async_copy(sent_ref.at[layer, rows], out_ref.at[layer, rows], sem_out).start()
+    first_scr, sem_c = refs[28:]
 
     x, y, c = (lax.axis_index(a) for a in ("x", "y", "c"))
     section = x * 2 + lax.axis_index("zl")
@@ -139,33 +136,13 @@
         one, two = partner(i, core, True), partner(i, core, False)
         return [i, one, two, partner(two, core, True)]
 
-    for target in range(4):
-        for kc in range(2):
-            cc = (c + kc) % 2
-            ys, xx = ring(y, cc), ring(x, cc)
-            slot = sum(jnp.where(xx[j] == target, j, 0) for j in range(4))
-            for i in range(4):
-                pltpu.make_async_copy(
-                    left[kc * 4 + i].at[slot],
-                    w_scr.at[2 * target : 2 * target + 2, :, ys[i], cc, :, :C],
-                    sem_a.at[target],
-                ).start()
-
-                @pl.when(xx[i] == target)
-                def _(i=i, kc=kc, cc=cc, ys=ys, target=target):
-                    for j in range(4):
-                        pltpu.make_async_copy(
-                            right[kc * 4 + i].at[j],
-                            w_scr.at[2 * target : 2 * target + 2, :, ys[j], cc, :, C:],
-                            sem_b.at[target],
-                        ).start()
-
-    def wait_layers(at):
-        for sem, src in ((sem_a, left[0]), (sem_b, right[0])):
-            for _ in range(8):
-                pltpu.make_async_copy(
-                    src.at[0], w_scr.at[0:2, :, 0, 0, :, :C], sem.at[at]
-                ).wait()
+    for kc in range(2):
+        cc = (c + kc) % 2
+        ys, xx = ring(y, cc), ring(x, cc)
+        for i in range(4):
+            for j in range(4):
+                w_scr[pl.ds(2 * xx[j], 2), :, ys[i], cc, :, :C] = left[kc * 4 + i][j]
+                w_scr[pl.ds(2 * xx[i], 2), :, ys[j], cc, :, C:] = right[kc * 4 + i][j]
 
     causal, diag, spread, block, tri, tri_back = masks()
 
@@ -174,10 +151,6 @@
         return jnp.concatenate(parts, axis=0)
 
     def forward(layer, stream):
-        @pl.when(layer % 2 == 0)
-        def _():
-            wait_layers(layer // 2)
-
         rows = assemble_rows(lambda d: w_scr[layer, d // 8, d // 2 % 4, d % 2, ROWS:])
         rows_low = rows.astype(BF16)
         rows_scr[layer] = rows_low
@@ -189,7 +162,6 @@
         ns[layer] = normed
         for m in range(BLOCKS):
             sent_ref[layer, T * m : T * (m + 1)] = normed[:, BLOCK * m : BLOCK * (m + 1)]
-        send(layer, pl.ds(0, TOK))
         logits = nt(normed, rows_low) + bias
         key_query = sum(
             nn(normed[:, BLOCK * m : BLOCK * (m + 1)], keys_of(layer, m)) for m in range(BLOCKS)
@@ -284,12 +256,10 @@
         sent_ref[layer, TOK + T :] = jnp.concatenate(
             [d[:, BLOCK * i : BLOCK * (i + 1)] for d in (d_gain, d_scale) for i in range(8)], axis=0
         ).astype(BF16)
-        send(layer, pl.ds(TOK, T + 16))
         return (dy + inv_rms * (d_hat - x_hat * mean)).astype(BF16)
 
     cot = jnp.where(section < SEQS, first_scr[1].astype(F32), 0.0).astype(BF16)
     lax.fori_loop(0, LAYERS, backward, cot, unroll=2)
-    pltpu.make_async_copy(sent_ref, out_ref, sem_out).wait()
 
 
 def weight_kernel(got_ref, keep_ref, send_ref, got, scr, sem_in, sem):
@@ -439,7 +409,7 @@
     sent = call(
         sequence_kernel,
         [shape(LAYERS, SENT, BLOCK)],
-        [ANY] * 18,
+        [VMEM] * 16 + [ANY] * 2,
         [
             pltpu.VMEM((LAYERS, 4, 4, 2, PIECE, 256), BF16),
             pltpu.VMEM((LAYERS, T, D), BF16),
@@ -451,13 +421,8 @@
             pltpu.VMEM((LAYERS, T, 256), F32),
             pltpu.VMEM((LAYERS, T, 256), F32),
             pltpu.VMEM((2, T, D), BF16),
-            pltpu.VMEM((LAYERS, SENT, BLOCK), BF16),
-            pltpu.SemaphoreType.DMA((4,)),
-            pltpu.SemaphoreType.DMA((4,)),
             pltpu.SemaphoreType.DMA((2,)),
-            pltpu.SemaphoreType.DMA,
         ],
-        [ANY],
         cost=(8_000_000_000, 30_000_000),
     )(*left, *right, entries, cotangents)[0]
 

time: 174 us -> 170 us (0.977)
  Pallas kernels: 31.1 us -> 27.4 us
    pallas_call x1, Pallas kernels: 26.9 us -> 23.3 us  [per_device(): call(sequence_kernel, [shape(LAYERS, SENT, BLOCK)], [VMEM] * 16 + [ANY] *...]
where the time goes in v8:
time: 170 us; the launch traced here: 169 us
  waiting for transfers between devices  64.8 us (38%)
  starting transfers between devices  43.8 us (26%)
  blocking collectives  28.5 us (17%)
  Pallas kernels  27.4 us (16%)
  other arithmetic  2.97 us (2%)
    ppermute x18, waiting for transfers between devices, swap(): return lax.ppermute(array, (axis, 'c'), ring_pairs(first))  49.8 us
    ppermute x18, starting transfers between devices, swap(): return lax.ppermute(array, (axis, 'c'), ring_pairs(first))  38.5 us
    all_to_all x1, blocking collectives, per_device(): lax.all_to_all(sent, ('x', 'zl', 'zh', 'y', 'c'), 0, 0, axis_index_groups...  28.5 us
    pallas_call x1, Pallas kernels, per_device(): call(sequence_kernel, [shape(LAYERS, SENT, BLOCK)], [VMEM] * 16 + [ANY] *...  23.3 us
    ppermute x2, waiting for transfers between devices, opposite(): return lax.ppermute(array, axis, [(i, i ^ 2) for i in range(4)])  5.31 us
    ppermute x9, waiting for transfers between devices, other_core(): return lax.ppermute(array, 'c', [(0, 1), (1, 0)])  4.92 us
    ppermute x1, waiting for transfers between devices, per_device(): other = lax.ppermute(along, ('zl', 'zh', 'c'), pairs)  4.83 us
    pallas_call x1, Pallas kernels, per_device(): call(weight_kernel, [half, half], [ANY], [pltpu.VMEM((LAYERS, SENT, BLOCK...  3.45 us
  transfers between devices with their start and end apart: 30, of which 18 were waited for; matrix products, arithmetic and copies ran while one was open for 1% of the time, Pallas kernels for 0%

profile of v8, /device:TPU:2, one launch (start us, length us, event | category | flops | bytes accessed | tf_op | source)
XLA Modules:
  0.0 169.0 jit_solution(10498390838194063213)
XLA Ops:
  0.6 0.9 fusion.6
  1.6 6.3 %collective-permute-start.1 = (bf16[112,256]{1,0:T(8,128)(2,1)S(1)}, bf16[112,256]{1,0:T(8,128)(2,1)S(1)}, u32[]{:S(2)}, u32[]{:S(2)}) collective-permute-start(bf16[112,256]{1,0:T(8,128)(2,1)S(1)} %fusion.6), channel_id=1, source_target_pairs={{0,24},{1,9},{8,16},{9,1},{16,8},{17,25},{24,0},{25,17},{2,26},{3,... | collective-permute-start | bytes 172040 | tf_op jit(solution)/shard_map/ppermute | solution.py:355
  7.9 1.5 collective-permute-start
  9.4 1.0 collective-permute-start.2
  10.4 0.9 fusion.8
  11.5 1.6 collective-permute-done.1
  13.1 1.1 collective-permute-done
  14.2 3.6 %collective-permute-done.2 = bf16[112,256]{1,0:T(8,128)(2,1)S(1)} collective-permute-done((bf16[112,256]{1,0:T(8,128)(2,1)S(1)}, bf16[112,256]{1,0:T(8,128)(2,1)S(1)}, u32[]{:S(2)}, u32[]{:S(2)}) %collective-permute-start.2) | collective-permute-done | bytes 57376 | tf_op jit(solution)/shard_map/ppermute | solution.py:363
  17.9 0.6 gather_fusion
  18.5 1.2 collective-permute-start.3
  19.8 4.8 %collective-permute-done.3 = bf16[4,112,256]{2,1,0:T(8,128)(2,1)S(1)} collective-permute-done((bf16[4,112,256]{2,1,0:T(8,128)(2,1)S(1)}, bf16[4,112,256]{2,1,0:T(8,128)(2,1)S(1)}, u32[]{:S(2)}, u32[]{:S(2)}) %collective-permute-start.3) | collective-permute-done | bytes 229408 | tf_op jit(solution)/shard_map/ppermute | solution.py:399
  24.9 0.6 collective-permute-start.4
  25.5 1.6 collective-permute-start.14
  27.1 2.2 %collective-permute-start.5 = (bf16[2,4,112,128]{3,2,1,0:T(8,128)(2,1)S(1)}, bf16[2,4,112,128]{3,2,1,0:T(8,128)(2,1)S(1)}, u32[]{:S(2)}, u32[]{:S(2)}) collective-permute-start(bf16[2,4,112,128]{3,2,1,0:T(8,128)(2,1)S(1)} %get-tuple-element.21), channel_id=1, source_target_pairs={{0,192},{1,65},{64,128},{65,1},{128,64},{129,193},{192,0},{193,129... | collective-permute-start | bytes 688136 | tf_op jit(solution)/shard_map/ppermute | solution.py:355
  29.2 2.3 %collective-permute-done.4 = bf16[2,4,112,128]{3,2,1,0:T(8,128)(2,1)S(1)} collective-permute-done((bf16[2,4,112,128]{3,2,1,0:T(8,128)(2,1)S(1)}, bf16[2,4,112,128]{3,2,1,0:T(8,128)(2,1)S(1)}, u32[]{:S(2)}, u32[]{:S(2)}) %collective-permute-start.4) | collective-permute-done | bytes 229408 | tf_op jit(solution)/shard_map/ppermute | solution.py:355
  31.6 2.6 %collective-permute-start.6 = (bf16[2,4,112,128]{3,2,1,0:T(8,128)(2,1)S(1)}, bf16[2,4,112,128]{3,2,1,0:T(8,128)(2,1)S(1)}, u32[]{:S(2)}, u32[]{:S(2)}) collective-permute-start(bf16[2,4,112,128]{3,2,1,0:T(8,128)(2,1)S(1)} %collective-permute-done.4), channel_id=1, source_target_pairs={{0,192},{1,65},{64,128},{65,1},{128,64},{129,193},{192,0},{193,129... | collective-permute-start | bytes 688136 | tf_op jit(solution)/shard_map/ppermute | solution.py:355
  34.2 2.3 %collective-permute-start.15 = (bf16[2,4,112,128]{3,2,1,0:T(8,128)(2,1)S(1)}, bf16[2,4,112,128]{3,2,1,0:T(8,128)(2,1)S(1)}, u32[]{:S(2)}, u32[]{:S(2)}) collective-permute-start(bf16[2,4,112,128]{3,2,1,0:T(8,128)(2,1)S(1)} %get-tuple-element.20), channel_id=1, source_target_pairs={{0,6},{1,3},{2,4},{3,1},{4,2},{5,7},{6,0},{7,5},{8,14},{9,11},{10,... | collective-permute-start | bytes 688136 | tf_op jit(solution)/shard_map/ppermute | solution.py:355
  36.4 1.0 collective-permute-start.16
  37.4 0.8 collective-permute-done.6
  38.4 4.4 %collective-permute-start.8 = (bf16[4,2,4,112,128]{4,3,2,1,0:T(8,128)(2,1)S(1)}, bf16[4,2,4,112,128]{4,3,2,1,0:T(8,128)(2,1)S(1)}, u32[]{:S(2)}, u32[]{:S(2)}) collective-permute-start(bf16[4,2,4,112,128]{4,3,2,1,0:T(8,128)(2,1)S(1)} %pad_maximum_fusion.refs_0_), channel_id=1, source_target_pairs={{0,6},{1,3},{2,4},{3,1},{4,2},{5,7},{6,0},{7,5},{8,14},{9,11},{10,... | collective-permute-start | bytes 2752520 | tf_op jit(solution)/shard_map/ppermute | solution.py:355
  42.9 1.0 collective-permute-done.16
  44.0 1.9 %collective-permute-start.17 = (bf16[4,2,4,112,128]{4,3,2,1,0:T(8,128)(2,1)S(1)}, bf16[4,2,4,112,128]{4,3,2,1,0:T(8,128)(2,1)S(1)}, u32[]{:S(2)}, u32[]{:S(2)}) collective-permute-start(bf16[4,2,4,112,128]{4,3,2,1,0:T(8,128)(2,1)S(1)} %pad_maximum_fusion.1.refs_8_), channel_id=1, source_target_pairs={{0,64},{1,193},{64,0},{65,129},{128,192},{129,65},{192,128},{193,1... | collective-permute-start | bytes 2752520 | tf_op jit(solution)/shard_map/ppermute | solution.py:355
  45.9 0.8 collective-permute-start.18
  46.8 16.6 %collective-permute-done.8.refs_2_ = bf16[4,2,4,112,128]{4,3,2,1,0:T(8,128)(2,1)S(1)} collective-permute-done((bf16[4,2,4,112,128]{4,3,2,1,0:T(8,128)(2,1)S(1)}, bf16[4,2,4,112,128]{4,3,2,1,0:T(8,128)(2,1)S(1)}, u32[]{:S(2)}, u32[]{:S(2)}) %collective-permute-start.8) | collective-permute-done | bytes 917536 | tf_op jit(solution)/shard_map/ppermute | solution.py:355
  63.4 3.7 %collective-permute-start.9 = (bf16[4,2,4,112,128]{4,3,2,1,0:T(8,128)(2,1)S(1)}, bf16[4,2,4,112,128]{4,3,2,1,0:T(8,128)(2,1)S(1)}, u32[]{:S(2)}, u32[]{:S(2)}) collective-permute-start(bf16[4,2,4,112,128]{4,3,2,1,0:T(8,128)(2,1)S(1)} %collective-permute-done.7.refs_1_), channel_id=1, source_target_pairs={{0,6},{1,3},{2,4},{3,1},{4,2},{5,7},{6,0},{7,5},{8,14},{9,11},{10,... | collective-permute-start | bytes 2752520 | tf_op jit(solution)/shard_map/ppermute | solution.py:355
  67.1 1.7 %collective-permute-start.19 = (bf16[4,2,4,112,128]{4,3,2,1,0:T(8,128)(2,1)S(1)}, bf16[4,2,4,112,128]{4,3,2,1,0:T(8,128)(2,1)S(1)}, u32[]{:S(2)}, u32[]{:S(2)}) collective-permute-start(bf16[4,2,4,112,128]{4,3,2,1,0:T(8,128)(2,1)S(1)} %collective-permute-done.17.refs_9_), channel_id=1, source_target_pairs={{0,192},{1,65},{64,128},{65,1},{128,64},{129,193},{192,0},{193,129... | collective-permute-start | bytes 2752520 | tf_op jit(solution)/shard_map/ppermute | solution.py:355
  68.8 0.5 collective-permute-start.21
  69.3 0.3 collective-permute-start.22
  69.6 8.9 %collective-permute-done.9.refs_3_ = bf16[4,2,4,112,128]{4,3,2,1,0:T(8,128)(2,1)S(1)} collective-permute-done((bf16[4,2,4,112,128]{4,3,2,1,0:T(8,128)(2,1)S(1)}, bf16[4,2,4,112,128]{4,3,2,1,0:T(8,128)(2,1)S(1)}, u32[]{:S(2)}, u32[]{:S(2)}) %collective-permute-start.9) | collective-permute-done | bytes 917536 | tf_op jit(solution)/shard_map/ppermute | solution.py:355
  78.5 2.0 %collective-permute-done.19.refs_11_ = bf16[4,2,4,112,128]{4,3,2,1,0:T(8,128)(2,1)S(1)} collective-permute-done((bf16[4,2,4,112,128]{4,3,2,1,0:T(8,128)(2,1)S(1)}, bf16[4,2,4,112,128]{4,3,2,1,0:T(8,128)(2,1)S(1)}, u32[]{:S(2)}, u32[]{:S(2)}) %collective-permute-start.19) | collective-permute-done | bytes 917536 | tf_op jit(solution)/shard_map/ppermute | solution.py:355
  80.5 0.4 collective-permute-done.13.refs_7_
  80.9 2.0 %collective-permute-done.23.refs_15_ = bf16[4,2,4,112,128]{4,3,2,1,0:T(8,128)(2,1)S(1)} collective-permute-done((bf16[4,2,4,112,128]{4,3,2,1,0:T(8,128)(2,1)S(1)}, bf16[4,2,4,112,128]{4,3,2,1,0:T(8,128)(2,1)S(1)}, u32[]{:S(2)}, u32[]{:S(2)}) %collective-permute-start.23) | collective-permute-done | bytes 917536 | tf_op jit(solution)/shard_map/ppermute | solution.py:359
  83.0 23.3 %shard_map.93 = bf16[8,304,384]{2,1,0:T(8,128)(2,1)S(1)} custom-call(bf16[4,2,4,112,128]{4,3,2,1,0:T(8,128)(2,1)S(1)} %pad_maximum_fusion.refs_0_, bf16[4,2,4,112,128]{4,3,2,1,0:T(8,128)(2,1)S(1)} %collective-permute-done.7.refs_1_, bf16[4,2,4,112,128]{4,3,2,1,0:T(8,128)(2,1)S(1)} %collective-permute-done.8.refs_2_, ...), custom_call_target="tpu_custom_call" | custom-call | flops 8000000000 | bytes 30000000 | tf_op jit(solution)/shard_map/pallas_call | solution.py:409
  106.2 28.5 %all_to_all.5.got_ref = bf16[8,304,384]{2,1,0:T(8,128)(2,1)S(1)} all-to-all(bf16[8,304,384]{2,1,0:T(8,128)(2,1)S(1)} %shard_map.93), channel_id=1, replica_groups={{0,32,64,96,128,160,192,224},{1,57,65,121,129,185,193,249},{2,34,66,98,..., dimensions={0} | all-to-all | bytes 3735552 | tf_op jit(solution)/shard_map/all_to_all | solution.py:438
  134.7 3.4 %shard_map.94 = (bf16[4,4,112,256]{3,2,1,0:T(8,128)(2,1)S(1)}, bf16[4,4,112,256]{3,2,1,0:T(8,128)(2,1)S(1)}) custom-call(bf16[8,304,384]{2,1,0:T(8,128)(2,1)S(1)} %all_to_all.5.got_ref), custom_call_target="tpu_custom_call" | custom-call | flops 600000000 | bytes 4000000 | tf_op jit(solution)/shard_map/pallas_call | solution.py:442
  138.3 2.5 %collective-permute-done.24 = bf16[4,4,112,256]{3,2,1,0:T(8,128)(2,1)S(1)} collective-permute-done((bf16[4,4,112,256]{3,2,1,0:T(8,128)(2,1)S(1)}, bf16[4,4,112,256]{3,2,1,0:T(8,128)(2,1)S(1)}, u32[]{:S(2)}, u32[]{:S(2)}) %collective-permute-start.24) | collective-permute-done | bytes 917536 | tf_op jit(solution)/shard_map/ppermute | solution.py:359
  140.7 0.3 add_convert_fusion.1
  141.0 0.8 collective-permute-start.25
  141.8 7.8 %collective-permute-done.25 = bf16[2,4,112,256]{3,2,1,0:T(8,128)(2,1)S(1)} collective-permute-done((bf16[2,4,112,256]{3,2,1,0:T(8,128)(2,1)S(1)}, bf16[2,4,112,256]{3,2,1,0:T(8,128)(2,1)S(1)}, u32[]{:S(2)}, u32[]{:S(2)}) %collective-permute-start.25) | collective-permute-done | bytes 458784 | tf_op jit(solution)/shard_map/ppermute | solution.py:355
  149.6 2.6 %collective-permute-start.26 = (bf16[4,112,256]{2,1,0:T(8,128)(2,1)S(1)}, bf16[4,112,256]{2,1,0:T(8,128)(2,1)S(1)}, u32[]{:S(2)}, u32[]{:S(2)}) collective-permute-start(bf16[4,112,256]{2,1,0:T(8,128)(2,1)S(1)} %fusion.2), channel_id=1, source_target_pairs={{0,6},{1,3},{2,4},{3,1},{4,2},{5,7},{6,0},{7,5},{8,14},{9,11},{10,... | collective-permute-start | bytes 688136 | tf_op jit(solution)/shard_map/ppermute | solution.py:355
  152.2 4.7 %collective-permute-done.26 = bf16[4,112,256]{2,1,0:T(8,128)(2,1)S(1)} collective-permute-done((bf16[4,112,256]{2,1,0:T(8,128)(2,1)S(1)}, bf16[4,112,256]{2,1,0:T(8,128)(2,1)S(1)}, u32[]{:S(2)}, u32[]{:S(2)}) %collective-permute-start.26) | collective-permute-done | bytes 229408 | tf_op jit(solution)/shard_map/ppermute | solution.py:355
  157.1 2.1 %collective-permute-start.29 = (bf16[112,256]{1,0:T(8,128)(2,1)S(1)}, bf16[112,256]{1,0:T(8,128)(2,1)S(1)}, u32[]{:S(2)}, u32[]{:S(2)}) collective-permute-start(bf16[112,256]{1,0:T(8,128)(2,1)S(1)} %get-tuple-element.22), channel_id=1, source_target_pairs={{0,16},{8,24},{16,0},{24,8},{1,17},{9,25},{17,1},{25,9},{2,18},{10... | collective-permute-start | bytes 172040 | tf_op jit(solution)/shard_map/ppermute | solution.py:363
  159.2 4.0 %collective-permute-start.28 = (bf16[112,256]{1,0:T(8,128)(2,1)S(1)}, bf16[112,256]{1,0:T(8,128)(2,1)S(1)}, u32[]{:S(2)}, u32[]{:S(2)}) collective-permute-start(bf16[112,256]{1,0:T(8,128)(2,1)S(1)} %get-tuple-element.23), channel_id=1, source_target_pairs={{0,24},{1,9},{8,16},{9,1},{16,8},{17,25},{24,0},{25,17},{2,26},{3,... | collective-permute-start | bytes 172040 | tf_op jit(solution)/shard_map/ppermute | solution.py:355
  163.2 0.4 collective-permute-start.27
  163.6 1.7 collective-permute-done.29.d_ref
  165.3 1.7 %collective-permute-done.28.c_ref = bf16[112,256]{1,0:T(8,128)(2,1)S(1)} collective-permute-done((bf16[112,256]{1,0:T(8,128)(2,1)S(1)}, bf16[112,256]{1,0:T(8,128)(2,1)S(1)}, u32[]{:S(2)}, u32[]{:S(2)}) %collective-permute-start.28) | collective-permute-done | bytes 57376 | tf_op jit(solution)/shard_map/ppermute | solution.py:355
  167.1 1.2 collective-permute-done.27.b_ref
  168.3 0.7 shard_map.95
  (38 shorter events, 1.3 us)
Async XLA Ops:
  1.6 11.5 %collective-permute-start.1 = (bf16[112,256]{1,0:T(8,128)(2,1)S(1)}, bf16[112,256]{1,0:T(8,128)(2,1)S(1)}, u32[]{:S(2)}, u32[]{:S(2)}) collective-permute-start(bf16[112,256]{1,0:T(8,128)(2,1)S(1)} %fusion.6), channel_id=1, source_target_pairs={{0,24},{1,9},{8,16},{9,1},{16,8},{17,25},{24,0},{25,17},{2,26},{3,... | collective-permute-start | bytes 172040 | tf_op jit(solution)/shard_map/ppermute | solution.py:355
  7.9 6.3 %collective-permute-start = (bf16[112,256]{1,0:T(8,128)(2,1)S(1)}, bf16[112,256]{1,0:T(8,128)(2,1)S(1)}, u32[]{:S(2)}, u32[]{:S(2)}) collective-permute-start(bf16[112,256]{1,0:T(8,128)(2,1)S(1)} %fusion.6), channel_id=1, source_target_pairs={{0,8},{1,25},{8,0},{9,17},{16,24},{17,9},{24,16},{25,1},{2,10},{3,... | collective-permute-start | bytes 172040 | tf_op jit(solution)/shard_map/ppermute | solution.py:355
  9.4 8.5 %collective-permute-start.2 = (bf16[112,256]{1,0:T(8,128)(2,1)S(1)}, bf16[112,256]{1,0:T(8,128)(2,1)S(1)}, u32[]{:S(2)}, u32[]{:S(2)}) collective-permute-start(bf16[112,256]{1,0:T(8,128)(2,1)S(1)} %fusion.6), channel_id=1, source_target_pairs={{0,16},{8,24},{16,0},{24,8},{1,17},{9,25},{17,1},{25,9},{2,18},{10... | collective-permute-start | bytes 172040 | tf_op jit(solution)/shard_map/ppermute | solution.py:363
  18.5 6.1 %collective-permute-start.3 = (bf16[4,112,256]{2,1,0:T(8,128)(2,1)S(1)}, bf16[4,112,256]{2,1,0:T(8,128)(2,1)S(1)}, u32[]{:S(2)}, u32[]{:S(2)}) collective-permute-start(bf16[4,112,256]{2,1,0:T(8,128)(2,1)S(1)} %broadcast_select_fusion), channel_id=1, source_target_pairs={{0,32},{1,57},{32,0},{33,9},{8,40},{9,33},{40,8},{41,17},{16,48},{... | collective-permute-start | bytes 688136 | tf_op jit(solution)/shard_map/ppermute | solution.py:399
  24.9 58.1 %copy-start = (bf16[2,3,32,3072]{3,2,1,0:T(8,128)(2,1)S(1)}, bf16[2,3,32,3072]{3,2,1,0:T(8,128)(2,1)}, u32[]{:S(2)}) copy-start(bf16[2,3,32,3072]{3,2,1,0:T(8,128)(2,1)} %refs_16_.1) | copy-start | bytes 3538948
  24.9 58.1 %copy-start.1 = (bf16[2,3,32,3072]{3,2,1,0:T(8,128)(2,1)S(1)}, bf16[2,3,32,3072]{3,2,1,0:T(8,128)(2,1)}, u32[]{:S(2)}) copy-start(bf16[2,3,32,3072]{3,2,1,0:T(8,128)(2,1)} %refs_17_.1) | copy-start | bytes 3538948
  24.9 6.7 %collective-permute-start.4 = (bf16[2,4,112,128]{3,2,1,0:T(8,128)(2,1)S(1)}, bf16[2,4,112,128]{3,2,1,0:T(8,128)(2,1)S(1)}, u32[]{:S(2)}, u32[]{:S(2)}) collective-permute-start(bf16[2,4,112,128]{3,2,1,0:T(8,128)(2,1)S(1)} %get-tuple-element.21), channel_id=1, source_target_pairs={{0,64},{1,193},{64,0},{65,129},{128,192},{129,65},{192,128},{193,1... | collective-permute-start | bytes 688136 | tf_op jit(solution)/shard_map/ppermute | solution.py:355
  25.5 10.9 %collective-permute-start.14 = (bf16[2,4,112,128]{3,2,1,0:T(8,128)(2,1)S(1)}, bf16[2,4,112,128]{3,2,1,0:T(8,128)(2,1)S(1)}, u32[]{:S(2)}, u32[]{:S(2)}) collective-permute-start(bf16[2,4,112,128]{3,2,1,0:T(8,128)(2,1)S(1)} %get-tuple-element.20), channel_id=1, source_target_pairs={{0,2},{1,7},{2,0},{3,5},{4,6},{5,3},{6,4},{7,1},{8,10},{9,15},{10,... | collective-permute-start | bytes 688136 | tf_op jit(solution)/shard_map/ppermute | solution.py:355
  27.1 10.3 %collective-permute-start.5 = (bf16[2,4,112,128]{3,2,1,0:T(8,128)(2,1)S(1)}, bf16[2,4,112,128]{3,2,1,0:T(8,128)(2,1)S(1)}, u32[]{:S(2)}, u32[]{:S(2)}) collective-permute-start(bf16[2,4,112,128]{3,2,1,0:T(8,128)(2,1)S(1)} %get-tuple-element.21), channel_id=1, source_target_pairs={{0,192},{1,65},{64,128},{65,1},{128,64},{129,193},{192,0},{193,129... | collective-permute-start | bytes 688136 | tf_op jit(solution)/shard_map/ppermute | solution.py:355
  31.6 6.6 %collective-permute-start.6 = (bf16[2,4,112,128]{3,2,1,0:T(8,128)(2,1)S(1)}, bf16[2,4,112,128]{3,2,1,0:T(8,128)(2,1)S(1)}, u32[]{:S(2)}, u32[]{:S(2)}) collective-permute-start(bf16[2,4,112,128]{3,2,1,0:T(8,128)(2,1)S(1)} %collective-permute-done.4), channel_id=1, source_target_pairs={{0,192},{1,65},{64,128},{65,1},{128,64},{129,193},{192,0},{193,129... | collective-permute-start | bytes 688136 | tf_op jit(solution)/shard_map/ppermute | solution.py:355
  34.2 8.7 %collective-permute-start.15 = (bf16[2,4,112,128]{3,2,1,0:T(8,128)(2,1)S(1)}, bf16[2,4,112,128]{3,2,1,0:T(8,128)(2,1)S(1)}, u32[]{:S(2)}, u32[]{:S(2)}) collective-permute-start(bf16[2,4,112,128]{3,2,1,0:T(8,128)(2,1)S(1)} %get-tuple-element.20), channel_id=1, source_target_pairs={{0,6},{1,3},{2,4},{3,1},{4,2},{5,7},{6,0},{7,5},{8,14},{9,11},{10,... | collective-permute-start | bytes 688136 | tf_op jit(solution)/shard_map/ppermute | solution.py:355
  36.4 7.4 %collective-permute-start.16 = (bf16[2,4,112,128]{3,2,1,0:T(8,128)(2,1)S(1)}, bf16[2,4,112,128]{3,2,1,0:T(8,128)(2,1)S(1)}, u32[]{:S(2)}, u32[]{:S(2)}) collective-permute-start(bf16[2,4,112,128]{3,2,1,0:T(8,128)(2,1)S(1)} %collective-permute-done.14), channel_id=1, source_target_pairs={{0,6},{1,3},{2,4},{3,1},{4,2},{5,7},{6,0},{7,5},{8,14},{9,11},{10,... | collective-permute-start | bytes 688136 | tf_op jit(solution)/shard_map/ppermute | solution.py:355
  38.3 7.6 %collective-permute-start.10 = (bf16[4,2,4,112,128]{4,3,2,1,0:T(8,128)(2,1)S(1)}, bf16[4,2,4,112,128]{4,3,2,1,0:T(8,128)(2,1)S(1)}, u32[]{:S(2)}, u32[]{:S(2)}) collective-permute-start(bf16[4,2,4,112,128]{4,3,2,1,0:T(8,128)(2,1)S(1)} %pad_maximum_fusion.refs_0_), channel_id=1, source_target_pairs={{0,1},{1,0},{2,3},{3,2},{4,5},{5,4},{6,7},{7,6},{8,9},{9,8},{10,11... | collective-permute-start | bytes 2752520 | tf_op jit(solution)/shard_map/ppermute | solution.py:359
  38.4 25.0 %collective-permute-start.8 = (bf16[4,2,4,112,128]{4,3,2,1,0:T(8,128)(2,1)S(1)}, bf16[4,2,4,112,128]{4,3,2,1,0:T(8,128)(2,1)S(1)}, u32[]{:S(2)}, u32[]{:S(2)}) collective-permute-start(bf16[4,2,4,112,128]{4,3,2,1,0:T(8,128)(2,1)S(1)} %pad_maximum_fusion.refs_0_), channel_id=1, source_target_pairs={{0,6},{1,3},{2,4},{3,1},{4,2},{5,7},{6,0},{7,5},{8,14},{9,11},{10,... | collective-permute-start | bytes 2752520 | tf_op jit(solution)/shard_map/ppermute | solution.py:355
  42.8 20.6 %collective-permute-start.7 = (bf16[4,2,4,112,128]{4,3,2,1,0:T(8,128)(2,1)S(1)}, bf16[4,2,4,112,128]{4,3,2,1,0:T(8,128)(2,1)S(1)}, u32[]{:S(2)}, u32[]{:S(2)}) collective-permute-start(bf16[4,2,4,112,128]{4,3,2,1,0:T(8,128)(2,1)S(1)} %pad_maximum_fusion.refs_0_), channel_id=1, source_target_pairs={{0,2},{1,7},{2,0},{3,5},{4,6},{5,3},{6,4},{7,1},{8,10},{9,15},{10,... | collective-permute-start | bytes 2752520 | tf_op jit(solution)/shard_map/ppermute | solution.py:355
  44.0 23.1 %collective-permute-start.17 = (bf16[4,2,4,112,128]{4,3,2,1,0:T(8,128)(2,1)S(1)}, bf16[4,2,4,112,128]{4,3,2,1,0:T(8,128)(2,1)S(1)}, u32[]{:S(2)}, u32[]{:S(2)}) collective-permute-start(bf16[4,2,4,112,128]{4,3,2,1,0:T(8,128)(2,1)S(1)} %pad_maximum_fusion.1.refs_8_), channel_id=1, source_target_pairs={{0,64},{1,193},{64,0},{65,129},{128,192},{129,65},{192,128},{193,1... | collective-permute-start | bytes 2752520 | tf_op jit(solution)/shard_map/ppermute | solution.py:355
  45.9 22.9 %collective-permute-start.20 = (bf16[4,2,4,112,128]{4,3,2,1,0:T(8,128)(2,1)S(1)}, bf16[4,2,4,112,128]{4,3,2,1,0:T(8,128)(2,1)S(1)}, u32[]{:S(2)}, u32[]{:S(2)}) collective-permute-start(bf16[4,2,4,112,128]{4,3,2,1,0:T(8,128)(2,1)S(1)} %pad_maximum_fusion.1.refs_8_), channel_id=1, source_target_pairs={{0,1},{1,0},{2,3},{3,2},{4,5},{5,4},{6,7},{7,6},{8,9},{9,8},{10,11... | collective-permute-start | bytes 2752520 | tf_op jit(solution)/shard_map/ppermute | solution.py:359
  45.9 22.9 %collective-permute-start.18 = (bf16[4,2,4,112,128]{4,3,2,1,0:T(8,128)(2,1)S(1)}, bf16[4,2,4,112,128]{4,3,2,1,0:T(8,128)(2,1)S(1)}, u32[]{:S(2)}, u32[]{:S(2)}) collective-permute-start(bf16[4,2,4,112,128]{4,3,2,1,0:T(8,128)(2,1)S(1)} %pad_maximum_fusion.1.refs_8_), channel_id=1, source_target_pairs={{0,192},{1,65},{64,128},{65,1},{128,64},{129,193},{192,0},{193,129... | collective-permute-start | bytes 2752520 | tf_op jit(solution)/shard_map/ppermute | solution.py:355
  63.4 5.9 %collective-permute-start.12 = (bf16[4,2,4,112,128]{4,3,2,1,0:T(8,128)(2,1)S(1)}, bf16[4,2,4,112,128]{4,3,2,1,0:T(8,128)(2,1)S(1)}, u32[]{:S(2)}, u32[]{:S(2)}) collective-permute-start(bf16[4,2,4,112,128]{4,3,2,1,0:T(8,128)(2,1)S(1)} %collective-permute-done.8.refs_2_), channel_id=1, source_target_pairs={{0,1},{1,0},{2,3},{3,2},{4,5},{5,4},{6,7},{7,6},{8,9},{9,8},{10,11... | collective-permute-start | bytes 2752520 | tf_op jit(solution)/shard_map/ppermute | solution.py:359
  63.4 15.1 %collective-permute-start.9 = (bf16[4,2,4,112,128]{4,3,2,1,0:T(8,128)(2,1)S(1)}, bf16[4,2,4,112,128]{4,3,2,1,0:T(8,128)(2,1)S(1)}, u32[]{:S(2)}, u32[]{:S(2)}) collective-permute-start(bf16[4,2,4,112,128]{4,3,2,1,0:T(8,128)(2,1)S(1)} %collective-permute-done.7.refs_1_), channel_id=1, source_target_pairs={{0,6},{1,3},{2,4},{3,1},{4,2},{5,7},{6,0},{7,5},{8,14},{9,11},{10,... | collective-permute-start | bytes 2752520 | tf_op jit(solution)/shard_map/ppermute | solution.py:355
  67.1 13.4 %collective-permute-start.19 = (bf16[4,2,4,112,128]{4,3,2,1,0:T(8,128)(2,1)S(1)}, bf16[4,2,4,112,128]{4,3,2,1,0:T(8,128)(2,1)S(1)}, u32[]{:S(2)}, u32[]{:S(2)}) collective-permute-start(bf16[4,2,4,112,128]{4,3,2,1,0:T(8,128)(2,1)S(1)} %collective-permute-done.17.refs_9_), channel_id=1, source_target_pairs={{0,192},{1,65},{64,128},{65,1},{128,64},{129,193},{192,0},{193,129... | collective-permute-start | bytes 2752520 | tf_op jit(solution)/shard_map/ppermute | solution.py:355
  68.8 11.7 %collective-permute-start.11 = (bf16[4,2,4,112,128]{4,3,2,1,0:T(8,128)(2,1)S(1)}, bf16[4,2,4,112,128]{4,3,2,1,0:T(8,128)(2,1)S(1)}, u32[]{:S(2)}, u32[]{:S(2)}) collective-permute-start(bf16[4,2,4,112,128]{4,3,2,1,0:T(8,128)(2,1)S(1)} %collective-permute-done.7.refs_1_), channel_id=1, source_target_pairs={{0,1},{1,0},{2,3},{3,2},{4,5},{5,4},{6,7},{7,6},{8,9},{9,8},{10,11... | collective-permute-start | bytes 2752520 | tf_op jit(solution)/shard_map/ppermute | solution.py:359
  68.8 11.7 %collective-permute-start.21 = (bf16[4,2,4,112,128]{4,3,2,1,0:T(8,128)(2,1)S(1)}, bf16[4,2,4,112,128]{4,3,2,1,0:T(8,128)(2,1)S(1)}, u32[]{:S(2)}, u32[]{:S(2)}) collective-permute-start(bf16[4,2,4,112,128]{4,3,2,1,0:T(8,128)(2,1)S(1)} %collective-permute-done.17.refs_9_), channel_id=1, source_target_pairs={{0,1},{1,0},{2,3},{3,2},{4,5},{5,4},{6,7},{7,6},{8,9},{9,8},{10,11... | collective-permute-start | bytes 2752520 | tf_op jit(solution)/shard_map/ppermute | solution.py:359
  69.3 11.2 %collective-permute-start.22 = (bf16[4,2,4,112,128]{4,3,2,1,0:T(8,128)(2,1)S(1)}, bf16[4,2,4,112,128]{4,3,2,1,0:T(8,128)(2,1)S(1)}, u32[]{:S(2)}, u32[]{:S(2)}) collective-permute-start(bf16[4,2,4,112,128]{4,3,2,1,0:T(8,128)(2,1)S(1)} %collective-permute-done.18.refs_10_), channel_id=1, source_target_pairs={{0,1},{1,0},{2,3},{3,2},{4,5},{5,4},{6,7},{7,6},{8,9},{9,8},{10,11... | collective-permute-start | bytes 2752520 | tf_op jit(solution)/shard_map/ppermute | solution.py:359
  78.5 2.5 %collective-permute-start.13 = (bf16[4,2,4,112,128]{4,3,2,1,0:T(8,128)(2,1)S(1)}, bf16[4,2,4,112,128]{4,3,2,1,0:T(8,128)(2,1)S(1)}, u32[]{:S(2)}, u32[]{:S(2)}) collective-permute-start(bf16[4,2,4,112,128]{4,3,2,1,0:T(8,128)(2,1)S(1)} %collective-permute-done.9.refs_3_), channel_id=1, source_target_pairs={{0,1},{1,0},{2,3},{3,2},{4,5},{5,4},{6,7},{7,6},{8,9},{9,8},{10,11... | collective-permute-start | bytes 2752520 | tf_op jit(solution)/shard_map/ppermute | solution.py:359
  80.5 2.5 %collective-permute-start.23 = (bf16[4,2,4,112,128]{4,3,2,1,0:T(8,128)(2,1)S(1)}, bf16[4,2,4,112,128]{4,3,2,1,0:T(8,128)(2,1)S(1)}, u32[]{:S(2)}, u32[]{:S(2)}) collective-permute-start(bf16[4,2,4,112,128]{4,3,2,1,0:T(8,128)(2,1)S(1)} %collective-permute-done.19.refs_11_), channel_id=1, source_target_pairs={{0,1},{1,0},{2,3},{3,2},{4,5},{5,4},{6,7},{7,6},{8,9},{9,8},{10,11... | collective-permute-start | bytes 2752520 | tf_op jit(solution)/shard_map/ppermute | solution.py:359
  138.2 2.6 %collective-permute-start.24 = (bf16[4,4,112,256]{3,2,1,0:T(8,128)(2,1)S(1)}, bf16[4,4,112,256]{3,2,1,0:T(8,128)(2,1)S(1)}, u32[]{:S(2)}, u32[]{:S(2)}) collective-permute-start(bf16[4,4,112,256]{3,2,1,0:T(8,128)(2,1)S(1)} %get-tuple-element.11), channel_id=1, source_target_pairs={{0,1},{1,0},{2,3},{3,2},{4,5},{5,4},{6,7},{7,6},{8,9},{9,8},{10,11... | collective-permute-start | bytes 2752520 | tf_op jit(solution)/shard_map/ppermute | solution.py:359
  141.0 8.6 %collective-permute-start.25 = (bf16[2,4,112,256]{3,2,1,0:T(8,128)(2,1)S(1)}, bf16[2,4,112,256]{3,2,1,0:T(8,128)(2,1)S(1)}, u32[]{:S(2)}, u32[]{:S(2)}) collective-permute-start(bf16[2,4,112,256]{3,2,1,0:T(8,128)(2,1)S(1)} %get-tuple-element.17), channel_id=1, source_target_pairs={{0,2},{1,7},{2,0},{3,5},{4,6},{5,3},{6,4},{7,1},{8,10},{9,15},{10,... | collective-permute-start | bytes 1376264 | tf_op jit(solution)/shard_map/ppermute | solution.py:355
  149.6 7.3 %collective-permute-start.26 = (bf16[4,112,256]{2,1,0:T(8,128)(2,1)S(1)}, bf16[4,112,256]{2,1,0:T(8,128)(2,1)S(1)}, u32[]{:S(2)}, u32[]{:S(2)}) collective-permute-start(bf16[4,112,256]{2,1,0:T(8,128)(2,1)S(1)} %fusion.2), channel_id=1, source_target_pairs={{0,6},{1,3},{2,4},{3,1},{4,2},{5,7},{6,0},{7,5},{8,14},{9,11},{10,... | collective-permute-start | bytes 688136 | tf_op jit(solution)/shard_map/ppermute | solution.py:355
  157.1 8.3 %collective-permute-start.29 = (bf16[112,256]{1,0:T(8,128)(2,1)S(1)}, bf16[112,256]{1,0:T(8,128)(2,1)S(1)}, u32[]{:S(2)}, u32[]{:S(2)}) collective-permute-start(bf16[112,256]{1,0:T(8,128)(2,1)S(1)} %get-tuple-element.22), channel_id=1, source_target_pairs={{0,16},{8,24},{16,0},{24,8},{1,17},{9,25},{17,1},{25,9},{2,18},{10... | collective-permute-start | bytes 172040 | tf_op jit(solution)/shard_map/ppermute | solution.py:363
  159.2 7.9 %collective-permute-start.28 = (bf16[112,256]{1,0:T(8,128)(2,1)S(1)}, bf16[112,256]{1,0:T(8,128)(2,1)S(1)}, u32[]{:S(2)}, u32[]{:S(2)}) collective-permute-start(bf16[112,256]{1,0:T(8,128)(2,1)S(1)} %get-tuple-element.23), channel_id=1, source_target_pairs={{0,24},{1,9},{8,16},{9,1},{16,8},{17,25},{24,0},{25,17},{2,26},{3,... | collective-permute-start | bytes 172040 | tf_op jit(solution)/shard_map/ppermute | solution.py:355
  163.2 5.1 %collective-permute-start.27 = (bf16[112,256]{1,0:T(8,128)(2,1)S(1)}, bf16[112,256]{1,0:T(8,128)(2,1)S(1)}, u32[]{:S(2)}, u32[]{:S(2)}) collective-permute-start(bf16[112,256]{1,0:T(8,128)(2,1)S(1)} %get-tuple-element.24), channel_id=1, source_target_pairs={{0,8},{1,25},{8,0},{9,17},{16,24},{17,9},{24,16},{25,1},{2,10},{3,... | collective-permute-start | bytes 172040 | tf_op jit(solution)/shard_map/ppermute | solution.py:355

commit v9 on v8

--- a/solution.py
+++ b/solution.py
@@ -399,8 +399,8 @@
     other = lax.ppermute(along, ("zl", "zh", "c"), pairs)
     both = jnp.where(zl == 0, jnp.stack([along, other]), jnp.stack([other, along]))
 
-    left = jnp.stack(gather_ring(both[..., :C], "x"))
-    right = jnp.stack(gather_ring(both[..., C:], "y"))
+    left = jnp.stack(gather_ring(both[..., :C], "x", direct=True))
+    right = jnp.stack(gather_ring(both[..., C:], "y", direct=True))
     left = gather_ring(left, "y")
     right = gather_ring(right, "x")
     left = left + [other_core(a) for a in left]

time: 170 us -> 174 us (1.024); the launches traced: 169 us -> 171 us
  waiting for transfers between devices: 64.8 us -> 66.8 us
    ppermute x18 -> x16, starting transfers between devices: 38.5 us -> 32.9 us  [swap(): return lax.ppermute(array, (axis, 'c'), ring_pairs(first))]
    ppermute x2 -> x4, starting transfers between devices: 3.11 us -> 7.42 us  [opposite(): return lax.ppermute(array, axis, [(i, i ^ 2) for i in range(4)])]
    ppermute x2 -> x4, waiting for transfers between devices: 5.31 us -> 9.34 us  [opposite(): return lax.ppermute(array, axis, [(i, i ^ 2) for i in range(4)])]
    ppermute x18 -> x16, waiting for transfers between devices: 49.8 us -> 47.7 us  [swap(): return lax.ppermute(array, (axis, 'c'), ring_pairs(first))]
  transfers between devices with their start and end apart: 30 -> 30, of which waited for: 18 -> 16; matrix products, arithmetic and copies ran while one was open for 1% -> 1% of each run, Pallas kernels for 0% -> 0%
where the time goes in v9:
time: 174 us; the launch traced here: 171 us
  waiting for transfers between devices  66.8 us (38%)
  starting transfers between devices  42.5 us (24%)
  blocking collectives  29.6 us (17%)
  Pallas kernels  27.4 us (16%)
  other arithmetic  2.97 us (2%)
    ppermute x16, waiting for transfers between devices, swap(): return lax.ppermute(array, (axis, 'c'), ring_pairs(first))  47.7 us
    ppermute x16, starting transfers between devices, swap(): return lax.ppermute(array, (axis, 'c'), ring_pairs(first))  32.9 us
    all_to_all x1, blocking collectives, per_device(): lax.all_to_all(sent, ('x', 'zl', 'zh', 'y', 'c'), 0, 0, axis_index_groups...  29.6 us
    pallas_call x1, Pallas kernels, per_device(): call(sequence_kernel, [shape(LAYERS, SENT, BLOCK)], [VMEM] * 16 + [ANY] *...  23.3 us
    ppermute x4, waiting for transfers between devices, opposite(): return lax.ppermute(array, axis, [(i, i ^ 2) for i in range(4)])  9.34 us
    ppermute x4, starting transfers between devices, opposite(): return lax.ppermute(array, axis, [(i, i ^ 2) for i in range(4)])  7.42 us
    ppermute x9, waiting for transfers between devices, other_core(): return lax.ppermute(array, 'c', [(0, 1), (1, 0)])  4.92 us
    ppermute x1, waiting for transfers between devices, per_device(): other = lax.ppermute(along, ('zl', 'zh', 'c'), pairs)  4.83 us
  transfers between devices with their start and end apart: 30, of which 16 were waited for; matrix products, arithmetic and copies ran while one was open for 1% of the time, Pallas kernels for 0%

profile of v9, /device:TPU:2, one launch (start us, length us, event | category | flops | bytes accessed | tf_op | source)
XLA Modules:
  0.0 170.7 jit_solution(3285279536216017107)
XLA Ops:
  0.6 0.9 fusion.6
  1.6 6.3 %collective-permute-start.1 = (bf16[112,256]{1,0:T(8,128)(2,1)S(1)}, bf16[112,256]{1,0:T(8,128)(2,1)S(1)}, u32[]{:S(2)}, u32[]{:S(2)}) collective-permute-start(bf16[112,256]{1,0:T(8,128)(2,1)S(1)} %fusion.6), channel_id=1, source_target_pairs={{0,24},{1,9},{8,16},{9,1},{16,8},{17,25},{24,0},{25,17},{2,26},{3,... | collective-permute-start | bytes 172040 | tf_op jit(solution)/shard_map/ppermute | solution.py:355
  7.9 1.5 collective-permute-start
  9.4 1.0 collective-permute-start.2
  10.4 0.9 fusion.8
  11.5 1.6 collective-permute-done.1
  13.1 1.1 collective-permute-done
  14.2 3.6 %collective-permute-done.2 = bf16[112,256]{1,0:T(8,128)(2,1)S(1)} collective-permute-done((bf16[112,256]{1,0:T(8,128)(2,1)S(1)}, bf16[112,256]{1,0:T(8,128)(2,1)S(1)}, u32[]{:S(2)}, u32[]{:S(2)}) %collective-permute-start.2) | collective-permute-done | bytes 57376 | tf_op jit(solution)/shard_map/ppermute | solution.py:363
  17.9 0.6 gather_fusion
  18.5 1.2 collective-permute-start.3
  19.8 4.8 %collective-permute-done.3 = bf16[4,112,256]{2,1,0:T(8,128)(2,1)S(1)} collective-permute-done((bf16[4,112,256]{2,1,0:T(8,128)(2,1)S(1)}, bf16[4,112,256]{2,1,0:T(8,128)(2,1)S(1)}, u32[]{:S(2)}, u32[]{:S(2)}) %collective-permute-start.3) | collective-permute-done | bytes 229408 | tf_op jit(solution)/shard_map/ppermute | solution.py:399
  24.7 0.1 slice_bitcast_fusion.4
  24.9 1.6 collective-permute-start.5
  26.5 1.8 %collective-permute-start.4 = (bf16[2,4,112,128]{3,2,1,0:T(8,128)(2,1)S(1)}, bf16[2,4,112,128]{3,2,1,0:T(8,128)(2,1)S(1)}, u32[]{:S(2)}, u32[]{:S(2)}) collective-permute-start(bf16[2,4,112,128]{3,2,1,0:T(8,128)(2,1)S(1)} %get-tuple-element.21), channel_id=1, source_target_pairs={{0,64},{1,193},{64,0},{65,129},{128,192},{129,65},{192,128},{193,1... | collective-permute-start | bytes 688136 | tf_op jit(solution)/shard_map/ppermute | solution.py:355
  28.3 0.2 collective-permute-start.6
  28.5 3.0 %collective-permute-start.15 = (bf16[2,4,112,128]{3,2,1,0:T(8,128)(2,1)S(1)}, bf16[2,4,112,128]{3,2,1,0:T(8,128)(2,1)S(1)}, u32[]{:S(2)}, u32[]{:S(2)}) collective-permute-start(bf16[2,4,112,128]{3,2,1,0:T(8,128)(2,1)S(1)} %get-tuple-element.20), channel_id=1, source_target_pairs={{0,6},{1,3},{2,4},{3,1},{4,2},{5,7},{6,0},{7,5},{8,14},{9,11},{10,... | collective-permute-start | bytes 688136 | tf_op jit(solution)/shard_map/ppermute | solution.py:355
  31.5 0.1 collective-permute-start.14
  31.6 4.5 %collective-permute-done.5 = bf16[2,4,112,128]{3,2,1,0:T(8,128)(2,1)S(1)} collective-permute-done((bf16[2,4,112,128]{3,2,1,0:T(8,128)(2,1)S(1)}, bf16[2,4,112,128]{3,2,1,0:T(8,128)(2,1)S(1)}, u32[]{:S(2)}, u32[]{:S(2)}) %collective-permute-start.5) | collective-permute-done | bytes 229408 | tf_op jit(solution)/shard_map/ppermute | solution.py:355
  36.1 3.2 %collective-permute-start.16 = (bf16[2,4,112,128]{3,2,1,0:T(8,128)(2,1)S(1)}, bf16[2,4,112,128]{3,2,1,0:T(8,128)(2,1)S(1)}, u32[]{:S(2)}, u32[]{:S(2)}) collective-permute-start(bf16[2,4,112,128]{3,2,1,0:T(8,128)(2,1)S(1)} %get-tuple-element.20), channel_id=1, source_target_pairs={{0,4},{2,6},{4,0},{6,2},{1,5},{3,7},{5,1},{7,3},{8,12},{10,14},{12... | collective-permute-start | bytes 688136 | tf_op jit(solution)/shard_map/ppermute | solution.py:363
  39.3 0.1 pad_maximum_fusion.refs_0_
  39.5 1.1 collective-permute-start.8
  40.7 0.1 collective-permute-start.7
  40.8 4.1 %collective-permute-done.16 = bf16[2,4,112,128]{3,2,1,0:T(8,128)(2,1)S(1)} collective-permute-done((bf16[2,4,112,128]{3,2,1,0:T(8,128)(2,1)S(1)}, bf16[2,4,112,128]{3,2,1,0:T(8,128)(2,1)S(1)}, u32[]{:S(2)}, u32[]{:S(2)}) %collective-permute-start.16) | collective-permute-done | bytes 229408 | tf_op jit(solution)/shard_map/ppermute | solution.py:363
  45.1 3.1 %collective-permute-start.17 = (bf16[4,2,4,112,128]{4,3,2,1,0:T(8,128)(2,1)S(1)}, bf16[4,2,4,112,128]{4,3,2,1,0:T(8,128)(2,1)S(1)}, u32[]{:S(2)}, u32[]{:S(2)}) collective-permute-start(bf16[4,2,4,112,128]{4,3,2,1,0:T(8,128)(2,1)S(1)} %pad_maximum_fusion.1.refs_8_), channel_id=1, source_target_pairs={{0,64},{1,193},{64,0},{65,129},{128,192},{129,65},{192,128},{193,1... | collective-permute-start | bytes 2752520 | tf_op jit(solution)/shard_map/ppermute | solution.py:355
  48.2 1.5 collective-permute-start.18
  49.7 14.2 %collective-permute-done.8.refs_2_ = bf16[4,2,4,112,128]{4,3,2,1,0:T(8,128)(2,1)S(1)} collective-permute-done((bf16[4,2,4,112,128]{4,3,2,1,0:T(8,128)(2,1)S(1)}, bf16[4,2,4,112,128]{4,3,2,1,0:T(8,128)(2,1)S(1)}, u32[]{:S(2)}, u32[]{:S(2)}) %collective-permute-start.8) | collective-permute-done | bytes 917536 | tf_op jit(solution)/shard_map/ppermute | solution.py:355
  63.9 2.4 %collective-permute-start.9 = (bf16[4,2,4,112,128]{4,3,2,1,0:T(8,128)(2,1)S(1)}, bf16[4,2,4,112,128]{4,3,2,1,0:T(8,128)(2,1)S(1)}, u32[]{:S(2)}, u32[]{:S(2)}) collective-permute-start(bf16[4,2,4,112,128]{4,3,2,1,0:T(8,128)(2,1)S(1)} %collective-permute-done.7.refs_1_), channel_id=1, source_target_pairs={{0,6},{1,3},{2,4},{3,1},{4,2},{5,7},{6,0},{7,5},{8,14},{9,11},{10,... | collective-permute-start | bytes 2752520 | tf_op jit(solution)/shard_map/ppermute | solution.py:355
  66.3 2.6 %collective-permute-done.17.refs_9_ = bf16[4,2,4,112,128]{4,3,2,1,0:T(8,128)(2,1)S(1)} collective-permute-done((bf16[4,2,4,112,128]{4,3,2,1,0:T(8,128)(2,1)S(1)}, bf16[4,2,4,112,128]{4,3,2,1,0:T(8,128)(2,1)S(1)}, u32[]{:S(2)}, u32[]{:S(2)}) %collective-permute-start.17) | collective-permute-done | bytes 917536 | tf_op jit(solution)/shard_map/ppermute | solution.py:355
  68.9 1.5 collective-permute-start.19
  70.4 0.5 collective-permute-start.21
  70.9 0.3 collective-permute-start.22
  71.2 7.3 %collective-permute-done.9.refs_3_ = bf16[4,2,4,112,128]{4,3,2,1,0:T(8,128)(2,1)S(1)} collective-permute-done((bf16[4,2,4,112,128]{4,3,2,1,0:T(8,128)(2,1)S(1)}, bf16[4,2,4,112,128]{4,3,2,1,0:T(8,128)(2,1)S(1)}, u32[]{:S(2)}, u32[]{:S(2)}) %collective-permute-start.9) | collective-permute-done | bytes 917536 | tf_op jit(solution)/shard_map/ppermute | solution.py:355
  78.5 3.8 %collective-permute-done.19.refs_11_ = bf16[4,2,4,112,128]{4,3,2,1,0:T(8,128)(2,1)S(1)} collective-permute-done((bf16[4,2,4,112,128]{4,3,2,1,0:T(8,128)(2,1)S(1)}, bf16[4,2,4,112,128]{4,3,2,1,0:T(8,128)(2,1)S(1)}, u32[]{:S(2)}, u32[]{:S(2)}) %collective-permute-start.19) | collective-permute-done | bytes 917536 | tf_op jit(solution)/shard_map/ppermute | solution.py:355
  82.3 2.4 %collective-permute-done.23.refs_15_ = bf16[4,2,4,112,128]{4,3,2,1,0:T(8,128)(2,1)S(1)} collective-permute-done((bf16[4,2,4,112,128]{4,3,2,1,0:T(8,128)(2,1)S(1)}, bf16[4,2,4,112,128]{4,3,2,1,0:T(8,128)(2,1)S(1)}, u32[]{:S(2)}, u32[]{:S(2)}) %collective-permute-start.23) | collective-permute-done | bytes 917536 | tf_op jit(solution)/shard_map/ppermute | solution.py:359
  84.8 23.3 %shard_map.93 = bf16[8,304,384]{2,1,0:T(8,128)(2,1)S(1)} custom-call(bf16[4,2,4,112,128]{4,3,2,1,0:T(8,128)(2,1)S(1)} %pad_maximum_fusion.refs_0_, bf16[4,2,4,112,128]{4,3,2,1,0:T(8,128)(2,1)S(1)} %collective-permute-done.7.refs_1_, bf16[4,2,4,112,128]{4,3,2,1,0:T(8,128)(2,1)S(1)} %collective-permute-done.8.refs_2_, ...), custom_call_target="tpu_custom_call" | custom-call | flops 8000000000 | bytes 30000000 | tf_op jit(solution)/shard_map/pallas_call | solution.py:409
  108.0 29.6 %all_to_all.5.got_ref = bf16[8,304,384]{2,1,0:T(8,128)(2,1)S(1)} all-to-all(bf16[8,304,384]{2,1,0:T(8,128)(2,1)S(1)} %shard_map.93), channel_id=1, replica_groups={{0,32,64,96,128,160,192,224},{1,57,65,121,129,185,193,249},{2,34,66,98,..., dimensions={0} | all-to-all | bytes 3735552 | tf_op jit(solution)/shard_map/all_to_all | solution.py:438
  137.6 3.4 %shard_map.94 = (bf16[4,4,112,256]{3,2,1,0:T(8,128)(2,1)S(1)}, bf16[4,4,112,256]{3,2,1,0:T(8,128)(2,1)S(1)}) custom-call(bf16[8,304,384]{2,1,0:T(8,128)(2,1)S(1)} %all_to_all.5.got_ref), custom_call_target="tpu_custom_call" | custom-call | flops 600000000 | bytes 4000000 | tf_op jit(solution)/shard_map/pallas_call | solution.py:442
  141.2 2.5 %collective-permute-done.24 = bf16[4,4,112,256]{3,2,1,0:T(8,128)(2,1)S(1)} collective-permute-done((bf16[4,4,112,256]{3,2,1,0:T(8,128)(2,1)S(1)}, bf16[4,4,112,256]{3,2,1,0:T(8,128)(2,1)S(1)}, u32[]{:S(2)}, u32[]{:S(2)}) %collective-permute-start.24) | collective-permute-done | bytes 917536 | tf_op jit(solution)/shard_map/ppermute | solution.py:359
  143.6 0.3 add_convert_fusion.1
  143.9 2.8 %collective-permute-start.25 = (bf16[2,4,112,256]{3,2,1,0:T(8,128)(2,1)S(1)}, bf16[2,4,112,256]{3,2,1,0:T(8,128)(2,1)S(1)}, u32[]{:S(2)}, u32[]{:S(2)}) collective-permute-start(bf16[2,4,112,256]{3,2,1,0:T(8,128)(2,1)S(1)} %get-tuple-element.17), channel_id=1, source_target_pairs={{0,2},{1,7},{2,0},{3,5},{4,6},{5,3},{6,4},{7,1},{8,10},{9,15},{10,... | collective-permute-start | bytes 1376264 | tf_op jit(solution)/shard_map/ppermute | solution.py:355
  146.7 6.5 %collective-permute-done.25 = bf16[2,4,112,256]{3,2,1,0:T(8,128)(2,1)S(1)} collective-permute-done((bf16[2,4,112,256]{3,2,1,0:T(8,128)(2,1)S(1)}, bf16[2,4,112,256]{3,2,1,0:T(8,128)(2,1)S(1)}, u32[]{:S(2)}, u32[]{:S(2)}) %collective-permute-start.25) | collective-permute-done | bytes 458784 | tf_op jit(solution)/shard_map/ppermute | solution.py:355
  153.2 2.5 %collective-permute-start.26 = (bf16[4,112,256]{2,1,0:T(8,128)(2,1)S(1)}, bf16[4,112,256]{2,1,0:T(8,128)(2,1)S(1)}, u32[]{:S(2)}, u32[]{:S(2)}) collective-permute-start(bf16[4,112,256]{2,1,0:T(8,128)(2,1)S(1)} %fusion.2), channel_id=1, source_target_pairs={{0,6},{1,3},{2,4},{3,1},{4,2},{5,7},{6,0},{7,5},{8,14},{9,11},{10,... | collective-permute-start | bytes 688136 | tf_op jit(solution)/shard_map/ppermute | solution.py:355
  155.6 4.8 %collective-permute-done.26 = bf16[4,112,256]{2,1,0:T(8,128)(2,1)S(1)} collective-permute-done((bf16[4,112,256]{2,1,0:T(8,128)(2,1)S(1)}, bf16[4,112,256]{2,1,0:T(8,128)(2,1)S(1)}, u32[]{:S(2)}, u32[]{:S(2)}) %collective-permute-start.26) | collective-permute-done | bytes 229408 | tf_op jit(solution)/shard_map/ppermute | solution.py:355
  160.6 3.0 %collective-permute-start.29 = (bf16[112,256]{1,0:T(8,128)(2,1)S(1)}, bf16[112,256]{1,0:T(8,128)(2,1)S(1)}, u32[]{:S(2)}, u32[]{:S(2)}) collective-permute-start(bf16[112,256]{1,0:T(8,128)(2,1)S(1)} %get-tuple-element.22), channel_id=1, source_target_pairs={{0,16},{8,24},{16,0},{24,8},{1,17},{9,25},{17,1},{25,9},{2,18},{10... | collective-permute-start | bytes 172040 | tf_op jit(solution)/shard_map/ppermute | solution.py:363
  163.6 3.6 %collective-permute-start.27 = (bf16[112,256]{1,0:T(8,128)(2,1)S(1)}, bf16[112,256]{1,0:T(8,128)(2,1)S(1)}, u32[]{:S(2)}, u32[]{:S(2)}) collective-permute-start(bf16[112,256]{1,0:T(8,128)(2,1)S(1)} %get-tuple-element.24), channel_id=1, source_target_pairs={{0,8},{1,25},{8,0},{9,17},{16,24},{17,9},{24,16},{25,1},{2,10},{3,... | collective-permute-start | bytes 172040 | tf_op jit(solution)/shard_map/ppermute | solution.py:355
  167.2 1.6 collective-permute-done.29.d_ref
  168.8 1.2 collective-permute-done.28.c_ref
  170.0 0.7 shard_map.95
  (38 shorter events, 1.0 us)
Async XLA Ops:
  1.6 11.5 %collective-permute-start.1 = (bf16[112,256]{1,0:T(8,128)(2,1)S(1)}, bf16[112,256]{1,0:T(8,128)(2,1)S(1)}, u32[]{:S(2)}, u32[]{:S(2)}) collective-permute-start(bf16[112,256]{1,0:T(8,128)(2,1)S(1)} %fusion.6), channel_id=1, source_target_pairs={{0,24},{1,9},{8,16},{9,1},{16,8},{17,25},{24,0},{25,17},{2,26},{3,... | collective-permute-start | bytes 172040 | tf_op jit(solution)/shard_map/ppermute | solution.py:355
  7.9 6.3 %collective-permute-start = (bf16[112,256]{1,0:T(8,128)(2,1)S(1)}, bf16[112,256]{1,0:T(8,128)(2,1)S(1)}, u32[]{:S(2)}, u32[]{:S(2)}) collective-permute-start(bf16[112,256]{1,0:T(8,128)(2,1)S(1)} %fusion.6), channel_id=1, source_target_pairs={{0,8},{1,25},{8,0},{9,17},{16,24},{17,9},{24,16},{25,1},{2,10},{3,... | collective-permute-start | bytes 172040 | tf_op jit(solution)/shard_map/ppermute | solution.py:355
  9.4 8.5 %collective-permute-start.2 = (bf16[112,256]{1,0:T(8,128)(2,1)S(1)}, bf16[112,256]{1,0:T(8,128)(2,1)S(1)}, u32[]{:S(2)}, u32[]{:S(2)}) collective-permute-start(bf16[112,256]{1,0:T(8,128)(2,1)S(1)} %fusion.6), channel_id=1, source_target_pairs={{0,16},{8,24},{16,0},{24,8},{1,17},{9,25},{17,1},{25,9},{2,18},{10... | collective-permute-start | bytes 172040 | tf_op jit(solution)/shard_map/ppermute | solution.py:363
  18.5 6.1 %collective-permute-start.3 = (bf16[4,112,256]{2,1,0:T(8,128)(2,1)S(1)}, bf16[4,112,256]{2,1,0:T(8,128)(2,1)S(1)}, u32[]{:S(2)}, u32[]{:S(2)}) collective-permute-start(bf16[4,112,256]{2,1,0:T(8,128)(2,1)S(1)} %broadcast_select_fusion), channel_id=1, source_target_pairs={{0,32},{1,57},{32,0},{33,9},{8,40},{9,33},{40,8},{41,17},{16,48},{... | collective-permute-start | bytes 688136 | tf_op jit(solution)/shard_map/ppermute | solution.py:399
  24.9 59.9 %copy-start = (bf16[2,3,32,3072]{3,2,1,0:T(8,128)(2,1)S(1)}, bf16[2,3,32,3072]{3,2,1,0:T(8,128)(2,1)}, u32[]{:S(2)}) copy-start(bf16[2,3,32,3072]{3,2,1,0:T(8,128)(2,1)} %refs_16_.1) | copy-start | bytes 3538948
  24.9 59.9 %copy-start.1 = (bf16[2,3,32,3072]{3,2,1,0:T(8,128)(2,1)S(1)}, bf16[2,3,32,3072]{3,2,1,0:T(8,128)(2,1)}, u32[]{:S(2)}) copy-start(bf16[2,3,32,3072]{3,2,1,0:T(8,128)(2,1)} %refs_17_.1) | copy-start | bytes 3538948
  24.9 11.2 %collective-permute-start.5 = (bf16[2,4,112,128]{3,2,1,0:T(8,128)(2,1)S(1)}, bf16[2,4,112,128]{3,2,1,0:T(8,128)(2,1)S(1)}, u32[]{:S(2)}, u32[]{:S(2)}) collective-permute-start(bf16[2,4,112,128]{3,2,1,0:T(8,128)(2,1)S(1)} %get-tuple-element.21), channel_id=1, source_target_pairs={{0,192},{1,65},{64,128},{65,1},{128,64},{129,193},{192,0},{193,129... | collective-permute-start | bytes 688136 | tf_op jit(solution)/shard_map/ppermute | solution.py:355
  26.5 12.8 %collective-permute-start.4 = (bf16[2,4,112,128]{3,2,1,0:T(8,128)(2,1)S(1)}, bf16[2,4,112,128]{3,2,1,0:T(8,128)(2,1)S(1)}, u32[]{:S(2)}, u32[]{:S(2)}) collective-permute-start(bf16[2,4,112,128]{3,2,1,0:T(8,128)(2,1)S(1)} %get-tuple-element.21), channel_id=1, source_target_pairs={{0,64},{1,193},{64,0},{65,129},{128,192},{129,65},{192,128},{193,1... | collective-permute-start | bytes 688136 | tf_op jit(solution)/shard_map/ppermute | solution.py:355
  28.3 11.0 %collective-permute-start.6 = (bf16[2,4,112,128]{3,2,1,0:T(8,128)(2,1)S(1)}, bf16[2,4,112,128]{3,2,1,0:T(8,128)(2,1)S(1)}, u32[]{:S(2)}, u32[]{:S(2)}) collective-permute-start(bf16[2,4,112,128]{3,2,1,0:T(8,128)(2,1)S(1)} %get-tuple-element.21), channel_id=1, source_target_pairs={{0,128},{64,192},{128,0},{192,64},{1,129},{65,193},{129,1},{193,65... | collective-permute-start | bytes 688136 | tf_op jit(solution)/shard_map/ppermute | solution.py:363
  28.5 12.2 %collective-permute-start.15 = (bf16[2,4,112,128]{3,2,1,0:T(8,128)(2,1)S(1)}, bf16[2,4,112,128]{3,2,1,0:T(8,128)(2,1)S(1)}, u32[]{:S(2)}, u32[]{:S(2)}) collective-permute-start(bf16[2,4,112,128]{3,2,1,0:T(8,128)(2,1)S(1)} %get-tuple-element.20), channel_id=1, source_target_pairs={{0,6},{1,3},{2,4},{3,1},{4,2},{5,7},{6,0},{7,5},{8,14},{9,11},{10,... | collective-permute-start | bytes 688136 | tf_op jit(solution)/shard_map/ppermute | solution.py:355
  31.5 9.3 %collective-permute-start.14 = (bf16[2,4,112,128]{3,2,1,0:T(8,128)(2,1)S(1)}, bf16[2,4,112,128]{3,2,1,0:T(8,128)(2,1)S(1)}, u32[]{:S(2)}, u32[]{:S(2)}) collective-permute-start(bf16[2,4,112,128]{3,2,1,0:T(8,128)(2,1)S(1)} %get-tuple-element.20), channel_id=1, source_target_pairs={{0,2},{1,7},{2,0},{3,5},{4,6},{5,3},{6,4},{7,1},{8,10},{9,15},{10,... | collective-permute-start | bytes 688136 | tf_op jit(solution)/shard_map/ppermute | solution.py:355
  36.1 8.8 %collective-permute-start.16 = (bf16[2,4,112,128]{3,2,1,0:T(8,128)(2,1)S(1)}, bf16[2,4,112,128]{3,2,1,0:T(8,128)(2,1)S(1)}, u32[]{:S(2)}, u32[]{:S(2)}) collective-permute-start(bf16[2,4,112,128]{3,2,1,0:T(8,128)(2,1)S(1)} %get-tuple-element.20), channel_id=1, source_target_pairs={{0,4},{2,6},{4,0},{6,2},{1,5},{3,7},{5,1},{7,3},{8,12},{10,14},{12... | collective-permute-start | bytes 688136 | tf_op jit(solution)/shard_map/ppermute | solution.py:363
  39.4 8.8 %collective-permute-start.10 = (bf16[4,2,4,112,128]{4,3,2,1,0:T(8,128)(2,1)S(1)}, bf16[4,2,4,112,128]{4,3,2,1,0:T(8,128)(2,1)S(1)}, u32[]{:S(2)}, u32[]{:S(2)}) collective-permute-start(bf16[4,2,4,112,128]{4,3,2,1,0:T(8,128)(2,1)S(1)} %pad_maximum_fusion.refs_0_), channel_id=1, source_target_pairs={{0,1},{1,0},{2,3},{3,2},{4,5},{5,4},{6,7},{7,6},{8,9},{9,8},{10,11... | collective-permute-start | bytes 2752520 | tf_op jit(solution)/shard_map/ppermute | solution.py:359
  39.5 24.4 %collective-permute-start.8 = (bf16[4,2,4,112,128]{4,3,2,1,0:T(8,128)(2,1)S(1)}, bf16[4,2,4,112,128]{4,3,2,1,0:T(8,128)(2,1)S(1)}, u32[]{:S(2)}, u32[]{:S(2)}) collective-permute-start(bf16[4,2,4,112,128]{4,3,2,1,0:T(8,128)(2,1)S(1)} %pad_maximum_fusion.refs_0_), channel_id=1, source_target_pairs={{0,6},{1,3},{2,4},{3,1},{4,2},{5,7},{6,0},{7,5},{8,14},{9,11},{10,... | collective-permute-start | bytes 2752520 | tf_op jit(solution)/shard_map/ppermute | solution.py:355
  40.7 23.2 %collective-permute-start.7 = (bf16[4,2,4,112,128]{4,3,2,1,0:T(8,128)(2,1)S(1)}, bf16[4,2,4,112,128]{4,3,2,1,0:T(8,128)(2,1)S(1)}, u32[]{:S(2)}, u32[]{:S(2)}) collective-permute-start(bf16[4,2,4,112,128]{4,3,2,1,0:T(8,128)(2,1)S(1)} %pad_maximum_fusion.refs_0_), channel_id=1, source_target_pairs={{0,2},{1,7},{2,0},{3,5},{4,6},{5,3},{6,4},{7,1},{8,10},{9,15},{10,... | collective-permute-start | bytes 2752520 | tf_op jit(solution)/shard_map/ppermute | solution.py:355
  45.1 23.9 %collective-permute-start.17 = (bf16[4,2,4,112,128]{4,3,2,1,0:T(8,128)(2,1)S(1)}, bf16[4,2,4,112,128]{4,3,2,1,0:T(8,128)(2,1)S(1)}, u32[]{:S(2)}, u32[]{:S(2)}) collective-permute-start(bf16[4,2,4,112,128]{4,3,2,1,0:T(8,128)(2,1)S(1)} %pad_maximum_fusion.1.refs_8_), channel_id=1, source_target_pairs={{0,64},{1,193},{64,0},{65,129},{128,192},{129,65},{192,128},{193,1... | collective-permute-start | bytes 2752520 | tf_op jit(solution)/shard_map/ppermute | solution.py:355
  48.2 22.2 %collective-permute-start.20 = (bf16[4,2,4,112,128]{4,3,2,1,0:T(8,128)(2,1)S(1)}, bf16[4,2,4,112,128]{4,3,2,1,0:T(8,128)(2,1)S(1)}, u32[]{:S(2)}, u32[]{:S(2)}) collective-permute-start(bf16[4,2,4,112,128]{4,3,2,1,0:T(8,128)(2,1)S(1)} %pad_maximum_fusion.1.refs_8_), channel_id=1, source_target_pairs={{0,1},{1,0},{2,3},{3,2},{4,5},{5,4},{6,7},{7,6},{8,9},{9,8},{10,11... | collective-permute-start | bytes 2752520 | tf_op jit(solution)/shard_map/ppermute | solution.py:359
  48.2 22.2 %collective-permute-start.18 = (bf16[4,2,4,112,128]{4,3,2,1,0:T(8,128)(2,1)S(1)}, bf16[4,2,4,112,128]{4,3,2,1,0:T(8,128)(2,1)S(1)}, u32[]{:S(2)}, u32[]{:S(2)}) collective-permute-start(bf16[4,2,4,112,128]{4,3,2,1,0:T(8,128)(2,1)S(1)} %pad_maximum_fusion.1.refs_8_), channel_id=1, source_target_pairs={{0,192},{1,65},{64,128},{65,1},{128,64},{129,193},{192,0},{193,129... | collective-permute-start | bytes 2752520 | tf_op jit(solution)/shard_map/ppermute | solution.py:355
  63.9 7.0 %collective-permute-start.12 = (bf16[4,2,4,112,128]{4,3,2,1,0:T(8,128)(2,1)S(1)}, bf16[4,2,4,112,128]{4,3,2,1,0:T(8,128)(2,1)S(1)}, u32[]{:S(2)}, u32[]{:S(2)}) collective-permute-start(bf16[4,2,4,112,128]{4,3,2,1,0:T(8,128)(2,1)S(1)} %collective-permute-done.8.refs_2_), channel_id=1, source_target_pairs={{0,1},{1,0},{2,3},{3,2},{4,5},{5,4},{6,7},{7,6},{8,9},{9,8},{10,11... | collective-permute-start | bytes 2752520 | tf_op jit(solution)/shard_map/ppermute | solution.py:359
  63.9 14.6 %collective-permute-start.9 = (bf16[4,2,4,112,128]{4,3,2,1,0:T(8,128)(2,1)S(1)}, bf16[4,2,4,112,128]{4,3,2,1,0:T(8,128)(2,1)S(1)}, u32[]{:S(2)}, u32[]{:S(2)}) collective-permute-start(bf16[4,2,4,112,128]{4,3,2,1,0:T(8,128)(2,1)S(1)} %collective-permute-done.7.refs_1_), channel_id=1, source_target_pairs={{0,6},{1,3},{2,4},{3,1},{4,2},{5,7},{6,0},{7,5},{8,14},{9,11},{10,... | collective-permute-start | bytes 2752520 | tf_op jit(solution)/shard_map/ppermute | solution.py:355
  68.9 13.4 %collective-permute-start.19 = (bf16[4,2,4,112,128]{4,3,2,1,0:T(8,128)(2,1)S(1)}, bf16[4,2,4,112,128]{4,3,2,1,0:T(8,128)(2,1)S(1)}, u32[]{:S(2)}, u32[]{:S(2)}) collective-permute-start(bf16[4,2,4,112,128]{4,3,2,1,0:T(8,128)(2,1)S(1)} %collective-permute-done.17.refs_9_), channel_id=1, source_target_pairs={{0,192},{1,65},{64,128},{65,1},{128,64},{129,193},{192,0},{193,129... | collective-permute-start | bytes 2752520 | tf_op jit(solution)/shard_map/ppermute | solution.py:355
  70.4 11.9 %collective-permute-start.11 = (bf16[4,2,4,112,128]{4,3,2,1,0:T(8,128)(2,1)S(1)}, bf16[4,2,4,112,128]{4,3,2,1,0:T(8,128)(2,1)S(1)}, u32[]{:S(2)}, u32[]{:S(2)}) collective-permute-start(bf16[4,2,4,112,128]{4,3,2,1,0:T(8,128)(2,1)S(1)} %collective-permute-done.7.refs_1_), channel_id=1, source_target_pairs={{0,1},{1,0},{2,3},{3,2},{4,5},{5,4},{6,7},{7,6},{8,9},{9,8},{10,11... | collective-permute-start | bytes 2752520 | tf_op jit(solution)/shard_map/ppermute | solution.py:359
  70.4 11.9 %collective-permute-start.21 = (bf16[4,2,4,112,128]{4,3,2,1,0:T(8,128)(2,1)S(1)}, bf16[4,2,4,112,128]{4,3,2,1,0:T(8,128)(2,1)S(1)}, u32[]{:S(2)}, u32[]{:S(2)}) collective-permute-start(bf16[4,2,4,112,128]{4,3,2,1,0:T(8,128)(2,1)S(1)} %collective-permute-done.17.refs_9_), channel_id=1, source_target_pairs={{0,1},{1,0},{2,3},{3,2},{4,5},{5,4},{6,7},{7,6},{8,9},{9,8},{10,11... | collective-permute-start | bytes 2752520 | tf_op jit(solution)/shard_map/ppermute | solution.py:359
  70.9 11.4 %collective-permute-start.22 = (bf16[4,2,4,112,128]{4,3,2,1,0:T(8,128)(2,1)S(1)}, bf16[4,2,4,112,128]{4,3,2,1,0:T(8,128)(2,1)S(1)}, u32[]{:S(2)}, u32[]{:S(2)}) collective-permute-start(bf16[4,2,4,112,128]{4,3,2,1,0:T(8,128)(2,1)S(1)} %collective-permute-done.18.refs_10_), channel_id=1, source_target_pairs={{0,1},{1,0},{2,3},{3,2},{4,5},{5,4},{6,7},{7,6},{8,9},{9,8},{10,11... | collective-permute-start | bytes 2752520 | tf_op jit(solution)/shard_map/ppermute | solution.py:359
  78.5 3.8 %collective-permute-start.13 = (bf16[4,2,4,112,128]{4,3,2,1,0:T(8,128)(2,1)S(1)}, bf16[4,2,4,112,128]{4,3,2,1,0:T(8,128)(2,1)S(1)}, u32[]{:S(2)}, u32[]{:S(2)}) collective-permute-start(bf16[4,2,4,112,128]{4,3,2,1,0:T(8,128)(2,1)S(1)} %collective-permute-done.9.refs_3_), channel_id=1, source_target_pairs={{0,1},{1,0},{2,3},{3,2},{4,5},{5,4},{6,7},{7,6},{8,9},{9,8},{10,11... | collective-permute-start | bytes 2752520 | tf_op jit(solution)/shard_map/ppermute | solution.py:359
  82.3 2.5 %collective-permute-start.23 = (bf16[4,2,4,112,128]{4,3,2,1,0:T(8,128)(2,1)S(1)}, bf16[4,2,4,112,128]{4,3,2,1,0:T(8,128)(2,1)S(1)}, u32[]{:S(2)}, u32[]{:S(2)}) collective-permute-start(bf16[4,2,4,112,128]{4,3,2,1,0:T(8,128)(2,1)S(1)} %collective-permute-done.19.refs_11_), channel_id=1, source_target_pairs={{0,1},{1,0},{2,3},{3,2},{4,5},{5,4},{6,7},{7,6},{8,9},{9,8},{10,11... | collective-permute-start | bytes 2752520 | tf_op jit(solution)/shard_map/ppermute | solution.py:359
  141.1 2.6 %collective-permute-start.24 = (bf16[4,4,112,256]{3,2,1,0:T(8,128)(2,1)S(1)}, bf16[4,4,112,256]{3,2,1,0:T(8,128)(2,1)S(1)}, u32[]{:S(2)}, u32[]{:S(2)}) collective-permute-start(bf16[4,4,112,256]{3,2,1,0:T(8,128)(2,1)S(1)} %get-tuple-element.11), channel_id=1, source_target_pairs={{0,1},{1,0},{2,3},{3,2},{4,5},{5,4},{6,7},{7,6},{8,9},{9,8},{10,11... | collective-permute-start | bytes 2752520 | tf_op jit(solution)/shard_map/ppermute | solution.py:359
  143.9 9.2 %collective-permute-start.25 = (bf16[2,4,112,256]{3,2,1,0:T(8,128)(2,1)S(1)}, bf16[2,4,112,256]{3,2,1,0:T(8,128)(2,1)S(1)}, u32[]{:S(2)}, u32[]{:S(2)}) collective-permute-start(bf16[2,4,112,256]{3,2,1,0:T(8,128)(2,1)S(1)} %get-tuple-element.17), channel_id=1, source_target_pairs={{0,2},{1,7},{2,0},{3,5},{4,6},{5,3},{6,4},{7,1},{8,10},{9,15},{10,... | collective-permute-start | bytes 1376264 | tf_op jit(solution)/shard_map/ppermute | solution.py:355
  153.2 7.3 %collective-permute-start.26 = (bf16[4,112,256]{2,1,0:T(8,128)(2,1)S(1)}, bf16[4,112,256]{2,1,0:T(8,128)(2,1)S(1)}, u32[]{:S(2)}, u32[]{:S(2)}) collective-permute-start(bf16[4,112,256]{2,1,0:T(8,128)(2,1)S(1)} %fusion.2), channel_id=1, source_target_pairs={{0,6},{1,3},{2,4},{3,1},{4,2},{5,7},{6,0},{7,5},{8,14},{9,11},{10,... | collective-permute-start | bytes 688136 | tf_op jit(solution)/shard_map/ppermute | solution.py:355
  160.6 8.2 %collective-permute-start.29 = (bf16[112,256]{1,0:T(8,128)(2,1)S(1)}, bf16[112,256]{1,0:T(8,128)(2,1)S(1)}, u32[]{:S(2)}, u32[]{:S(2)}) collective-permute-start(bf16[112,256]{1,0:T(8,128)(2,1)S(1)} %get-tuple-element.22), channel_id=1, source_target_pairs={{0,16},{8,24},{16,0},{24,8},{1,17},{9,25},{17,1},{25,9},{2,18},{10... | collective-permute-start | bytes 172040 | tf_op jit(solution)/shard_map/ppermute | solution.py:363
  163.6 6.4 %collective-permute-start.28 = (bf16[112,256]{1,0:T(8,128)(2,1)S(1)}, bf16[112,256]{1,0:T(8,128)(2,1)S(1)}, u32[]{:S(2)}, u32[]{:S(2)}) collective-permute-start(bf16[112,256]{1,0:T(8,128)(2,1)S(1)} %get-tuple-element.23), channel_id=1, source_target_pairs={{0,24},{1,9},{8,16},{9,1},{16,8},{17,25},{24,0},{25,17},{2,26},{3,... | collective-permute-start | bytes 172040 | tf_op jit(solution)/shard_map/ppermute | solution.py:355
  163.6 6.4 %collective-permute-start.27 = (bf16[112,256]{1,0:T(8,128)(2,1)S(1)}, bf16[112,256]{1,0:T(8,128)(2,1)S(1)}, u32[]{:S(2)}, u32[]{:S(2)}) collective-permute-start(bf16[112,256]{1,0:T(8,128)(2,1)S(1)} %get-tuple-element.24), channel_id=1, source_target_pairs={{0,8},{1,25},{8,0},{9,17},{16,24},{17,9},{24,16},{25,1},{2,10},{3,... | collective-permute-start | bytes 172040 | tf_op jit(solution)/shard_map/ppermute | solution.py:355
